TPU v7x, 512 devices: a whole 4x4x16 slice. The times are simulated.
512 devices in a mesh: phase: 8 (over y, core), tensor: 16 (over x, z_lo), seq: 4 (over z_hi).
Axes of the slice: x: 4, y: 4, z: 16 (z_hi: 4, z_lo: 4; z = z_hi * 4 + z_lo), core: 2. Of those that a mesh axis runs over, the one named last changes fastest.
Arguments:
- hidden: bfloat16 [8, 512, 8192], P('phase', 'seq', 'tensor'), may hold values from -52 to 52
- segment_ids: int32 [8, 512], P('phase', 'seq'), may hold values from 0 to 1, never falling along the last dimension, each value on 1 to 320 neighbouring positions
- gain_attn: bfloat16 [8, 8192], P('phase', 'tensor'), may hold values from 0.5 to 1.5
- gain_ffn: bfloat16 [8, 8192], P('phase', 'tensor'), may hold values from 0.5 to 1.5
- w_query: bfloat16 [8, 8192, 8192], P('phase', 'seq', 'tensor'), may hold values from -2 to 2
- w_key: bfloat16 [8, 8192, 1024], P('phase', 'seq', 'tensor'), may hold values from -2 to 2
- w_value: bfloat16 [8, 8192, 1024], P('phase', 'seq', 'tensor'), may hold values from -0.0625 to 0.0625
Outputs:
- passed: bfloat16 [8, 512, 8192], P('phase', 'seq', 'tensor')
- hessians: bfloat16 [8, 8192, 8192], P('phase', 'tensor', 'seq')
- ffn_diagonal: float32 [8, 8192], P('phase', ('tensor', 'seq'))
Inputs may be any that keep to these rules, and one draw needn't show every extreme that they name: `segment_ids`: in each section the tokens form two contiguous documents, document 0 first, each holding at least one token.
All inputs are finite; a program needn't handle non-finite values.
Results may differ from a plain program's by a relative error of at most 0.017.
Values may be sent and summed in bfloat16 or wider, within the bound.
No kernel may reach another device: no remote copies, remote signals or barrier semaphores. Data moves between devices by JAX's collectives and lax.ppermute only.
A program may use at most 64 MiB of HBM per device.

v0:
```python
import jax
import jax.numpy as jnp
from jax import lax
from jax.sharding import PartitionSpec as P

D = 8192
HD = 128


norm_eps = 1e-05
rope_base = 500000.0


def swapped(value, axis, distance):
    mask = 2**distance
    pairs = [(source, source ^ mask) for source in range(lax.axis_size(axis))]
    return lax.ppermute(value, axis, pairs)


def from_behind(value, axis, steps):
    count = lax.axis_size(axis)
    pairs = [(source, (source + steps) % count) for source in range(count)]
    return lax.ppermute(value, axis, pairs)


def scale_rows(values, total_sq, gain):
    return (values * lax.rsqrt(total_sq / D + norm_eps) * gain.astype(jnp.float32)).astype(
        jnp.bfloat16
    )


def rotate_pairs(values, positions):
    half_dim = values.shape[-1] // 2
    freq = rope_base ** (-(jnp.arange(half_dim, dtype=jnp.float32) * 2.0 / values.shape[-1]))
    angle = positions[:, None] * freq[None, :]
    cosine = jnp.cos(angle)[:, None, :]
    sine = jnp.sin(angle)[:, None, :]
    first = values[..., :half_dim]
    second = values[..., half_dim:]
    return jnp.concatenate(
        [first * cosine - second * sine, second * cosine + first * sine], axis=-1
    )


def on_device(hidden, segment_ids, gain_attn, gain_ffn, w_query, w_key, w_value):
    seq_count = lax.axis_size("seq")
    tensor_pos = lax.axis_index("tensor")
    seq_pos = lax.axis_index("seq")
    tok_rows = hidden.shape[1]
    feat_shard = hidden.shape[2]
    all_tokens = tok_rows * seq_count
    resid = hidden[0].astype(jnp.float32)
    attn_sq = lax.psum(jnp.sum(resid * resid, axis=1), "tensor")
    normed_attn = scale_rows(resid, attn_sq[:, None], gain_attn[0][None, :])
    attn_whole = lax.all_gather(normed_attn, "tensor", axis=1, tiled=True)
    attn_columns = lax.all_to_all(attn_whole, "seq", split_axis=1, concat_axis=0, tiled=True)
    query_cols = w_query.shape[2]
    pieces = (
        lax.all_gather(w_query[0], "seq", axis=0, tiled=True),
        lax.all_gather(w_key[0], "seq", axis=0, tiled=True),
        lax.all_gather(w_value[0], "seq", axis=0, tiled=True),
    )
    query, key_part, value_part = tuple(
        (jnp.dot(attn_whole, piece, preferred_element_type=jnp.float32) for piece in pieces)
    )
    key_other, value_other = swapped((key_part, value_part), "tensor", 0)
    lower_half = tensor_pos % 2 == 0
    key_head = jnp.where(
        lower_half,
        jnp.concatenate([key_part, key_other], 1),
        jnp.concatenate([key_other, key_part], 1),
    )
    value_head = jnp.where(
        lower_half,
        jnp.concatenate([value_part, value_other], 1),
        jnp.concatenate([value_other, value_part], 1),
    )
    kv_local = 1
    group_local = query_cols // HD // kv_local
    own_ids = seq_pos * tok_rows + jnp.arange(tok_rows, dtype=jnp.int32)
    positions = own_ids.astype(jnp.float32)
    query = rotate_pairs(query.reshape(tok_rows, kv_local * group_local, HD), positions)
    query = query.reshape(tok_rows, kv_local, group_local, HD)
    key_head = rotate_pairs(key_head.reshape(tok_rows, kv_local, HD), positions)
    value_head = value_head.reshape(tok_rows, kv_local, HD)
    own_docs = segment_ids[0].astype(jnp.float32)
    inv_root = 1.0 / jnp.sqrt(jnp.float32(HD))
    keys = lax.all_gather(key_head, "seq", axis=0, tiled=True)
    values = lax.all_gather(value_head, "seq", axis=0, tiled=True)
    docs = lax.all_gather(own_docs, "seq", axis=0, tiled=True)
    key_ids = jnp.arange(keys.shape[0], dtype=jnp.int32)
    allowed = (key_ids[None, :] <= own_ids[:, None]) & (docs[None, :] == own_docs[:, None])
    allowed = allowed[:, None, None, :]
    scores = jnp.einsum("rkgd,nkd->rkgn", query, keys, precision=lax.Precision.HIGHEST) * inv_root
    scores = jnp.where(allowed, scores, jnp.float32(-1e30))
    peak = jnp.full((tok_rows, kv_local, group_local), -1e30, jnp.float32)
    new_peak = jnp.maximum(peak, jnp.max(scores, axis=-1))
    weights = jnp.where(allowed, jnp.exp(scores - new_peak[..., None]), jnp.float32(0.0))
    accum = jnp.einsum("rkgn,nkd->rkgd", weights, values, precision=lax.Precision.HIGHEST)
    peak, total, accum = (new_peak, jnp.sum(weights, axis=-1), accum)
    context = (accum / total[..., None]).reshape(tok_rows, query_cols)
    section_out = (resid + context).astype(jnp.bfloat16)
    passed = from_behind(section_out, "phase", 1)[None]
    out_float = section_out.astype(jnp.float32)
    ffn_sq = lax.psum(jnp.sum(out_float * out_float, axis=1), "tensor")
    normed_ffn = scale_rows(out_float, ffn_sq[:, None], gain_ffn[0][None, :])
    ffn_whole = lax.all_gather(normed_ffn, "tensor", axis=1, tiled=True)
    ffn_columns = lax.all_to_all(ffn_whole, "seq", split_axis=1, concat_axis=0, tiled=True)
    attn_rows, ffn_rows = (
        lax.all_gather(normed_attn, "seq", axis=0, tiled=True),
        lax.all_gather(normed_ffn, "seq", axis=0, tiled=True),
    )
    contract = (((0,), (0,)), ((), ()))
    scale = 2.0 / all_tokens
    upper_part = (
        lax.dot_general(attn_rows, attn_columns, contract, preferred_element_type=jnp.float32)
        * scale
    )
    lower_part = (
        lax.dot_general(ffn_rows, ffn_columns, contract, preferred_element_type=jnp.float32) * scale
    )
    col_width = attn_columns.shape[1]
    row_ids = tensor_pos * feat_shard + jnp.arange(feat_shard, dtype=jnp.int32)
    col_ids = seq_pos * col_width + jnp.arange(col_width, dtype=jnp.int32)
    hessians = jnp.where(row_ids[:, None] <= col_ids[None, :], upper_part, lower_part).astype(
        jnp.bfloat16
    )[None]
    diag_width = feat_shard // seq_count
    own_cols = lax.dynamic_slice_in_dim(ffn_rows, seq_pos * diag_width, diag_width, 1).astype(
        jnp.float32
    )
    ffn_diagonal = (jnp.sum(own_cols * own_cols, axis=0) * scale)[None]
    return (passed, hessians, ffn_diagonal)


def solution(mesh):
    return jax.shard_map(
        on_device,
        mesh=mesh,
        in_specs=(
            P("phase", "seq", "tensor"),
            P("phase", "seq"),
            P("phase", "tensor"),
            P("phase", "tensor"),
            P("phase", "seq", "tensor"),
            P("phase", "seq", "tensor"),
            P("phase", "seq", "tensor"),
        ),
        out_specs=(
            P("phase", "seq", "tensor"),
            P("phase", "tensor", "seq"),
            P("phase", ("tensor", "seq")),
        ),
        check_vma=False,
    )
```

profile of v0, /device:TPU:1, one launch (start us, length us, event | category | flops | bytes accessed | tf_op | source)
XLA Modules:
  0.0 963.2 jit_solution(4333614558954208742)
XLA Ops:
  9.8 43.8 %psum.14 = f32[128]{0:T(128)S(1)} all-reduce(f32[128]{0:T(128)S(1)} %fusion.22), channel_id=1, replica_groups=mesh['phase'=8,'tensor'=16,'seq'=4] {'tensor'}, use_global_device_ids=true, to_apply=%region_1.0 | all-reduce | flops 128 | bytes 1024 | tf_op jit(solution)/shard_map/psum | solution.py:53
  55.8 21.8 %all-gather.1 = f32[1,512]{1,0:T(1,128)S(1)} all-gather(f32[1,128]{1,0:T(1,128)S(1)} %get-tuple-element.16), channel_id=3, replica_groups=mesh['phase'=8,'tensor'=16,'seq'=4] {'seq'}, dimensions={1}, use_global_device_ids=true | all-gather | bytes 2560 | tf_op jit(solution)/shard_map/all_gather | solution.py:90
  78.1 82.5 %all-gather.10.cloned.1.call-done = bf16[128,8192]{0,1:T(8,128)(2,1)} async-done(((bf16[128,512]{0,1:T(8,128)(2,1)}), bf16[128,8192]{0,1:T(8,128)(2,1)}) %all-gather.10.cloned.1.call-update) | async-done | bytes 2097168 | tf_op jit(solution)/shard_map/all_gather | solution.py:55
  160.6 2.4 fusion.7
  163.0 1.9 collective-permute-start.1
  164.9 66.8 %all-gather.14.cloned.1.call-done = bf16[1,8192,64]{1,2,0:T(8,128)(2,1)} async-done(((bf16[1,2048,64]{1,2,0:T(8,128)(2,1)}), bf16[1,8192,64]{1,2,0:T(8,128)(2,1)}) %all-gather.14.cloned.1.call-update) | async-done | bytes 1048592 | tf_op jit(solution)/shard_map/all_gather | solution.py:61
  231.7 2.4 fusion.9
  234.1 1.9 collective-permute-start
  236.0 4.4 all-to-all-start
  240.7 78.2 %all_gather.35 = f32[512,1,128]{0,2,1:T(8,128)S(1)} all-gather(f32[128,1,128]{0,2,1:T(8,128)S(1)} %pad_maximum_fusion), channel_id=1, replica_groups=mesh['phase'=8,'tensor'=16,'seq'=4] {'seq'}, dimensions={0}, use_global_device_ids=true | all-gather | bytes 327680 | tf_op jit(solution)/shard_map/all_gather | solution.py:88
  319.0 24.4 %all_gather.32 = f32[512,1,128]{0,2,1:T(8,128)S(1)} all-gather(f32[128,1,128]{0,2,1:T(8,128)S(1)} %maximum_select_fusion), channel_id=1, replica_groups=mesh['phase'=8,'tensor'=16,'seq'=4] {'seq'}, dimensions={0}, use_global_device_ids=true | all-gather | bytes 327680 | tf_op jit(solution)/shard_map/all_gather | solution.py:89
  343.4 128.6 %all-gather.18.cloned.1.call-done = bf16[1,8192,512]{2,1,0:T(8,128)(2,1)} async-done(((bf16[1,2048,512]{2,1,0:T(8,128)(2,1)}), bf16[1,8192,512]{2,1,0:T(8,128)(2,1)}) %all-gather.18.cloned.1.call-update) | async-done | bytes 8388624 | tf_op jit(solution)/shard_map/all_gather | solution.py:59
  472.0 5.3 fusion
  477.7 1.2 fusion.38
  480.0 199.6 %psum.15 = f32[128]{0:T(128)S(1)} all-reduce(f32[128]{0:T(128)S(1)} %get-tuple-element.20), channel_id=1, replica_groups=mesh['phase'=8,'tensor'=16,'seq'=4] {'tensor'}, use_global_device_ids=true, to_apply=%region_5.6 | all-reduce | flops 128 | bytes 1024 | tf_op jit(solution)/shard_map/psum | solution.py:105
  680.4 86.6 %all-gather.12.cloned.1.call-done = bf16[128,8192]{0,1:T(8,128)(2,1)} async-done(((bf16[128,512]{0,1:T(8,128)(2,1)}), bf16[128,8192]{0,1:T(8,128)(2,1)}) %all-gather.12.cloned.1.call-update) | async-done | bytes 2097168 | tf_op jit(solution)/shard_map/all_gather | solution.py:107
  767.0 9.8 %all-to-all-start.1 = ((bf16[128,4,2048]{0,2,1:T(8,128)(2,1)}), bf16[128,4,2048]{0,2,1:T(8,128)(2,1)}, u32[]{:S(2)}, u32[]{:S(2)}) async-start(bf16[128,4,2048]{0,2,1:T(8,128)(2,1)} %bitcast.91), calls=%async_computation.1 | async-start | bytes 4194304 | tf_op jit(solution)/shard_map/all_to_all | solution.py:108
  776.9 111.4 %all_gather.37 = bf16[512,512]{0,1:T(8,128)(2,1)S(1)} all-gather(bf16[128,512]{0,1:T(8,128)(2,1)S(1)} %copy-done), channel_id=1, replica_groups=mesh['phase'=8,'tensor'=16,'seq'=4] {'seq'}, dimensions={0}, use_global_device_ids=true | all-gather | bytes 655360 | tf_op jit(solution)/shard_map/all_gather | solution.py:110
  888.3 2.6 copy.27
  890.9 4.8 fusion.39
  895.7 18.1 %collective-permute-start.2 = (bf16[128,512]{0,1:T(8,128)(2,1)S(1)}, bf16[128,512]{0,1:T(8,128)(2,1)S(1)}, u32[]{:S(2)}, u32[]{:S(2)}) collective-permute-start(bf16[128,512]{0,1:T(8,128)(2,1)S(1)} %get-tuple-element.7), channel_id=1, source_target_pairs={{0,64},{64,128},{128,192},{192,256},{256,320},{320,384},{384,448},... | collective-permute-start | bytes 393224 | tf_op jit(solution)/shard_map/ppermute | solution.py:23
  913.9 33.5 %all_gather.38 = bf16[512,512]{0,1:T(8,128)(2,1)S(1)} all-gather(bf16[128,512]{0,1:T(8,128)(2,1)S(1)} %copy-done.1), channel_id=1, replica_groups=mesh['phase'=8,'tensor'=16,'seq'=4] {'seq'}, dimensions={0}, use_global_device_ids=true | all-gather | bytes 655360 | tf_op jit(solution)/shard_map/all_gather | solution.py:111
  948.8 2.9 copy.28
  951.8 4.9 fusion.2
  (53 shorter events, 9.1 us)
Async XLA Ops:
  7.2 48.6 %copy-start.2 = (bf16[1,512]{1,0:T(2,128)(2,1)S(1)}, bf16[1,512]{1,0:T(2,128)(2,1)}, u32[]{:S(2)}) copy-start(bf16[1,512]{1,0:T(2,128)(2,1)} %param.10) | copy-start | bytes 3076
  7.2 48.6 %copy-start.3 = (s32[1,128]{1,0:T(1,128)S(1)}, s32[1,128]{1,0:T(1,128)}, u32[]{:S(2)}) copy-start(s32[1,128]{1,0:T(1,128)} %param.8) | copy-start | bytes 1540
  7.2 70.9 %all-gather.16.cloned.1.call-start = ((), (), s32[]{:S(2)}) async-start(), calls=%async_computation.5 | async-start | bytes 1310720 | tf_op jit(solution)/shard_map/all_gather | solution.py:60
  7.9 152.7 %all-gather.10.cloned.1.call-start = ((), (), s32[]{:S(2)}) async-start(), calls=%async_computation.2 | async-start | bytes 2228224 | tf_op jit(solution)/shard_map/all_gather | solution.py:55
  54.4 177.3 %all-gather.14.cloned.1.call-start = ((), (), s32[]{:S(2)}) async-start(), calls=%async_computation.4 | async-start | bytes 1310720 | tf_op jit(solution)/shard_map/all_gather | solution.py:61
  55.2 416.9 %all-gather.18.cloned.1.call-start = ((), (), s32[]{:S(2)}) async-start(), calls=%async_computation.6 | async-start | bytes 10485760 | tf_op jit(solution)/shard_map/all_gather | solution.py:59
  163.0 77.5 %collective-permute-start.1 = (f32[128,64]{0,1:T(8,128)S(1)}, f32[128,64]{0,1:T(8,128)S(1)}, u32[]{:S(2)}, u32[]{:S(2)}) collective-permute-start(f32[128,64]{0,1:T(8,128)S(1)} %fusion.7), channel_id=1, source_target_pairs={{0,4},{4,0},{8,12},{12,8},{16,20},{20,16},{24,28},{28,24},{32,36},... | collective-permute-start | bytes 98312 | tf_op jit(solution)/shard_map/ppermute | solution.py:17
  234.1 84.8 %collective-permute-start = (f32[128,64]{0,1:T(8,128)S(1)}, f32[128,64]{0,1:T(8,128)S(1)}, u32[]{:S(2)}, u32[]{:S(2)}) collective-permute-start(f32[128,64]{0,1:T(8,128)S(1)} %fusion.9), channel_id=1, source_target_pairs={{0,4},{4,0},{8,12},{12,8},{16,20},{20,16},{24,28},{28,24},{32,36},... | collective-permute-start | bytes 98312 | tf_op jit(solution)/shard_map/ppermute | solution.py:17
  236.0 444.4 %all-to-all-start = ((bf16[128,4,2048]{0,2,1:T(8,128)(2,1)}), bf16[128,4,2048]{0,2,1:T(8,128)(2,1)S(1)}, u32[]{:S(2)}, u32[]{:S(2)}) async-start(bf16[128,4,2048]{0,2,1:T(8,128)(2,1)} %bitcast.22), calls=%async_computation | async-start | bytes 4194304 | tf_op jit(solution)/shard_map/all_to_all | solution.py:56
  240.5 526.6 %all-gather.12.cloned.1.call-start = ((), (), s32[]{:S(2)}) async-start(), calls=%async_computation.3 | async-start | bytes 2228224 | tf_op jit(solution)/shard_map/all_gather | solution.py:107
  767.0 9.8 %copy-start = (bf16[128,512]{0,1:T(8,128)(2,1)S(1)}, bf16[128,512]{0,1:T(8,128)(2,1)}, u32[]{:S(2)}) copy-start(bf16[128,512]{0,1:T(8,128)(2,1)} %fusion.24) | copy-start | bytes 393220
  767.0 181.8 %all-to-all-start.1 = ((bf16[128,4,2048]{0,2,1:T(8,128)(2,1)}), bf16[128,4,2048]{0,2,1:T(8,128)(2,1)}, u32[]{:S(2)}, u32[]{:S(2)}) async-start(bf16[128,4,2048]{0,2,1:T(8,128)(2,1)} %bitcast.91), calls=%async_computation.1 | async-start | bytes 4194304 | tf_op jit(solution)/shard_map/all_to_all | solution.py:108
  890.9 23.0 %copy-start.1 = (bf16[128,512]{0,1:T(8,128)(2,1)S(1)}, bf16[128,512]{0,1:T(8,128)(2,1)}, u32[]{:S(2)}) copy-start(bf16[128,512]{0,1:T(8,128)(2,1)} %get-tuple-element.6) | copy-start | bytes 393220
  895.7 52.3 %collective-permute-start.2 = (bf16[128,512]{0,1:T(8,128)(2,1)S(1)}, bf16[128,512]{0,1:T(8,128)(2,1)S(1)}, u32[]{:S(2)}, u32[]{:S(2)}) collective-permute-start(bf16[128,512]{0,1:T(8,128)(2,1)S(1)} %get-tuple-element.7), channel_id=1, source_target_pairs={{0,64},{64,128},{128,192},{192,256},{256,320},{320,384},{384,448},... | collective-permute-start | bytes 393224 | tf_op jit(solution)/shard_map/ppermute | solution.py:23
Sparse Core Ops, SparseCore 0:
  10.1 67.2 all-gather.15
  80.0 80.5 all-gather.9
  162.7 68.9 all-gather.13
  233.7 238.3 all-gather.17
  680.5 86.4 all-gather.11
where the time goes:
time: 969 us; the launch traced here: 963 us
  blocking collectives  513 us (53%)
  waiting for transfers between devices  366 us (38%)
  starting transfers between devices  36.4 us (4%)
  matrix products  21.9 us (2%)
  between operations  14 us (1%)
    psum x1, blocking collectives, on_device(): ffn_sq = lax.psum(jnp.sum(out_float * out_float, axis=1), 'tensor')  200 us
    all_gather x1, waiting for transfers between devices, on_device(): lax.all_gather(w_query[0], 'seq', axis=0, tiled=True)  129 us
    all_gather x1, blocking collectives, on_device(): lax.all_gather(normed_attn, 'seq', axis=0, tiled=True)  111 us
    all_gather x1, waiting for transfers between devices, on_device(): ffn_whole = lax.all_gather(normed_ffn, 'tensor', axis=1, tiled=True)  86.6 us
    all_gather x1, waiting for transfers between devices, on_device(): attn_whole = lax.all_gather(normed_attn, 'tensor', axis=1, tiled=True)  82.5 us
    all_gather x1, blocking collectives, on_device(): keys = lax.all_gather(key_head, 'seq', axis=0, tiled=True)  78.2 us
    all_gather x1, waiting for transfers between devices, on_device(): lax.all_gather(w_value[0], 'seq', axis=0, tiled=True)  66.8 us
    psum x1, blocking collectives, on_device(): attn_sq = lax.psum(jnp.sum(resid * resid, axis=1), 'tensor')  43.8 us
  transfers between devices with their start and end apart: 10, of which 4 were waited for; matrix products, arithmetic and copies ran while one was open for 3% of the time, Pallas kernels for 0%

commit v1 on v0

v1 whole, which is shorter than its diff:
```python
import jax
import jax.numpy as jnp
from jax import lax
from jax.sharding import Mesh, PartitionSpec as P

HD = 128
norm_eps = 1e-05
rope_base = 500000.0
ZL = ("za", "zb")
TENSOR = ("x", "za", "zb")
GROUP = TENSOR + ("seq",)
ALL = ("phase",) + GROUP
f32 = jnp.float32
bf16 = jnp.bfloat16


def spread(value, axis):
    count = lax.axis_size(axis)
    copies = jnp.broadcast_to(value[None], (count,) + value.shape)
    return lax.all_to_all(copies, axis, 0, 0)


def swap_x_seq(value):
    nx, nz, ns = lax.axis_size("x"), lax.axis_size(ZL), lax.axis_size("seq")
    pairs = [
        ((x * nz + z) * ns + s, (s * nz + z) * ns + x)
        for x in range(nx)
        for z in range(nz)
        for s in range(ns)
    ]
    return lax.ppermute(value, GROUP, pairs)


def swap_and_pass(value):
    np_, nx, nz, ns = (lax.axis_size(a) for a in ("phase", "x", ZL, "seq"))
    pairs = [
        (
            ((p * nx + x) * nz + z) * ns + s,
            ((((p + 1) % np_) * nx + s) * nz + z) * ns + x,
        )
        for p in range(np_)
        for x in range(nx)
        for z in range(nz)
        for s in range(ns)
    ]
    return lax.ppermute(value, ALL, pairs)


def three_parts(value):
    parts = []
    for _ in range(3):
        part = lax.reduce_precision(value, 8, 7)
        parts.append(part.astype(bf16))
        value = value - part
    return jnp.stack(parts)


def padded_rows(rows, count):
    return jnp.concatenate([rows, jnp.zeros((count - rows.shape[0], rows.shape[1]), rows.dtype)])


def rotate(values, positions):
    half = HD // 2
    freq = rope_base ** (-(jnp.arange(half, dtype=f32) * 2.0 / HD))
    angle = positions[:, None] * freq[None, :]
    cosine, sine = jnp.cos(angle), jnp.sin(angle)
    first, second = values[..., :half], values[..., half:]
    return jnp.concatenate(
        [first * cosine - second * sine, second * cosine + first * sine], axis=-1
    )


def on_device(hidden, segment_ids, gain_attn, gain_ffn, w_query, w_key, w_value):
    x_pos = lax.axis_index("x")
    zl_pos = lax.axis_index(ZL)
    seq_pos = lax.axis_index("seq")
    ns = lax.axis_size("seq")
    rows, feats = hidden.shape[1:]
    tokens = rows * ns
    width = feats * lax.axis_size(TENSOR)
    heads = feats // HD

    extra = jnp.concatenate(
        [gain_attn, gain_ffn, jnp.pad(segment_ids.astype(bf16), ((0, 0), (0, feats - rows)))]
    )
    swapped = swap_x_seq(jnp.concatenate([hidden[0], padded_rows(extra, 16)]))
    resid = swapped[:rows].astype(f32)
    gain_a = swapped[rows].astype(f32)
    gain_f = swapped[rows + 1].astype(f32)
    docs_own = swapped[rows + 2, :rows]

    scaled = (resid * gain_a[None, :]).astype(bf16)
    part_sq = jnp.sum(resid * resid, axis=1)
    attn_lo = lax.all_gather(scaled, ZL)
    attn_cols = spread(attn_lo, "x")
    attn_sq = lax.psum(part_sq, ZL)

    def project(weight):
        w = weight[0].reshape(4, feats, weight.shape[2])
        return lax.dot_general(
            attn_cols, w, (((1, 3), (0, 1)), ((), ())), preferred_element_type=f32
        ).astype(bf16)

    q_part = project(w_query)
    k_part, v_part = project(w_key), project(w_value)
    q_part = q_part.reshape(ns, rows, heads, HD).transpose(0, 2, 1, 3).reshape(ns, heads * rows, HD)
    message = jnp.concatenate([q_part, jnp.concatenate([k_part, v_part], 2)], 1)
    by_block = lax.all_to_all(message, "x", 0, 0)
    sq_rows = padded_rows(three_parts(attn_sq), 16)
    message = jnp.concatenate([by_block, jnp.broadcast_to(sq_rows[None], (ns, 16, rows))], 1)
    arrived = jnp.sum(lax.all_to_all(message, "seq", 0, 0).astype(f32), axis=0)
    query = arrived[: heads * rows].reshape(heads, rows, HD)
    kv = arrived[heads * rows : (heads + 1) * rows]
    total_sq = jnp.sum(arrived[(heads + 1) * rows : (heads + 1) * rows + 3], axis=0)
    r_own = lax.rsqrt(total_sq / width + norm_eps)
    query = query * r_own[None, :, None]
    kv = (kv * r_own[:, None]).astype(bf16)
    tail = jnp.concatenate([three_parts(r_own), docs_own[None]])
    kv_all = spread(jnp.concatenate([kv, padded_rows(tail, 16)]), ("x", "zb"))
    kv_all = kv_all.reshape(ns, 2, rows + 16, HD)
    kv_both = kv_all[:, :, :rows].astype(f32)
    keys = jnp.concatenate([kv_both[:, 0, :, : HD // 2], kv_both[:, 1, :, : HD // 2]], -1)
    values = jnp.concatenate([kv_both[:, 0, :, HD // 2 :], kv_both[:, 1, :, HD // 2 :]], -1)
    keys, values = keys.reshape(tokens, HD), values.reshape(tokens, HD)
    r_attn = jnp.sum(kv_all[:, 0, rows : rows + 3].astype(f32), axis=1).reshape(tokens)
    docs = kv_all[:, 0, rows + 3].reshape(tokens)

    key_ids = jnp.arange(tokens, dtype=jnp.int32)
    own_ids = x_pos * rows + jnp.arange(rows, dtype=jnp.int32)
    inv_root = 1.0 / jnp.sqrt(f32(HD))
    query = rotate(query, own_ids.astype(f32)) * inv_root
    keys = rotate(keys, key_ids.astype(f32))
    allowed = (key_ids[None, :] <= own_ids[:, None]) & (docs[None, :] == docs_own[:, None])
    scores = jnp.einsum("hrd,nd->hrn", query, keys, precision=lax.Precision.HIGHEST)
    scores = jnp.where(allowed[None], scores, f32(-1e30))
    peak = jnp.max(scores, axis=-1, keepdims=True)
    weights = jnp.where(allowed[None], jnp.exp(scores - peak), f32(0.0))
    total = jnp.sum(weights, axis=-1, keepdims=True)
    context = jnp.einsum("hrn,nd->hrd", weights, values, precision=lax.Precision.HIGHEST) / total
    context = context.transpose(1, 0, 2).reshape(rows, feats)
    section_out = (resid + context).astype(bf16)
    passed = swap_and_pass(section_out)[None]

    out_float = section_out.astype(f32)
    out_sq = jnp.sum(out_float * out_float, axis=1)
    out_scaled = (out_float * gain_f[None, :]).astype(bf16)
    ffn_lo = lax.all_gather(out_scaled, ZL)
    ffn_cols = spread(ffn_lo, "x")
    sq_all = jnp.sum(spread(out_sq[None], ZL + ("seq",)), axis=(0, 1))
    r_ffn = lax.rsqrt(spread(sq_all[None], "x").reshape(tokens) / width + norm_eps)
    ffn_rows = lax.all_gather(swap_x_seq(out_scaled), "seq", axis=0, tiled=True)
    attn_own = (hidden[0].astype(f32) * gain_attn.astype(f32)).astype(bf16)
    attn_rows = lax.all_gather(attn_own, "seq", axis=0, tiled=True)

    scale = 2.0 / tokens

    def hessian(rows_, r, cols):
        left = (rows_.astype(f32) * (r * r * scale)[:, None]).astype(bf16)
        return lax.dot_general(
            left.reshape(ns, rows, feats), cols, (((0, 1), (0, 2)), ((), ())),
            preferred_element_type=f32,
        )

    upper_part = hessian(attn_rows, r_attn, attn_cols)
    lower_part = hessian(ffn_rows, r_ffn, ffn_cols)
    row_ids = (x_pos * 4 + zl_pos) * feats + jnp.arange(feats, dtype=jnp.int32)
    col_ids = seq_pos * 4 * feats + jnp.arange(4 * feats, dtype=jnp.int32).reshape(4, feats)
    hessians = jnp.where(row_ids[:, None, None] <= col_ids[None], upper_part, lower_part)
    hessians = hessians.astype(bf16).reshape(1, feats, 4 * feats)
    diag_width = feats // ns
    own_cols = lax.dynamic_slice_in_dim(ffn_rows, seq_pos * diag_width, diag_width, 1).astype(f32)
    own_cols = own_cols * r_ffn[:, None]
    ffn_diagonal = (jnp.sum(own_cols * own_cols, axis=0) * scale)[None]
    return (passed, hessians, ffn_diagonal)


def solution(mesh):
    phase, tensor, seq = (mesh.shape[a] for a in ("phase", "tensor", "seq"))
    lines = Mesh(
        mesh.devices.reshape(phase, tensor // 4, 2, 2, seq), ("phase", "x", "za", "zb", "seq")
    )
    tiled = P("phase", "seq", TENSOR)
    return jax.shard_map(
        on_device,
        mesh=lines,
        in_specs=(
            tiled,
            P("phase", "seq"),
            P("phase", TENSOR),
            P("phase", TENSOR),
            tiled,
            tiled,
            tiled,
        ),
        out_specs=(tiled, P("phase", TENSOR, "seq"), P("phase", GROUP)),
        check_vma=False,
    )
```

time: 969 us -> 297 us (0.31)
  blocking collectives: 513 us -> 105 us
  waiting for transfers between devices: 366 us -> 62.6 us
  starting transfers between devices: 36.4 us -> 76.8 us
  between operations: 14 us -> 1.11 us
    all_gather x5 -> x0, waiting for transfers between devices: 365 us -> none  [the longest x1 129 us: on_device(): lax.all_gather(w_query[0], 'seq', axis=0, tiled=True)]
    psum x2 -> x1, blocking collectives: 243 us -> 6.6 us  [on_device(): attn_sq = lax.psum(part_sq, ZL)]
    all_gather x5 -> x4, blocking collectives: 269 us -> 98.9 us  [the longest x1 27.8 us: on_device(): ffn_rows = lax.all_gather(swap_x_seq(out_scaled), 'seq', axis=0, tiled=True)]
    all_to_all x2 -> x7, waiting for transfers between devices: 0.01 us -> 62.6 us  [the longest x1 32.8 us: on_device(): arrived = jnp.sum(lax.all_to_all(message, 'seq', 0, 0).astype(f32), axis=0)]
    all_to_all x2 -> x7, starting transfers between devices: 14.3 us -> 71.2 us  [the longest x5 57.5 us: spread(): return lax.all_to_all(copies, axis, 0, 0)]
    ppermute x3, starting transfers between devices: 22 us -> 5.61 us  [the longest x1 4.27 us: swap_and_pass(): return lax.ppermute(value, ALL, pairs)]
  transfers between devices with their start and end apart: 10 -> 10, of which waited for: 4 -> 4; matrix products, arithmetic and copies ran while one was open for 3% -> 4% of each run, Pallas kernels for 0% -> 0%
where the time goes in v1:
time: 297 us; the launch traced here: 294 us
  blocking collectives  105 us (35%)
  starting transfers between devices  76.8 us (26%)
  waiting for transfers between devices  62.6 us (21%)
  matrix products  19.3 us (6%)
  local copies, waits for them, and re-layouts  17.2 us (6%)
  other arithmetic  11.3 us (4%)
    all_to_all x5, starting transfers between devices, spread(): return lax.all_to_all(copies, axis, 0, 0)  57.5 us
    all_to_all x1, waiting for transfers between devices, on_device(): arrived = jnp.sum(lax.all_to_all(message, 'seq', 0, 0).astype(f32), axis=0)  32.8 us
    all_to_all x5, waiting for transfers between devices, spread(): return lax.all_to_all(copies, axis, 0, 0)  29 us
    all_gather x1, blocking collectives, on_device(): ffn_rows = lax.all_gather(swap_x_seq(out_scaled), 'seq', axis=0, tiled=True)  27.8 us
    all_gather x1, blocking collectives, on_device(): ffn_lo = lax.all_gather(out_scaled, ZL)  25.3 us
    all_gather x1, blocking collectives, on_device(): attn_rows = lax.all_gather(attn_own, 'seq', axis=0, tiled=True)  23.4 us
    all_gather x1, blocking collectives, on_device(): attn_lo = lax.all_gather(scaled, ZL)  22.3 us
    all_to_all x1, starting transfers between devices, on_device(): arrived = jnp.sum(lax.all_to_all(message, 'seq', 0, 0).astype(f32), axis=0)  10.1 us
  transfers between devices with their start and end apart: 10, of which 4 were waited for; matrix products, arithmetic and copies ran while one was open for 4% of the time, Pallas kernels for 0%

profile of v1, /device:TPU:1, one launch (start us, length us, event | category | flops | bytes accessed | tf_op | source)
XLA Modules:
  0.0 293.7 jit_solution(5495500779574066225)
XLA Ops:
  1.5 1.8 concatenate.38
  4.1 22.3 %all-gather = bf16[512,512]{1,0:T(8,128)(2,1)S(1)} all-gather(bf16[128,512]{1,0:T(8,128)(2,1)S(1)} %get-tuple-element.34), channel_id=2, replica_groups=mesh['phase'=8,'x'=4,'za'=2,'zb'=2,'seq'=4] {'za','zb'}, dimensions={0}, use_global_device_ids=true | all-gather | bytes 655360 | tf_op jit(solution)/shard_map/all_gather | solution.py:94
  27.9 26.5 %all-to-all-start = ((bf16[4,4,128,512]{3,2,1,0:T(8,128)(2,1)}), bf16[4,4,128,512]{3,2,1,0:T(8,128)(2,1)}, u32[]{:S(2)}, u32[]{:S(2)}) async-start(bf16[4,4,128,512]{3,2,1,0:T(8,128)(2,1)} %broadcast_in_dim.39), calls=%async_computation | async-start | bytes 4194304 | tf_op jit(solution)/shard_map/all_to_all | solution.py:20
  54.9 23.7 %all-to-all-done = bf16[4,4,128,512]{3,2,1,0:T(8,128)(2,1)} async-done(((bf16[4,4,128,512]{3,2,1,0:T(8,128)(2,1)}), bf16[4,4,128,512]{3,2,1,0:T(8,128)(2,1)}, u32[]{:S(2)}, u32[]{:S(2)}) %all-to-all-start) | async-done | bytes 2097184 | tf_op jit(solution)/shard_map/all_to_all | solution.py:20
  78.6 2.3 fusion.5
  80.9 2.3 fusion.4
  83.4 2.8 fusion.2
  87.3 3.6 %all-to-all-start.1 = ((bf16[4,640,128]{2,1,0:T(8,128)(2,1)}), bf16[4,640,128]{2,1,0:T(8,128)(2,1)S(1)}, u32[]{:S(2)}, u32[]{:S(2)}) async-start(bf16[4,640,128]{2,1,0:T(8,128)(2,1)} %pad_maximum_fusion.1), calls=%async_computation.1 | async-start | bytes 1310720 | tf_op jit(solution)/shard_map/all_to_all | solution.py:108
  91.0 6.6 %psum.7 = f32[128]{0:T(128)S(1)} all-reduce(f32[128]{0:T(128)S(1)} %get-tuple-element.35), channel_id=1, replica_groups=mesh['phase'=8,'x'=4,'za'=2,'zb'=2,'seq'=4] {'za','zb'}, use_global_device_ids=true, to_apply=%region_1.2 | all-reduce | flops 128 | bytes 1024 | tf_op jit(solution)/shard_map/psum | solution.py:96
  99.4 10.1 %all-to-all-start.2 = ((bf16[4,656,128]{2,1,0:T(8,128)(2,1)}), bf16[4,656,128]{2,1,0:T(8,128)(2,1)S(1)}, u32[]{:S(2)}, u32[]{:S(2)}) async-start(bf16[4,656,128]{2,1,0:T(8,128)(2,1)} %pad_maximum_fusion), calls=%async_computation.2 | async-start | bytes 1343488 | tf_op jit(solution)/shard_map/all_to_all | solution.py:111
  110.6 32.8 %all-to-all-done.2 = bf16[4,656,128]{2,1,0:T(8,128)(2,1)S(1)} async-done(((bf16[4,656,128]{2,1,0:T(8,128)(2,1)}), bf16[4,656,128]{2,1,0:T(8,128)(2,1)S(1)}, u32[]{:S(2)}, u32[]{:S(2)}) %all-to-all-start.2) | async-done | bytes 671776 | tf_op jit(solution)/shard_map/all_to_all | solution.py:111
  144.6 4.1 %all-to-all-start.3 = ((bf16[8,144,128]{2,1,0:T(8,128)(2,1)}), bf16[8,144,128]{2,1,0:T(8,128)(2,1)S(1)}, u32[]{:S(2)}, u32[]{:S(2)}) async-start(bf16[8,144,128]{2,1,0:T(8,128)(2,1)} %broadcast_in_dim.43), calls=%async_computation.3 | async-start | bytes 589824 | tf_op jit(solution)/shard_map/all_to_all | solution.py:20
  149.7 23.4 %all_gather.20 = bf16[512,512]{1,0:T(8,128)(2,1)S(1)} all-gather(bf16[128,512]{1,0:T(8,128)(2,1)S(1)} %multiply_convert_fusion.2), channel_id=1, replica_groups=mesh['phase'=8,'x'=4,'za'=2,'zb'=2,'seq'=4] {'seq'}, dimensions={0}, use_global_device_ids=true | all-gather | bytes 655360 | tf_op jit(solution)/shard_map/all_gather | solution.py:153
  178.2 2.2 fusion.16
  184.3 9.7 %all-to-all-start.4 = ((f32[16,1,128]{2,1,0:T(1,128)}), f32[16,1,128]{2,1,0:T(1,128)S(1)}, u32[]{:S(2)}, u32[]{:S(2)}) async-start(f32[16,1,128]{2,1,0:T(1,128)} %broadcast_in_dim.48), calls=%async_computation.4 | async-start | bytes 16384 | tf_op jit(solution)/shard_map/all_to_all | solution.py:20
  194.0 4.3 %collective-permute-start.1 = (bf16[128,512]{1,0:T(8,128)(2,1)S(1)}, bf16[128,512]{1,0:T(8,128)(2,1)}, u32[]{:S(2)}, u32[]{:S(2)}) collective-permute-start(bf16[128,512]{1,0:T(8,128)(2,1)S(1)} %get-tuple-element.19), channel_id=1, source_target_pairs={{0,64},{1,80},{2,96},{3,112},{4,68},{5,84},{6,100},{7,116},{8,72},... | collective-permute-start | bytes 393224 | tf_op jit(solution)/shard_map/ppermute | solution.py:46
  199.9 5.3 %all-to-all-done.4 = f32[16,1,128]{2,1,0:T(1,128)S(1)} async-done(((f32[16,1,128]{2,1,0:T(1,128)}), f32[16,1,128]{2,1,0:T(1,128)S(1)}, u32[]{:S(2)}, u32[]{:S(2)}) %all-to-all-start.4) | async-done | bytes 8224 | tf_op jit(solution)/shard_map/all_to_all | solution.py:20
  205.8 12.7 %all-to-all-start.5 = ((f32[4,1,128]{2,1,0:T(1,128)}), f32[4,1,128]{2,1,0:T(1,128)S(1)}, u32[]{:S(2)}, u32[]{:S(2)}) async-start(f32[4,1,128]{2,1,0:T(1,128)} %broadcast_in_dim.49), calls=%async_computation.5 | async-start | bytes 4096 | tf_op jit(solution)/shard_map/all_to_all | solution.py:20
  218.5 25.3 %all-gather.1 = bf16[512,512]{1,0:T(8,128)(2,1)S(1)} all-gather(bf16[128,512]{1,0:T(8,128)(2,1)S(1)} %fusion.14), channel_id=3, replica_groups=mesh['phase'=8,'x'=4,'za'=2,'zb'=2,'seq'=4] {'za','zb'}, dimensions={0}, use_global_device_ids=true | all-gather | bytes 655360 | tf_op jit(solution)/shard_map/all_gather | solution.py:147
  245.8 4.6 %all-to-all-start.6 = ((bf16[4,4,128,512]{2,3,1,0:T(8,128)(2,1)}), bf16[4,4,128,512]{2,3,1,0:T(8,128)(2,1)}, u32[]{:S(2)}, u32[]{:S(2)}) async-start(bf16[4,4,128,512]{2,3,1,0:T(8,128)(2,1)} %broadcast_in_dim.50), calls=%async_computation.6 | async-start | bytes 4194304 | tf_op jit(solution)/shard_map/all_to_all | solution.py:20
  250.4 4.2 %fusion.49 = bf16[512,4,512,1]{0,2,1,3:T(8,128)(2,1)} fusion(bf16[4,128,512,1]{2,1,3,0:T(8,128)(2,1)S(1)} %bitcast.135, bf16[4,4,128,512]{3,2,1,0:T(8,128)(2,1)} %all-to-all-done), kind=kOutput, calls=%fused_computation.107 | convolution fusion | flops 1073741824 | bytes 4718592 | tf_op jit(solution)/shard_map/dot_general | solution.py:159
  254.7 27.8 %all_gather.21 = bf16[512,512]{1,0:T(8,128)(2,1)S(1)} all-gather(bf16[128,512]{1,0:T(8,128)(2,1)S(1)} %collective-permute-done.2), channel_id=1, replica_groups=mesh['phase'=8,'x'=4,'za'=2,'zb'=2,'seq'=4] {'seq'}, dimensions={0}, use_global_device_ids=true | all-gather | bytes 655360 | tf_op jit(solution)/shard_map/all_gather | solution.py:151
  283.3 4.9 %fusion = bf16[512,4,512]{0,2,1:T(8,128)(2,1)} fusion(bf16[512,4,512,1]{0,2,1,3:T(8,128)(2,1)} %fusion.49, bf16[4,128,512,1]{2,1,3,0:T(8,128)(2,1)S(1)} %bitcast.136, bf16[4,4,128,512]{2,3,1,0:T(8,128)(2,1)} %all-to-all-done.6, s32[4,512]{1,0:T(4,128)S(1)} %copy-done.10, s32[512]{0:T(512)S(1)} %copy-done.12), kind=kOutput, calls=%fused_computation.1 | convolution fusion | flops 1075838976 | bytes 6825984 | tf_op jit(solution)/shard_map/dot_general | solution.py:159
  288.2 3.9 %copy.62 = bf16[1,512,2048]{2,1,0:T(8,128)(2,1)} copy(bf16[1,512,2048]{1,2,0:T(8,128)(2,1)} %bitcast.126) | data formatting | bytes 4194304
  (100 shorter events, 25.4 us)
Async XLA Ops:
  0.6 82.8 %copy-start = (bf16[1,2048,512]{2,1,0:T(8,128)(2,1)S(1)}, bf16[1,2048,512]{2,1,0:T(8,128)(2,1)}, u32[]{:S(2)}) copy-start(bf16[1,2048,512]{2,1,0:T(8,128)(2,1)} %param.11) | copy-start | bytes 6291460
  3.2 0.7 collective-permute-start
  3.9 106.2 %copy-start.4 = (bf16[144,512]{1,0:T(8,128)(2,1)}, bf16[144,512]{1,0:T(8,128)(2,1)S(1)}, u32[]{:S(2)}) copy-start(bf16[144,512]{1,0:T(8,128)(2,1)S(1)} %collective-permute-done) | copy-start | bytes 442372
  27.9 26.5 %copy-start.6 = (bf16[1,2048,64]{1,2,0:T(8,128)(2,1)S(1)}, bf16[1,2048,64]{1,2,0:T(8,128)(2,1)}, u32[]{:S(2)}) copy-start(bf16[1,2048,64]{1,2,0:T(8,128)(2,1)} %param.12) | copy-start | bytes 786436
  27.9 26.7 %copy-start.7 = (bf16[1,2048,64]{1,2,0:T(8,128)(2,1)S(1)}, bf16[1,2048,64]{1,2,0:T(8,128)(2,1)}, u32[]{:S(2)}) copy-start(bf16[1,2048,64]{1,2,0:T(8,128)(2,1)} %param.13) | copy-start | bytes 786436
  27.9 50.7 %all-to-all-start = ((bf16[4,4,128,512]{3,2,1,0:T(8,128)(2,1)}), bf16[4,4,128,512]{3,2,1,0:T(8,128)(2,1)}, u32[]{:S(2)}, u32[]{:S(2)}) async-start(bf16[4,4,128,512]{3,2,1,0:T(8,128)(2,1)} %broadcast_in_dim.39), calls=%async_computation | async-start | bytes 4194304 | tf_op jit(solution)/shard_map/all_to_all | solution.py:20
  87.3 22.2 %copy-start.9 = (bf16[1,512]{1,0:T(2,128)(2,1)S(1)}, bf16[1,512]{1,0:T(2,128)(2,1)}, u32[]{:S(2)}) copy-start(bf16[1,512]{1,0:T(2,128)(2,1)} %param.9) | copy-start | bytes 3076
  87.3 22.8 %copy-start.2 = (bf16[1,128,512]{2,1,0:T(8,128)(2,1)S(1)}, bf16[1,128,512]{2,1,0:T(8,128)(2,1)}, u32[]{:S(2)}) copy-start(bf16[1,128,512]{2,1,0:T(8,128)(2,1)} %param.7) | copy-start | bytes 393220
  87.3 11.2 %all-to-all-start.1 = ((bf16[4,640,128]{2,1,0:T(8,128)(2,1)}), bf16[4,640,128]{2,1,0:T(8,128)(2,1)S(1)}, u32[]{:S(2)}, u32[]{:S(2)}) async-start(bf16[4,640,128]{2,1,0:T(8,128)(2,1)} %pad_maximum_fusion.1), calls=%async_computation.1 | async-start | bytes 1310720 | tf_op jit(solution)/shard_map/all_to_all | solution.py:108
  99.4 44.0 %all-to-all-start.2 = ((bf16[4,656,128]{2,1,0:T(8,128)(2,1)}), bf16[4,656,128]{2,1,0:T(8,128)(2,1)S(1)}, u32[]{:S(2)}, u32[]{:S(2)}) async-start(bf16[4,656,128]{2,1,0:T(8,128)(2,1)} %pad_maximum_fusion), calls=%async_computation.2 | async-start | bytes 1343488 | tf_op jit(solution)/shard_map/all_to_all | solution.py:111
  109.5 64.0 %copy-start.11 = (f32[64]{0:T(128)}, f32[64]{0:T(128)S(1)}, u32[]{:S(2)}) copy-start(f32[64]{0:T(128)S(1)} %negate_power_fusion) | copy-start | bytes 772
  144.6 29.8 %all-to-all-start.3 = ((bf16[8,144,128]{2,1,0:T(8,128)(2,1)}), bf16[8,144,128]{2,1,0:T(8,128)(2,1)S(1)}, u32[]{:S(2)}, u32[]{:S(2)}) async-start(bf16[8,144,128]{2,1,0:T(8,128)(2,1)} %broadcast_in_dim.43), calls=%async_computation.3 | async-start | bytes 589824 | tf_op jit(solution)/shard_map/all_to_all | solution.py:20
  174.5 5.9 %copy-start.1 = (f32[4,128,64]{2,1,0:T(8,128)S(1)}, f32[4,128,64]{2,1,0:T(8,128)}, u32[]{:S(2)}) copy-start(f32[4,128,64]{2,1,0:T(8,128)} %get-tuple-element.29) | copy-start | bytes 393220
  178.1 3.8 %copy-start.8 = (f32[512,64]{0,1:T(8,128)S(1)}, f32[512,64]{0,1:T(8,128)}, u32[]{:S(2)}) copy-start(f32[512,64]{0,1:T(8,128)} %copy.70) | copy-start | bytes 393220
  181.6 1.9 copy-start.5
  184.3 20.9 %all-to-all-start.4 = ((f32[16,1,128]{2,1,0:T(1,128)}), f32[16,1,128]{2,1,0:T(1,128)S(1)}, u32[]{:S(2)}, u32[]{:S(2)}) async-start(f32[16,1,128]{2,1,0:T(1,128)} %broadcast_in_dim.48), calls=%async_computation.4 | async-start | bytes 16384 | tf_op jit(solution)/shard_map/all_to_all | solution.py:20
  194.0 60.7 %collective-permute-start.1 = (bf16[128,512]{1,0:T(8,128)(2,1)S(1)}, bf16[128,512]{1,0:T(8,128)(2,1)}, u32[]{:S(2)}, u32[]{:S(2)}) collective-permute-start(bf16[128,512]{1,0:T(8,128)(2,1)S(1)} %get-tuple-element.19), channel_id=1, source_target_pairs={{0,64},{1,80},{2,96},{3,112},{4,68},{5,84},{6,100},{7,116},{8,72},... | collective-permute-start | bytes 393224 | tf_op jit(solution)/shard_map/ppermute | solution.py:46
  198.3 56.4 %collective-permute-start.2 = (bf16[128,512]{1,0:T(8,128)(2,1)S(1)}, bf16[128,512]{1,0:T(8,128)(2,1)S(1)}, u32[]{:S(2)}, u32[]{:S(2)}) collective-permute-start(bf16[128,512]{1,0:T(8,128)(2,1)S(1)} %fusion.14), channel_id=1, source_target_pairs={{0,0},{1,16},{2,32},{3,48},{4,4},{5,20},{6,36},{7,52},{8,8},{9,24}... | collective-permute-start | bytes 393224 | tf_op jit(solution)/shard_map/ppermute | solution.py:31
  205.8 38.3 %all-to-all-start.5 = ((f32[4,1,128]{2,1,0:T(1,128)}), f32[4,1,128]{2,1,0:T(1,128)S(1)}, u32[]{:S(2)}, u32[]{:S(2)}) async-start(f32[4,1,128]{2,1,0:T(1,128)} %broadcast_in_dim.49), calls=%async_computation.5 | async-start | bytes 4096 | tf_op jit(solution)/shard_map/all_to_all | solution.py:20
  245.8 4.6 %copy-start.3 = (bf16[512,512]{1,0:T(8,128)(2,1)S(1)}, bf16[512,512]{1,0:T(8,128)(2,1)}, u32[]{:S(2)}) copy-start(bf16[512,512]{1,0:T(8,128)(2,1)} %multiply_convert_fusion.1) | copy-start | bytes 1572868
  245.8 37.5 %all-to-all-start.6 = ((bf16[4,4,128,512]{2,3,1,0:T(8,128)(2,1)}), bf16[4,4,128,512]{2,3,1,0:T(8,128)(2,1)}, u32[]{:S(2)}, u32[]{:S(2)}) async-start(bf16[4,4,128,512]{2,3,1,0:T(8,128)(2,1)} %broadcast_in_dim.50), calls=%async_computation.6 | async-start | bytes 4194304 | tf_op jit(solution)/shard_map/all_to_all | solution.py:20
  250.4 32.9 %copy-start.10 = (s32[4,512]{1,0:T(4,128)S(1)}, s32[4,512]{1,0:T(4,128)}, u32[]{:S(2)}) copy-start(s32[4,512]{1,0:T(4,128)} %add_add_fusion) | copy-start | bytes 24580
  250.4 32.9 %copy-start.12 = (s32[512]{0:T(512)S(1)}, s32[512]{0:T(512)}, u32[]{:S(2)}) copy-start(s32[512]{0:T(512)} %iota_add_fusion) | copy-start | bytes 6148

commit v2 on v1

v2 whole, which is shorter than its diff:
```python
import functools

import jax
import jax.numpy as jnp
from jax import lax
from jax.experimental import pallas as pl
from jax.experimental.pallas import tpu as pltpu
from jax.sharding import Mesh, PartitionSpec as P

HD = 128
norm_eps = 1e-05
rope_base = 500000.0
ZL = ("za", "zb")
TENSOR = ("x", "za", "zb")
GROUP = TENSOR + ("seq",)
ALL = ("phase",) + GROUP
f32 = jnp.float32
bf16 = jnp.bfloat16
LIMIT = 24 * 1024 * 1024


def spread(value, axis):
    count = lax.axis_size(axis)
    copies = jnp.broadcast_to(value[None], (count,) + value.shape)
    return lax.all_to_all(copies, axis, 0, 0)


def swap_x_seq(value):
    nx, nz, ns = lax.axis_size("x"), lax.axis_size(ZL), lax.axis_size("seq")
    pairs = [
        ((x * nz + z) * ns + s, (s * nz + z) * ns + x)
        for x in range(nx)
        for z in range(nz)
        for s in range(ns)
    ]
    return lax.ppermute(value, GROUP, pairs)


def swap_and_pass(value):
    np_, nx, nz, ns = (lax.axis_size(a) for a in ("phase", "x", ZL, "seq"))
    pairs = [
        (
            ((p * nx + x) * nz + z) * ns + s,
            ((((p + 1) % np_) * nx + s) * nz + z) * ns + x,
        )
        for p in range(np_)
        for x in range(nx)
        for z in range(nz)
        for s in range(ns)
    ]
    return lax.ppermute(value, ALL, pairs)


def project_kernel(cols, wq, wk, wv, q_out, kv_out, q_acc, kv_acc):
    step = pl.program_id(0)
    blocks, rows, feats = cols.shape
    left = cols[...].reshape(blocks * rows, feats)
    kv_w = jnp.concatenate([wk[...], wv[...]], 0)
    kv = lax.dot_general(left, kv_w, (((1,), (1,)), ((), ())), preferred_element_type=f32)
    q = jnp.dot(left, wq[...], preferred_element_type=f32)

    @pl.when(step == 0)
    def _():
        q_acc[...] = q
        kv_acc[...] = kv

    @pl.when(step > 0)
    def _():
        q_acc[...] += q
        kv_acc[...] += kv

    @pl.when(step == pl.num_programs(0) - 1)
    def _():
        for k in range(blocks):
            block = pl.ds(k * rows, rows)
            kv_out[k] = kv_acc[block, :].astype(bf16)
            for h in range(q_acc.shape[1] // HD):
                q_out[k, pl.ds(h * rows, rows), :] = q_acc[block, pl.ds(h * HD, HD)].astype(bf16)


def project(cols, w_query, w_key, w_value):
    blocks, parts, rows, feats = cols.shape
    q_width, kv_width = w_query.shape[2], 2 * w_key.shape[2]
    heads = q_width // HD
    kv_spec = pl.BlockSpec((None, w_key.shape[2], feats), lambda z: (0, 0, z))
    return pl.pallas_call(
        project_kernel,
        grid=(parts,),
        in_specs=[
            pl.BlockSpec((blocks, None, rows, feats), lambda z: (0, z, 0, 0)),
            pl.BlockSpec((None, feats, q_width), lambda z: (0, z, 0)),
            kv_spec,
            kv_spec,
        ],
        out_specs=[
            pl.BlockSpec((blocks, heads * rows, HD), lambda z: (0, 0, 0)),
            pl.BlockSpec((blocks, rows, kv_width), lambda z: (0, 0, 0)),
        ],
        out_shape=[
            jax.ShapeDtypeStruct((blocks, heads * rows, HD), bf16),
            jax.ShapeDtypeStruct((blocks, rows, kv_width), bf16),
        ],
        scratch_shapes=[
            pltpu.VMEM((blocks * rows, q_width), f32),
            pltpu.VMEM((blocks * rows, kv_width), f32),
        ],
        compiler_params=pltpu.CompilerParams(vmem_limit_bytes=LIMIT),
        name="project",
    )(cols, w_query, w_key.swapaxes(1, 2), w_value.swapaxes(1, 2))


def rotate(values, cosine, sine):
    return values * cosine + pltpu.roll(values, HD // 2, 1) * sine


def attend_kernel(
    place, q_in, kv_in, r_own, r_all, docs_own, docs_all, cos_own, sin_own, cos_all, sin_all,
    resid, out, keys, values,
):
    rows = out.shape[0]
    tokens = keys.shape[0]

    @pl.when(pl.program_id(0) == 0)
    def _():
        lower = lax.broadcasted_iota(jnp.int32, (rows, HD), 1) < HD // 2
        for k in range(tokens // rows):
            first = kv_in[2 * k].astype(f32)
            second = kv_in[2 * k + 1].astype(f32)
            block = pl.ds(k * rows, rows)
            key = jnp.where(lower, first, pltpu.roll(second, HD // 2, 1))
            keys[block, :] = rotate(key, cos_all[block, :], sin_all[block, :])
            values[block, :] = jnp.where(lower, pltpu.roll(first, HD // 2, 1), second)

    query = jnp.sum(q_in[...].astype(f32), axis=0)
    query = rotate(query, cos_own[...], sin_own[...]) * r_own[...]
    scores = lax.dot_general(
        query, keys[...], (((1,), (1,)), ((), ())),
        preferred_element_type=f32, precision=lax.Precision.HIGHEST,
    )
    scores = scores * r_all[...]
    key_ids = lax.broadcasted_iota(jnp.int32, scores.shape, 1)
    own_ids = lax.broadcasted_iota(jnp.int32, scores.shape, 0) + place[0] * rows
    allowed = (key_ids <= own_ids) & (docs_all[...] == docs_own[...])
    scores = jnp.where(allowed, scores, f32(-1e30))
    peak = jnp.max(scores, axis=-1, keepdims=True)
    weights = jnp.where(allowed, jnp.exp(scores - peak), f32(0.0))
    total = jnp.sum(weights, axis=-1, keepdims=True)
    context = jnp.dot(
        weights * r_all[...], values[...],
        preferred_element_type=f32, precision=lax.Precision.HIGHEST,
    ) / total
    out[...] = (resid[...].astype(f32) + context).astype(bf16)


def attend(place, q_in, kv_in, r_own, r_all, docs_own, docs_all, tables_own, tables_all, resid):
    rows, feats = resid.shape
    tokens = r_all.shape[1]
    whole = pl.BlockSpec(memory_space=pltpu.VMEM)
    return pl.pallas_call(
        attend_kernel,
        grid=(feats // HD,),
        in_specs=[
            pl.BlockSpec(memory_space=pltpu.SMEM),
            pl.BlockSpec((q_in.shape[0], rows, HD), lambda h: (0, h, 0)),
        ]
        + [whole] * 9
        + [pl.BlockSpec((rows, HD), lambda h: (0, h))],
        out_specs=pl.BlockSpec((rows, HD), lambda h: (0, h)),
        out_shape=jax.ShapeDtypeStruct((rows, feats), bf16),
        scratch_shapes=[pltpu.VMEM((tokens, HD), f32), pltpu.VMEM((tokens, HD), f32)],
        compiler_params=pltpu.CompilerParams(vmem_limit_bytes=LIMIT),
        name="attend",
    )(place, q_in, kv_in, r_own, r_all, docs_own, docs_all, *tables_own, *tables_all, resid)


def product(left, cols):
    blocks, rows, feats = cols.shape
    return jnp.dot(left[...], cols[...].reshape(blocks * rows, feats), preferred_element_type=f32)


def upper_kernel(place, left, cols, out):
    @pl.when(place[1] <= place[2] + pl.program_id(0))
    def _():
        out[...] = product(left, cols).astype(bf16)


def lower_kernel(place, left, cols, upper, out):
    row, col = place[1], place[2] + pl.program_id(0)

    @pl.when(row < col)
    def _():
        out[...] = upper[...]

    @pl.when(row > col)
    def _():
        out[...] = product(left, cols).astype(bf16)

    @pl.when(row == col)
    def _():
        lower = product(left, cols).astype(bf16)
        row_ids = lax.broadcasted_iota(jnp.int32, lower.shape, 0)
        col_ids = lax.broadcasted_iota(jnp.int32, lower.shape, 1)
        out[...] = jnp.where(row_ids <= col_ids, upper[...], lower)


def hessian(kernel, place, left, cols, *upper):
    blocks, parts, rows, feats = cols.shape
    tile = pl.BlockSpec((feats, feats), lambda z: (0, z))
    return pl.pallas_call(
        kernel,
        grid=(parts,),
        in_specs=[
            pl.BlockSpec(memory_space=pltpu.SMEM),
            pl.BlockSpec((feats, blocks * rows), lambda z: (0, 0)),
            pl.BlockSpec((blocks, None, rows, feats), lambda z: (0, z, 0, 0)),
        ]
        + [tile] * len(upper),
        out_specs=tile,
        out_shape=jax.ShapeDtypeStruct((feats, parts * feats), bf16),
        compiler_params=pltpu.CompilerParams(vmem_limit_bytes=LIMIT),
        name="hessian",
    )(place, left, cols, *upper)


def on_device(hidden, segment_ids, gain_attn, gain_ffn, w_query, w_key, w_value):
    x_pos = lax.axis_index("x")
    zl_pos = lax.axis_index(ZL)
    seq_pos = lax.axis_index("seq")
    nx, nz, ns = lax.axis_size("x"), lax.axis_size(ZL), lax.axis_size("seq")
    rows, feats = hidden.shape[1:]
    tokens = rows * ns
    width = feats * nx * nz
    scale = 2.0 / tokens
    place = jnp.stack([x_pos, x_pos * nz + zl_pos, seq_pos * nz]).astype(jnp.int32)

    resid = swap_x_seq(hidden[0])
    gains = spread(jnp.concatenate([gain_attn, gain_ffn]), TENSOR)
    gains = lax.dynamic_slice_in_dim(gains.astype(f32), seq_pos * nz, nz, 0)

    def columns(block, gain):
        group = spread(block, ZL).astype(f32)
        cols = spread((group * gain[:, None, :]).astype(bf16), "x")
        small = jnp.stack([jnp.sum(group * group, axis=(0, 2)), segment_ids[0].astype(f32)])
        small = spread(small, ("x", "seq")).reshape(nx, ns, 2, rows)
        total = jnp.sum(small[:, :, 0], axis=1).reshape(tokens)
        return cols, lax.rsqrt(total / width + norm_eps), small[0, :, 1].reshape(tokens)

    def left_side(blocks, gain, r):
        left = blocks.astype(f32).reshape(tokens, feats) * (r * r * scale)[:, None]
        return (left * gain.astype(f32)).astype(bf16).T

    attn_cols, r_attn, docs = columns(resid, gains[:, 0])
    q_part, kv_part = project(attn_cols, w_query, w_key, w_value)
    kv = lax.all_to_all(lax.all_to_all(kv_part, "x", 0, 0), "seq", 0, 0)
    kv = spread(jnp.sum(kv.astype(f32), axis=0).astype(bf16), ("x", "zb"))
    query = lax.all_to_all(lax.all_to_all(q_part, "x", 0, 0), "seq", 0, 0)

    half = HD // 2
    freq = rope_base ** (-(jnp.arange(half, dtype=f32) * 2.0 / HD))
    angle = jnp.arange(tokens, dtype=f32)[:, None] * freq[None, :]
    cosine, sine = jnp.cos(angle), jnp.sin(angle)
    tables = (jnp.concatenate([cosine] * 2, 1), jnp.concatenate([-sine, sine], 1))
    own = functools.partial(lax.dynamic_slice_in_dim, start_index=x_pos * rows, slice_size=rows)
    inv_root = 1.0 / jnp.sqrt(f32(HD))
    section_out = attend(
        place,
        query,
        kv,
        own(r_attn * inv_root)[:, None],
        r_attn[None],
        own(docs)[:, None],
        docs[None],
        tuple(own(t) for t in tables),
        tables,
        resid,
    )
    attn_rows = spread(hidden[0], "seq")
    attn_left = left_side(attn_rows, gain_attn, r_attn)
    upper = hessian(upper_kernel, place, attn_left, attn_cols)

    passed = swap_and_pass(section_out)[None]
    ffn_cols, r_ffn, _ = columns(section_out, gains[:, 1])
    ffn_rows = lax.all_to_all(spread(section_out, "seq"), "x", 0, 0)
    ffn_left = left_side(ffn_rows, gain_ffn, r_ffn)
    hessians = hessian(lower_kernel, place, ffn_left, ffn_cols, upper)[None]
    diag_width = feats // ns
    own_cols = lax.dynamic_slice_in_dim(
        ffn_rows.reshape(tokens, feats), seq_pos * diag_width, diag_width, 1
    ).astype(f32)
    own_gain = lax.dynamic_slice_in_dim(gain_ffn[0], seq_pos * diag_width, diag_width)
    own_cols = own_cols * r_ffn[:, None] * own_gain.astype(f32)
    ffn_diagonal = (jnp.sum(own_cols * own_cols, axis=0) * scale)[None]
    return (passed, hessians, ffn_diagonal)


def solution(mesh):
    phase, tensor, seq = (mesh.shape[a] for a in ("phase", "tensor", "seq"))
    lines = Mesh(
        mesh.devices.reshape(phase, tensor // 4, 2, 2, seq), ("phase", "x", "za", "zb", "seq")
    )
    tiled = P("phase", "seq", TENSOR)
    return jax.shard_map(
        on_device,
        mesh=lines,
        in_specs=(
            tiled,
            P("phase", "seq"),
            P("phase", TENSOR),
            P("phase", TENSOR),
            tiled,
            tiled,
            tiled,
        ),
        out_specs=(tiled, P("phase", TENSOR, "seq"), P("phase", GROUP)),
        check_vma=False,
    )
```

time: 297 us -> 338 us (1.14)
  the two profiles are of different devices: /device:TPU:1 before, /device:TPU:2 now
where the time goes in v2:
time: 338 us; the launch traced here: 337 us
  blocking collectives  117 us (35%)
  waiting for transfers between devices  111 us (33%)
  starting transfers between devices  67.2 us (20%)
  local copies, waits for them, and re-layouts  20.8 us (6%)
  Pallas kernels  13.8 us (4%)
  other arithmetic  6.45 us (2%)
    all_to_all x4, blocking collectives, spread(): return lax.all_to_all(copies, axis, 0, 0)  80.3 us
    all_to_all x6, waiting for transfers between devices, spread(): return lax.all_to_all(copies, axis, 0, 0)  69.8 us
    all_to_all x6, starting transfers between devices, spread(): return lax.all_to_all(copies, axis, 0, 0)  47.1 us
    all_to_all x2, blocking collectives, on_device(): kv = lax.all_to_all(lax.all_to_all(kv_part, 'x', 0, 0), 'seq', 0, 0)  25.7 us
    all_to_all x2, waiting for transfers between devices, on_device(): query = lax.all_to_all(lax.all_to_all(q_part, 'x', 0, 0), 'seq', 0, 0)  25 us
    ppermute x1, waiting for transfers between devices, swap_and_pass(): return lax.ppermute(value, ALL, pairs)  15.9 us
    all_to_all x1, blocking collectives, on_device(): ffn_rows = lax.all_to_all(spread(section_out, 'seq'), 'x', 0, 0)  11.2 us
    ppermute x1, starting transfers between devices, swap_x_seq(): return lax.ppermute(value, GROUP, pairs)  9.07 us
  transfers between devices with their start and end apart: 10, of which 8 were waited for; matrix products, arithmetic and copies ran while one was open for 3% of the time, Pallas kernels for 3%

profile of v2, /device:TPU:2, one launch (start us, length us, event | category | flops | bytes accessed | tf_op | source)
XLA Modules:
  0.0 337.0 jit_solution(1586564104211195270)
XLA Ops:
  0.6 9.1 %collective-permute-start = (bf16[128,512]{1,0:T(8,128)(2,1)}, bf16[128,512]{1,0:T(8,128)(2,1)S(1)}, u32[]{:S(2)}, u32[]{:S(2)}) collective-permute-start(bf16[128,512]{1,0:T(8,128)(2,1)} %bitcast.69), channel_id=1, source_target_pairs={{0,0},{1,16},{2,32},{3,48},{4,4},{5,20},{6,36},{7,52},{8,8},{9,24}... | collective-permute-start | bytes 393224 | tf_op jit(solution)/shard_map/ppermute | solution.py:36
  10.4 20.6 %all_to_all.75 = bf16[16,2,512]{2,1,0:T(2,128)(2,1)S(1)} all-to-all(bf16[16,2,512]{2,1,0:T(2,128)(2,1)S(1)} %broadcast_in_dim.27), channel_id=1, replica_groups=mesh['phase'=8,'x'=4,'za'=2,'zb'=2,'seq'=4] {'x','za','zb'}, dimensions={0} | all-to-all | bytes 65536 | tf_op jit(solution)/shard_map/all_to_all | solution.py:25
  36.1 13.7 %all-to-all-done = bf16[4,128,512]{2,1,0:T(8,128)(2,1)S(1)} async-done(((bf16[4,128,512]{2,1,0:T(8,128)(2,1)}), bf16[4,128,512]{2,1,0:T(8,128)(2,1)S(1)}, u32[]{:S(2)}, u32[]{:S(2)}) %all-to-all-start) | async-done | bytes 524320 | tf_op jit(solution)/shard_map/all_to_all | solution.py:25
  51.6 5.0 %all-to-all-start.2 = ((bf16[4,4,128,512]{3,2,1,0:T(8,128)(2,1)}), bf16[4,4,128,512]{3,2,1,0:T(8,128)(2,1)S(1)}, u32[]{:S(2)}, u32[]{:S(2)}) async-start(bf16[4,4,128,512]{3,2,1,0:T(8,128)(2,1)} %broadcast_in_dim.28), calls=%async_computation.2 | async-start | bytes 4194304 | tf_op jit(solution)/shard_map/all_to_all | solution.py:25
  57.2 23.5 %all-to-all-done.2.cols = bf16[4,4,128,512]{3,2,1,0:T(8,128)(2,1)S(1)} async-done(((bf16[4,4,128,512]{3,2,1,0:T(8,128)(2,1)}), bf16[4,4,128,512]{3,2,1,0:T(8,128)(2,1)S(1)}, u32[]{:S(2)}, u32[]{:S(2)}) %all-to-all-start.2) | async-done | bytes 2097184 | tf_op jit(solution)/shard_map/all_to_all | solution.py:25
  81.3 12.8 %all-to-all-start.8 = ((f32[16,2,128]{2,1,0:T(2,128)}), f32[16,2,128]{2,1,0:T(2,128)S(1)}, u32[]{:S(2)}, u32[]{:S(2)}) async-start(f32[16,2,128]{2,1,0:T(2,128)} %broadcast_in_dim.30), calls=%async_computation.8 | async-start | bytes 32768 | tf_op jit(solution)/shard_map/all_to_all | solution.py:25
  99.6 8.0 %all-to-all-done.8 = f32[16,2,128]{2,1,0:T(2,128)S(1)} async-done(((f32[16,2,128]{2,1,0:T(2,128)}), f32[16,2,128]{2,1,0:T(2,128)S(1)}, u32[]{:S(2)}, u32[]{:S(2)}) %all-to-all-start.8) | async-done | bytes 16416 | tf_op jit(solution)/shard_map/all_to_all | solution.py:25
  107.5 8.4 %all_to_all.76 = bf16[4,128,128]{2,1,0:T(8,128)(2,1)S(1)} all-to-all(bf16[4,128,128]{2,1,0:T(8,128)(2,1)S(1)} %get-tuple-element.6), channel_id=1, replica_groups=mesh['phase'=8,'x'=4,'za'=2,'zb'=2,'seq'=4] {'x'}, dimensions={0} | all-to-all | bytes 262144 | tf_op jit(solution)/shard_map/all_to_all | solution.py:254
  115.9 17.3 %all_to_all.77 = bf16[4,128,128]{2,1,0:T(8,128)(2,1)S(1)} all-to-all(bf16[4,128,128]{2,1,0:T(8,128)(2,1)S(1)} %all_to_all.76), channel_id=1, replica_groups=mesh['phase'=8,'x'=4,'za'=2,'zb'=2,'seq'=4] {'seq'}, dimensions={0} | all-to-all | bytes 262144 | tf_op jit(solution)/shard_map/all_to_all | solution.py:254
  133.2 5.6 %all-to-all-start.3 = ((bf16[4,512,128]{2,1,0:T(8,128)(2,1)}), bf16[4,512,128]{2,1,0:T(8,128)(2,1)}, u32[]{:S(2)}, u32[]{:S(2)}) async-start(bf16[4,512,128]{2,1,0:T(8,128)(2,1)} %get-tuple-element.5), calls=%async_computation.3 | async-start | bytes 1048576 | tf_op jit(solution)/shard_map/all_to_all | solution.py:256
  138.8 6.8 %all-to-all-done.3 = bf16[4,512,128]{2,1,0:T(8,128)(2,1)} async-done(((bf16[4,512,128]{2,1,0:T(8,128)(2,1)}), bf16[4,512,128]{2,1,0:T(8,128)(2,1)}, u32[]{:S(2)}, u32[]{:S(2)}) %all-to-all-start.3) | async-done | bytes 524320 | tf_op jit(solution)/shard_map/all_to_all | solution.py:256
  145.6 13.9 %all_to_all.78.kv_in = bf16[8,128,128]{2,1,0:T(8,128)(2,1)S(1)} all-to-all(bf16[8,128,128]{2,1,0:T(8,128)(2,1)S(1)} %broadcast_in_dim.29), channel_id=1, replica_groups=mesh['phase'=8,'x'=4,'za'=2,'zb'=2,'seq'=4] {'x','zb'}, dimensions={0} | all-to-all | bytes 524288 | tf_op jit(solution)/shard_map/all_to_all | solution.py:25
  163.2 18.2 %all-to-all-done.4.q_in = bf16[4,512,128]{2,1,0:T(8,128)(2,1)S(1)} async-done(((bf16[4,512,128]{2,1,0:T(8,128)(2,1)}), bf16[4,512,128]{2,1,0:T(8,128)(2,1)S(1)}, u32[]{:S(2)}, u32[]{:S(2)}) %all-to-all-start.4) | async-done | bytes 524320 | tf_op jit(solution)/shard_map/all_to_all | solution.py:256
  182.3 7.2 %all-to-all-start.14 = ((bf16[4,128,512]{1,2,0:T(8,128)(2,1)}), bf16[4,128,512]{1,2,0:T(8,128)(2,1)}, u32[]{:S(2)}, u32[]{:S(2)}) async-start(bf16[4,128,512]{1,2,0:T(8,128)(2,1)} %broadcast_in_dim.37), calls=%async_computation.14 | async-start | bytes 1048576 | tf_op jit(solution)/shard_map/all_to_all | solution.py:25
  199.0 4.4 %attend.1 = bf16[128,512]{1,0:T(8,128)(2,1)S(1)} custom-call(s32[3]{0:T(128)S(1)} %pad_add_fusion.place, bf16[4,512,128]{2,1,0:T(8,128)(2,1)S(1)} %all-to-all-done.4.q_in, bf16[8,128,128]{2,1,0:T(8,128)(2,1)S(1)} %all_to_all.78.kv_in, f32[128,1]{1,0:T(8,128)S(1)} %copy-done.10, f32[1,512]{1,0:T(1,128)S(1)} %bitcast.66, f32[128,1]{1,0:T(8,128)S(1)} %copy-done.9, ...), custom_call_target="tpu_custom_call" | custom-call | tf_op jit(solution)/shard_map/attend/pallas_call | solution.py:159
  204.1 4.1 %all-to-all-done.14 = bf16[4,128,512]{1,2,0:T(8,128)(2,1)} async-done(((bf16[4,128,512]{1,2,0:T(8,128)(2,1)}), bf16[4,128,512]{1,2,0:T(8,128)(2,1)}, u32[]{:S(2)}, u32[]{:S(2)}) %all-to-all-start.14) | async-done | bytes 524320 | tf_op jit(solution)/shard_map/all_to_all | solution.py:25
  209.9 21.3 %all_to_all.79 = bf16[4,128,512]{2,1,0:T(8,128)(2,1)} all-to-all(bf16[4,128,512]{2,1,0:T(8,128)(2,1)} %broadcast_in_dim.34), channel_id=1, replica_groups=mesh['phase'=8,'x'=4,'za'=2,'zb'=2,'seq'=4] {'za','zb'}, dimensions={0} | all-to-all | bytes 1048576 | tf_op jit(solution)/shard_map/all_to_all | solution.py:25
  231.3 12.4 %all-to-all-start.9 = ((bf16[4,128,512]{2,1,0:T(8,128)(2,1)}), bf16[4,128,512]{2,1,0:T(8,128)(2,1)S(1)}, u32[]{:S(2)}, u32[]{:S(2)}) async-start(bf16[4,128,512]{2,1,0:T(8,128)(2,1)} %broadcast_in_dim.34), calls=%async_computation.9 | async-start | bytes 1048576 | tf_op jit(solution)/shard_map/all_to_all | solution.py:25
  245.0 20.6 %all-to-all-done.9 = bf16[4,128,512]{2,1,0:T(8,128)(2,1)S(1)} async-done(((bf16[4,128,512]{2,1,0:T(8,128)(2,1)}), bf16[4,128,512]{2,1,0:T(8,128)(2,1)S(1)}, u32[]{:S(2)}, u32[]{:S(2)}) %all-to-all-start.9) | async-done | bytes 524320 | tf_op jit(solution)/shard_map/all_to_all | solution.py:25
  265.5 24.5 %all_to_all.80 = f32[16,2,128]{2,1,0:T(2,128)S(1)} all-to-all(f32[16,2,128]{2,1,0:T(2,128)S(1)} %broadcast_in_dim.35), channel_id=1, replica_groups=mesh['phase'=8,'x'=4,'za'=2,'zb'=2,'seq'=4] {'x','seq'}, dimensions={0} | all-to-all | bytes 32768 | tf_op jit(solution)/shard_map/all_to_all | solution.py:25
  290.0 11.2 %all_to_all.81 = bf16[4,128,512]{2,1,0:T(8,128)(2,1)} all-to-all(bf16[4,128,512]{2,1,0:T(8,128)(2,1)S(1)} %all-to-all-done.9), channel_id=1, replica_groups=mesh['phase'=8,'x'=4,'za'=2,'zb'=2,'seq'=4] {'x'}, dimensions={0} | all-to-all | bytes 1048576 | tf_op jit(solution)/shard_map/all_to_all | solution.py:283
  302.7 6.0 %all-to-all-start.13 = ((bf16[4,4,128,512]{3,2,1,0:T(8,128)(2,1)}), bf16[4,4,128,512]{3,2,1,0:T(8,128)(2,1)}, u32[]{:S(2)}, u32[]{:S(2)}) async-start(bf16[4,4,128,512]{3,2,1,0:T(8,128)(2,1)} %broadcast_in_dim.36), calls=%async_computation.13 | async-start | bytes 4194304 | tf_op jit(solution)/shard_map/all_to_all | solution.py:25
  314.2 15.9 %collective-permute-done.1 = bf16[128,512]{1,0:T(8,128)(2,1)S(1)} collective-permute-done((bf16[128,512]{1,0:T(8,128)(2,1)S(1)}, bf16[128,512]{1,0:T(8,128)(2,1)S(1)}, u32[]{:S(2)}, u32[]{:S(2)}) %collective-permute-start.1) | collective-permute-done | bytes 131104 | tf_op jit(solution)/shard_map/ppermute | solution.py:51
  331.7 4.6 %hessian.3 = bf16[512,2048]{1,0:T(8,128)(2,1)} custom-call(s32[3]{0:T(128)S(1)} %pad_add_fusion.place, bf16[512,512]{1,0:T(8,128)(2,1)S(1)} %fusion.6.left, bf16[4,4,128,512]{3,2,1,0:T(8,128)(2,1)} %all-to-all-done.13.cols, bf16[512,2048]{1,0:T(8,128)(2,1)S(1)} %copy-done.1), custom_call_target="tpu_custom_call" | custom-call | tf_op jit(solution)/shard_map/hessian/pallas_call | solution.py:209
  (93 shorter events, 41.0 us)
Async XLA Ops:
  0.6 30.4 %collective-permute-start = (bf16[128,512]{1,0:T(8,128)(2,1)}, bf16[128,512]{1,0:T(8,128)(2,1)S(1)}, u32[]{:S(2)}, u32[]{:S(2)}) collective-permute-start(bf16[128,512]{1,0:T(8,128)(2,1)} %bitcast.69), channel_id=1, source_target_pairs={{0,0},{1,16},{2,32},{3,48},{4,4},{5,20},{6,36},{7,52},{8,8},{9,24}... | collective-permute-start | bytes 393224 | tf_op jit(solution)/shard_map/ppermute | solution.py:36
  31.9 17.9 %all-to-all-start = ((bf16[4,128,512]{2,1,0:T(8,128)(2,1)}), bf16[4,128,512]{2,1,0:T(8,128)(2,1)S(1)}, u32[]{:S(2)}, u32[]{:S(2)}) async-start(bf16[4,128,512]{2,1,0:T(8,128)(2,1)} %broadcast_in_dim.26), calls=%async_computation | async-start | bytes 1048576 | tf_op jit(solution)/shard_map/all_to_all | solution.py:25
  51.6 5.0 %copy-start.19 = (s32[1,128]{1,0:T(1,128)S(1)}, s32[1,128]{1,0:T(1,128)}, u32[]{:S(2)}) copy-start(s32[1,128]{1,0:T(1,128)} %param.8) | copy-start | bytes 1540
  51.6 42.5 %copy-start.5 = (bf16[1,2048,64]{1,2,0:T(8,128)(2,1)S(1)}, bf16[1,2048,64]{1,2,0:T(8,128)(2,1)}, u32[]{:S(2)}) copy-start(bf16[1,2048,64]{1,2,0:T(8,128)(2,1)} %param.12) | copy-start | bytes 786436
  51.6 42.5 %copy-start.6 = (bf16[1,2048,64]{1,2,0:T(8,128)(2,1)S(1)}, bf16[1,2048,64]{1,2,0:T(8,128)(2,1)}, u32[]{:S(2)}) copy-start(bf16[1,2048,64]{1,2,0:T(8,128)(2,1)} %param.13) | copy-start | bytes 786436
  51.6 29.1 %all-to-all-start.2 = ((bf16[4,4,128,512]{3,2,1,0:T(8,128)(2,1)}), bf16[4,4,128,512]{3,2,1,0:T(8,128)(2,1)S(1)}, u32[]{:S(2)}, u32[]{:S(2)}) async-start(bf16[4,4,128,512]{3,2,1,0:T(8,128)(2,1)} %broadcast_in_dim.28), calls=%async_computation.2 | async-start | bytes 4194304 | tf_op jit(solution)/shard_map/all_to_all | solution.py:25
  81.3 26.3 %all-to-all-start.8 = ((f32[16,2,128]{2,1,0:T(2,128)}), f32[16,2,128]{2,1,0:T(2,128)S(1)}, u32[]{:S(2)}, u32[]{:S(2)}) async-start(f32[16,2,128]{2,1,0:T(2,128)} %broadcast_in_dim.30), calls=%async_computation.8 | async-start | bytes 32768 | tf_op jit(solution)/shard_map/all_to_all | solution.py:25
  94.1 1.6 copy-start.2
  99.6 63.5 %copy-start.12 = (bf16[1,128,512]{2,1,0:T(8,128)(2,1)S(1)}, bf16[1,128,512]{2,1,0:T(8,128)(2,1)}, u32[]{:S(2)}) copy-start(bf16[1,128,512]{2,1,0:T(8,128)(2,1)} %param.7) | copy-start | bytes 393220
  107.5 52.0 %copy-start.13 = (f32[16,2,128]{2,1,0:T(2,128)}, f32[16,2,128]{2,1,0:T(2,128)S(1)}, u32[]{:S(2)}) copy-start(f32[16,2,128]{2,1,0:T(2,128)S(1)} %all-to-all-done.8) | copy-start | bytes 49156
  133.2 12.3 %all-to-all-start.3 = ((bf16[4,512,128]{2,1,0:T(8,128)(2,1)}), bf16[4,512,128]{2,1,0:T(8,128)(2,1)}, u32[]{:S(2)}, u32[]{:S(2)}) async-start(bf16[4,512,128]{2,1,0:T(8,128)(2,1)} %get-tuple-element.5), calls=%async_computation.3 | async-start | bytes 1048576 | tf_op jit(solution)/shard_map/all_to_all | solution.py:256
  159.6 21.9 %all-to-all-start.4 = ((bf16[4,512,128]{2,1,0:T(8,128)(2,1)}), bf16[4,512,128]{2,1,0:T(8,128)(2,1)S(1)}, u32[]{:S(2)}, u32[]{:S(2)}) async-start(bf16[4,512,128]{2,1,0:T(8,128)(2,1)} %all-to-all-done.3), calls=%async_computation.4 | async-start | bytes 1048576 | tf_op jit(solution)/shard_map/all_to_all | solution.py:256
  182.3 25.9 %all-to-all-start.14 = ((bf16[4,128,512]{1,2,0:T(8,128)(2,1)}), bf16[4,128,512]{1,2,0:T(8,128)(2,1)}, u32[]{:S(2)}, u32[]{:S(2)}) async-start(bf16[4,128,512]{1,2,0:T(8,128)(2,1)} %broadcast_in_dim.37), calls=%async_computation.14 | async-start | bytes 1048576 | tf_op jit(solution)/shard_map/all_to_all | solution.py:25
  204.1 39.6 %copy-start.14 = (f32[4,1,512]{2,1,0:T(1,128)S(1)}, f32[4,1,512]{2,1,0:T(1,128)}, u32[]{:S(2)}) copy-start(f32[4,1,512]{2,1,0:T(1,128)} %get-tuple-element.11) | copy-start | bytes 24580
  204.1 40.9 %copy-start.18 = (f32[1,128]{1,0:T(1,128)S(1)}, f32[1,128]{1,0:T(1,128)}, u32[]{:S(2)}) copy-start(f32[1,128]{1,0:T(1,128)} %copy-done.17) | copy-start | bytes 1540
  231.3 34.2 %all-to-all-start.9 = ((bf16[4,128,512]{2,1,0:T(8,128)(2,1)}), bf16[4,128,512]{2,1,0:T(8,128)(2,1)S(1)}, u32[]{:S(2)}, u32[]{:S(2)}) async-start(bf16[4,128,512]{2,1,0:T(8,128)(2,1)} %broadcast_in_dim.34), calls=%async_computation.9 | async-start | bytes 1048576 | tf_op jit(solution)/shard_map/all_to_all | solution.py:25
  302.7 6.0 %copy-start.15 = (bf16[1,512]{1,0:T(2,128)(2,1)S(1)}, bf16[1,512]{1,0:T(2,128)(2,1)}, u32[]{:S(2)}) copy-start(bf16[1,512]{1,0:T(2,128)(2,1)} %param.9) | copy-start | bytes 3076
  302.7 6.0 %copy-start.16 = (bf16[1,512]{1,0:T(2,128)(2,1)S(1)}, bf16[1,512]{1,0:T(2,128)(2,1)}, u32[]{:S(2)}) copy-start(bf16[1,512]{1,0:T(2,128)(2,1)} %param.10) | copy-start | bytes 3076
  302.7 6.1 %copy-start.4 = (bf16[128,512]{1,0:T(8,128)(2,1)S(1)}, bf16[128,512]{1,0:T(8,128)(2,1)}, u32[]{:S(2)}) copy-start(bf16[128,512]{1,0:T(8,128)(2,1)} %copy-done.3) | copy-start | bytes 393220
  302.7 28.5 %all-to-all-start.13 = ((bf16[4,4,128,512]{3,2,1,0:T(8,128)(2,1)}), bf16[4,4,128,512]{3,2,1,0:T(8,128)(2,1)}, u32[]{:S(2)}, u32[]{:S(2)}) async-start(bf16[4,4,128,512]{3,2,1,0:T(8,128)(2,1)} %broadcast_in_dim.36), calls=%async_computation.13 | async-start | bytes 4194304 | tf_op jit(solution)/shard_map/all_to_all | solution.py:25
  308.8 21.3 %collective-permute-start.1 = (bf16[128,512]{1,0:T(8,128)(2,1)S(1)}, bf16[128,512]{1,0:T(8,128)(2,1)S(1)}, u32[]{:S(2)}, u32[]{:S(2)}) collective-permute-start(bf16[128,512]{1,0:T(8,128)(2,1)S(1)} %copy-done.4), channel_id=1, source_target_pairs={{0,64},{1,80},{2,96},{3,112},{4,68},{5,84},{6,100},{7,116},{8,72},... | collective-permute-start | bytes 393224 | tf_op jit(solution)/shard_map/ppermute | solution.py:51
  311.9 18.3 %copy-start.11 = (bf16[4,128,512]{2,1,0:T(8,128)(2,1)S(1)}, bf16[4,128,512]{2,1,0:T(8,128)(2,1)}, u32[]{:S(2)}) copy-start(bf16[4,128,512]{2,1,0:T(8,128)(2,1)} %all_to_all.81) | copy-start | bytes 1572868
  312.9 1.3 copy-start
  330.1 1.6 copy-start.1
  (6 other events, 4.6 us)

commit v3 on v2

v3 whole, which is shorter than its diff:
```python
import jax
import jax.numpy as jnp
from jax import lax
from jax.experimental import pallas as pl
from jax.experimental.pallas import tpu as pltpu
from jax.sharding import Mesh, PartitionSpec as P

HD = 128
norm_eps = 1e-05
rope_base = 500000.0
ZL = ("za", "zb")
TENSOR = ("x", "za", "zb")
GROUP = TENSOR + ("seq",)
f32 = jnp.float32
bf16 = jnp.bfloat16
LIMIT = 24 * 1024 * 1024


def swap_x_seq(value):
    nx, nz, ns = lax.axis_size("x"), lax.axis_size(ZL), lax.axis_size("seq")
    pairs = [
        ((x * nz + z) * ns + s, (s * nz + z) * ns + x)
        for x in range(nx)
        for z in range(nz)
        for s in range(ns)
    ]
    return lax.ppermute(value, GROUP, pairs)


def three_parts(value):
    parts = []
    for _ in range(3):
        part = lax.reduce_precision(value, 8, 7)
        parts.append(part.astype(bf16))
        value = value - part
    return jnp.stack(parts)


def pad_to(rows, count, width):
    return jnp.pad(rows, ((0, count - rows.shape[0]), (0, width - rows.shape[1])))


def project_kernel(cols, gain, wq, wk, wv, out, q_acc, kv_acc):
    step = pl.program_id(0)
    blocks, rows, feats = cols.shape
    left = (cols[...].reshape(blocks * rows, feats).astype(f32) * gain[...]).astype(bf16)
    kv_w = jnp.concatenate([wk[...], wv[...]], 0)
    kv = lax.dot_general(left, kv_w, (((1,), (1,)), ((), ())), preferred_element_type=f32)
    q = jnp.dot(left, wq[...], preferred_element_type=f32)

    @pl.when(step == 0)
    def _():
        q_acc[...] = q
        kv_acc[...] = kv

    @pl.when(step > 0)
    def _():
        q_acc[...] += q
        kv_acc[...] += kv

    @pl.when(step == pl.num_programs(0) - 1)
    def _():
        heads = q_acc.shape[1] // HD
        for k in range(blocks):
            block = pl.ds(k * rows, rows)
            out[k, pl.ds(heads * rows, rows), :] = kv_acc[block, :].astype(bf16)
            for h in range(heads):
                out[k, pl.ds(h * rows, rows), :] = q_acc[block, pl.ds(h * HD, HD)].astype(bf16)


def project(cols, gain, w_query, w_key, w_value):
    blocks, parts, rows, feats = cols.shape
    q_width, kv_width = w_query.shape[2], 2 * w_key.shape[2]
    heads = q_width // HD
    kv_spec = pl.BlockSpec((None, w_key.shape[2], feats), lambda z: (0, 0, z))
    return pl.pallas_call(
        project_kernel,
        grid=(parts,),
        in_specs=[
            pl.BlockSpec((blocks, None, rows, feats), lambda z: (0, z, 0, 0)),
            pl.BlockSpec((None, 1, feats), lambda z: (z, 0, 0)),
            pl.BlockSpec((None, feats, q_width), lambda z: (0, z, 0)),
            kv_spec,
            kv_spec,
        ],
        out_specs=pl.BlockSpec((blocks, (heads + 1) * rows, HD), lambda z: (0, 0, 0)),
        out_shape=jax.ShapeDtypeStruct((blocks, (heads + 1) * rows, HD), bf16),
        scratch_shapes=[
            pltpu.VMEM((blocks * rows, q_width), f32),
            pltpu.VMEM((blocks * rows, kv_width), f32),
        ],
        compiler_params=pltpu.CompilerParams(vmem_limit_bytes=LIMIT),
        name="project",
    )(cols, gain, w_query, w_key.swapaxes(1, 2), w_value.swapaxes(1, 2))


def rotate(values, cosine, sine):
    return values * cosine + pltpu.roll(values, HD // 2, 1) * sine


def column_of(row):
    n = row.shape[1]
    same = lax.broadcasted_iota(jnp.int32, (n, n), 0) == lax.broadcasted_iota(jnp.int32, (n, n), 1)
    return jnp.sum(jnp.where(same, row, f32(0.0)), axis=1, keepdims=True)


def attend_kernel(
    place, q_in, kv_in, cos_own, sin_own, cos_all, sin_all, resid, copies, out,
    keys, values, r_all, docs_all, r_own, docs_own,
):
    rows = out.shape[0]
    tokens = keys.shape[0]

    @pl.when(pl.program_id(0) == 0)
    def _():
        lower = lax.broadcasted_iota(jnp.int32, (rows, HD), 1) < HD // 2
        for k in range(tokens // rows):
            first = kv_in[2 * k, pl.ds(0, rows), :].astype(f32)
            second = kv_in[2 * k + 1, pl.ds(0, rows), :].astype(f32)
            tail = kv_in[2 * k, pl.ds(rows, 16), :].astype(f32)
            block = pl.ds(k * rows, rows)
            key = jnp.where(lower, first, pltpu.roll(second, HD // 2, 1))
            keys[block, :] = rotate(key, cos_all[block, :], sin_all[block, :])
            values[block, :] = jnp.where(lower, pltpu.roll(first, HD // 2, 1), second)
            r = tail[0:1] + tail[1:2] + tail[2:3]
            r_all[:, block] = r
            docs_all[:, block] = tail[3:4]

            @pl.when(place[0] == k)
            def _():
                r_own[...] = column_of(r) * (1.0 / HD**0.5)
                docs_own[...] = column_of(tail[3:4])

    query = jnp.sum(q_in[...].astype(f32), axis=0)
    query = rotate(query, cos_own[...], sin_own[...]) * r_own[...]
    scores = lax.dot_general(
        query, keys[...], (((1,), (1,)), ((), ())),
        preferred_element_type=f32, precision=lax.Precision.HIGHEST,
    )
    scores = scores * r_all[...]
    key_ids = lax.broadcasted_iota(jnp.int32, scores.shape, 1)
    own_ids = lax.broadcasted_iota(jnp.int32, scores.shape, 0) + place[0] * rows
    allowed = (key_ids <= own_ids) & (docs_all[...] == docs_own[...])
    scores = jnp.where(allowed, scores, f32(-1e30))
    peak = jnp.max(scores, axis=-1, keepdims=True)
    weights = jnp.where(allowed, jnp.exp(scores - peak), f32(0.0))
    total = jnp.sum(weights, axis=-1, keepdims=True)
    context = jnp.dot(
        weights * r_all[...], values[...],
        preferred_element_type=f32, precision=lax.Precision.HIGHEST,
    ) / total
    result = (resid[...].astype(f32) + context).astype(bf16)
    out[...] = result
    for copy in range(copies.shape[0]):
        copies[copy] = result


def attend(place, q_in, kv_in, tables_own, tables_all, resid, copies):
    heads = q_in.shape[1] // HD - 1
    rows, feats, tokens = q_in.shape[1] // (heads + 1), heads * HD, tables_all[0].shape[0]
    whole = pl.BlockSpec(memory_space=pltpu.VMEM)
    return pl.pallas_call(
        attend_kernel,
        grid=(heads,),
        in_specs=[
            pl.BlockSpec(memory_space=pltpu.SMEM),
            pl.BlockSpec((q_in.shape[0], rows, HD), lambda h: (0, h, 0)),
        ]
        + [whole] * 5
        + [pl.BlockSpec((rows, HD), lambda h: (0, h))],
        out_specs=[
            pl.BlockSpec((copies, rows, HD), lambda h: (0, 0, h)),
            pl.BlockSpec((rows, HD), lambda h: (0, h)),
        ],
        out_shape=[
            jax.ShapeDtypeStruct((copies, rows, feats), bf16),
            jax.ShapeDtypeStruct((rows, feats), bf16),
        ],
        scratch_shapes=[
            pltpu.VMEM((tokens, HD), f32),
            pltpu.VMEM((tokens, HD), f32),
            pltpu.VMEM((1, tokens), f32),
            pltpu.VMEM((1, tokens), f32),
            pltpu.VMEM((rows, 1), f32),
            pltpu.VMEM((rows, 1), f32),
        ],
        compiler_params=pltpu.CompilerParams(vmem_limit_bytes=LIMIT),
        name="attend",
    )(place, q_in, kv_in, *tables_own, *tables_all, resid)


def product(left, cols, gain):
    blocks, rows, feats = cols.shape
    right = cols[...].reshape(blocks * rows, feats)
    return (jnp.dot(left[...], right, preferred_element_type=f32) * gain[...]).astype(bf16)


def upper_kernel(place, left, cols, gain, out):
    @pl.when(place[1] <= place[2] + pl.program_id(0))
    def _():
        out[...] = product(left, cols, gain)


def lower_kernel(place, left, cols, gain, upper, out):
    row, col = place[1], place[2] + pl.program_id(0)

    @pl.when(row < col)
    def _():
        out[...] = upper[...]

    @pl.when(row > col)
    def _():
        out[...] = product(left, cols, gain)

    @pl.when(row == col)
    def _():
        lower = product(left, cols, gain)
        row_ids = lax.broadcasted_iota(jnp.int32, lower.shape, 0)
        col_ids = lax.broadcasted_iota(jnp.int32, lower.shape, 1)
        out[...] = jnp.where(row_ids <= col_ids, upper[...], lower)


def hessian(kernel, place, left, cols, gain, *upper):
    blocks, parts, rows, feats = cols.shape
    tile = pl.BlockSpec((feats, feats), lambda z: (0, z))
    return pl.pallas_call(
        kernel,
        grid=(parts,),
        in_specs=[
            pl.BlockSpec(memory_space=pltpu.SMEM),
            pl.BlockSpec((feats, blocks * rows), lambda z: (0, 0)),
            pl.BlockSpec((blocks, None, rows, feats), lambda z: (0, z, 0, 0)),
            pl.BlockSpec((None, 1, feats), lambda z: (z, 0, 0)),
        ]
        + [tile] * len(upper),
        out_specs=tile,
        out_shape=jax.ShapeDtypeStruct((feats, parts * feats), bf16),
        compiler_params=pltpu.CompilerParams(vmem_limit_bytes=LIMIT),
        name="hessian",
    )(place, left, cols, gain, *upper)


def on_device(hidden, segment_ids, gain_attn, gain_ffn, w_query, w_key, w_value):
    x_pos = lax.axis_index("x")
    zl_pos = lax.axis_index(ZL)
    seq_pos = lax.axis_index("seq")
    nx, nz, ns = lax.axis_size("x"), lax.axis_size(ZL), lax.axis_size("seq")
    rows, feats = hidden.shape[1:]
    tokens = rows * ns
    width = feats * nx * nz
    scale = 2.0 / tokens
    place = jnp.stack([x_pos, x_pos * nz + zl_pos, seq_pos * nz]).astype(jnp.int32)

    def copied(value, count):
        return jnp.broadcast_to(value[None], (count,) + value.shape)

    def square_rows(group):
        group = group.astype(f32)
        return pad_to(three_parts(jnp.sum(group * group, axis=(0, 2))), 16, feats)

    def r_of(parts):
        return lax.rsqrt(jnp.sum(parts.astype(f32), axis=(0, 1)) / width + norm_eps)

    def left_side(blocks, gain, r):
        left = blocks.astype(f32).reshape(tokens, feats) * (r * r * scale)[:, None]
        return (left * gain.astype(f32)).astype(bf16).T

    resid = swap_x_seq(hidden[0])
    extra = swap_x_seq(
        pad_to(
            jnp.concatenate([gain_attn, gain_ffn, pad_to(segment_ids.astype(bf16), 1, feats)]),
            16,
            feats,
        )
    )
    group = lax.all_to_all(copied(jnp.concatenate([resid, extra]), nz), ZL, 0, 0)
    gain_a = group[:, rows : rows + 1].astype(f32)
    gain_f = group[:, rows + 1 : rows + 2].astype(f32)
    docs_own = extra[2, :rows]
    group = group[:, :rows]
    attn_cols = lax.all_to_all(copied(group, nx), "x", 0, 0)
    attn_rows = lax.all_gather(jnp.concatenate([hidden[0], square_rows(group)]), "seq")
    r_own = r_of(attn_rows[:, rows : rows + 3, :rows])
    tail = jnp.concatenate([three_parts(r_own), docs_own[None]])
    tail = pad_to(tail, 16, HD)

    message = project(attn_cols, gain_a, w_query, w_key, w_value)
    message = lax.all_to_all(message, "x", 0, 0)
    arrived = lax.all_to_all(message, "seq", 0, 0)
    heads = feats // HD
    kv = jnp.sum(arrived[:, heads * rows :].astype(f32), axis=0).astype(bf16)
    kv_all = lax.all_to_all(copied(jnp.concatenate([kv, tail]), 2 * nx), ("x", "zb"), 0, 0)

    half = HD // 2
    freq = rope_base ** (-(jnp.arange(half, dtype=f32) * 2.0 / HD))
    angle = jnp.arange(tokens, dtype=f32)[:, None] * freq[None, :]
    cosine, sine = jnp.cos(angle), jnp.sin(angle)
    tables = (jnp.concatenate([cosine] * 2, 1), jnp.concatenate([-sine, sine], 1))
    own = tuple(lax.dynamic_slice_in_dim(t, x_pos * rows, rows) for t in tables)
    copies, section_out = attend(place, arrived, kv_all, own, tables, resid, nz)

    r_attn = jnp.sum(
        kv_all.reshape(nx, 2, rows + 16, HD)[:, 0, rows : rows + 3].astype(f32), axis=1
    ).reshape(tokens)
    attn_left = left_side(attn_rows[:, :rows], gain_attn, r_attn)
    upper = hessian(upper_kernel, place, attn_left, attn_cols, gain_a)

    group = lax.all_to_all(copies, ZL, 0, 0)
    out_rows = swap_x_seq(section_out)
    count = lax.axis_size("phase")
    passed = lax.ppermute(out_rows, "phase", [(p, (p + 1) % count) for p in range(count)])[None]
    ffn_cols = lax.all_to_all(copied(group, nx), "x", 0, 0)
    ffn_rows = lax.all_gather(jnp.concatenate([out_rows, square_rows(group)]), "seq")
    r_ffn = lax.all_gather(r_of(ffn_rows[:, rows : rows + 3, :rows]), "x", tiled=True)
    ffn_rows = ffn_rows[:, :rows]
    ffn_left = left_side(ffn_rows, gain_ffn, r_ffn)
    hessians = hessian(lower_kernel, place, ffn_left, ffn_cols, gain_f, upper)[None]
    diag_width = feats // ns
    own_cols = lax.dynamic_slice_in_dim(
        ffn_rows.reshape(tokens, feats), seq_pos * diag_width, diag_width, 1
    ).astype(f32)
    own_gain = lax.dynamic_slice_in_dim(gain_ffn[0], seq_pos * diag_width, diag_width)
    own_cols = own_cols * r_ffn[:, None] * own_gain.astype(f32)
    ffn_diagonal = (jnp.sum(own_cols * own_cols, axis=0) * scale)[None]
    return (passed, hessians, ffn_diagonal)


def solution(mesh):
    phase, tensor, seq = (mesh.shape[a] for a in ("phase", "tensor", "seq"))
    lines = Mesh(
        mesh.devices.reshape(phase, tensor // 4, 2, 2, seq), ("phase", "x", "za", "zb", "seq")
    )
    tiled = P("phase", "seq", TENSOR)
    return jax.shard_map(
        on_device,
        mesh=lines,
        in_specs=(
            tiled,
            P("phase", "seq"),
            P("phase", TENSOR),
            P("phase", TENSOR),
            tiled,
            tiled,
            tiled,
        ),
        out_specs=(tiled, P("phase", TENSOR, "seq"), P("phase", GROUP)),
        check_vma=False,
    )
```

time: 338 us -> 279 us (0.83)
  the two profiles are of different devices: /device:TPU:2 before, /device:TPU:1 now
where the time goes in v3:
time: 279 us; the launch traced here: 276 us
  blocking collectives  132 us (47%)
  starting transfers between devices  75.3 us (27%)
  waiting for transfers between devices  27.5 us (10%)
  local copies, waits for them, and re-layouts  15.1 us (5%)
  Pallas kernels  15.1 us (5%)
  other arithmetic  10.7 us (4%)
    all_gather x1, blocking collectives, on_device(): lax.all_gather(jnp.concatenate([hidden[0], square_rows(group)]), 'seq')  55.9 us
    all_gather x1, blocking collectives, on_device(): lax.all_gather(jnp.concatenate([out_rows, square_rows(group)]), 'seq')  36.1 us
    all_to_all x1, starting transfers between devices, on_device(): attn_cols = lax.all_to_all(copied(group, nx), 'x', 0, 0)  29.4 us
    all_to_all x1, waiting for transfers between devices, on_device(): attn_cols = lax.all_to_all(copied(group, nx), 'x', 0, 0)  23.8 us
    all_to_all x1, blocking collectives, on_device(): lax.all_to_all(copied(jnp.concatenate([resid, extra]), nz), ZL, 0, 0)  21.6 us
    all_to_all x1, starting transfers between devices, on_device(): ffn_cols = lax.all_to_all(copied(group, nx), 'x', 0, 0)  21.1 us
    all_to_all x1, starting transfers between devices, on_device(): arrived = lax.all_to_all(message, 'seq', 0, 0)  11.4 us
    unnamed x30, local copies, waits for them, and re-layouts  10.9 us
  transfers between devices with their start and end apart: 9, of which 2 were waited for; matrix products, arithmetic and copies ran while one was open for 5% of the time, Pallas kernels for 1%

profile of v3, /device:TPU:1, one launch (start us, length us, event | category | flops | bytes accessed | tf_op | source)
XLA Modules:
  0.0 276.4 jit_solution(17364875000994185920)
XLA Ops:
  0.6 1.6 collective-permute-start
  4.3 21.6 %all_to_all.35 = bf16[4,144,512]{2,1,0:T(8,128)(2,1)S(1)} all-to-all(bf16[4,144,512]{2,1,0:T(8,128)(2,1)S(1)} %broadcast_in_dim.12), channel_id=1, replica_groups=mesh['phase'=8,'x'=4,'za'=2,'zb'=2,'seq'=4] {'za','zb'}, dimensions={0} | all-to-all | bytes 1179648 | tf_op jit(solution)/shard_map/all_to_all | solution.py:276
  26.0 1.5 broadcast_in_dim.13
  27.5 29.4 %all-to-all-start.1 = ((bf16[4,4,128,512]{3,2,1,0:T(8,128)(2,1)}), bf16[4,4,128,512]{3,2,1,0:T(8,128)(2,1)S(1)}, u32[]{:S(2)}, u32[]{:S(2)}) async-start(bf16[4,4,128,512]{3,2,1,0:T(8,128)(2,1)} %broadcast_in_dim.13), calls=%async_computation.1 | async-start | bytes 4194304 | tf_op jit(solution)/shard_map/all_to_all | solution.py:281
  57.0 23.8 %all-to-all-done.1.cols = bf16[4,4,128,512]{3,2,1,0:T(8,128)(2,1)S(1)} async-done(((bf16[4,4,128,512]{3,2,1,0:T(8,128)(2,1)}), bf16[4,4,128,512]{3,2,1,0:T(8,128)(2,1)S(1)}, u32[]{:S(2)}, u32[]{:S(2)}) %all-to-all-start.1) | async-done | bytes 2097184 | tf_op jit(solution)/shard_map/all_to_all | solution.py:281
  80.8 1.6 copy-done.2
  82.4 3.1 %project.1 = bf16[4,640,128]{2,1,0:T(8,128)(2,1)S(1)} custom-call(bf16[4,4,128,512]{3,2,1,0:T(8,128)(2,1)S(1)} %all-to-all-done.1.cols, f32[4,1,512]{2,1,0:T(1,128)S(1)} %get-tuple-element.8.gain, bf16[1,2048,512]{2,1,0:T(8,128)(2,1)S(1)} %copy-done.2, bf16[1,64,2048]{2,1,0:T(8,128)(2,1)S(1)} %bitcast.63, bf16[1,64,2048]{2,1,0:T(8,128)(2,1)S(1)} %bitcast.64), custom_call_target="tpu_custom_call" | custom-call | tf_op jit(solution)/shard_map/project/pallas_call | solution.py:76
  85.5 10.7 %all_to_all.36 = bf16[4,640,128]{2,1,0:T(8,128)(2,1)} all-to-all(bf16[4,640,128]{2,1,0:T(8,128)(2,1)S(1)} %project.1), channel_id=1, replica_groups=mesh['phase'=8,'x'=4,'za'=2,'zb'=2,'seq'=4] {'x'}, dimensions={0} | all-to-all | bytes 1310720 | tf_op jit(solution)/shard_map/all_to_all | solution.py:288
  96.3 11.4 %all-to-all-start.3 = ((bf16[4,640,128]{2,1,0:T(8,128)(2,1)}), bf16[4,640,128]{2,1,0:T(8,128)(2,1)S(1)}, u32[]{:S(2)}, u32[]{:S(2)}) async-start(bf16[4,640,128]{2,1,0:T(8,128)(2,1)} %all_to_all.36), calls=%async_computation.3 | async-start | bytes 1310720 | tf_op jit(solution)/shard_map/all_to_all | solution.py:289
  108.8 55.9 %all-gather = bf16[576,512]{1,0:T(8,128)(2,1)S(1)} all-gather(bf16[144,512]{1,0:T(8,128)(2,1)S(1)} %pad_maximum_fusion.3), channel_id=2, replica_groups=mesh['phase'=8,'x'=4,'za'=2,'zb'=2,'seq'=4] {'seq'}, dimensions={0}, use_global_device_ids=true | all-gather | bytes 737280 | tf_op jit(solution)/shard_map/all_gather | solution.py:282
  166.4 3.4 %all-to-all-start.4 = ((bf16[8,144,128]{2,1,0:T(8,128)(2,1)}), bf16[8,144,128]{2,1,0:T(8,128)(2,1)S(1)}, u32[]{:S(2)}, u32[]{:S(2)}) async-start(bf16[8,144,128]{2,1,0:T(8,128)(2,1)} %broadcast_in_dim.14), calls=%async_computation.4 | async-start | bytes 589824 | tf_op jit(solution)/shard_map/all_to_all | solution.py:292
  172.5 3.6 %all-to-all-done.4.kv_in = bf16[8,144,128]{2,1,0:T(8,128)(2,1)S(1)} async-done(((bf16[8,144,128]{2,1,0:T(8,128)(2,1)}), bf16[8,144,128]{2,1,0:T(8,128)(2,1)S(1)}, u32[]{:S(2)}, u32[]{:S(2)}) %all-to-all-start.4) | async-done | bytes 294944 | tf_op jit(solution)/shard_map/all_to_all | solution.py:292
  177.9 5.0 %attend.1 = (bf16[4,128,512]{2,1,0:T(8,128)(2,1)S(1)}, bf16[128,512]{1,0:T(8,128)(2,1)S(1)}) custom-call(s32[3]{0:T(128)S(1)} %pad_add_fusion.place, bf16[4,640,128]{2,1,0:T(8,128)(2,1)S(1)} %all-to-all-done.3.q_in, bf16[8,144,128]{2,1,0:T(8,128)(2,1)S(1)} %all-to-all-done.4.kv_in, f32[128,128]{1,0:T(8,128)S(1)} %copy-done.5, ...), custom_call_target="tpu_custom_call" | custom-call | tf_op jit(solution)/shard_map/attend/pallas_call | solution.py:162
  184.4 3.5 %all-to-all-start.5 = ((bf16[4,128,512]{2,1,0:T(8,128)(2,1)}), bf16[4,128,512]{2,1,0:T(8,128)(2,1)S(1)}, u32[]{:S(2)}, u32[]{:S(2)}) async-start(bf16[4,128,512]{2,1,0:T(8,128)(2,1)} %copy-done.4), calls=%async_computation.5 | async-start | bytes 1048576 | tf_op jit(solution)/shard_map/all_to_all | solution.py:308
  188.0 2.1 slice_convert_fusion
  190.1 2.5 copy.18
  193.4 3.6 %collective-permute-start.3 = (bf16[128,512]{1,0:T(8,128)(2,1)S(1)}, bf16[128,512]{1,0:T(8,128)(2,1)S(1)}, u32[]{:S(2)}, u32[]{:S(2)}) collective-permute-start(bf16[128,512]{1,0:T(8,128)(2,1)S(1)} %collective-permute-done.2), channel_id=1, source_target_pairs={{0,64},{64,128},{128,192},{192,256},{256,320},{320,384},{384,448},... | collective-permute-start | bytes 393224 | tf_op jit(solution)/shard_map/ppermute | solution.py:311
  197.0 1.4 fusion.3.left
  198.4 2.7 hessian.2.upper
  202.6 1.5 broadcast_in_dim.16
  204.2 21.1 %all-to-all-start.6 = ((bf16[4,4,128,512]{3,2,1,0:T(8,128)(2,1)}), bf16[4,4,128,512]{3,2,1,0:T(8,128)(2,1)}, u32[]{:S(2)}, u32[]{:S(2)}) async-start(bf16[4,4,128,512]{3,2,1,0:T(8,128)(2,1)} %broadcast_in_dim.16), calls=%async_computation.6 | async-start | bytes 4194304 | tf_op jit(solution)/shard_map/all_to_all | solution.py:312
  225.3 36.1 %all-gather.1 = bf16[576,512]{1,0:T(8,128)(2,1)S(1)} all-gather(bf16[144,512]{1,0:T(8,128)(2,1)S(1)} %pad_maximum_fusion.4), channel_id=3, replica_groups=mesh['phase'=8,'x'=4,'za'=2,'zb'=2,'seq'=4] {'seq'}, dimensions={0}, use_global_device_ids=true | all-gather | bytes 737280 | tf_op jit(solution)/shard_map/all_gather | solution.py:313
  263.2 7.4 %all-gather.2 = f32[4,1,128]{2,1,0:T(1,128)S(1)} all-gather(f32[1,1,128]{2,1,0:T(1,128)S(1)} %rsqrt_bitcast_fusion), channel_id=1, replica_groups=mesh['phase'=8,'x'=4,'za'=2,'zb'=2,'seq'=4] {'x'}, dimensions={0}, use_global_device_ids=true | all-gather | bytes 2560 | tf_op jit(solution)/shard_map/all_gather | solution.py:314
  271.5 4.2 %hessian.3 = bf16[512,2048]{1,0:T(8,128)(2,1)} custom-call(s32[3]{0:T(128)S(1)} %pad_add_fusion.place, bf16[512,512]{1,0:T(8,128)(2,1)S(1)} %fusion.2.left, bf16[4,4,128,512]{3,2,1,0:T(8,128)(2,1)} %all-to-all-done.6.cols, f32[4,1,512]{2,1,0:T(1,128)S(1)} %get-tuple-element.7.gain, bf16[512,2048]{1,0:T(8,128)(2,1)S(1)} %copy-done.1), custom_call_target="tpu_custom_call" | custom-call | tf_op jit(solution)/shard_map/hessian/pallas_call | solution.py:226
  (77 shorter events, 16.4 us)
Async XLA Ops:
  0.6 3.6 %collective-permute-start = (bf16[128,512]{1,0:T(8,128)(2,1)}, bf16[128,512]{1,0:T(8,128)(2,1)S(1)}, u32[]{:S(2)}, u32[]{:S(2)}) collective-permute-start(bf16[128,512]{1,0:T(8,128)(2,1)} %bitcast.72), channel_id=1, source_target_pairs={{0,0},{1,16},{2,32},{3,48},{4,4},{5,20},{6,36},{7,52},{8,8},{9,24}... | collective-permute-start | bytes 393224 | tf_op jit(solution)/shard_map/ppermute | solution.py:27
  3.6 0.7 collective-permute-start.1
  27.5 53.3 %copy-start.6 = (bf16[1,2048,64]{1,2,0:T(8,128)(2,1)S(1)}, bf16[1,2048,64]{1,2,0:T(8,128)(2,1)}, u32[]{:S(2)}) copy-start(bf16[1,2048,64]{1,2,0:T(8,128)(2,1)} %param.12) | copy-start | bytes 786436
  27.5 53.3 %copy-start.7 = (bf16[1,2048,64]{1,2,0:T(8,128)(2,1)S(1)}, bf16[1,2048,64]{1,2,0:T(8,128)(2,1)}, u32[]{:S(2)}) copy-start(bf16[1,2048,64]{1,2,0:T(8,128)(2,1)} %param.13) | copy-start | bytes 786436
  27.5 53.3 %all-to-all-start.1 = ((bf16[4,4,128,512]{3,2,1,0:T(8,128)(2,1)}), bf16[4,4,128,512]{3,2,1,0:T(8,128)(2,1)S(1)}, u32[]{:S(2)}, u32[]{:S(2)}) async-start(bf16[4,4,128,512]{3,2,1,0:T(8,128)(2,1)} %broadcast_in_dim.13), calls=%async_computation.1 | async-start | bytes 4194304 | tf_op jit(solution)/shard_map/all_to_all | solution.py:281
  80.8 1.6 copy-start.2
  96.3 69.3 %all-to-all-start.3 = ((bf16[4,640,128]{2,1,0:T(8,128)(2,1)}), bf16[4,640,128]{2,1,0:T(8,128)(2,1)S(1)}, u32[]{:S(2)}, u32[]{:S(2)}) async-start(bf16[4,640,128]{2,1,0:T(8,128)(2,1)} %all_to_all.36), calls=%async_computation.3 | async-start | bytes 1310720 | tf_op jit(solution)/shard_map/all_to_all | solution.py:289
  164.7 0.8 copy-start.10
  166.4 9.8 %all-to-all-start.4 = ((bf16[8,144,128]{2,1,0:T(8,128)(2,1)}), bf16[8,144,128]{2,1,0:T(8,128)(2,1)S(1)}, u32[]{:S(2)}, u32[]{:S(2)}) async-start(bf16[8,144,128]{2,1,0:T(8,128)(2,1)} %broadcast_in_dim.14), calls=%async_computation.4 | async-start | bytes 589824 | tf_op jit(solution)/shard_map/all_to_all | solution.py:292
  171.6 16.3 %copy-start.12 = (bf16[1,512]{1,0:T(2,128)(2,1)S(1)}, bf16[1,512]{1,0:T(2,128)(2,1)}, u32[]{:S(2)}) copy-start(bf16[1,512]{1,0:T(2,128)(2,1)} %param.9) | copy-start | bytes 3076
  171.6 16.3 %copy-start.13 = (bf16[1,512]{1,0:T(2,128)(2,1)S(1)}, bf16[1,512]{1,0:T(2,128)(2,1)}, u32[]{:S(2)}) copy-start(bf16[1,512]{1,0:T(2,128)(2,1)} %param.10) | copy-start | bytes 3076
  176.2 1.0 copy-start.3
  177.1 0.8 copy-start.5
  183.0 0.8 copy-start.4
  183.8 0.7 copy-start.8
  184.4 18.0 %all-to-all-start.5 = ((bf16[4,128,512]{2,1,0:T(8,128)(2,1)}), bf16[4,128,512]{2,1,0:T(8,128)(2,1)S(1)}, u32[]{:S(2)}, u32[]{:S(2)}) async-start(bf16[4,128,512]{2,1,0:T(8,128)(2,1)} %copy-done.4), calls=%async_computation.5 | async-start | bytes 1048576 | tf_op jit(solution)/shard_map/all_to_all | solution.py:308
  187.9 4.8 %copy-start.9 = (bf16[128,512]{1,0:T(8,128)(2,1)S(1)}, bf16[128,512]{1,0:T(8,128)(2,1)}, u32[]{:S(2)}) copy-start(bf16[128,512]{1,0:T(8,128)(2,1)} %copy-done.8) | copy-start | bytes 393220
  192.7 0.7 collective-permute-start.2
  193.4 9.0 %collective-permute-start.3 = (bf16[128,512]{1,0:T(8,128)(2,1)S(1)}, bf16[128,512]{1,0:T(8,128)(2,1)S(1)}, u32[]{:S(2)}, u32[]{:S(2)}) collective-permute-start(bf16[128,512]{1,0:T(8,128)(2,1)S(1)} %collective-permute-done.2), channel_id=1, source_target_pairs={{0,64},{64,128},{128,192},{192,256},{256,320},{320,384},{384,448},... | collective-permute-start | bytes 393224 | tf_op jit(solution)/shard_map/ppermute | solution.py:311
  201.1 1.3 copy-start
  204.2 67.3 %all-to-all-start.6 = ((bf16[4,4,128,512]{3,2,1,0:T(8,128)(2,1)}), bf16[4,4,128,512]{3,2,1,0:T(8,128)(2,1)}, u32[]{:S(2)}, u32[]{:S(2)}) async-start(bf16[4,4,128,512]{3,2,1,0:T(8,128)(2,1)} %broadcast_in_dim.16), calls=%async_computation.6 | async-start | bytes 4194304 | tf_op jit(solution)/shard_map/all_to_all | solution.py:312
  225.3 46.2 %copy-start.1 = (bf16[512,2048]{1,0:T(8,128)(2,1)S(1)}, bf16[512,2048]{1,0:T(8,128)(2,1)}, u32[]{:S(2)}) copy-start(bf16[512,2048]{1,0:T(8,128)(2,1)} %copy-done) | copy-start | bytes 6291460
  261.4 0.8 copy-start.11

commit v4 on v3

--- a/solution.py
+++ b/solution.py
@@ -40,7 +40,7 @@
     return jnp.pad(rows, ((0, count - rows.shape[0]), (0, width - rows.shape[1])))
 
 
-def project_kernel(cols, gain, wq, wk, wv, out, q_acc, kv_acc):
+def project_kernel(cols, gain, wq, wk, wv, after, out, q_acc, kv_acc):
     step = pl.program_id(0)
     blocks, rows, feats = cols.shape
     left = (cols[...].reshape(blocks * rows, feats).astype(f32) * gain[...]).astype(bf16)
@@ -68,7 +68,7 @@
                 out[k, pl.ds(h * rows, rows), :] = q_acc[block, pl.ds(h * HD, HD)].astype(bf16)
 
 
-def project(cols, gain, w_query, w_key, w_value):
+def project(cols, gain, w_query, w_key, w_value, after):
     blocks, parts, rows, feats = cols.shape
     q_width, kv_width = w_query.shape[2], 2 * w_key.shape[2]
     heads = q_width // HD
@@ -82,6 +82,7 @@
             pl.BlockSpec((None, feats, q_width), lambda z: (0, z, 0)),
             kv_spec,
             kv_spec,
+            pl.BlockSpec(memory_space=pl.ANY),
         ],
         out_specs=pl.BlockSpec((blocks, (heads + 1) * rows, HD), lambda z: (0, 0, 0)),
         out_shape=jax.ShapeDtypeStruct((blocks, (heads + 1) * rows, HD), bf16),
@@ -91,7 +92,25 @@
         ],
         compiler_params=pltpu.CompilerParams(vmem_limit_bytes=LIMIT),
         name="project",
-    )(cols, gain, w_query, w_key.swapaxes(1, 2), w_value.swapaxes(1, 2))
+    )(cols, gain, w_query, w_key.swapaxes(1, 2), w_value.swapaxes(1, 2), after)
+
+
+def take_kernel(value, after, out):
+    out[...] = value[...]
+
+
+def take_after(value, count, after):
+    shape = (value.shape[0], count, value.shape[2])
+    spec = pl.BlockSpec((1, count, value.shape[2]), lambda i: (i, 0, 0))
+    return pl.pallas_call(
+        take_kernel,
+        grid=(value.shape[0],),
+        in_specs=[spec, pl.BlockSpec(memory_space=pl.ANY)],
+        out_specs=spec,
+        out_shape=jax.ShapeDtypeStruct(shape, value.dtype),
+        compiler_params=pltpu.CompilerParams(vmem_limit_bytes=LIMIT),
+        name="take_after",
+    )(value, after)
 
 
 def rotate(values, cosine, sine):
@@ -105,7 +124,7 @@
 
 
 def attend_kernel(
-    place, q_in, kv_in, cos_own, sin_own, cos_all, sin_all, resid, copies, out,
+    place, q_in, kv_own, kv_other, cos_own, sin_own, cos_all, sin_all, resid, copies, out,
     keys, values, r_all, docs_all, r_own, docs_own,
 ):
     rows = out.shape[0]
@@ -115,9 +134,11 @@
     def _():
         lower = lax.broadcasted_iota(jnp.int32, (rows, HD), 1) < HD // 2
         for k in range(tokens // rows):
-            first = kv_in[2 * k, pl.ds(0, rows), :].astype(f32)
-            second = kv_in[2 * k + 1, pl.ds(0, rows), :].astype(f32)
-            tail = kv_in[2 * k, pl.ds(rows, 16), :].astype(f32)
+            mine = kv_own[k, pl.ds(0, rows), :].astype(f32)
+            other = kv_other[k].astype(f32)
+            first = jnp.where(place[3] == 0, mine, other)
+            second = jnp.where(place[3] == 0, other, mine)
+            tail = kv_own[k, pl.ds(rows, 16), :].astype(f32)
             block = pl.ds(k * rows, rows)
             key = jnp.where(lower, first, pltpu.roll(second, HD // 2, 1))
             keys[block, :] = rotate(key, cos_all[block, :], sin_all[block, :])
@@ -155,9 +176,9 @@
         copies[copy] = result
 
 
-def attend(place, q_in, kv_in, tables_own, tables_all, resid, copies):
-    heads = q_in.shape[1] // HD - 1
-    rows, feats, tokens = q_in.shape[1] // (heads + 1), heads * HD, tables_all[0].shape[0]
+def attend(place, q_in, kv_own, kv_other, tables_own, tables_all, resid, copies):
+    rows, feats = resid.shape
+    heads, tokens = feats // HD, tables_all[0].shape[0]
     whole = pl.BlockSpec(memory_space=pltpu.VMEM)
     return pl.pallas_call(
         attend_kernel,
@@ -166,7 +187,7 @@
             pl.BlockSpec(memory_space=pltpu.SMEM),
             pl.BlockSpec((q_in.shape[0], rows, HD), lambda h: (0, h, 0)),
         ]
-        + [whole] * 5
+        + [whole] * 6
         + [pl.BlockSpec((rows, HD), lambda h: (0, h))],
         out_specs=[
             pl.BlockSpec((copies, rows, HD), lambda h: (0, 0, h)),
@@ -186,7 +207,7 @@
         ],
         compiler_params=pltpu.CompilerParams(vmem_limit_bytes=LIMIT),
         name="attend",
-    )(place, q_in, kv_in, *tables_own, *tables_all, resid)
+    )(place, q_in, kv_own, kv_other, *tables_own, *tables_all, resid)
 
 
 def product(left, cols, gain):
@@ -249,7 +270,8 @@
     tokens = rows * ns
     width = feats * nx * nz
     scale = 2.0 / tokens
-    place = jnp.stack([x_pos, x_pos * nz + zl_pos, seq_pos * nz]).astype(jnp.int32)
+    zb_pos = lax.axis_index("zb")
+    place = jnp.stack([x_pos, x_pos * nz + zl_pos, seq_pos * nz, zb_pos]).astype(jnp.int32)
 
     def copied(value, count):
         return jnp.broadcast_to(value[None], (count,) + value.shape)
@@ -284,12 +306,14 @@
     tail = jnp.concatenate([three_parts(r_own), docs_own[None]])
     tail = pad_to(tail, 16, HD)
 
-    message = project(attn_cols, gain_a, w_query, w_key, w_value)
+    message = project(attn_cols, gain_a, w_query, w_key, w_value, tail)
     message = lax.all_to_all(message, "x", 0, 0)
-    arrived = lax.all_to_all(message, "seq", 0, 0)
-    heads = feats // HD
-    kv = jnp.sum(arrived[:, heads * rows :].astype(f32), axis=0).astype(bf16)
-    kv_all = lax.all_to_all(copied(jnp.concatenate([kv, tail]), 2 * nx), ("x", "zb"), 0, 0)
+    q_rows = rows * feats // HD
+    kv = lax.all_to_all(message[:, q_rows:], "seq", 0, 0)
+    query = lax.all_to_all(take_after(message, q_rows, kv), "seq", 0, 0)
+    kv = jnp.sum(kv.astype(f32), axis=0).astype(bf16)
+    kv_all = lax.all_gather(jnp.concatenate([kv, tail]), "x")
+    kv_other = lax.ppermute(kv_all[:, :rows], "zb", [(0, 1), (1, 0)])
 
     half = HD // 2
     freq = rope_base ** (-(jnp.arange(half, dtype=f32) * 2.0 / HD))
@@ -297,22 +321,21 @@
     cosine, sine = jnp.cos(angle), jnp.sin(angle)
     tables = (jnp.concatenate([cosine] * 2, 1), jnp.concatenate([-sine, sine], 1))
     own = tuple(lax.dynamic_slice_in_dim(t, x_pos * rows, rows) for t in tables)
-    copies, section_out = attend(place, arrived, kv_all, own, tables, resid, nz)
-
-    r_attn = jnp.sum(
-        kv_all.reshape(nx, 2, rows + 16, HD)[:, 0, rows : rows + 3].astype(f32), axis=1
-    ).reshape(tokens)
+    copies, section_out = attend(place, query, kv_all, kv_other, own, tables, resid, nz)
+
+    r_attn = jnp.sum(kv_all[:, rows : rows + 3].astype(f32), axis=1).reshape(tokens)
     attn_left = left_side(attn_rows[:, :rows], gain_attn, r_attn)
     upper = hessian(upper_kernel, place, attn_left, attn_cols, gain_a)
 
     group = lax.all_to_all(copies, ZL, 0, 0)
     out_rows = swap_x_seq(section_out)
-    count = lax.axis_size("phase")
-    passed = lax.ppermute(out_rows, "phase", [(p, (p + 1) % count) for p in range(count)])[None]
     ffn_cols = lax.all_to_all(copied(group, nx), "x", 0, 0)
     ffn_rows = lax.all_gather(jnp.concatenate([out_rows, square_rows(group)]), "seq")
     r_ffn = lax.all_gather(r_of(ffn_rows[:, rows : rows + 3, :rows]), "x", tiled=True)
     ffn_rows = ffn_rows[:, :rows]
+    count = lax.axis_size("phase")
+    passed = lax.dynamic_slice_in_dim(ffn_rows, seq_pos, 1, 0)
+    passed = lax.ppermute(passed, "phase", [(p, (p + 1) % count) for p in range(count)])
     ffn_left = left_side(ffn_rows, gain_ffn, r_ffn)
     hessians = hessian(lower_kernel, place, ffn_left, ffn_cols, gain_f, upper)[None]
     diag_width = feats // ns

time: 279 us -> 254 us (0.910)
  waiting for transfers between devices: 27.5 us -> 11.6 us
  starting transfers between devices: 75.3 us -> 62.1 us
    all_to_all x1, waiting for transfers between devices: 23.8 us -> 0.01 us  [on_device(): attn_cols = lax.all_to_all(copied(group, nx), 'x', 0, 0)]
    all_gather x1, blocking collectives: 55.9 us -> 32.2 us  [on_device(): lax.all_gather(jnp.concatenate([hidden[0], square_rows(group)]), 'seq')]
    all_to_all x0 -> x1, blocking collectives: none -> 18.3 us  [on_device(): kv = lax.all_to_all(message[:, q_rows:], 'seq', 0, 0)]
    all_to_all x2 -> x1, starting transfers between devices: 14.8 us -> 3.47 us  [on_device(): query = lax.all_to_all(take_after(message, q_rows, kv), 'seq', 0, 0)]
    all_to_all x1, starting transfers between devices: 21.1 us -> 10.5 us  [on_device(): ffn_cols = lax.all_to_all(copied(group, nx), 'x', 0, 0)]
    all_gather x0 -> x1, blocking collectives: none -> 9.14 us  [on_device(): kv_all = lax.all_gather(jnp.concatenate([kv, tail]), 'x')]
    ppermute x1 -> x2, starting transfers between devices: 3.63 us -> 12.2 us  [the longest x1 10.3 us: on_device(): lax.ppermute(passed, 'phase', [(p, (p + 1) % count) for p in range(count)])]
    ppermute x1 -> x2, waiting for transfers between devices: 0.01 us -> 6.75 us  [the longest x1 6.75 us: on_device(): kv_other = lax.ppermute(kv_all[:, :rows], 'zb', [(0, 1), (1, 0)])]
  transfers between devices with their start and end apart: 9 -> 9, of which waited for: 2 -> 2; matrix products, arithmetic and copies ran while one was open for 5% -> 7% of each run, Pallas kernels for 1% -> 1%
where the time goes in v4:
time: 254 us; the launch traced here: 252 us
  blocking collectives  133 us (52%)
  starting transfers between devices  62.1 us (24%)
  Pallas kernels  16.4 us (6%)
  local copies, waits for them, and re-layouts  14.9 us (6%)
  other arithmetic  12.8 us (5%)
  waiting for transfers between devices  11.6 us (5%)
    all_gather x1, blocking collectives, on_device(): lax.all_gather(jnp.concatenate([out_rows, square_rows(group)]), 'seq')  36.6 us
    all_gather x1, blocking collectives, on_device(): lax.all_gather(jnp.concatenate([hidden[0], square_rows(group)]), 'seq')  32.2 us
    all_to_all x1, starting transfers between devices, on_device(): attn_cols = lax.all_to_all(copied(group, nx), 'x', 0, 0)  29.4 us
    all_to_all x1, blocking collectives, on_device(): lax.all_to_all(copied(jnp.concatenate([resid, extra]), nz), ZL, 0, 0)  21.6 us
    all_to_all x1, blocking collectives, on_device(): kv = lax.all_to_all(message[:, q_rows:], 'seq', 0, 0)  18.3 us
    unnamed x44, local copies, waits for them, and re-layouts  11.5 us
    all_to_all x1, starting transfers between devices, on_device(): ffn_cols = lax.all_to_all(copied(group, nx), 'x', 0, 0)  10.5 us
    ppermute x1, starting transfers between devices, on_device(): lax.ppermute(passed, 'phase', [(p, (p + 1) % count) for p in range(count)])  10.3 us
  transfers between devices with their start and end apart: 9, of which 2 were waited for; matrix products, arithmetic and copies ran while one was open for 7% of the time, Pallas kernels for 1%

profile of v4, /device:TPU:1, one launch (start us, length us, event | category | flops | bytes accessed | tf_op | source)
XLA Modules:
  0.0 251.9 jit_solution(12444425783316209345)
XLA Ops:
  0.6 1.6 collective-permute-start
  4.3 21.6 %all_to_all.35 = bf16[4,144,512]{2,1,0:T(8,128)(2,1)S(1)} all-to-all(bf16[4,144,512]{2,1,0:T(8,128)(2,1)S(1)} %broadcast_in_dim.8), channel_id=1, replica_groups=mesh['phase'=8,'x'=4,'za'=2,'zb'=2,'seq'=4] {'za','zb'}, dimensions={0} | all-to-all | bytes 1179648 | tf_op jit(solution)/shard_map/all_to_all | solution.py:298
  27.5 29.4 %all-to-all-start.1 = ((bf16[4,4,128,512]{3,2,1,0:T(8,128)(2,1)}), bf16[4,4,128,512]{3,2,1,0:T(8,128)(2,1)S(1)}, u32[]{:S(2)}, u32[]{:S(2)}) async-start(bf16[4,4,128,512]{3,2,1,0:T(8,128)(2,1)} %broadcast_in_dim.9), calls=%async_computation.1 | async-start | bytes 4194304 | tf_op jit(solution)/shard_map/all_to_all | solution.py:303
  57.2 32.2 %all-gather = bf16[576,512]{1,0:T(8,128)(2,1)S(1)} all-gather(bf16[144,512]{1,0:T(8,128)(2,1)S(1)} %pad_maximum_fusion.3), channel_id=2, replica_groups=mesh['phase'=8,'x'=4,'za'=2,'zb'=2,'seq'=4] {'seq'}, dimensions={0}, use_global_device_ids=true | all-gather | bytes 737280 | tf_op jit(solution)/shard_map/all_gather | solution.py:304
  90.9 1.6 copy-done.2
  92.5 3.1 %project.1 = bf16[4,640,128]{2,1,0:T(8,128)(2,1)S(1)} custom-call(bf16[4,4,128,512]{3,2,1,0:T(8,128)(2,1)S(1)} %all-to-all-done.1.cols, f32[4,1,512]{2,1,0:T(1,128)S(1)} %get-tuple-element.8.gain, bf16[1,2048,512]{2,1,0:T(8,128)(2,1)S(1)} %copy-done.2, bf16[1,64,2048]{2,1,0:T(8,128)(2,1)S(1)} %bitcast.65, bf16[1,64,2048]{2,1,0:T(8,128)(2,1)S(1)} %bitcast.66, ...), custom_call_target="tpu_custom_call" | custom-call | tf_op jit(solution)/shard_map/project/pallas_call | solution.py:76
  95.6 10.0 %all_to_all.36.value = bf16[4,640,128]{2,1,0:T(8,128)(2,1)S(1)} all-to-all(bf16[4,640,128]{2,1,0:T(8,128)(2,1)S(1)} %project.1), channel_id=1, replica_groups=mesh['phase'=8,'x'=4,'za'=2,'zb'=2,'seq'=4] {'x'}, dimensions={0} | all-to-all | bytes 1310720 | tf_op jit(solution)/shard_map/all_to_all | solution.py:310
  105.7 18.3 %all_to_all.37.after = bf16[4,128,128]{2,1,0:T(8,128)(2,1)S(1)} all-to-all(bf16[4,128,128]{2,1,0:T(8,128)(2,1)S(1)} %slice.48), channel_id=1, replica_groups=mesh['phase'=8,'x'=4,'za'=2,'zb'=2,'seq'=4] {'seq'}, dimensions={0} | all-to-all | bytes 262144 | tf_op jit(solution)/shard_map/all_to_all | solution.py:312
  125.4 3.5 %all-to-all-start.4 = ((bf16[4,512,128]{2,1,0:T(8,128)(2,1)}), bf16[4,512,128]{2,1,0:T(8,128)(2,1)S(1)}, u32[]{:S(2)}, u32[]{:S(2)}) async-start(bf16[4,512,128]{2,1,0:T(8,128)(2,1)} %take_after.1), calls=%async_computation.4 | async-start | bytes 1048576 | tf_op jit(solution)/shard_map/all_to_all | solution.py:313
  130.9 9.1 %all-gather.1 = bf16[576,128]{1,0:T(8,128)(2,1)S(1)} all-gather(bf16[144,128]{1,0:T(8,128)(2,1)S(1)} %pad_maximum_fusion.5), channel_id=3, replica_groups=mesh['phase'=8,'x'=4,'za'=2,'zb'=2,'seq'=4] {'x'}, dimensions={0}, use_global_device_ids=true | all-gather | bytes 184320 | tf_op jit(solution)/shard_map/all_gather | solution.py:315
  140.1 1.9 collective-permute-start.2
  144.1 6.8 %collective-permute-done.2.kv_other = bf16[4,128,128]{2,1,0:T(8,128)(2,1)S(1)} collective-permute-done((bf16[4,128,128]{2,1,0:T(8,128)(2,1)S(1)}, bf16[4,128,128]{2,1,0:T(8,128)(2,1)S(1)}, u32[]{:S(2)}, u32[]{:S(2)}) %collective-permute-start.2) | collective-permute-done | bytes 131104 | tf_op jit(solution)/shard_map/ppermute | solution.py:316
  151.5 4.8 %all-to-all-done.4.q_in = bf16[4,512,128]{2,1,0:T(8,128)(2,1)S(1)} async-done(((bf16[4,512,128]{2,1,0:T(8,128)(2,1)}), bf16[4,512,128]{2,1,0:T(8,128)(2,1)S(1)}, u32[]{:S(2)}, u32[]{:S(2)}) %all-to-all-start.4) | async-done | bytes 524320 | tf_op jit(solution)/shard_map/all_to_all | solution.py:313
  157.9 5.0 %attend.1 = (bf16[4,128,512]{2,1,0:T(8,128)(2,1)S(1)}, bf16[128,512]{1,0:T(8,128)(2,1)S(1)}) custom-call(s32[4]{0:T(128)S(1)} %copy-done.11, bf16[4,512,128]{2,1,0:T(8,128)(2,1)S(1)} %all-to-all-done.4.q_in, bf16[4,144,128]{2,1,0:T(8,128)(2,1)S(1)} %bitcast.63, bf16[4,128,128]{2,1,0:T(8,128)(2,1)S(1)} %copy-done.7, ...), custom_call_target="tpu_custom_call" | custom-call | tf_op jit(solution)/shard_map/attend/pallas_call | solution.py:183
  164.4 3.5 %all-to-all-start.5 = ((bf16[4,128,512]{2,1,0:T(8,128)(2,1)}), bf16[4,128,512]{2,1,0:T(8,128)(2,1)S(1)}, u32[]{:S(2)}, u32[]{:S(2)}) async-start(bf16[4,128,512]{2,1,0:T(8,128)(2,1)} %copy-done.3), calls=%async_computation.5 | async-start | bytes 1048576 | tf_op jit(solution)/shard_map/all_to_all | solution.py:330
  169.9 2.1 slice_convert_fusion
  172.0 2.6 %copy.17 = f32[4,128,512]{1,0,2:T(4,128)} copy(f32[4,128,512]{2,1,0:T(8,128)} %slice_convert_fusion) | data formatting | bytes 2097152
  176.0 2.7 %hessian.2.upper = bf16[512,2048]{1,0:T(8,128)(2,1)S(1)} custom-call(s32[4]{0:T(128)S(1)} %copy-done.12, bf16[512,512]{1,0:T(8,128)(2,1)S(1)} %fusion.3.left, bf16[4,4,128,512]{3,2,1,0:T(8,128)(2,1)S(1)} %all-to-all-done.1.cols, f32[4,1,512]{2,1,0:T(1,128)S(1)} %copy-done.9), custom_call_target="tpu_custom_call" | custom-call | tf_op jit(solution)/shard_map/hessian/pallas_call | solution.py:247
  180.9 1.5 broadcast_in_dim.10
  182.4 10.5 %all-to-all-start.6 = ((bf16[4,4,128,512]{3,2,1,0:T(8,128)(2,1)}), bf16[4,4,128,512]{3,2,1,0:T(8,128)(2,1)}, u32[]{:S(2)}, u32[]{:S(2)}) async-start(bf16[4,4,128,512]{3,2,1,0:T(8,128)(2,1)} %broadcast_in_dim.10), calls=%async_computation.6 | async-start | bytes 4194304 | tf_op jit(solution)/shard_map/all_to_all | solution.py:332
  193.0 36.6 %all-gather.2 = bf16[576,512]{1,0:T(8,128)(2,1)S(1)} all-gather(bf16[144,512]{1,0:T(8,128)(2,1)S(1)} %pad_maximum_fusion.4), channel_id=4, replica_groups=mesh['phase'=8,'x'=4,'za'=2,'zb'=2,'seq'=4] {'seq'}, dimensions={0}, use_global_device_ids=true | all-gather | bytes 737280 | tf_op jit(solution)/shard_map/all_gather | solution.py:333
  229.7 10.3 %collective-permute-start.4 = (bf16[1,128,512]{2,1,0:T(8,128)(2,1)S(1)}, bf16[1,128,512]{2,1,0:T(8,128)(2,1)S(1)}, u32[]{:S(2)}, u32[]{:S(2)}) collective-permute-start(bf16[1,128,512]{2,1,0:T(8,128)(2,1)S(1)} %constant_dynamic-slice_fusion.1), channel_id=1, source_target_pairs={{0,64},{64,128},{128,192},{192,256},{256,320},{320,384},{384,448},... | collective-permute-start | bytes 393224 | tf_op jit(solution)/shard_map/ppermute | solution.py:338
  241.0 5.2 %all-gather.3 = f32[4,1,128]{2,1,0:T(1,128)S(1)} all-gather(f32[1,1,128]{2,1,0:T(1,128)S(1)} %rsqrt_bitcast_fusion), channel_id=1, replica_groups=mesh['phase'=8,'x'=4,'za'=2,'zb'=2,'seq'=4] {'x'}, dimensions={0}, use_global_device_ids=true | all-gather | bytes 2560 | tf_op jit(solution)/shard_map/all_gather | solution.py:334
  247.0 4.2 %hessian.3 = bf16[512,2048]{1,0:T(8,128)(2,1)} custom-call(s32[4]{0:T(128)S(1)} %copy-done.12, bf16[512,512]{1,0:T(8,128)(2,1)S(1)} %fusion.2.left, bf16[4,4,128,512]{3,2,1,0:T(8,128)(2,1)} %all-to-all-done.6.cols, f32[4,1,512]{2,1,0:T(1,128)S(1)} %copy-done.10, bf16[512,2048]{1,0:T(8,128)(2,1)S(1)} %copy-done.1), custom_call_target="tpu_custom_call" | custom-call | tf_op jit(solution)/shard_map/hessian/pallas_call | solution.py:247
  (96 shorter events, 22.6 us)
Async XLA Ops:
  0.6 3.6 %collective-permute-start = (bf16[128,512]{1,0:T(8,128)(2,1)}, bf16[128,512]{1,0:T(8,128)(2,1)S(1)}, u32[]{:S(2)}, u32[]{:S(2)}) collective-permute-start(bf16[128,512]{1,0:T(8,128)(2,1)} %bitcast.74), channel_id=1, source_target_pairs={{0,0},{1,16},{2,32},{3,48},{4,4},{5,20},{6,36},{7,52},{8,8},{9,24}... | collective-permute-start | bytes 393224 | tf_op jit(solution)/shard_map/ppermute | solution.py:27
  3.6 0.7 collective-permute-start.1
  27.5 29.7 %copy-start.20 = (bf16[1,128,512]{2,1,0:T(8,128)(2,1)S(1)}, bf16[1,128,512]{2,1,0:T(8,128)(2,1)}, u32[]{:S(2)}) copy-start(bf16[1,128,512]{2,1,0:T(8,128)(2,1)} %param.7) | copy-start | bytes 393220
  27.5 63.4 %copy-start.4 = (bf16[1,2048,64]{1,2,0:T(8,128)(2,1)S(1)}, bf16[1,2048,64]{1,2,0:T(8,128)(2,1)}, u32[]{:S(2)}) copy-start(bf16[1,2048,64]{1,2,0:T(8,128)(2,1)} %param.12) | copy-start | bytes 786436
  27.5 63.4 %copy-start.5 = (bf16[1,2048,64]{1,2,0:T(8,128)(2,1)S(1)}, bf16[1,2048,64]{1,2,0:T(8,128)(2,1)}, u32[]{:S(2)}) copy-start(bf16[1,2048,64]{1,2,0:T(8,128)(2,1)} %param.13) | copy-start | bytes 786436
  27.5 63.4 %all-to-all-start.1 = ((bf16[4,4,128,512]{3,2,1,0:T(8,128)(2,1)}), bf16[4,4,128,512]{3,2,1,0:T(8,128)(2,1)S(1)}, u32[]{:S(2)}, u32[]{:S(2)}) async-start(bf16[4,4,128,512]{3,2,1,0:T(8,128)(2,1)} %broadcast_in_dim.9), calls=%async_computation.1 | async-start | bytes 4194304 | tf_op jit(solution)/shard_map/all_to_all | solution.py:303
  89.5 0.8 copy-start.18
  90.9 4.7 %copy-start.8 = (f32[4,1,512]{2,1,0:T(1,128)}, f32[4,1,512]{2,1,0:T(1,128)S(1)}, u32[]{:S(2)}) copy-start(f32[4,1,512]{2,1,0:T(1,128)S(1)} %get-tuple-element.8.gain) | copy-start | bytes 24580
  90.9 1.6 copy-start.2
  125.4 30.9 %all-to-all-start.4 = ((bf16[4,512,128]{2,1,0:T(8,128)(2,1)}), bf16[4,512,128]{2,1,0:T(8,128)(2,1)S(1)}, u32[]{:S(2)}, u32[]{:S(2)}) async-start(bf16[4,512,128]{2,1,0:T(8,128)(2,1)} %take_after.1), calls=%async_computation.4 | async-start | bytes 1048576 | tf_op jit(solution)/shard_map/all_to_all | solution.py:313
  129.9 0.9 copy-start.17
  140.1 10.7 %collective-permute-start.2 = (bf16[4,128,128]{2,1,0:T(8,128)(2,1)S(1)}, bf16[4,128,128]{2,1,0:T(8,128)(2,1)S(1)}, u32[]{:S(2)}, u32[]{:S(2)}) collective-permute-start(bf16[4,128,128]{2,1,0:T(8,128)(2,1)S(1)} %slice.49), channel_id=1, source_target_pairs={{0,4},{4,0},{1,5},{5,1},{2,6},{6,2},{3,7},{7,3},{8,12},{12,8},{9,1... | collective-permute-start | bytes 393224 | tf_op jit(solution)/shard_map/ppermute | solution.py:316
  156.3 0.9 copy-start.7
  164.4 16.3 %all-to-all-start.5 = ((bf16[4,128,512]{2,1,0:T(8,128)(2,1)}), bf16[4,128,512]{2,1,0:T(8,128)(2,1)S(1)}, u32[]{:S(2)}, u32[]{:S(2)}) async-start(bf16[4,128,512]{2,1,0:T(8,128)(2,1)} %copy-done.3), calls=%async_computation.5 | async-start | bytes 1048576 | tf_op jit(solution)/shard_map/all_to_all | solution.py:330
  172.0 4.0 %copy-start.9 = (f32[4,1,512]{2,1,0:T(1,128)S(1)}, f32[4,1,512]{2,1,0:T(1,128)}, u32[]{:S(2)}) copy-start(f32[4,1,512]{2,1,0:T(1,128)} %copy-done.8) | copy-start | bytes 24580
  172.0 4.0 %copy-start.12 = (s32[4]{0:T(128)S(1)}, s32[4]{0:T(128)}, u32[]{:S(2)}) copy-start(s32[4]{0:T(128)} %pad_add_fusion.place) | copy-start | bytes 52
  176.0 4.0 %copy-start.14 = (bf16[128,512]{1,0:T(8,128)(2,1)S(1)}, bf16[128,512]{1,0:T(8,128)(2,1)}, u32[]{:S(2)}) copy-start(bf16[128,512]{1,0:T(8,128)(2,1)} %copy-done.13) | copy-start | bytes 393220
  178.7 1.3 copy-start
  180.0 13.0 %collective-permute-start.3 = (bf16[128,512]{1,0:T(8,128)(2,1)S(1)}, bf16[128,512]{1,0:T(8,128)(2,1)S(1)}, u32[]{:S(2)}, u32[]{:S(2)}) collective-permute-start(bf16[128,512]{1,0:T(8,128)(2,1)S(1)} %copy-done.14), channel_id=1, source_target_pairs={{0,0},{1,16},{2,32},{3,48},{4,4},{5,20},{6,36},{7,52},{8,8},{9,24}... | collective-permute-start | bytes 393224 | tf_op jit(solution)/shard_map/ppermute | solution.py:27
  182.4 64.6 %all-to-all-start.6 = ((bf16[4,4,128,512]{3,2,1,0:T(8,128)(2,1)}), bf16[4,4,128,512]{3,2,1,0:T(8,128)(2,1)}, u32[]{:S(2)}, u32[]{:S(2)}) async-start(bf16[4,4,128,512]{3,2,1,0:T(8,128)(2,1)} %broadcast_in_dim.10), calls=%async_computation.6 | async-start | bytes 4194304 | tf_op jit(solution)/shard_map/all_to_all | solution.py:332
  193.0 54.0 %copy-start.1 = (bf16[512,2048]{1,0:T(8,128)(2,1)S(1)}, bf16[512,2048]{1,0:T(8,128)(2,1)}, u32[]{:S(2)}) copy-start(bf16[512,2048]{1,0:T(8,128)(2,1)} %copy-done) | copy-start | bytes 6291460
  193.0 54.0 %copy-start.10 = (f32[4,1,512]{2,1,0:T(1,128)S(1)}, f32[4,1,512]{2,1,0:T(1,128)}, u32[]{:S(2)}) copy-start(f32[4,1,512]{2,1,0:T(1,128)} %get-tuple-element.7.gain) | copy-start | bytes 24580
  229.6 10.4 %copy-start.19 = (bf16[576,512]{1,0:T(8,128)(2,1)}, bf16[576,512]{1,0:T(8,128)(2,1)S(1)}, u32[]{:S(2)}) copy-start(bf16[576,512]{1,0:T(8,128)(2,1)S(1)} %all-gather.2) | copy-start | bytes 1769476
  229.7 17.3 %collective-permute-start.4 = (bf16[1,128,512]{2,1,0:T(8,128)(2,1)S(1)}, bf16[1,128,512]{2,1,0:T(8,128)(2,1)S(1)}, u32[]{:S(2)}, u32[]{:S(2)}) collective-permute-start(bf16[1,128,512]{2,1,0:T(8,128)(2,1)S(1)} %constant_dynamic-slice_fusion.1), channel_id=1, source_target_pairs={{0,64},{64,128},{128,192},{192,256},{256,320},{320,384},{384,448},... | collective-permute-start | bytes 393224 | tf_op jit(solution)/shard_map/ppermute | solution.py:338
  (6 other events, 4.3 us)

commit v5 on v4

--- a/solution.py
+++ b/solution.py
@@ -1,3 +1,5 @@
+import functools
+
 import jax
 import jax.numpy as jnp
 from jax import lax
@@ -27,6 +29,18 @@
     return lax.ppermute(value, GROUP, pairs)
 
 
+def to_upper(value, away):
+    nx, nz, ns = lax.axis_size("x"), lax.axis_size(ZL), lax.axis_size("seq")
+    pairs = [
+        ((x * nz + z) * ns + s, (x * nz + z) * ns + (s + away) % ns)
+        for x in range(nx)
+        for z in range(nz)
+        for s in range(ns)
+        if (s + away) % ns >= x
+    ]
+    return lax.ppermute(value, GROUP, pairs)
+
+
 def three_parts(value):
     parts = []
     for _ in range(3):
@@ -40,7 +54,7 @@
     return jnp.pad(rows, ((0, count - rows.shape[0]), (0, width - rows.shape[1])))
 
 
-def project_kernel(cols, gain, wq, wk, wv, after, out, q_acc, kv_acc):
+def project_kernel(cols, gain, wq, wk, wv, out, q_acc, kv_acc):
     step = pl.program_id(0)
     blocks, rows, feats = cols.shape
     left = (cols[...].reshape(blocks * rows, feats).astype(f32) * gain[...]).astype(bf16)
@@ -68,7 +82,7 @@
                 out[k, pl.ds(h * rows, rows), :] = q_acc[block, pl.ds(h * HD, HD)].astype(bf16)
 
 
-def project(cols, gain, w_query, w_key, w_value, after):
+def project(cols, gain, w_query, w_key, w_value):
     blocks, parts, rows, feats = cols.shape
     q_width, kv_width = w_query.shape[2], 2 * w_key.shape[2]
     heads = q_width // HD
@@ -82,7 +96,6 @@
             pl.BlockSpec((None, feats, q_width), lambda z: (0, z, 0)),
             kv_spec,
             kv_spec,
-            pl.BlockSpec(memory_space=pl.ANY),
         ],
         out_specs=pl.BlockSpec((blocks, (heads + 1) * rows, HD), lambda z: (0, 0, 0)),
         out_shape=jax.ShapeDtypeStruct((blocks, (heads + 1) * rows, HD), bf16),
@@ -92,7 +105,7 @@
         ],
         compiler_params=pltpu.CompilerParams(vmem_limit_bytes=LIMIT),
         name="project",
-    )(cols, gain, w_query, w_key.swapaxes(1, 2), w_value.swapaxes(1, 2), after)
+    )(cols, gain, w_query, w_key.swapaxes(1, 2), w_value.swapaxes(1, 2))
 
 
 def take_kernel(value, after, out):
@@ -123,8 +136,14 @@
     return jnp.sum(jnp.where(same, row, f32(0.0)), axis=1, keepdims=True)
 
 
+def row_of(column):
+    n = column.shape[0]
+    same = lax.broadcasted_iota(jnp.int32, (n, n), 0) == lax.broadcasted_iota(jnp.int32, (n, n), 1)
+    return jnp.sum(jnp.where(same, column, f32(0.0)), axis=0, keepdims=True)
+
+
 def attend_kernel(
-    place, q_in, kv_own, kv_other, cos_own, sin_own, cos_all, sin_all, resid, copies, out,
+    place, q_in, kv_own, kv_other, cos_own, sin_own, cos_all, sin_all, resid, after, copies, out,
     keys, values, r_all, docs_all, r_own, docs_own,
 ):
     rows = out.shape[0]
@@ -176,7 +195,7 @@
         copies[copy] = result
 
 
-def attend(place, q_in, kv_own, kv_other, tables_own, tables_all, resid, copies):
+def attend(place, q_in, kv_own, kv_other, tables_own, tables_all, resid, after, copies):
     rows, feats = resid.shape
     heads, tokens = feats // HD, tables_all[0].shape[0]
     whole = pl.BlockSpec(memory_space=pltpu.VMEM)
@@ -188,7 +207,7 @@
             pl.BlockSpec((q_in.shape[0], rows, HD), lambda h: (0, h, 0)),
         ]
         + [whole] * 6
-        + [pl.BlockSpec((rows, HD), lambda h: (0, h))],
+        + [pl.BlockSpec((rows, HD), lambda h: (0, h)), pl.BlockSpec(memory_space=pl.ANY)],
         out_specs=[
             pl.BlockSpec((copies, rows, HD), lambda h: (0, 0, h)),
             pl.BlockSpec((rows, HD), lambda h: (0, h)),
@@ -207,58 +226,122 @@
         ],
         compiler_params=pltpu.CompilerParams(vmem_limit_bytes=LIMIT),
         name="attend",
-    )(place, q_in, kv_own, kv_other, *tables_own, *tables_all, resid)
-
-
-def product(left, cols, gain):
-    blocks, rows, feats = cols.shape
-    right = cols[...].reshape(blocks * rows, feats)
-    return (jnp.dot(left[...], right, preferred_element_type=f32) * gain[...]).astype(bf16)
-
-
-def upper_kernel(place, left, cols, gain, out):
-    @pl.when(place[1] <= place[2] + pl.program_id(0))
-    def _():
-        out[...] = product(left, cols, gain)
-
-
-def lower_kernel(place, left, cols, gain, upper, out):
+    )(place, q_in, kv_own, kv_other, *tables_own, *tables_all, resid, after)
+
+
+def left_block(block, gain, r, scale):
+    turned = (block.astype(f32) * gain).T
+    return turned, r * r * scale
+
+
+def attn_left_kernel(scale, place, own, one, two, three, gain, kv, out):
+    rows = own.shape[0]
+    blocks = kv.shape[0]
+    for away, ref in enumerate((own, one, two, three)):
+        k = lax.rem(place[4] + blocks - away, blocks)
+        parts = kv[k, pl.ds(rows, 16), :].astype(f32)
+        r = parts[0:1] + parts[1:2] + parts[2:3]
+        turned, weight = left_block(ref[...], gain[...].astype(f32), r, scale)
+        out[:, pl.ds(pl.multiple_of(k * rows, rows), rows)] = (turned * weight).astype(bf16)
+
+
+def attn_left(scale, place, rows, gain, kv_all):
+    feats = gain.shape[1]
+    tokens = rows[0].shape[0] * kv_all.shape[0]
+    whole = pl.BlockSpec(memory_space=pltpu.VMEM)
+    return pl.pallas_call(
+        functools.partial(attn_left_kernel, scale),
+        in_specs=[pl.BlockSpec(memory_space=pltpu.SMEM)] + [whole] * 6,
+        out_specs=whole,
+        out_shape=jax.ShapeDtypeStruct((feats, tokens), bf16),
+        compiler_params=pltpu.CompilerParams(vmem_limit_bytes=LIMIT),
+        name="attn_left",
+    )(place, *rows, gain, kv_all)
+
+
+def hessian_kernel(
+    scale, place, left_a, cols_a, gain_a, ffn_rows, gain_row, r_ffn, cols_f, gain_f,
+    out, diagonal, left_f, turned_f,
+):
+    blocks, rows, feats = cols_a.shape
     row, col = place[1], place[2] + pl.program_id(0)
 
+    @pl.when(pl.program_id(0) == 0)
+    def _():
+        squares = jnp.zeros((rows, 1), f32)
+        part = pl.multiple_of(place[4] * rows, rows)
+        for k in range(blocks):
+            turned, weight = left_block(
+                ffn_rows[k, pl.ds(0, rows), :], gain_row[...].astype(f32), r_ffn[k], scale
+            )
+            turned_f[...] = turned
+            mine = turned_f[pl.ds(part, rows), :]
+            squares += jnp.sum(mine * mine * weight, axis=1, keepdims=True)
+            left_f[:, pl.ds(k * rows, rows)] = (turned * weight).astype(bf16)
+        diagonal[...] = row_of(squares)
+
+    def product(left, cols, gain):
+        right = cols[...].reshape(blocks * rows, feats)
+        return (jnp.dot(left[...], right, preferred_element_type=f32) * gain[...]).astype(bf16)
+
     @pl.when(row < col)
     def _():
-        out[...] = upper[...]
+        out[...] = product(left_a, cols_a, gain_a)
 
     @pl.when(row > col)
     def _():
-        out[...] = product(left, cols, gain)
+        out[...] = product(left_f, cols_f, gain_f)
 
     @pl.when(row == col)
     def _():
-        lower = product(left, cols, gain)
+        upper = product(left_a, cols_a, gain_a)
+        lower = product(left_f, cols_f, gain_f)
         row_ids = lax.broadcasted_iota(jnp.int32, lower.shape, 0)
         col_ids = lax.broadcasted_iota(jnp.int32, lower.shape, 1)
-        out[...] = jnp.where(row_ids <= col_ids, upper[...], lower)
-
-
-def hessian(kernel, place, left, cols, gain, *upper):
-    blocks, parts, rows, feats = cols.shape
-    tile = pl.BlockSpec((feats, feats), lambda z: (0, z))
+        out[...] = jnp.where(row_ids <= col_ids, upper, lower)
+
+
+def hessian(scale, place, left_a, cols_a, gain_a, ffn_rows, gain_row, r_ffn, cols_f, gain_f):
+    blocks, parts, rows, feats = cols_a.shape
+    tokens = blocks * rows
+
+    def upper_at(z, at):
+        return jnp.clip(jnp.maximum(z, at[1] - at[2]), 0, parts - 1)
+
+    def lower_at(z, at):
+        return jnp.clip(jnp.minimum(z, at[1] - at[2]), 0, parts - 1)
+
+    def side(pick):
+        return [
+            pl.BlockSpec((blocks, None, rows, feats), lambda z, at: (0, pick(z, at), 0, 0)),
+            pl.BlockSpec((None, 1, feats), lambda z, at: (z, 0, 0)),
+        ]
+
+    def fixed(shape):
+        return pl.BlockSpec(shape, lambda z, at: (0,) * len(shape))
+
     return pl.pallas_call(
-        kernel,
-        grid=(parts,),
-        in_specs=[
-            pl.BlockSpec(memory_space=pltpu.SMEM),
-            pl.BlockSpec((feats, blocks * rows), lambda z: (0, 0)),
-            pl.BlockSpec((blocks, None, rows, feats), lambda z: (0, z, 0, 0)),
-            pl.BlockSpec((None, 1, feats), lambda z: (z, 0, 0)),
-        ]
-        + [tile] * len(upper),
-        out_specs=tile,
-        out_shape=jax.ShapeDtypeStruct((feats, parts * feats), bf16),
+        functools.partial(hessian_kernel, scale),
+        grid_spec=pltpu.PrefetchScalarGridSpec(
+            num_scalar_prefetch=1,
+            grid=(parts,),
+            in_specs=[fixed(left_a.shape)]
+            + side(upper_at)
+            + [fixed(ffn_rows.shape), fixed(gain_row.shape), fixed(r_ffn.shape)]
+            + side(lower_at),
+            out_specs=[
+                pl.BlockSpec((feats, feats), lambda z, at: (0, z)),
+                fixed((1, rows)),
+            ],
+            scratch_shapes=[pltpu.VMEM((feats, tokens), bf16), pltpu.VMEM((feats, rows), f32)],
+        ),
+        out_shape=[
+            jax.ShapeDtypeStruct((feats, parts * feats), bf16),
+            jax.ShapeDtypeStruct((1, rows), f32),
+        ],
         compiler_params=pltpu.CompilerParams(vmem_limit_bytes=LIMIT),
         name="hessian",
-    )(place, left, cols, gain, *upper)
+    )(place, left_a, cols_a, gain_a, ffn_rows, gain_row, r_ffn, cols_f, gain_f)
 
 
 def on_device(hidden, segment_ids, gain_attn, gain_ffn, w_query, w_key, w_value):
@@ -271,7 +354,8 @@
     width = feats * nx * nz
     scale = 2.0 / tokens
     zb_pos = lax.axis_index("zb")
-    place = jnp.stack([x_pos, x_pos * nz + zl_pos, seq_pos * nz, zb_pos]).astype(jnp.int32)
+    place = jnp.stack([x_pos, x_pos * nz + zl_pos, seq_pos * nz, zb_pos, seq_pos])
+    place = place.astype(jnp.int32)
 
     def copied(value, count):
         return jnp.broadcast_to(value[None], (count,) + value.shape)
@@ -282,10 +366,6 @@
 
     def r_of(parts):
         return lax.rsqrt(jnp.sum(parts.astype(f32), axis=(0, 1)) / width + norm_eps)
-
-    def left_side(blocks, gain, r):
-        left = blocks.astype(f32).reshape(tokens, feats) * (r * r * scale)[:, None]
-        return (left * gain.astype(f32)).astype(bf16).T
 
     resid = swap_x_seq(hidden[0])
     extra = swap_x_seq(
@@ -301,19 +381,20 @@
     docs_own = extra[2, :rows]
     group = group[:, :rows]
     attn_cols = lax.all_to_all(copied(group, nx), "x", 0, 0)
-    attn_rows = lax.all_gather(jnp.concatenate([hidden[0], square_rows(group)]), "seq")
-    r_own = r_of(attn_rows[:, rows : rows + 3, :rows])
-    tail = jnp.concatenate([three_parts(r_own), docs_own[None]])
-    tail = pad_to(tail, 16, HD)
-
-    message = project(attn_cols, gain_a, w_query, w_key, w_value, tail)
+    own_rows = take_after(hidden, rows, group)[0]
+    attn_rows = [own_rows] + [to_upper(own_rows, d) for d in range(1, ns)]
+
+    message = project(attn_cols, gain_a, w_query, w_key, w_value)
     message = lax.all_to_all(message, "x", 0, 0)
     q_rows = rows * feats // HD
-    kv = lax.all_to_all(message[:, q_rows:], "seq", 0, 0)
+    squares = copied(square_rows(group)[:, :HD], ns)
+    kv = lax.all_to_all(jnp.concatenate([message[:, q_rows:], squares], 1), "seq", 0, 0)
     query = lax.all_to_all(take_after(message, q_rows, kv), "seq", 0, 0)
-    kv = jnp.sum(kv.astype(f32), axis=0).astype(bf16)
-    kv_all = lax.all_gather(jnp.concatenate([kv, tail]), "x")
+    tail = jnp.concatenate([three_parts(r_of(kv[:, rows : rows + 3])), docs_own[None]])
+    kv = jnp.sum(kv[:, :rows].astype(f32), axis=0).astype(bf16)
+    kv_all = lax.all_gather(jnp.concatenate([kv, pad_to(tail, 16, HD)]), "x")
     kv_other = lax.ppermute(kv_all[:, :rows], "zb", [(0, 1), (1, 0)])
+    left_a = attn_left(scale, place, attn_rows, gain_attn, kv_all)
 
     half = HD // 2
     freq = rope_base ** (-(jnp.arange(half, dtype=f32) * 2.0 / HD))
@@ -321,31 +402,22 @@
     cosine, sine = jnp.cos(angle), jnp.sin(angle)
     tables = (jnp.concatenate([cosine] * 2, 1), jnp.concatenate([-sine, sine], 1))
     own = tuple(lax.dynamic_slice_in_dim(t, x_pos * rows, rows) for t in tables)
-    copies, section_out = attend(place, query, kv_all, kv_other, own, tables, resid, nz)
-
-    r_attn = jnp.sum(kv_all[:, rows : rows + 3].astype(f32), axis=1).reshape(tokens)
-    attn_left = left_side(attn_rows[:, :rows], gain_attn, r_attn)
-    upper = hessian(upper_kernel, place, attn_left, attn_cols, gain_a)
+    copies, section_out = attend(
+        place, query, kv_all, kv_other, own, tables, resid, left_a, nz
+    )
 
     group = lax.all_to_all(copies, ZL, 0, 0)
     out_rows = swap_x_seq(section_out)
     ffn_cols = lax.all_to_all(copied(group, nx), "x", 0, 0)
     ffn_rows = lax.all_gather(jnp.concatenate([out_rows, square_rows(group)]), "seq")
-    r_ffn = lax.all_gather(r_of(ffn_rows[:, rows : rows + 3, :rows]), "x", tiled=True)
-    ffn_rows = ffn_rows[:, :rows]
+    r_ffn = lax.all_gather(r_of(ffn_rows[:, rows : rows + 3, :rows])[None], "x")
     count = lax.axis_size("phase")
-    passed = lax.dynamic_slice_in_dim(ffn_rows, seq_pos, 1, 0)
+    passed = lax.dynamic_slice_in_dim(ffn_rows[:, :rows], seq_pos, 1, 0)
     passed = lax.ppermute(passed, "phase", [(p, (p + 1) % count) for p in range(count)])
-    ffn_left = left_side(ffn_rows, gain_ffn, r_ffn)
-    hessians = hessian(lower_kernel, place, ffn_left, ffn_cols, gain_f, upper)[None]
-    diag_width = feats // ns
-    own_cols = lax.dynamic_slice_in_dim(
-        ffn_rows.reshape(tokens, feats), seq_pos * diag_width, diag_width, 1
-    ).astype(f32)
-    own_gain = lax.dynamic_slice_in_dim(gain_ffn[0], seq_pos * diag_width, diag_width)
-    own_cols = own_cols * r_ffn[:, None] * own_gain.astype(f32)
-    ffn_diagonal = (jnp.sum(own_cols * own_cols, axis=0) * scale)[None]
-    return (passed, hessians, ffn_diagonal)
+    hessians, ffn_diagonal = hessian(
+        scale, place, left_a, attn_cols, gain_a, ffn_rows, gain_ffn, r_ffn, ffn_cols, gain_f
+    )
+    return (passed, hessians[None], ffn_diagonal)
 
 
 def solution(mesh):

time: 254 us -> 287 us (1.13)
  waiting for transfers between devices: 11.6 us -> 35.5 us
  local copies, waits for them, and re-layouts: 14.9 us -> 20.4 us
  starting transfers between devices: 62.1 us -> 67.1 us
  blocking collectives: 133 us -> 137 us
  other arithmetic: 12.8 us -> 9.33 us
    all_gather x3 -> x2, blocking collectives: 46.6 us -> 21 us  [the longest x1 11 us: on_device(): r_ffn = lax.all_gather(r_of(ffn_rows[:, rows:rows + 3, :rows])[None], 'x')]
    all_to_all x1, waiting for transfers between devices: 0.01 us -> 22.4 us  [on_device(): attn_cols = lax.all_to_all(copied(group, nx), 'x', 0, 0)]
    ppermute x0 -> x3, starting transfers between devices: none -> 21.2 us  [to_upper(): return lax.ppermute(value, GROUP, pairs)]
    all_gather x1, blocking collectives: 36.6 us -> 55.7 us  [on_device(): lax.all_gather(jnp.concatenate([out_rows, square_rows(group)]), 'seq')]
    ppermute x1, starting transfers between devices: 10.3 us -> 0.02 us  [on_device(): lax.ppermute(passed, 'phase', [(p, (p + 1) % count) for p in range(count)])]
    all_to_all x2, blocking collectives: 28.4 us -> 38.2 us  [the longest x1 23.4 us: on_device(): lax.all_to_all(jnp.concatenate([message[:, q_rows:], squares], 1), 'seq',...]
    ppermute x0 -> x3, waiting for transfers between devices: none -> 6.76 us  [to_upper(): return lax.ppermute(value, GROUP, pairs)]
    ppermute x1, waiting for transfers between devices: 6.75 us -> 0.01 us  [on_device(): kv_other = lax.ppermute(kv_all[:, :rows], 'zb', [(0, 1), (1, 0)])]
  transfers between devices with their start and end apart: 9 -> 12, of which waited for: 2 -> 3; matrix products, arithmetic and copies ran while one was open for 7% -> 4% of each run, Pallas kernels for 1% -> 1%
where the time goes in v5:
time: 287 us; the launch traced here: 286 us
  blocking collectives  137 us (48%)
  starting transfers between devices  67.1 us (23%)
  waiting for transfers between devices  35.5 us (12%)
  local copies, waits for them, and re-layouts  20.4 us (7%)
  Pallas kernels  15.9 us (6%)
  other arithmetic  9.33 us (3%)
    all_gather x1, blocking collectives, on_device(): lax.all_gather(jnp.concatenate([out_rows, square_rows(group)]), 'seq')  55.7 us
    all_to_all x1, starting transfers between devices, on_device(): attn_cols = lax.all_to_all(copied(group, nx), 'x', 0, 0)  29.5 us
    all_to_all x1, blocking collectives, on_device(): lax.all_to_all(jnp.concatenate([message[:, q_rows:], squares], 1), 'seq',...  23.4 us
    all_to_all x1, waiting for transfers between devices, on_device(): attn_cols = lax.all_to_all(copied(group, nx), 'x', 0, 0)  22.4 us
    all_to_all x1, blocking collectives, on_device(): lax.all_to_all(copied(jnp.concatenate([resid, extra]), nz), ZL, 0, 0)  21.6 us
    ppermute x3, starting transfers between devices, to_upper(): return lax.ppermute(value, GROUP, pairs)  21.2 us
    unnamed x65, local copies, waits for them, and re-layouts  15.9 us
    all_to_all x1, blocking collectives, on_device(): group = lax.all_to_all(copies, ZL, 0, 0)  14.9 us
  transfers between devices with their start and end apart: 12, of which 3 were waited for; matrix products, arithmetic and copies ran while one was open for 4% of the time, Pallas kernels for 1%

profile of v5, /device:TPU:1, one launch (start us, length us, event | category | flops | bytes accessed | tf_op | source)
XLA Modules:
  0.0 285.8 jit_solution(18441305436786783176)
XLA Ops:
  0.6 1.6 collective-permute-start
  4.3 21.6 %all_to_all.35 = bf16[4,144,512]{2,1,0:T(8,128)(2,1)S(1)} all-to-all(bf16[4,144,512]{2,1,0:T(8,128)(2,1)S(1)} %broadcast_in_dim.10), channel_id=1, replica_groups=mesh['phase'=8,'x'=4,'za'=2,'zb'=2,'seq'=4] {'za','zb'}, dimensions={0} | all-to-all | bytes 1179648 | tf_op jit(solution)/shard_map/all_to_all | solution.py:378
  26.0 1.5 broadcast_in_dim.11
  27.5 29.5 %all-to-all-start.1 = ((bf16[4,4,128,512]{3,2,1,0:T(8,128)(2,1)}), bf16[4,4,128,512]{3,2,1,0:T(8,128)(2,1)S(1)}, u32[]{:S(2)}, u32[]{:S(2)}) async-start(bf16[4,4,128,512]{3,2,1,0:T(8,128)(2,1)} %broadcast_in_dim.11), calls=%async_computation.1 | async-start | bytes 4194304 | tf_op jit(solution)/shard_map/all_to_all | solution.py:383
  58.4 22.4 %all-to-all-done.1.cols.cols_a = bf16[4,4,128,512]{3,2,1,0:T(8,128)(2,1)S(1)} async-done(((bf16[4,4,128,512]{3,2,1,0:T(8,128)(2,1)}), bf16[4,4,128,512]{3,2,1,0:T(8,128)(2,1)S(1)}, u32[]{:S(2)}, u32[]{:S(2)}) %all-to-all-start.1) | async-done | bytes 2097184 | tf_op jit(solution)/shard_map/all_to_all | solution.py:383
  80.9 1.6 copy-done.1
  82.5 3.1 %project.1 = bf16[4,640,128]{2,1,0:T(8,128)(2,1)S(1)} custom-call(bf16[4,4,128,512]{3,2,1,0:T(8,128)(2,1)S(1)} %all-to-all-done.1.cols.cols_a, f32[4,1,512]{2,1,0:T(1,128)S(1)} %get-tuple-element.12.gain.gain_a, bf16[1,2048,512]{2,1,0:T(8,128)(2,1)S(1)} %copy-done.1, bf16[1,64,2048]{2,1,0:T(8,128)(2,1)S(1)} %bitcast.41, bf16[1,64,2048]{2,1,0:T(8,128)(2,1)S(1)} %bitcast.42), custom_call_target="tpu_custom_call" | custom-call | tf_op jit(solution)/shard_map/project/pallas_call | solution.py:90
  86.4 3.5 %all-to-all-start.2 = ((bf16[4,640,128]{2,1,0:T(8,128)(2,1)}), bf16[4,640,128]{2,1,0:T(8,128)(2,1)S(1)}, u32[]{:S(2)}, u32[]{:S(2)}) async-start(bf16[4,640,128]{2,1,0:T(8,128)(2,1)} %copy-done), calls=%async_computation.2 | async-start | bytes 1310720 | tf_op jit(solution)/shard_map/all_to_all | solution.py:388
  91.2 6.3 %all-to-all-done.2.value = bf16[4,640,128]{2,1,0:T(8,128)(2,1)S(1)} async-done(((bf16[4,640,128]{2,1,0:T(8,128)(2,1)}), bf16[4,640,128]{2,1,0:T(8,128)(2,1)S(1)}, u32[]{:S(2)}, u32[]{:S(2)}) %all-to-all-start.2) | async-done | bytes 655392 | tf_op jit(solution)/shard_map/all_to_all | solution.py:388
  97.6 23.4 %all_to_all.36.after = bf16[4,144,128]{2,1,0:T(8,128)(2,1)S(1)} all-to-all(bf16[4,144,128]{2,1,0:T(8,128)(2,1)S(1)} %pad_maximum_fusion.3), channel_id=1, replica_groups=mesh['phase'=8,'x'=4,'za'=2,'zb'=2,'seq'=4] {'seq'}, dimensions={0} | all-to-all | bytes 294912 | tf_op jit(solution)/shard_map/all_to_all | solution.py:391
  121.8 3.5 %all-to-all-start.4 = ((bf16[4,512,128]{2,1,0:T(8,128)(2,1)}), bf16[4,512,128]{2,1,0:T(8,128)(2,1)S(1)}, u32[]{:S(2)}, u32[]{:S(2)}) async-start(bf16[4,512,128]{2,1,0:T(8,128)(2,1)} %copy-done.2), calls=%async_computation.4 | async-start | bytes 1048576 | tf_op jit(solution)/shard_map/all_to_all | solution.py:392
  128.1 7.2 %collective-permute-start.3 = (bf16[128,512]{1,0:T(8,128)(2,1)}, bf16[128,512]{1,0:T(8,128)(2,1)S(1)}, u32[]{:S(2)}, u32[]{:S(2)}) collective-permute-start(bf16[128,512]{1,0:T(8,128)(2,1)} %bitcast.11.own), channel_id=1, source_target_pairs={{0,1},{1,2},{2,3},{3,0},{4,5},{5,6},{6,7},{7,4},{8,9},{9,10},{10,1... | collective-permute-start | bytes 393224 | tf_op jit(solution)/shard_map/ppermute | solution.py:41
  135.3 7.0 %collective-permute-start.4 = (bf16[128,512]{1,0:T(8,128)(2,1)}, bf16[128,512]{1,0:T(8,128)(2,1)S(1)}, u32[]{:S(2)}, u32[]{:S(2)}) collective-permute-start(bf16[128,512]{1,0:T(8,128)(2,1)} %bitcast.11.own), channel_id=1, source_target_pairs={{0,2},{1,3},{2,0},{3,1},{4,6},{5,7},{6,4},{7,5},{8,10},{9,11},{10,... | collective-permute-start | bytes 393224 | tf_op jit(solution)/shard_map/ppermute | solution.py:41
  142.3 7.0 %collective-permute-start.5 = (bf16[128,512]{1,0:T(8,128)(2,1)}, bf16[128,512]{1,0:T(8,128)(2,1)S(1)}, u32[]{:S(2)}, u32[]{:S(2)}) collective-permute-start(bf16[128,512]{1,0:T(8,128)(2,1)} %bitcast.11.own), channel_id=1, source_target_pairs={{0,3},{1,0},{2,1},{3,2},{4,7},{5,4},{6,5},{7,6},{8,11},{9,8},{10,9... | collective-permute-start | bytes 393224 | tf_op jit(solution)/shard_map/ppermute | solution.py:41
  149.4 10.0 %all-gather = bf16[576,128]{1,0:T(8,128)(2,1)S(1)} all-gather(bf16[144,128]{1,0:T(8,128)(2,1)S(1)} %pad_maximum_fusion.5), channel_id=2, replica_groups=mesh['phase'=8,'x'=4,'za'=2,'zb'=2,'seq'=4] {'x'}, dimensions={0}, use_global_device_ids=true | all-gather | bytes 184320 | tf_op jit(solution)/shard_map/all_gather | solution.py:395
  160.1 1.9 collective-permute-start.2
  163.5 2.1 pad_maximum_fusion
  166.9 6.8 %collective-permute-done.5.three = bf16[128,512]{1,0:T(8,128)(2,1)S(1)} collective-permute-done((bf16[128,512]{1,0:T(8,128)(2,1)}, bf16[128,512]{1,0:T(8,128)(2,1)S(1)}, u32[]{:S(2)}, u32[]{:S(2)}) %collective-permute-start.5) | collective-permute-done | bytes 131104 | tf_op jit(solution)/shard_map/ppermute | solution.py:41
  183.8 5.4 %attend.1 = (bf16[4,128,512]{2,1,0:T(8,128)(2,1)S(1)}, bf16[128,512]{1,0:T(8,128)(2,1)S(1)}) custom-call(s32[5]{0:T(128)S(1)} %copy-done.21, bf16[4,512,128]{2,1,0:T(8,128)(2,1)S(1)} %all-to-all-done.4.q_in, bf16[4,144,128]{2,1,0:T(8,128)(2,1)S(1)} %bitcast.40, bf16[4,128,128]{2,1,0:T(8,128)(2,1)} %collective-permute-done.2.kv_other, ...), custom_call_target="tpu_custom_call" | custom-call | tf_op jit(solution)/shard_map/attend/pallas_call | solution.py:202
  189.2 14.9 %all_to_all.37 = bf16[4,128,512]{2,1,0:T(8,128)(2,1)S(1)} all-to-all(bf16[4,128,512]{2,1,0:T(8,128)(2,1)S(1)} %get-tuple-element.8), channel_id=1, replica_groups=mesh['phase'=8,'x'=4,'za'=2,'zb'=2,'seq'=4] {'za','zb'}, dimensions={0} | all-to-all | bytes 1048576 | tf_op jit(solution)/shard_map/all_to_all | solution.py:409
  206.4 4.6 %all-to-all-start.6 = ((bf16[4,4,128,512]{3,2,1,0:T(8,128)(2,1)}), bf16[4,4,128,512]{3,2,1,0:T(8,128)(2,1)}, u32[]{:S(2)}, u32[]{:S(2)}) async-start(bf16[4,4,128,512]{3,2,1,0:T(8,128)(2,1)} %broadcast_in_dim.13), calls=%async_computation.6 | async-start | bytes 4194304 | tf_op jit(solution)/shard_map/all_to_all | solution.py:411
  213.0 55.7 %all-gather.1 = bf16[576,512]{1,0:T(8,128)(2,1)S(1)} all-gather(bf16[144,512]{1,0:T(8,128)(2,1)S(1)} %pad_maximum_fusion.4), channel_id=3, replica_groups=mesh['phase'=8,'x'=4,'za'=2,'zb'=2,'seq'=4] {'seq'}, dimensions={0}, use_global_device_ids=true | all-gather | bytes 737280 | tf_op jit(solution)/shard_map/all_gather | solution.py:412
  268.8 11.0 %all-gather.3.r_ffn = f32[4,1,128]{2,1,0:T(1,128)S(1)} all-gather(f32[1,1,128]{2,1,0:T(1,128)S(1)} %rsqrt_bitcast_fusion), channel_id=4, replica_groups=mesh['phase'=8,'x'=4,'za'=2,'zb'=2,'seq'=4] {'x'}, dimensions={0}, use_global_device_ids=true | all-gather | bytes 2560 | tf_op jit(solution)/shard_map/all_gather | solution.py:413
  279.8 5.4 %hessian.1 = (bf16[512,2048]{1,0:T(8,128)(2,1)}, f32[1,128]{1,0:T(1,128)}) custom-call(s32[5]{0:T(128)S(1)} %copy-done.22, bf16[512,512]{1,0:T(8,128)(2,1)S(1)} %attn_left.1.after.left_a, bf16[4,4,128,512]{3,2,1,0:T(8,128)(2,1)S(1)} %all-to-all-done.1.cols.cols_a, f32[4,1,512]{2,1,0:T(1,128)S(1)} %copy-done.18, bf16[4,144,512]{2,1,0:T(8,128)(2,1)S(1)} %bitcast.37, ...), custom_call_target="tpu_custom_call" | custom-call | tf_op jit(solution)/shard_map/hessian/pallas_call | solution.py:323
  (112 shorter events, 27.9 us)
Async XLA Ops:
  0.6 3.6 %collective-permute-start = (bf16[128,512]{1,0:T(8,128)(2,1)}, bf16[128,512]{1,0:T(8,128)(2,1)S(1)}, u32[]{:S(2)}, u32[]{:S(2)}) collective-permute-start(bf16[128,512]{1,0:T(8,128)(2,1)} %bitcast.43), channel_id=1, source_target_pairs={{0,0},{1,16},{2,32},{3,48},{4,4},{5,20},{6,36},{7,52},{8,8},{9,24}... | collective-permute-start | bytes 393224 | tf_op jit(solution)/shard_map/ppermute | solution.py:29
  3.6 0.7 collective-permute-start.1
  4.3 23.2 %copy-start.4 = (bf16[128,512]{1,0:T(8,128)(2,1)}, bf16[128,512]{1,0:T(8,128)(2,1)S(1)}, u32[]{:S(2)}) copy-start(bf16[128,512]{1,0:T(8,128)(2,1)S(1)} %collective-permute-done.resid) | copy-start | bytes 393220
  27.5 53.3 %copy-start.8 = (bf16[1,2048,64]{1,2,0:T(8,128)(2,1)S(1)}, bf16[1,2048,64]{1,2,0:T(8,128)(2,1)}, u32[]{:S(2)}) copy-start(bf16[1,2048,64]{1,2,0:T(8,128)(2,1)} %param.12) | copy-start | bytes 786436
  27.5 53.3 %copy-start.9 = (bf16[1,2048,64]{1,2,0:T(8,128)(2,1)S(1)}, bf16[1,2048,64]{1,2,0:T(8,128)(2,1)}, u32[]{:S(2)}) copy-start(bf16[1,2048,64]{1,2,0:T(8,128)(2,1)} %param.13) | copy-start | bytes 786436
  27.5 53.3 %all-to-all-start.1 = ((bf16[4,4,128,512]{3,2,1,0:T(8,128)(2,1)}), bf16[4,4,128,512]{3,2,1,0:T(8,128)(2,1)S(1)}, u32[]{:S(2)}, u32[]{:S(2)}) async-start(bf16[4,4,128,512]{3,2,1,0:T(8,128)(2,1)} %broadcast_in_dim.11), calls=%async_computation.1 | async-start | bytes 4194304 | tf_op jit(solution)/shard_map/all_to_all | solution.py:383
  58.4 27.2 %copy-start.17 = (f32[4,1,512]{2,1,0:T(1,128)}, f32[4,1,512]{2,1,0:T(1,128)S(1)}, u32[]{:S(2)}) copy-start(f32[4,1,512]{2,1,0:T(1,128)S(1)} %get-tuple-element.12.gain.gain_a) | copy-start | bytes 24580
  86.4 11.1 %all-to-all-start.2 = ((bf16[4,640,128]{2,1,0:T(8,128)(2,1)}), bf16[4,640,128]{2,1,0:T(8,128)(2,1)S(1)}, u32[]{:S(2)}, u32[]{:S(2)}) async-start(bf16[4,640,128]{2,1,0:T(8,128)(2,1)} %copy-done), calls=%async_computation.2 | async-start | bytes 1310720 | tf_op jit(solution)/shard_map/all_to_all | solution.py:388
  121.8 57.8 %all-to-all-start.4 = ((bf16[4,512,128]{2,1,0:T(8,128)(2,1)}), bf16[4,512,128]{2,1,0:T(8,128)(2,1)S(1)}, u32[]{:S(2)}, u32[]{:S(2)}) async-start(bf16[4,512,128]{2,1,0:T(8,128)(2,1)} %copy-done.2), calls=%async_computation.4 | async-start | bytes 1048576 | tf_op jit(solution)/shard_map/all_to_all | solution.py:392
  126.3 35.7 %copy-start.29 = (f32[512,64]{1,0:T(8,128)}, f32[512,64]{1,0:T(8,128)S(1)}, u32[]{:S(2)}) copy-start(f32[512,64]{1,0:T(8,128)S(1)} %get-tuple-element.16) | copy-start | bytes 393220
  126.3 35.7 %copy-start.30 = (f32[512,64]{1,0:T(8,128)}, f32[512,64]{1,0:T(8,128)S(1)}, u32[]{:S(2)}) copy-start(f32[512,64]{1,0:T(8,128)S(1)} %get-tuple-element.17) | copy-start | bytes 393220
  126.3 35.7 %copy-start.31 = (f32[512,64]{1,0:T(8,128)}, f32[512,64]{1,0:T(8,128)S(1)}, u32[]{:S(2)}) copy-start(f32[512,64]{1,0:T(8,128)S(1)} %get-tuple-element.18) | copy-start | bytes 393220
  128.1 37.5 %collective-permute-start.3 = (bf16[128,512]{1,0:T(8,128)(2,1)}, bf16[128,512]{1,0:T(8,128)(2,1)S(1)}, u32[]{:S(2)}, u32[]{:S(2)}) collective-permute-start(bf16[128,512]{1,0:T(8,128)(2,1)} %bitcast.11.own), channel_id=1, source_target_pairs={{0,1},{1,2},{2,3},{3,0},{4,5},{5,6},{6,7},{7,4},{8,9},{9,10},{10,1... | collective-permute-start | bytes 393224 | tf_op jit(solution)/shard_map/ppermute | solution.py:41
  135.3 30.9 %collective-permute-start.4 = (bf16[128,512]{1,0:T(8,128)(2,1)}, bf16[128,512]{1,0:T(8,128)(2,1)S(1)}, u32[]{:S(2)}, u32[]{:S(2)}) collective-permute-start(bf16[128,512]{1,0:T(8,128)(2,1)} %bitcast.11.own), channel_id=1, source_target_pairs={{0,2},{1,3},{2,0},{3,1},{4,6},{5,7},{6,4},{7,5},{8,10},{9,11},{10,... | collective-permute-start | bytes 393224 | tf_op jit(solution)/shard_map/ppermute | solution.py:41
  142.3 31.3 %collective-permute-start.5 = (bf16[128,512]{1,0:T(8,128)(2,1)}, bf16[128,512]{1,0:T(8,128)(2,1)S(1)}, u32[]{:S(2)}, u32[]{:S(2)}) collective-permute-start(bf16[128,512]{1,0:T(8,128)(2,1)} %bitcast.11.own), channel_id=1, source_target_pairs={{0,3},{1,0},{2,1},{3,2},{4,7},{5,4},{6,5},{7,6},{8,11},{9,8},{10,9... | collective-permute-start | bytes 393224 | tf_op jit(solution)/shard_map/ppermute | solution.py:41
  160.1 19.5 %collective-permute-start.2 = (bf16[4,128,128]{2,1,0:T(8,128)(2,1)}, bf16[4,128,128]{2,1,0:T(8,128)(2,1)}, u32[]{:S(2)}, u32[]{:S(2)}) collective-permute-start(bf16[4,128,128]{2,1,0:T(8,128)(2,1)} %slice.50), channel_id=1, source_target_pairs={{0,4},{4,0},{1,5},{5,1},{2,6},{6,2},{3,7},{7,3},{8,12},{12,8},{9,1... | collective-permute-start | bytes 393224 | tf_op jit(solution)/shard_map/ppermute | solution.py:396
  189.2 14.9 %copy-start.25 = (bf16[128,512]{1,0:T(8,128)(2,1)}, bf16[128,512]{1,0:T(8,128)(2,1)S(1)}, u32[]{:S(2)}) copy-start(bf16[128,512]{1,0:T(8,128)(2,1)S(1)} %get-tuple-element.7) | copy-start | bytes 393220
  206.4 73.4 %all-to-all-start.6 = ((bf16[4,4,128,512]{3,2,1,0:T(8,128)(2,1)}), bf16[4,4,128,512]{3,2,1,0:T(8,128)(2,1)}, u32[]{:S(2)}, u32[]{:S(2)}) async-start(bf16[4,4,128,512]{3,2,1,0:T(8,128)(2,1)} %broadcast_in_dim.13), calls=%async_computation.6 | async-start | bytes 4194304 | tf_op jit(solution)/shard_map/all_to_all | solution.py:411
  210.9 68.8 %copy-start.18 = (f32[4,1,512]{2,1,0:T(1,128)S(1)}, f32[4,1,512]{2,1,0:T(1,128)}, u32[]{:S(2)}) copy-start(f32[4,1,512]{2,1,0:T(1,128)} %copy-done.17) | copy-start | bytes 24580
  210.9 68.8 %copy-start.19 = (f32[4,1,512]{2,1,0:T(1,128)S(1)}, f32[4,1,512]{2,1,0:T(1,128)}, u32[]{:S(2)}) copy-start(f32[4,1,512]{2,1,0:T(1,128)} %get-tuple-element.11.gain_f) | copy-start | bytes 24580
  211.0 68.8 %copy-start.22 = (s32[5]{0:T(128)S(1)}, s32[5]{0:T(128)}, u32[]{:S(2)}) copy-start(s32[5]{0:T(128)} %stack.38.place) | copy-start | bytes 64
  211.0 68.8 %copy-start.24 = (bf16[1,512]{1,0:T(2,128)(2,1)S(1)}, bf16[1,512]{1,0:T(2,128)(2,1)}, u32[]{:S(2)}) copy-start(bf16[1,512]{1,0:T(2,128)(2,1)} %gain_row.1) | copy-start | bytes 3076
  211.0 1.9 collective-permute-start.6
  268.7 11.0 %collective-permute-start.7 = (bf16[1,128,512]{2,1,0:T(8,128)(2,1)S(1)}, bf16[1,128,512]{2,1,0:T(8,128)(2,1)S(1)}, u32[]{:S(2)}, u32[]{:S(2)}) collective-permute-start(bf16[1,128,512]{2,1,0:T(8,128)(2,1)S(1)} %constant_dynamic-slice_fusion), channel_id=1, source_target_pairs={{0,64},{64,128},{128,192},{192,256},{256,320},{320,384},{384,448},... | collective-permute-start | bytes 393224 | tf_op jit(solution)/shard_map/ppermute | solution.py:416
  (20 other events, 21.4 us)

commit v6 on v5

--- a/solution.py
+++ b/solution.py
@@ -41,20 +41,7 @@
     return lax.ppermute(value, GROUP, pairs)
 
 
-def three_parts(value):
-    parts = []
-    for _ in range(3):
-        part = lax.reduce_precision(value, 8, 7)
-        parts.append(part.astype(bf16))
-        value = value - part
-    return jnp.stack(parts)
-
-
-def pad_to(rows, count, width):
-    return jnp.pad(rows, ((0, count - rows.shape[0]), (0, width - rows.shape[1])))
-
-
-def project_kernel(cols, gain, wq, wk, wv, out, q_acc, kv_acc):
+def project_kernel(cols, gain, wq, wk, wv, first, second, out, q_acc, kv_acc):
     step = pl.program_id(0)
     blocks, rows, feats = cols.shape
     left = (cols[...].reshape(blocks * rows, feats).astype(f32) * gain[...]).astype(bf16)
@@ -82,7 +69,7 @@
                 out[k, pl.ds(h * rows, rows), :] = q_acc[block, pl.ds(h * HD, HD)].astype(bf16)
 
 
-def project(cols, gain, w_query, w_key, w_value):
+def project(cols, gain, w_query, w_key, w_value, *after):
     blocks, parts, rows, feats = cols.shape
     q_width, kv_width = w_query.shape[2], 2 * w_key.shape[2]
     heads = q_width // HD
@@ -96,16 +83,162 @@
             pl.BlockSpec((None, feats, q_width), lambda z: (0, z, 0)),
             kv_spec,
             kv_spec,
-        ],
+        ]
+        + [pl.BlockSpec(memory_space=pl.ANY)] * len(after),
         out_specs=pl.BlockSpec((blocks, (heads + 1) * rows, HD), lambda z: (0, 0, 0)),
         out_shape=jax.ShapeDtypeStruct((blocks, (heads + 1) * rows, HD), bf16),
         scratch_shapes=[
             pltpu.VMEM((blocks * rows, q_width), f32),
             pltpu.VMEM((blocks * rows, kv_width), f32),
         ],
-        compiler_params=pltpu.CompilerParams(vmem_limit_bytes=LIMIT),
+        compiler_params=params(),
         name="project",
-    )(cols, gain, w_query, w_key.swapaxes(1, 2), w_value.swapaxes(1, 2))
+    )(cols, gain, w_query, w_key.swapaxes(1, 2), w_value.swapaxes(1, 2), *after)
+
+
+def fixed(shape):
+    return pl.BlockSpec(shape, lambda *at: (0,) * len(shape))
+
+
+def params():
+    return pltpu.CompilerParams(vmem_limit_bytes=LIMIT)
+
+
+def three_parts(value):
+    parts = []
+    for _ in range(3):
+        part = value.astype(bf16)
+        parts.append(part)
+        value = value - part.astype(f32)
+    return parts
+
+
+def row_of(column):
+    n = column.shape[0]
+    same = lax.broadcasted_iota(jnp.int32, (n, n), 0) == lax.broadcasted_iota(jnp.int32, (n, n), 1)
+    return jnp.sum(jnp.where(same, column, f32(0.0)), axis=0, keepdims=True)
+
+
+def stacked(parts, more=()):
+    rows = list(parts) + list(more)
+    rows.append(jnp.zeros((16 - len(rows), rows[0].shape[1]), f32))
+    return jnp.concatenate([row.astype(f32) for row in rows]).astype(bf16)
+
+
+def add_squares(group, squares):
+    rows = squares.shape[0]
+    block = group[pl.ds(0, rows), :].astype(f32)
+    part = jnp.sum(block * block, axis=1, keepdims=True)
+
+    @pl.when(pl.program_id(0) == 0)
+    def _():
+        squares[...] = part
+
+    @pl.when(pl.program_id(0) > 0)
+    def _():
+        squares[...] += part
+
+
+def attn_copies_kernel(group, own, copies, kept, sums, gain_a, gain_f, squares):
+    rows = own.shape[0]
+    for k in range(copies.shape[0]):
+        copies[k] = group[pl.ds(0, rows), :]
+    gains = group[pl.ds(rows, 16), :].astype(f32)
+    gain_a[...] = gains[0:1]
+    gain_f[...] = gains[1:2]
+    add_squares(group, squares)
+
+    @pl.when(pl.program_id(0) == pl.num_programs(0) - 1)
+    def _():
+        kept[...] = own[...]
+        sums[...] = stacked(three_parts(row_of(squares[...])))
+
+
+def attn_copies(group, own, count):
+    parts, tall, feats = group.shape
+    rows = own.shape[0]
+    gain = pl.BlockSpec((None, 1, feats), lambda z: (z, 0, 0))
+    gain_shape = jax.ShapeDtypeStruct((parts, 1, feats), f32)
+    return pl.pallas_call(
+        attn_copies_kernel,
+        grid=(parts,),
+        in_specs=[pl.BlockSpec((None, tall, feats), lambda z: (z, 0, 0)), fixed(own.shape)],
+        out_specs=[
+            pl.BlockSpec((count, None, rows, feats), lambda z: (0, z, 0, 0)),
+            fixed(own.shape),
+            fixed((16, rows)),
+            gain,
+            gain,
+        ],
+        out_shape=[
+            pltpu.HBM((count, parts, rows, feats), bf16),
+            jax.ShapeDtypeStruct(own.shape, bf16),
+            jax.ShapeDtypeStruct((16, rows), bf16),
+            gain_shape,
+            gain_shape,
+        ],
+        scratch_shapes=[pltpu.VMEM((rows, 1), f32)],
+        compiler_params=params(),
+        name="attn_copies",
+    )(group, own)
+
+
+def ffn_copies_kernel(group, own, copies, message, squares):
+    rows, feats = own.shape
+    for k in range(copies.shape[0]):
+        copies[k] = group[...]
+    add_squares(group, squares)
+
+    @pl.when(pl.program_id(0) == pl.num_programs(0) - 1)
+    def _():
+        message[pl.ds(0, rows), :] = own[...]
+        sums = stacked(three_parts(row_of(squares[...])))
+        message[pl.ds(rows, 16), :] = jnp.concatenate([sums] * (feats // rows), 1)
+
+
+def ffn_copies(group, own, count):
+    parts, rows, feats = group.shape
+    return pl.pallas_call(
+        ffn_copies_kernel,
+        grid=(parts,),
+        in_specs=[pl.BlockSpec((None, rows, feats), lambda z: (z, 0, 0)), fixed(own.shape)],
+        out_specs=[
+            pl.BlockSpec((count, None, rows, feats), lambda z: (0, z, 0, 0)),
+            fixed((rows + 16, feats)),
+        ],
+        out_shape=[
+            pltpu.HBM((count, parts, rows, feats), bf16),
+            jax.ShapeDtypeStruct((rows + 16, feats), bf16),
+        ],
+        scratch_shapes=[pltpu.VMEM((rows, 1), f32)],
+        compiler_params=params(),
+        name="ffn_copies",
+    )(group, own)
+
+
+def kv_message_kernel(message, sums, after, out):
+    rows = message.shape[0]
+    out[pl.ds(0, rows), :] = message[...]
+    out[pl.ds(rows, 16), :] = sums[...]
+
+
+def kv_message(message, sums, after):
+    blocks, tall, width = message.shape
+    rows = sums.shape[1]
+    last = tall // rows - 1
+    return pl.pallas_call(
+        kv_message_kernel,
+        grid=(blocks,),
+        in_specs=[
+            pl.BlockSpec((None, rows, width), lambda i: (i, last, 0)),
+            fixed(sums.shape),
+            pl.BlockSpec(memory_space=pl.ANY),
+        ],
+        out_specs=pl.BlockSpec((None, rows + 16, width), lambda i: (i, 0, 0)),
+        out_shape=jax.ShapeDtypeStruct((blocks, rows + 16, width), bf16),
+        compiler_params=params(),
+        name="kv_message",
+    )(message, sums, after)
 
 
 def take_kernel(value, after, out):
@@ -120,13 +253,38 @@
         grid=(value.shape[0],),
         in_specs=[spec, pl.BlockSpec(memory_space=pl.ANY)],
         out_specs=spec,
-        out_shape=jax.ShapeDtypeStruct(shape, value.dtype),
-        compiler_params=pltpu.CompilerParams(vmem_limit_bytes=LIMIT),
+        out_shape=pltpu.HBM(shape, value.dtype),
+        compiler_params=params(),
         name="take_after",
     )(value, after)
 
 
-def rotate(values, cosine, sine):
+def kv_sum_kernel(width, arrived, docs, out):
+    rows = out.shape[0] - 16
+    out[pl.ds(0, rows), :] = jnp.sum(arrived[:, pl.ds(0, rows), :].astype(f32), axis=0).astype(bf16)
+    sums = jnp.sum(arrived[:, pl.ds(rows, 16), :].astype(f32), axis=0)
+    r = lax.rsqrt((sums[0:1] + sums[1:2] + sums[2:3]) / width + norm_eps)
+    own = docs[...].astype(f32)[2:3, :rows]
+    out[pl.ds(rows, 16), :] = stacked(three_parts(r), [own])
+
+
+def kv_sum(width, arrived, docs):
+    return pl.pallas_call(
+        functools.partial(kv_sum_kernel, width),
+        grid=(1,),
+        in_specs=[fixed(arrived.shape), fixed(docs.shape)],
+        out_specs=fixed(arrived.shape[1:]),
+        out_shape=jax.ShapeDtypeStruct(arrived.shape[1:], bf16),
+        compiler_params=params(),
+        name="kv_sum",
+    )(arrived, docs)
+
+
+def rotate(values, table):
+    lower = lax.broadcasted_iota(jnp.int32, table.shape, 1) < HD // 2
+    swapped = pltpu.roll(table, HD // 2, 1)
+    cosine = jnp.where(lower, table, swapped)
+    sine = jnp.where(lower, -swapped, table)
     return values * cosine + pltpu.roll(values, HD // 2, 1) * sine
 
 
@@ -136,50 +294,46 @@
     return jnp.sum(jnp.where(same, row, f32(0.0)), axis=1, keepdims=True)
 
 
-def row_of(column):
-    n = column.shape[0]
-    same = lax.broadcasted_iota(jnp.int32, (n, n), 0) == lax.broadcasted_iota(jnp.int32, (n, n), 1)
-    return jnp.sum(jnp.where(same, column, f32(0.0)), axis=0, keepdims=True)
-
-
 def attend_kernel(
-    place, q_in, kv_own, kv_other, cos_own, sin_own, cos_all, sin_all, resid, after, copies, out,
+    q_in, kv_own, kv_other, table, resid, after, copies, out,
     keys, values, r_all, docs_all, r_own, docs_own,
 ):
     rows = out.shape[0]
     tokens = keys.shape[0]
+    x_pos, zb_pos = lax.axis_index("x"), lax.axis_index("zb")
 
     @pl.when(pl.program_id(0) == 0)
     def _():
         lower = lax.broadcasted_iota(jnp.int32, (rows, HD), 1) < HD // 2
         for k in range(tokens // rows):
             mine = kv_own[k, pl.ds(0, rows), :].astype(f32)
-            other = kv_other[k].astype(f32)
-            first = jnp.where(place[3] == 0, mine, other)
-            second = jnp.where(place[3] == 0, other, mine)
+            other = kv_other[k, pl.ds(0, rows), :].astype(f32)
+            first = jnp.where(zb_pos == 0, mine, other)
+            second = jnp.where(zb_pos == 0, other, mine)
             tail = kv_own[k, pl.ds(rows, 16), :].astype(f32)
             block = pl.ds(k * rows, rows)
             key = jnp.where(lower, first, pltpu.roll(second, HD // 2, 1))
-            keys[block, :] = rotate(key, cos_all[block, :], sin_all[block, :])
+            keys[block, :] = rotate(key, table[block, :])
             values[block, :] = jnp.where(lower, pltpu.roll(first, HD // 2, 1), second)
             r = tail[0:1] + tail[1:2] + tail[2:3]
             r_all[:, block] = r
             docs_all[:, block] = tail[3:4]
 
-            @pl.when(place[0] == k)
+            @pl.when(x_pos == k)
             def _():
                 r_own[...] = column_of(r) * (1.0 / HD**0.5)
                 docs_own[...] = column_of(tail[3:4])
 
     query = jnp.sum(q_in[...].astype(f32), axis=0)
-    query = rotate(query, cos_own[...], sin_own[...]) * r_own[...]
+    own = pl.ds(pl.multiple_of(x_pos * rows, rows), rows)
+    query = rotate(query, table[own, :]) * r_own[...]
     scores = lax.dot_general(
         query, keys[...], (((1,), (1,)), ((), ())),
         preferred_element_type=f32, precision=lax.Precision.HIGHEST,
     )
     scores = scores * r_all[...]
     key_ids = lax.broadcasted_iota(jnp.int32, scores.shape, 1)
-    own_ids = lax.broadcasted_iota(jnp.int32, scores.shape, 0) + place[0] * rows
+    own_ids = lax.broadcasted_iota(jnp.int32, scores.shape, 0) + x_pos * rows
     allowed = (key_ids <= own_ids) & (docs_all[...] == docs_own[...])
     scores = jnp.where(allowed, scores, f32(-1e30))
     peak = jnp.max(scores, axis=-1, keepdims=True)
@@ -195,26 +349,24 @@
         copies[copy] = result
 
 
-def attend(place, q_in, kv_own, kv_other, tables_own, tables_all, resid, after, copies):
+def attend(q_in, kv_own, kv_other, table, resid, after, copies):
     rows, feats = resid.shape
-    heads, tokens = feats // HD, tables_all[0].shape[0]
-    whole = pl.BlockSpec(memory_space=pltpu.VMEM)
+    heads, tokens = feats // HD, table.shape[0]
     return pl.pallas_call(
         attend_kernel,
         grid=(heads,),
         in_specs=[
-            pl.BlockSpec(memory_space=pltpu.SMEM),
             pl.BlockSpec((q_in.shape[0], rows, HD), lambda h: (0, h, 0)),
         ]
-        + [whole] * 6
+        + [fixed(kv_own.shape), fixed(kv_other.shape), fixed(table.shape)]
         + [pl.BlockSpec((rows, HD), lambda h: (0, h)), pl.BlockSpec(memory_space=pl.ANY)],
         out_specs=[
             pl.BlockSpec((copies, rows, HD), lambda h: (0, 0, h)),
             pl.BlockSpec((rows, HD), lambda h: (0, h)),
         ],
         out_shape=[
-            jax.ShapeDtypeStruct((copies, rows, feats), bf16),
-            jax.ShapeDtypeStruct((rows, feats), bf16),
+            pltpu.HBM((copies, rows, feats), bf16),
+            pltpu.HBM((rows, feats), bf16),
         ],
         scratch_shapes=[
             pltpu.VMEM((tokens, HD), f32),
@@ -224,9 +376,9 @@
             pltpu.VMEM((rows, 1), f32),
             pltpu.VMEM((rows, 1), f32),
         ],
-        compiler_params=pltpu.CompilerParams(vmem_limit_bytes=LIMIT),
+        compiler_params=params(),
         name="attend",
-    )(place, q_in, kv_own, kv_other, *tables_own, *tables_all, resid, after)
+    )(q_in, kv_own, kv_other, table, resid, after)
 
 
 def left_block(block, gain, r, scale):
@@ -234,29 +386,31 @@
     return turned, r * r * scale
 
 
-def attn_left_kernel(scale, place, own, one, two, three, gain, kv, out):
+def attn_left_kernel(scale, own, one, two, three, gain, kv, out):
     rows = own.shape[0]
     blocks = kv.shape[0]
+    seq_pos = lax.axis_index("seq")
     for away, ref in enumerate((own, one, two, three)):
-        k = lax.rem(place[4] + blocks - away, blocks)
+        k = lax.rem(seq_pos + blocks - away, blocks)
         parts = kv[k, pl.ds(rows, 16), :].astype(f32)
         r = parts[0:1] + parts[1:2] + parts[2:3]
         turned, weight = left_block(ref[...], gain[...].astype(f32), r, scale)
         out[:, pl.ds(pl.multiple_of(k * rows, rows), rows)] = (turned * weight).astype(bf16)
 
 
-def attn_left(scale, place, rows, gain, kv_all):
+def attn_left(scale, rows, gain, kv_all):
     feats = gain.shape[1]
     tokens = rows[0].shape[0] * kv_all.shape[0]
-    whole = pl.BlockSpec(memory_space=pltpu.VMEM)
+    arrays = (*rows, gain, kv_all)
     return pl.pallas_call(
         functools.partial(attn_left_kernel, scale),
-        in_specs=[pl.BlockSpec(memory_space=pltpu.SMEM)] + [whole] * 6,
-        out_specs=whole,
+        grid=(1,),
+        in_specs=[fixed(a.shape) for a in arrays],
+        out_specs=fixed((feats, tokens)),
         out_shape=jax.ShapeDtypeStruct((feats, tokens), bf16),
-        compiler_params=pltpu.CompilerParams(vmem_limit_bytes=LIMIT),
+        compiler_params=params(),
         name="attn_left",
-    )(place, *rows, gain, kv_all)
+    )(*arrays)
 
 
 def hessian_kernel(
@@ -264,12 +418,12 @@
     out, diagonal, left_f, turned_f,
 ):
     blocks, rows, feats = cols_a.shape
-    row, col = place[1], place[2] + pl.program_id(0)
+    row, col = place[0], place[1] + pl.program_id(0)
 
     @pl.when(pl.program_id(0) == 0)
     def _():
         squares = jnp.zeros((rows, 1), f32)
-        part = pl.multiple_of(place[4] * rows, rows)
+        part = pl.multiple_of(lax.axis_index("seq") * rows, rows)
         for k in range(blocks):
             turned, weight = left_block(
                 ffn_rows[k, pl.ds(0, rows), :], gain_row[...].astype(f32), r_ffn[k], scale
@@ -306,19 +460,16 @@
     tokens = blocks * rows
 
     def upper_at(z, at):
-        return jnp.clip(jnp.maximum(z, at[1] - at[2]), 0, parts - 1)
+        return jnp.clip(jnp.maximum(z, at[0] - at[1]), 0, parts - 1)
 
     def lower_at(z, at):
-        return jnp.clip(jnp.minimum(z, at[1] - at[2]), 0, parts - 1)
+        return jnp.clip(jnp.minimum(z, at[0] - at[1]), 0, parts - 1)
 
     def side(pick):
         return [
             pl.BlockSpec((blocks, None, rows, feats), lambda z, at: (0, pick(z, at), 0, 0)),
             pl.BlockSpec((None, 1, feats), lambda z, at: (z, 0, 0)),
         ]
-
-    def fixed(shape):
-        return pl.BlockSpec(shape, lambda z, at: (0,) * len(shape))
 
     return pl.pallas_call(
         functools.partial(hessian_kernel, scale),
@@ -339,7 +490,7 @@
             jax.ShapeDtypeStruct((feats, parts * feats), bf16),
             jax.ShapeDtypeStruct((1, rows), f32),
         ],
-        compiler_params=pltpu.CompilerParams(vmem_limit_bytes=LIMIT),
+        compiler_params=params(),
         name="hessian",
     )(place, left_a, cols_a, gain_a, ffn_rows, gain_row, r_ffn, cols_f, gain_f)
 
@@ -353,63 +504,41 @@
     tokens = rows * ns
     width = feats * nx * nz
     scale = 2.0 / tokens
-    zb_pos = lax.axis_index("zb")
-    place = jnp.stack([x_pos, x_pos * nz + zl_pos, seq_pos * nz, zb_pos, seq_pos])
+    place = jnp.stack([x_pos * nz + zl_pos, seq_pos * nz])
     place = place.astype(jnp.int32)
 
     def copied(value, count):
         return jnp.broadcast_to(value[None], (count,) + value.shape)
 
-    def square_rows(group):
-        group = group.astype(f32)
-        return pad_to(three_parts(jnp.sum(group * group, axis=(0, 2))), 16, feats)
-
     def r_of(parts):
         return lax.rsqrt(jnp.sum(parts.astype(f32), axis=(0, 1)) / width + norm_eps)
 
     resid = swap_x_seq(hidden[0])
-    extra = swap_x_seq(
-        pad_to(
-            jnp.concatenate([gain_attn, gain_ffn, pad_to(segment_ids.astype(bf16), 1, feats)]),
-            16,
-            feats,
-        )
-    )
+    docs = jnp.pad(segment_ids.astype(bf16), ((0, 13), (0, feats - rows)))
+    extra = swap_x_seq(jnp.concatenate([gain_attn, gain_ffn, docs]))
     group = lax.all_to_all(copied(jnp.concatenate([resid, extra]), nz), ZL, 0, 0)
-    gain_a = group[:, rows : rows + 1].astype(f32)
-    gain_f = group[:, rows + 1 : rows + 2].astype(f32)
-    docs_own = extra[2, :rows]
-    group = group[:, :rows]
-    attn_cols = lax.all_to_all(copied(group, nx), "x", 0, 0)
-    own_rows = take_after(hidden, rows, group)[0]
+    copies, own_rows, sums, gain_a, gain_f = attn_copies(group, hidden[0], nx)
     attn_rows = [own_rows] + [to_upper(own_rows, d) for d in range(1, ns)]
-
-    message = project(attn_cols, gain_a, w_query, w_key, w_value)
+    attn_cols = lax.all_to_all(copies, "x", 0, 0)
+
+    message = project(attn_cols, gain_a, w_query, w_key, w_value, *attn_rows[1:3])
     message = lax.all_to_all(message, "x", 0, 0)
-    q_rows = rows * feats // HD
-    squares = copied(square_rows(group)[:, :HD], ns)
-    kv = lax.all_to_all(jnp.concatenate([message[:, q_rows:], squares], 1), "seq", 0, 0)
-    query = lax.all_to_all(take_after(message, q_rows, kv), "seq", 0, 0)
-    tail = jnp.concatenate([three_parts(r_of(kv[:, rows : rows + 3])), docs_own[None]])
-    kv = jnp.sum(kv[:, :rows].astype(f32), axis=0).astype(bf16)
-    kv_all = lax.all_gather(jnp.concatenate([kv, pad_to(tail, 16, HD)]), "x")
-    kv_other = lax.ppermute(kv_all[:, :rows], "zb", [(0, 1), (1, 0)])
-    left_a = attn_left(scale, place, attn_rows, gain_attn, kv_all)
+    kv = lax.all_to_all(kv_message(message, sums, attn_rows[3]), "seq", 0, 0)
+    query = lax.all_to_all(take_after(message, rows * feats // HD, kv), "seq", 0, 0)
+    kv_all = lax.all_gather(kv_sum(width, kv, extra), "x")
+    kv_other = lax.ppermute(kv_all, "zb", [(0, 1), (1, 0)])
+    left_a = attn_left(scale, attn_rows, gain_attn, kv_all)
 
     half = HD // 2
     freq = rope_base ** (-(jnp.arange(half, dtype=f32) * 2.0 / HD))
     angle = jnp.arange(tokens, dtype=f32)[:, None] * freq[None, :]
-    cosine, sine = jnp.cos(angle), jnp.sin(angle)
-    tables = (jnp.concatenate([cosine] * 2, 1), jnp.concatenate([-sine, sine], 1))
-    own = tuple(lax.dynamic_slice_in_dim(t, x_pos * rows, rows) for t in tables)
-    copies, section_out = attend(
-        place, query, kv_all, kv_other, own, tables, resid, left_a, nz
-    )
+    table = jnp.concatenate([jnp.cos(angle), jnp.sin(angle)], 1)
+    copies, section_out = attend(query, kv_all, kv_other, table, resid, left_a, nz)
 
     group = lax.all_to_all(copies, ZL, 0, 0)
-    out_rows = swap_x_seq(section_out)
-    ffn_cols = lax.all_to_all(copied(group, nx), "x", 0, 0)
-    ffn_rows = lax.all_gather(jnp.concatenate([out_rows, square_rows(group)]), "seq")
+    copies, message = ffn_copies(group, swap_x_seq(section_out), nx)
+    ffn_cols = lax.all_to_all(copies, "x", 0, 0)
+    ffn_rows = lax.all_gather(message, "seq")
     r_ffn = lax.all_gather(r_of(ffn_rows[:, rows : rows + 3, :rows])[None], "x")
     count = lax.axis_size("phase")
     passed = lax.dynamic_slice_in_dim(ffn_rows[:, :rows], seq_pos, 1, 0)

time: 287 us -> 260 us (0.906)
  blocking collectives: 137 us -> 87.7 us
  waiting for transfers between devices: 35.5 us -> 54.3 us
  starting transfers between devices: 67.1 us -> 80.1 us
  local copies, waits for them, and re-layouts: 20.4 us -> 9.83 us
  other arithmetic: 9.33 us -> 3.3 us
  Pallas kernels: 15.9 us -> 20.4 us
    all_gather x2, blocking collectives: 65.7 us -> 33.7 us  [the longest x1 20 us: on_device(): ffn_rows = lax.all_gather(message, 'seq')]
    ppermute x3, waiting for transfers between devices: 6.76 us -> 29.3 us  [to_upper(): return lax.ppermute(value, GROUP, pairs)]
    all_to_all x2 -> x1, blocking collectives: 38.2 us -> 16.5 us  [on_device(): kv = lax.all_to_all(kv_message(message, sums, attn_rows[3]), 'seq', 0, 0)]
    ppermute x1, starting transfers between devices: 0.02 us -> 9.12 us  [on_device(): lax.ppermute(passed, 'phase', [(p, (p + 1) % count) for p in range(count)])]
    all_to_all x1, waiting for transfers between devices: 6.34 us -> 0.01 us  [on_device(): message = lax.all_to_all(message, 'x', 0, 0)]
    unnamed x65 -> x35, local copies, waits for them, and re-layouts: 15.9 us -> 9.74 us
    all_to_all x1, blocking collectives: 21.6 us -> 26.9 us  [on_device(): lax.all_to_all(copied(jnp.concatenate([resid, extra]), nz), ZL, 0, 0)]
    ppermute x1, waiting for transfers between devices: 0.01 us -> 5 us  [on_device(): kv_other = lax.ppermute(kv_all, 'zb', [(0, 1), (1, 0)])]
  transfers between devices with their start and end apart: 12 -> 13, of which waited for: 3 -> 4; matrix products, arithmetic and copies ran while one was open for 4% -> 1% of each run, Pallas kernels for 1% -> 0%
where the time goes in v6:
time: 260 us; the launch traced here: 257 us
  blocking collectives  87.7 us (34%)
  starting transfers between devices  80.1 us (31%)
  waiting for transfers between devices  54.3 us (21%)
  Pallas kernels  20.4 us (8%)
  local copies, waits for them, and re-layouts  9.83 us (4%)
  other arithmetic  3.3 us (1%)
    ppermute x3, waiting for transfers between devices, to_upper(): return lax.ppermute(value, GROUP, pairs)  29.3 us
    all_to_all x1, blocking collectives, on_device(): lax.all_to_all(copied(jnp.concatenate([resid, extra]), nz), ZL, 0, 0)  26.9 us
    all_to_all x1, starting transfers between devices, on_device(): attn_cols = lax.all_to_all(copies, 'x', 0, 0)  24.1 us
    ppermute x3, starting transfers between devices, to_upper(): return lax.ppermute(value, GROUP, pairs)  20.5 us
    all_gather x1, blocking collectives, on_device(): ffn_rows = lax.all_gather(message, 'seq')  20 us
    all_to_all x1, waiting for transfers between devices, on_device(): group = lax.all_to_all(copies, ZL, 0, 0)  19.9 us
    all_to_all x1, blocking collectives, on_device(): kv = lax.all_to_all(kv_message(message, sums, attn_rows[3]), 'seq', 0, 0)  16.5 us
    all_gather x1, blocking collectives, on_device(): kv_all = lax.all_gather(kv_sum(width, kv, extra), 'x')  13.7 us
  transfers between devices with their start and end apart: 13, of which 4 were waited for; matrix products, arithmetic and copies ran while one was open for 1% of the time, Pallas kernels for 0%

profile of v6, /device:TPU:1, one launch (start us, length us, event | category | flops | bytes accessed | tf_op | source)
XLA Modules:
  0.0 256.5 jit_solution(6411125169879145669)
XLA Ops:
  5.1 26.9 %all_to_all.35.group = bf16[4,144,512]{2,1,0:T(8,128)(2,1)S(1)} all-to-all(bf16[4,144,512]{2,1,0:T(8,128)(2,1)S(1)} %broadcast_in_dim.4), channel_id=1, replica_groups=mesh['phase'=8,'x'=4,'za'=2,'zb'=2,'seq'=4] {'za','zb'}, dimensions={0} | all-to-all | bytes 1179648 | tf_op jit(solution)/shard_map/all_to_all | solution.py:519
  32.1 2.1 attn_copies.1
  34.1 24.1 %all-to-all-start.1 = ((bf16[4,4,128,512]{3,2,1,0:T(8,128)(2,1)}), bf16[4,4,128,512]{3,2,1,0:T(8,128)(2,1)S(1)}, u32[]{:S(2)}, u32[]{:S(2)}) async-start(bf16[4,4,128,512]{3,2,1,0:T(8,128)(2,1)} %get-tuple-element.14), calls=%async_computation.1 | async-start | bytes 4194304 | tf_op jit(solution)/shard_map/all_to_all | solution.py:522
  58.3 11.3 %collective-permute-start.3 = (bf16[128,512]{1,0:T(8,128)(2,1)S(1)}, bf16[128,512]{1,0:T(8,128)(2,1)S(1)}, u32[]{:S(2)}, u32[]{:S(2)}) collective-permute-start(bf16[128,512]{1,0:T(8,128)(2,1)S(1)} %get-tuple-element.16.own), channel_id=1, source_target_pairs={{0,2},{1,3},{2,0},{3,1},{4,6},{5,7},{6,4},{7,5},{8,10},{9,11},{10,... | collective-permute-start | bytes 393224 | tf_op jit(solution)/shard_map/ppermute | solution.py:41
  69.6 5.0 %collective-permute-start.2 = (bf16[128,512]{1,0:T(8,128)(2,1)S(1)}, bf16[128,512]{1,0:T(8,128)(2,1)S(1)}, u32[]{:S(2)}, u32[]{:S(2)}) collective-permute-start(bf16[128,512]{1,0:T(8,128)(2,1)S(1)} %get-tuple-element.16.own), channel_id=1, source_target_pairs={{0,1},{1,2},{2,3},{3,0},{4,5},{5,6},{6,7},{7,4},{8,9},{9,10},{10,1... | collective-permute-start | bytes 393224 | tf_op jit(solution)/shard_map/ppermute | solution.py:41
  74.6 16.2 %collective-permute-done.2.first.one = bf16[128,512]{1,0:T(8,128)(2,1)S(1)} collective-permute-done((bf16[128,512]{1,0:T(8,128)(2,1)S(1)}, bf16[128,512]{1,0:T(8,128)(2,1)S(1)}, u32[]{:S(2)}, u32[]{:S(2)}) %collective-permute-start.2) | collective-permute-done | bytes 131104 | tf_op jit(solution)/shard_map/ppermute | solution.py:41
  92.5 3.9 %project.1 = bf16[4,640,128]{2,1,0:T(8,128)(2,1)} custom-call(bf16[4,4,128,512]{3,2,1,0:T(8,128)(2,1)S(1)} %all-to-all-done.1.cols.cols_a, f32[4,1,512]{2,1,0:T(1,128)S(1)} %get-tuple-element.15.gain.gain_a, bf16[1,2048,512]{2,1,0:T(8,128)(2,1)S(1)} %copy-done, bf16[1,64,2048]{2,1,0:T(8,128)(2,1)S(1)} %bitcast.16, bf16[1,64,2048]{2,1,0:T(8,128)(2,1)S(1)} %bitcast.17, ...), custom_call_target="tpu_custom_call" | custom-call | tf_op jit(solution)/shard_map/project/pallas_call | solution.py:77
  96.4 3.5 %all-to-all-start.2 = ((bf16[4,640,128]{2,1,0:T(8,128)(2,1)}), bf16[4,640,128]{2,1,0:T(8,128)(2,1)S(1)}, u32[]{:S(2)}, u32[]{:S(2)}) async-start(bf16[4,640,128]{2,1,0:T(8,128)(2,1)} %project.1), calls=%async_computation.2 | async-start | bytes 1310720 | tf_op jit(solution)/shard_map/all_to_all | solution.py:525
  99.9 4.2 %collective-permute-start.4 = (bf16[128,512]{1,0:T(8,128)(2,1)S(1)}, bf16[128,512]{1,0:T(8,128)(2,1)S(1)}, u32[]{:S(2)}, u32[]{:S(2)}) collective-permute-start(bf16[128,512]{1,0:T(8,128)(2,1)S(1)} %get-tuple-element.16.own), channel_id=1, source_target_pairs={{0,3},{1,0},{2,1},{3,2},{4,7},{5,4},{6,5},{7,6},{8,11},{9,8},{10,9... | collective-permute-start | bytes 393224 | tf_op jit(solution)/shard_map/ppermute | solution.py:41
  104.2 13.1 %collective-permute-done.4.after.three = bf16[128,512]{1,0:T(8,128)(2,1)S(1)} collective-permute-done((bf16[128,512]{1,0:T(8,128)(2,1)S(1)}, bf16[128,512]{1,0:T(8,128)(2,1)S(1)}, u32[]{:S(2)}, u32[]{:S(2)}) %collective-permute-start.4) | collective-permute-done | bytes 131104 | tf_op jit(solution)/shard_map/ppermute | solution.py:41
  118.0 16.5 %all_to_all.36.after.arrived = bf16[4,144,128]{2,1,0:T(8,128)(2,1)S(1)} all-to-all(bf16[4,144,128]{2,1,0:T(8,128)(2,1)S(1)} %kv_message.1), channel_id=1, replica_groups=mesh['phase'=8,'x'=4,'za'=2,'zb'=2,'seq'=4] {'seq'}, dimensions={0} | all-to-all | bytes 294912 | tf_op jit(solution)/shard_map/all_to_all | solution.py:526
  135.8 3.5 %all-to-all-start.4 = ((bf16[4,512,128]{2,1,0:T(8,128)(2,1)}), bf16[4,512,128]{2,1,0:T(8,128)(2,1)S(1)}, u32[]{:S(2)}, u32[]{:S(2)}) async-start(bf16[4,512,128]{2,1,0:T(8,128)(2,1)} %take_after.1), calls=%async_computation.4 | async-start | bytes 1048576 | tf_op jit(solution)/shard_map/all_to_all | solution.py:527
  139.4 13.7 %all-gather = bf16[576,128]{1,0:T(8,128)(2,1)S(1)} all-gather(bf16[144,128]{1,0:T(8,128)(2,1)S(1)} %kv_sum.1), channel_id=2, replica_groups=mesh['phase'=8,'x'=4,'za'=2,'zb'=2,'seq'=4] {'x'}, dimensions={0}, use_global_device_ids=true | all-gather | bytes 184320 | tf_op jit(solution)/shard_map/all_gather | solution.py:528
  153.1 5.6 %collective-permute-start.5 = (bf16[4,144,128]{2,1,0:T(8,128)(2,1)S(1)}, bf16[4,144,128]{2,1,0:T(8,128)(2,1)S(1)}, u32[]{:S(2)}, u32[]{:S(2)}) collective-permute-start(bf16[4,144,128]{2,1,0:T(8,128)(2,1)S(1)} %bitcast.13), channel_id=1, source_target_pairs={{0,4},{4,0},{1,5},{5,1},{2,6},{6,2},{3,7},{7,3},{8,12},{12,8},{9,1... | collective-permute-start | bytes 442376 | tf_op jit(solution)/shard_map/ppermute | solution.py:529
  163.5 5.0 %collective-permute-done.5.kv_other = bf16[4,144,128]{2,1,0:T(8,128)(2,1)S(1)} collective-permute-done((bf16[4,144,128]{2,1,0:T(8,128)(2,1)S(1)}, bf16[4,144,128]{2,1,0:T(8,128)(2,1)S(1)}, u32[]{:S(2)}, u32[]{:S(2)}) %collective-permute-start.5) | collective-permute-done | bytes 147488 | tf_op jit(solution)/shard_map/ppermute | solution.py:529
  172.0 5.0 %attend.1 = (bf16[4,128,512]{2,1,0:T(8,128)(2,1)}, bf16[128,512]{1,0:T(8,128)(2,1)}) custom-call(bf16[4,512,128]{2,1,0:T(8,128)(2,1)S(1)} %all-to-all-done.4.q_in, bf16[4,144,128]{2,1,0:T(8,128)(2,1)S(1)} %bitcast.15, bf16[4,144,128]{2,1,0:T(8,128)(2,1)S(1)} %copy-done.11, f32[512,128]{1,0:T(8,128)S(1)} %copy-done.1, bf16[128,512]{1,0:T(8,128)(2,1)S(1)} %copy-done.7, ...), custom_call_target="tpu_custom_call" | custom-call | tf_op jit(solution)/shard_map/attend/pallas_call | solution.py:355
  177.0 5.4 %all-to-all-start.5 = ((bf16[4,128,512]{2,1,0:T(8,128)(2,1)}), bf16[4,128,512]{2,1,0:T(8,128)(2,1)S(1)}, u32[]{:S(2)}, u32[]{:S(2)}) async-start(bf16[4,128,512]{2,1,0:T(8,128)(2,1)} %get-tuple-element.18), calls=%async_computation.5 | async-start | bytes 1048576 | tf_op jit(solution)/shard_map/all_to_all | solution.py:538
  184.0 19.9 %all-to-all-done.5.group = bf16[4,128,512]{2,1,0:T(8,128)(2,1)S(1)} async-done(((bf16[4,128,512]{2,1,0:T(8,128)(2,1)}), bf16[4,128,512]{2,1,0:T(8,128)(2,1)S(1)}, u32[]{:S(2)}, u32[]{:S(2)}) %all-to-all-start.5) | async-done | bytes 524320 | tf_op jit(solution)/shard_map/all_to_all | solution.py:538
  203.9 2.1 ffn_copies.1
  206.0 4.4 %all-to-all-start.6 = ((bf16[4,4,128,512]{3,2,1,0:T(8,128)(2,1)}), bf16[4,4,128,512]{3,2,1,0:T(8,128)(2,1)}, u32[]{:S(2)}, u32[]{:S(2)}) async-start(bf16[4,4,128,512]{3,2,1,0:T(8,128)(2,1)} %get-tuple-element.21), calls=%async_computation.6 | async-start | bytes 4194304 | tf_op jit(solution)/shard_map/all_to_all | solution.py:540
  210.6 20.0 %all-gather.1 = bf16[576,512]{1,0:T(8,128)(2,1)S(1)} all-gather(bf16[144,512]{1,0:T(8,128)(2,1)S(1)} %get-tuple-element.20), channel_id=3, replica_groups=mesh['phase'=8,'x'=4,'za'=2,'zb'=2,'seq'=4] {'seq'}, dimensions={0}, use_global_device_ids=true | all-gather | bytes 737280 | tf_op jit(solution)/shard_map/all_gather | solution.py:541
  230.7 9.1 %collective-permute-start.7 = (bf16[1,128,512]{2,1,0:T(8,128)(2,1)S(1)}, bf16[1,128,512]{2,1,0:T(8,128)(2,1)S(1)}, u32[]{:S(2)}, u32[]{:S(2)}) collective-permute-start(bf16[1,128,512]{2,1,0:T(8,128)(2,1)S(1)} %constant_dynamic-slice_fusion), channel_id=1, source_target_pairs={{0,64},{64,128},{128,192},{192,256},{256,320},{320,384},{384,448},... | collective-permute-start | bytes 393224 | tf_op jit(solution)/shard_map/ppermute | solution.py:545
  239.8 10.6 %all-gather.3.r_ffn = f32[4,1,128]{2,1,0:T(1,128)S(1)} all-gather(f32[1,1,128]{2,1,0:T(1,128)S(1)} %rsqrt_bitcast_fusion), channel_id=4, replica_groups=mesh['phase'=8,'x'=4,'za'=2,'zb'=2,'seq'=4] {'x'}, dimensions={0}, use_global_device_ids=true | all-gather | bytes 2560 | tf_op jit(solution)/shard_map/all_gather | solution.py:542
  250.4 5.5 %hessian.1 = (bf16[512,2048]{1,0:T(8,128)(2,1)}, f32[1,128]{1,0:T(1,128)}) custom-call(s32[2]{0:T(128)S(1)} %pad_add_fusion.place, bf16[512,512]{1,0:T(8,128)(2,1)S(1)} %attn_left.1.after.left_a, bf16[4,4,128,512]{3,2,1,0:T(8,128)(2,1)S(1)} %all-to-all-done.1.cols.cols_a, f32[4,1,512]{2,1,0:T(1,128)S(1)} %get-tuple-element.15.gain.gain_a, ...), custom_call_target="tpu_custom_call" | custom-call | tf_op jit(solution)/shard_map/hessian/pallas_call | solution.py:474
  (63 shorter events, 18.9 us)
Async XLA Ops:
  0.6 31.4 %copy-start.14 = (bf16[1,128,512]{2,1,0:T(8,128)(2,1)S(1)}, bf16[1,128,512]{2,1,0:T(8,128)(2,1)}, u32[]{:S(2)}) copy-start(bf16[1,128,512]{2,1,0:T(8,128)(2,1)} %param.7) | copy-start | bytes 393220
  0.6 3.7 %collective-permute-start = (bf16[128,512]{1,0:T(8,128)(2,1)}, bf16[128,512]{1,0:T(8,128)(2,1)S(1)}, u32[]{:S(2)}, u32[]{:S(2)}) collective-permute-start(bf16[128,512]{1,0:T(8,128)(2,1)} %bitcast.18), channel_id=1, source_target_pairs={{0,0},{1,16},{2,32},{3,48},{4,4},{5,20},{6,36},{7,52},{8,8},{9,24}... | collective-permute-start | bytes 393224 | tf_op jit(solution)/shard_map/ppermute | solution.py:29
  3.7 0.7 collective-permute-start.1
  34.1 65.8 %copy-start.12 = (bf16[128,512]{1,0:T(8,128)(2,1)}, bf16[128,512]{1,0:T(8,128)(2,1)S(1)}, u32[]{:S(2)}) copy-start(bf16[128,512]{1,0:T(8,128)(2,1)S(1)} %get-tuple-element.16.own) | copy-start | bytes 393220
  34.1 56.7 %copy-start.8 = (bf16[1,2048,64]{1,2,0:T(8,128)(2,1)S(1)}, bf16[1,2048,64]{1,2,0:T(8,128)(2,1)}, u32[]{:S(2)}) copy-start(bf16[1,2048,64]{1,2,0:T(8,128)(2,1)} %param.12) | copy-start | bytes 786436
  34.1 56.7 %copy-start.9 = (bf16[1,2048,64]{1,2,0:T(8,128)(2,1)S(1)}, bf16[1,2048,64]{1,2,0:T(8,128)(2,1)}, u32[]{:S(2)}) copy-start(bf16[1,2048,64]{1,2,0:T(8,128)(2,1)} %param.13) | copy-start | bytes 786436
  34.1 56.7 %all-to-all-start.1 = ((bf16[4,4,128,512]{3,2,1,0:T(8,128)(2,1)}), bf16[4,4,128,512]{3,2,1,0:T(8,128)(2,1)S(1)}, u32[]{:S(2)}, u32[]{:S(2)}) async-start(bf16[4,4,128,512]{3,2,1,0:T(8,128)(2,1)} %get-tuple-element.14), calls=%async_computation.1 | async-start | bytes 4194304 | tf_op jit(solution)/shard_map/all_to_all | solution.py:522
  58.3 16.3 %collective-permute-start.3 = (bf16[128,512]{1,0:T(8,128)(2,1)S(1)}, bf16[128,512]{1,0:T(8,128)(2,1)S(1)}, u32[]{:S(2)}, u32[]{:S(2)}) collective-permute-start(bf16[128,512]{1,0:T(8,128)(2,1)S(1)} %get-tuple-element.16.own), channel_id=1, source_target_pairs={{0,2},{1,3},{2,0},{3,1},{4,6},{5,7},{6,4},{7,5},{8,10},{9,11},{10,... | collective-permute-start | bytes 393224 | tf_op jit(solution)/shard_map/ppermute | solution.py:41
  69.6 21.3 %collective-permute-start.2 = (bf16[128,512]{1,0:T(8,128)(2,1)S(1)}, bf16[128,512]{1,0:T(8,128)(2,1)S(1)}, u32[]{:S(2)}, u32[]{:S(2)}) collective-permute-start(bf16[128,512]{1,0:T(8,128)(2,1)S(1)} %get-tuple-element.16.own), channel_id=1, source_target_pairs={{0,1},{1,2},{2,3},{3,0},{4,5},{5,6},{6,7},{7,4},{8,9},{9,10},{10,1... | collective-permute-start | bytes 393224 | tf_op jit(solution)/shard_map/ppermute | solution.py:41
  90.8 5.6 %copy-start.2 = (bf16[128,512]{1,0:T(8,128)(2,1)}, bf16[128,512]{1,0:T(8,128)(2,1)S(1)}, u32[]{:S(2)}) copy-start(bf16[128,512]{1,0:T(8,128)(2,1)S(1)} %collective-permute-done.2.first.one) | copy-start | bytes 393220
  90.8 1.6 copy-start
  96.4 20.8 %all-to-all-start.2 = ((bf16[4,640,128]{2,1,0:T(8,128)(2,1)}), bf16[4,640,128]{2,1,0:T(8,128)(2,1)S(1)}, u32[]{:S(2)}, u32[]{:S(2)}) async-start(bf16[4,640,128]{2,1,0:T(8,128)(2,1)} %project.1), calls=%async_computation.2 | async-start | bytes 1310720 | tf_op jit(solution)/shard_map/all_to_all | solution.py:525
  99.9 17.3 %collective-permute-start.4 = (bf16[128,512]{1,0:T(8,128)(2,1)S(1)}, bf16[128,512]{1,0:T(8,128)(2,1)S(1)}, u32[]{:S(2)}, u32[]{:S(2)}) collective-permute-start(bf16[128,512]{1,0:T(8,128)(2,1)S(1)} %get-tuple-element.16.own), channel_id=1, source_target_pairs={{0,3},{1,0},{2,1},{3,2},{4,7},{5,4},{6,5},{7,6},{8,11},{9,8},{10,9... | collective-permute-start | bytes 393224 | tf_op jit(solution)/shard_map/ppermute | solution.py:41
  134.4 26.0 %copy-start.15 = (bf16[1,512]{1,0:T(2,128)(2,1)S(1)}, bf16[1,512]{1,0:T(2,128)(2,1)}, u32[]{:S(2)}) copy-start(bf16[1,512]{1,0:T(2,128)(2,1)} %gain.1) | copy-start | bytes 3076
  135.8 33.4 %all-to-all-start.4 = ((bf16[4,512,128]{2,1,0:T(8,128)(2,1)}), bf16[4,512,128]{2,1,0:T(8,128)(2,1)S(1)}, u32[]{:S(2)}, u32[]{:S(2)}) async-start(bf16[4,512,128]{2,1,0:T(8,128)(2,1)} %take_after.1), calls=%async_computation.4 | async-start | bytes 1048576 | tf_op jit(solution)/shard_map/all_to_all | solution.py:527
  153.1 15.5 %collective-permute-start.5 = (bf16[4,144,128]{2,1,0:T(8,128)(2,1)S(1)}, bf16[4,144,128]{2,1,0:T(8,128)(2,1)S(1)}, u32[]{:S(2)}, u32[]{:S(2)}) collective-permute-start(bf16[4,144,128]{2,1,0:T(8,128)(2,1)S(1)} %bitcast.13), channel_id=1, source_target_pairs={{0,4},{4,0},{1,5},{5,1},{2,6},{6,2},{3,7},{7,3},{8,12},{12,8},{9,1... | collective-permute-start | bytes 442376 | tf_op jit(solution)/shard_map/ppermute | solution.py:529
  160.5 0.9 copy-start.3
  169.2 1.0 copy-start.1
  171.1 0.9 copy-start.11
  177.0 26.9 %all-to-all-start.5 = ((bf16[4,128,512]{2,1,0:T(8,128)(2,1)}), bf16[4,128,512]{2,1,0:T(8,128)(2,1)S(1)}, u32[]{:S(2)}, u32[]{:S(2)}) async-start(bf16[4,128,512]{2,1,0:T(8,128)(2,1)} %get-tuple-element.18), calls=%async_computation.5 | async-start | bytes 1048576 | tf_op jit(solution)/shard_map/all_to_all | solution.py:538
  182.5 1.6 collective-permute-start.6
  206.0 44.4 %all-to-all-start.6 = ((bf16[4,4,128,512]{3,2,1,0:T(8,128)(2,1)}), bf16[4,4,128,512]{3,2,1,0:T(8,128)(2,1)}, u32[]{:S(2)}, u32[]{:S(2)}) async-start(bf16[4,4,128,512]{3,2,1,0:T(8,128)(2,1)} %get-tuple-element.21), calls=%async_computation.6 | async-start | bytes 4194304 | tf_op jit(solution)/shard_map/all_to_all | solution.py:540
  210.5 39.9 %copy-start.16 = (bf16[1,512]{1,0:T(2,128)(2,1)S(1)}, bf16[1,512]{1,0:T(2,128)(2,1)}, u32[]{:S(2)}) copy-start(bf16[1,512]{1,0:T(2,128)(2,1)} %gain_row.1) | copy-start | bytes 3076
  230.7 19.7 %collective-permute-start.7 = (bf16[1,128,512]{2,1,0:T(8,128)(2,1)S(1)}, bf16[1,128,512]{2,1,0:T(8,128)(2,1)S(1)}, u32[]{:S(2)}, u32[]{:S(2)}) collective-permute-start(bf16[1,128,512]{2,1,0:T(8,128)(2,1)S(1)} %constant_dynamic-slice_fusion), channel_id=1, source_target_pairs={{0,64},{64,128},{128,192},{192,256},{256,320},{320,384},{384,448},... | collective-permute-start | bytes 393224 | tf_op jit(solution)/shard_map/ppermute | solution.py:545
  (6 other events, 4.7 us)

commit v7 on v6

--- a/solution.py
+++ b/solution.py
@@ -29,22 +29,12 @@
     return lax.ppermute(value, GROUP, pairs)
 
 
-def to_upper(value, away):
-    nx, nz, ns = lax.axis_size("x"), lax.axis_size(ZL), lax.axis_size("seq")
-    pairs = [
-        ((x * nz + z) * ns + s, (x * nz + z) * ns + (s + away) % ns)
-        for x in range(nx)
-        for z in range(nz)
-        for s in range(ns)
-        if (s + away) % ns >= x
-    ]
-    return lax.ppermute(value, GROUP, pairs)
-
-
-def project_kernel(cols, gain, wq, wk, wv, first, second, out, q_acc, kv_acc):
+def project_kernel(cols, gain, wq, wk, wv, first, second, out, q_acc, kv_acc, squares):
     step = pl.program_id(0)
     blocks, rows, feats = cols.shape
-    left = (cols[...].reshape(blocks * rows, feats).astype(f32) * gain[...]).astype(bf16)
+    raw = cols[...].reshape(blocks * rows, feats).astype(f32)
+    left = (raw * gain[...]).astype(bf16)
+    part = jnp.sum(raw * raw, axis=1, keepdims=True)
     kv_w = jnp.concatenate([wk[...], wv[...]], 0)
     kv = lax.dot_general(left, kv_w, (((1,), (1,)), ((), ())), preferred_element_type=f32)
     q = jnp.dot(left, wq[...], preferred_element_type=f32)
@@ -53,11 +43,13 @@
     def _():
         q_acc[...] = q
         kv_acc[...] = kv
+        squares[...] = part
 
     @pl.when(step > 0)
     def _():
         q_acc[...] += q
         kv_acc[...] += kv
+        squares[...] += part
 
     @pl.when(step == pl.num_programs(0) - 1)
     def _():
@@ -65,6 +57,8 @@
         for k in range(blocks):
             block = pl.ds(k * rows, rows)
             out[k, pl.ds(heads * rows, rows), :] = kv_acc[block, :].astype(bf16)
+            sums = stacked(three_parts(row_of(squares[block, :])))
+            out[k, pl.ds((heads + 1) * rows, 16), :] = sums
             for h in range(heads):
                 out[k, pl.ds(h * rows, rows), :] = q_acc[block, pl.ds(h * HD, HD)].astype(bf16)
 
@@ -85,11 +79,12 @@
             kv_spec,
         ]
         + [pl.BlockSpec(memory_space=pl.ANY)] * len(after),
-        out_specs=pl.BlockSpec((blocks, (heads + 1) * rows, HD), lambda z: (0, 0, 0)),
-        out_shape=jax.ShapeDtypeStruct((blocks, (heads + 1) * rows, HD), bf16),
+        out_specs=fixed((blocks, (heads + 1) * rows + 16, HD)),
+        out_shape=pltpu.HBM((blocks, (heads + 1) * rows + 16, HD), bf16),
         scratch_shapes=[
             pltpu.VMEM((blocks * rows, q_width), f32),
             pltpu.VMEM((blocks * rows, kv_width), f32),
+            pltpu.VMEM((blocks * rows, 1), f32),
         ],
         compiler_params=params(),
         name="project",
@@ -139,26 +134,24 @@
         squares[...] += part
 
 
-def attn_copies_kernel(group, own, copies, kept, sums, gain_a, gain_f, squares):
+def attn_copies_kernel(group, own, copies, kept, gain_a, gain_f):
     rows = own.shape[0]
     for k in range(copies.shape[0]):
         copies[k] = group[pl.ds(0, rows), :]
     gains = group[pl.ds(rows, 16), :].astype(f32)
     gain_a[...] = gains[0:1]
     gain_f[...] = gains[1:2]
-    add_squares(group, squares)
-
-    @pl.when(pl.program_id(0) == pl.num_programs(0) - 1)
+
+    @pl.when(pl.program_id(0) == 0)
     def _():
         kept[...] = own[...]
-        sums[...] = stacked(three_parts(row_of(squares[...])))
 
 
 def attn_copies(group, own, count):
     parts, tall, feats = group.shape
     rows = own.shape[0]
     gain = pl.BlockSpec((None, 1, feats), lambda z: (z, 0, 0))
-    gain_shape = jax.ShapeDtypeStruct((parts, 1, feats), f32)
+    gain_shape = pltpu.HBM((parts, 1, feats), f32)
     return pl.pallas_call(
         attn_copies_kernel,
         grid=(parts,),
@@ -166,24 +159,21 @@
         out_specs=[
             pl.BlockSpec((count, None, rows, feats), lambda z: (0, z, 0, 0)),
             fixed(own.shape),
-            fixed((16, rows)),
             gain,
             gain,
         ],
         out_shape=[
             pltpu.HBM((count, parts, rows, feats), bf16),
-            jax.ShapeDtypeStruct(own.shape, bf16),
-            jax.ShapeDtypeStruct((16, rows), bf16),
+            pltpu.HBM(own.shape, bf16),
             gain_shape,
             gain_shape,
         ],
-        scratch_shapes=[pltpu.VMEM((rows, 1), f32)],
         compiler_params=params(),
         name="attn_copies",
     )(group, own)
 
 
-def ffn_copies_kernel(group, own, copies, message, squares):
+def ffn_copies_kernel(group, own, after, copies, message, squares):
     rows, feats = own.shape
     for k in range(copies.shape[0]):
         copies[k] = group[...]
@@ -196,12 +186,16 @@
         message[pl.ds(rows, 16), :] = jnp.concatenate([sums] * (feats // rows), 1)
 
 
-def ffn_copies(group, own, count):
+def ffn_copies(group, own, after, count):
     parts, rows, feats = group.shape
     return pl.pallas_call(
         ffn_copies_kernel,
         grid=(parts,),
-        in_specs=[pl.BlockSpec((None, rows, feats), lambda z: (z, 0, 0)), fixed(own.shape)],
+        in_specs=[
+            pl.BlockSpec((None, rows, feats), lambda z: (z, 0, 0)),
+            fixed(own.shape),
+            pl.BlockSpec(memory_space=pl.ANY),
+        ],
         out_specs=[
             pl.BlockSpec((count, None, rows, feats), lambda z: (0, z, 0, 0)),
             fixed((rows + 16, feats)),
@@ -213,68 +207,36 @@
         scratch_shapes=[pltpu.VMEM((rows, 1), f32)],
         compiler_params=params(),
         name="ffn_copies",
-    )(group, own)
-
-
-def kv_message_kernel(message, sums, after, out):
-    rows = message.shape[0]
-    out[pl.ds(0, rows), :] = message[...]
-    out[pl.ds(rows, 16), :] = sums[...]
-
-
-def kv_message(message, sums, after):
-    blocks, tall, width = message.shape
-    rows = sums.shape[1]
-    last = tall // rows - 1
-    return pl.pallas_call(
-        kv_message_kernel,
-        grid=(blocks,),
-        in_specs=[
-            pl.BlockSpec((None, rows, width), lambda i: (i, last, 0)),
-            fixed(sums.shape),
-            pl.BlockSpec(memory_space=pl.ANY),
-        ],
-        out_specs=pl.BlockSpec((None, rows + 16, width), lambda i: (i, 0, 0)),
-        out_shape=jax.ShapeDtypeStruct((blocks, rows + 16, width), bf16),
-        compiler_params=params(),
-        name="kv_message",
-    )(message, sums, after)
-
-
-def take_kernel(value, after, out):
-    out[...] = value[...]
-
-
-def take_after(value, count, after):
-    shape = (value.shape[0], count, value.shape[2])
-    spec = pl.BlockSpec((1, count, value.shape[2]), lambda i: (i, 0, 0))
-    return pl.pallas_call(
-        take_kernel,
-        grid=(value.shape[0],),
-        in_specs=[spec, pl.BlockSpec(memory_space=pl.ANY)],
-        out_specs=spec,
-        out_shape=pltpu.HBM(shape, value.dtype),
-        compiler_params=params(),
-        name="take_after",
-    )(value, after)
+    )(group, own, after)
 
 
 def kv_sum_kernel(width, arrived, docs, out):
-    rows = out.shape[0] - 16
-    out[pl.ds(0, rows), :] = jnp.sum(arrived[:, pl.ds(0, rows), :].astype(f32), axis=0).astype(bf16)
+    rows = out.shape[1] - 16
+    kv = jnp.sum(arrived[:, pl.ds(0, rows), :].astype(f32), axis=0).astype(bf16)
     sums = jnp.sum(arrived[:, pl.ds(rows, 16), :].astype(f32), axis=0)
     r = lax.rsqrt((sums[0:1] + sums[1:2] + sums[2:3]) / width + norm_eps)
-    own = docs[...].astype(f32)[2:3, :rows]
-    out[pl.ds(rows, 16), :] = stacked(three_parts(r), [own])
-
-
-def kv_sum(width, arrived, docs):
+    tail = stacked(three_parts(r), [docs[...].astype(f32)[2:3, :rows]])
+    for copy in range(out.shape[0]):
+        out[copy, pl.ds(0, rows), :] = kv
+        out[copy, pl.ds(rows, 16), :] = tail
+
+
+def kv_sum(width, arrived, docs, copies):
+    blocks, tall, lanes = arrived.shape
+    rows = HD
+    last = tall - rows - 16
     return pl.pallas_call(
         functools.partial(kv_sum_kernel, width),
         grid=(1,),
-        in_specs=[fixed(arrived.shape), fixed(docs.shape)],
-        out_specs=fixed(arrived.shape[1:]),
-        out_shape=jax.ShapeDtypeStruct(arrived.shape[1:], bf16),
+        in_specs=[
+            pl.BlockSpec(
+                (pl.Element(blocks), pl.Element(rows + 16), pl.Element(lanes)),
+                lambda i: (0, last, 0),
+            ),
+            fixed(docs.shape),
+        ],
+        out_specs=fixed((copies, rows + 16, lanes)),
+        out_shape=pltpu.HBM((copies, rows + 16, lanes), bf16),
         compiler_params=params(),
         name="kv_sum",
     )(arrived, docs)
@@ -295,22 +257,20 @@
 
 
 def attend_kernel(
-    q_in, kv_own, kv_other, table, resid, after, copies, out,
+    q_in, kv_in, table, resid, copies, out,
     keys, values, r_all, docs_all, r_own, docs_own,
 ):
     rows = out.shape[0]
     tokens = keys.shape[0]
-    x_pos, zb_pos = lax.axis_index("x"), lax.axis_index("zb")
+    x_pos = lax.axis_index("x")
 
     @pl.when(pl.program_id(0) == 0)
     def _():
         lower = lax.broadcasted_iota(jnp.int32, (rows, HD), 1) < HD // 2
         for k in range(tokens // rows):
-            mine = kv_own[k, pl.ds(0, rows), :].astype(f32)
-            other = kv_other[k, pl.ds(0, rows), :].astype(f32)
-            first = jnp.where(zb_pos == 0, mine, other)
-            second = jnp.where(zb_pos == 0, other, mine)
-            tail = kv_own[k, pl.ds(rows, 16), :].astype(f32)
+            first = kv_in[2 * k, pl.ds(0, rows), :].astype(f32)
+            second = kv_in[2 * k + 1, pl.ds(0, rows), :].astype(f32)
+            tail = kv_in[2 * k, pl.ds(rows, 16), :].astype(f32)
             block = pl.ds(k * rows, rows)
             key = jnp.where(lower, first, pltpu.roll(second, HD // 2, 1))
             keys[block, :] = rotate(key, table[block, :])
@@ -349,7 +309,7 @@
         copies[copy] = result
 
 
-def attend(q_in, kv_own, kv_other, table, resid, after, copies):
+def attend(q_in, kv_in, table, resid, copies):
     rows, feats = resid.shape
     heads, tokens = feats // HD, table.shape[0]
     return pl.pallas_call(
@@ -358,8 +318,8 @@
         in_specs=[
             pl.BlockSpec((q_in.shape[0], rows, HD), lambda h: (0, h, 0)),
         ]
-        + [fixed(kv_own.shape), fixed(kv_other.shape), fixed(table.shape)]
-        + [pl.BlockSpec((rows, HD), lambda h: (0, h)), pl.BlockSpec(memory_space=pl.ANY)],
+        + [fixed(kv_in.shape), fixed(table.shape)]
+        + [pl.BlockSpec((rows, HD), lambda h: (0, h))],
         out_specs=[
             pl.BlockSpec((copies, rows, HD), lambda h: (0, 0, h)),
             pl.BlockSpec((rows, HD), lambda h: (0, h)),
@@ -378,7 +338,7 @@
         ],
         compiler_params=params(),
         name="attend",
-    )(q_in, kv_own, kv_other, table, resid, after)
+    )(q_in, kv_in, table, resid)
 
 
 def left_block(block, gain, r, scale):
@@ -386,28 +346,24 @@
     return turned, r * r * scale
 
 
-def attn_left_kernel(scale, own, one, two, three, gain, kv, out):
-    rows = own.shape[0]
-    blocks = kv.shape[0]
-    seq_pos = lax.axis_index("seq")
-    for away, ref in enumerate((own, one, two, three)):
-        k = lax.rem(seq_pos + blocks - away, blocks)
-        parts = kv[k, pl.ds(rows, 16), :].astype(f32)
+def attn_left_kernel(scale, own_rows, gain, kv, out):
+    blocks, rows, feats = own_rows.shape
+    for k in range(blocks):
+        parts = kv[2 * k, pl.ds(rows, 16), :].astype(f32)
         r = parts[0:1] + parts[1:2] + parts[2:3]
-        turned, weight = left_block(ref[...], gain[...].astype(f32), r, scale)
-        out[:, pl.ds(pl.multiple_of(k * rows, rows), rows)] = (turned * weight).astype(bf16)
-
-
-def attn_left(scale, rows, gain, kv_all):
-    feats = gain.shape[1]
-    tokens = rows[0].shape[0] * kv_all.shape[0]
-    arrays = (*rows, gain, kv_all)
+        turned, weight = left_block(own_rows[k], gain[...].astype(f32), r, scale)
+        out[:, pl.ds(k * rows, rows)] = (turned * weight).astype(bf16)
+
+
+def attn_left(scale, own_rows, gain, kv_all):
+    blocks, rows, feats = own_rows.shape
+    arrays = (own_rows, gain, kv_all)
     return pl.pallas_call(
         functools.partial(attn_left_kernel, scale),
         grid=(1,),
         in_specs=[fixed(a.shape) for a in arrays],
-        out_specs=fixed((feats, tokens)),
-        out_shape=jax.ShapeDtypeStruct((feats, tokens), bf16),
+        out_specs=fixed((feats, blocks * rows)),
+        out_shape=jax.ShapeDtypeStruct((feats, blocks * rows), bf16),
         compiler_params=params(),
         name="attn_left",
     )(*arrays)
@@ -517,26 +473,22 @@
     docs = jnp.pad(segment_ids.astype(bf16), ((0, 13), (0, feats - rows)))
     extra = swap_x_seq(jnp.concatenate([gain_attn, gain_ffn, docs]))
     group = lax.all_to_all(copied(jnp.concatenate([resid, extra]), nz), ZL, 0, 0)
-    copies, own_rows, sums, gain_a, gain_f = attn_copies(group, hidden[0], nx)
-    attn_rows = [own_rows] + [to_upper(own_rows, d) for d in range(1, ns)]
+    copies, own_rows, gain_a, gain_f = attn_copies(group, hidden[0], nx)
+    attn_rows = lax.all_gather(own_rows, "seq")
     attn_cols = lax.all_to_all(copies, "x", 0, 0)
-
-    message = project(attn_cols, gain_a, w_query, w_key, w_value, *attn_rows[1:3])
-    message = lax.all_to_all(message, "x", 0, 0)
-    kv = lax.all_to_all(kv_message(message, sums, attn_rows[3]), "seq", 0, 0)
-    query = lax.all_to_all(take_after(message, rows * feats // HD, kv), "seq", 0, 0)
-    kv_all = lax.all_gather(kv_sum(width, kv, extra), "x")
-    kv_other = lax.ppermute(kv_all, "zb", [(0, 1), (1, 0)])
-    left_a = attn_left(scale, attn_rows, gain_attn, kv_all)
 
     half = HD // 2
     freq = rope_base ** (-(jnp.arange(half, dtype=f32) * 2.0 / HD))
     angle = jnp.arange(tokens, dtype=f32)[:, None] * freq[None, :]
     table = jnp.concatenate([jnp.cos(angle), jnp.sin(angle)], 1)
-    copies, section_out = attend(query, kv_all, kv_other, table, resid, left_a, nz)
+    message = project(attn_cols, gain_a, w_query, w_key, w_value, attn_rows, table)
+    arrived = lax.all_to_all(lax.all_to_all(message, "x", 0, 0), "seq", 0, 0)
+    kv = lax.all_to_all(kv_sum(width, arrived, extra, 2 * nx), ("x", "zb"), 0, 0)
+    copies, section_out = attend(arrived, kv, table, resid, nz)
+    left_a = attn_left(scale, attn_rows, gain_attn, kv)
 
     group = lax.all_to_all(copies, ZL, 0, 0)
-    copies, message = ffn_copies(group, swap_x_seq(section_out), nx)
+    copies, message = ffn_copies(group, swap_x_seq(section_out), left_a, nx)
     ffn_cols = lax.all_to_all(copies, "x", 0, 0)
     ffn_rows = lax.all_gather(message, "seq")
     r_ffn = lax.all_gather(r_of(ffn_rows[:, rows : rows + 3, :rows])[None], "x")

time: 260 us -> 248 us (0.954)
  blocking collectives: 87.7 us -> 136 us
  waiting for transfers between devices: 54.3 us -> 13.6 us
  starting transfers between devices: 80.1 us -> 67.6 us
  local copies, waits for them, and re-layouts: 9.83 us -> 4.62 us
    all_to_all x1 -> x3, blocking collectives: 16.5 us -> 54.8 us  [the longest x2 43.7 us: on_device(): arrived = lax.all_to_all(lax.all_to_all(message, 'x', 0, 0), 'seq', 0, 0)]
    ppermute x4 -> x0, waiting for transfers between devices: 34.3 us -> none  [the longest x3 29.3 us: to_upper(): return lax.ppermute(value, GROUP, pairs)]
    ppermute x4 -> x0, starting transfers between devices: 26.1 us -> none  [the longest x3 20.5 us: to_upper(): return lax.ppermute(value, GROUP, pairs)]
    all_gather x1, blocking collectives: 13.7 us -> 27.3 us  [on_device(): attn_rows = lax.all_gather(own_rows, 'seq')]
    all_to_all x1, starting transfers between devices: 5.44 us -> 13.2 us  [on_device(): group = lax.all_to_all(copies, ZL, 0, 0)]
    ppermute x1, starting transfers between devices: 9.12 us -> 16.5 us  [on_device(): lax.ppermute(passed, 'phase', [(p, (p + 1) % count) for p in range(count)])]
    all_to_all x2 -> x0, starting transfers between devices: 6.96 us -> none  [the longest x1 3.48 us: on_device(): message = lax.all_to_all(message, 'x', 0, 0)]
    all_to_all x1, waiting for transfers between devices: 19.9 us -> 13.6 us  [on_device(): group = lax.all_to_all(copies, ZL, 0, 0)]
  transfers between devices with their start and end apart: 13 -> 7, of which waited for: 4 -> 1; matrix products, arithmetic and copies ran while one was open for 1% -> 1% of each run, Pallas kernels for 0% -> 0%
where the time goes in v7:
time: 248 us; the launch traced here: 247 us
  blocking collectives  136 us (55%)
  starting transfers between devices  67.6 us (27%)
  Pallas kernels  21.5 us (9%)
  waiting for transfers between devices  13.6 us (5%)
  local copies, waits for them, and re-layouts  4.62 us (2%)
  other arithmetic  2.61 us (1%)
    all_to_all x2, blocking collectives, on_device(): arrived = lax.all_to_all(lax.all_to_all(message, 'x', 0, 0), 'seq', 0, 0)  43.7 us
    all_to_all x1, starting transfers between devices, on_device(): attn_cols = lax.all_to_all(copies, 'x', 0, 0)  29.4 us
    all_gather x1, blocking collectives, on_device(): attn_rows = lax.all_gather(own_rows, 'seq')  27.3 us
    all_gather x1, blocking collectives, on_device(): ffn_rows = lax.all_gather(message, 'seq')  23.8 us
    all_to_all x1, blocking collectives, on_device(): lax.all_to_all(copied(jnp.concatenate([resid, extra]), nz), ZL, 0, 0)  21.7 us
    ppermute x1, starting transfers between devices, on_device(): lax.ppermute(passed, 'phase', [(p, (p + 1) % count) for p in range(count)])  16.5 us
    all_to_all x1, waiting for transfers between devices, on_device(): group = lax.all_to_all(copies, ZL, 0, 0)  13.6 us
    all_to_all x1, starting transfers between devices, on_device(): group = lax.all_to_all(copies, ZL, 0, 0)  13.2 us
  transfers between devices with their start and end apart: 7, of which 1 were waited for; matrix products, arithmetic and copies ran while one was open for 1% of the time, Pallas kernels for 0%

profile of v7, /device:TPU:1, one launch (start us, length us, event | category | flops | bytes accessed | tf_op | source)
XLA Modules:
  0.0 246.7 jit_solution(2461246452430786634)
XLA Ops:
  0.6 1.7 collective-permute-start
  3.0 0.7 fusion.3
  4.5 21.7 %all_to_all.35.group = bf16[4,144,512]{2,1,0:T(8,128)(2,1)S(1)} all-to-all(bf16[4,144,512]{2,1,0:T(8,128)(2,1)S(1)} %broadcast_in_dim.4), channel_id=1, replica_groups=mesh['phase'=8,'x'=4,'za'=2,'zb'=2,'seq'=4] {'za','zb'}, dimensions={0} | all-to-all | bytes 1179648 | tf_op jit(solution)/shard_map/all_to_all | solution.py:475
  26.1 1.9 attn_copies.1
  28.1 29.4 %all-to-all-start.1 = ((bf16[4,4,128,512]{3,2,1,0:T(8,128)(2,1)}), bf16[4,4,128,512]{3,2,1,0:T(8,128)(2,1)S(1)}, u32[]{:S(2)}, u32[]{:S(2)}) async-start(bf16[4,4,128,512]{3,2,1,0:T(8,128)(2,1)} %get-tuple-element.13), calls=%async_computation.1 | async-start | bytes 4194304 | tf_op jit(solution)/shard_map/all_to_all | solution.py:478
  57.5 1.0 fusion.1
  58.6 27.3 %all-gather = bf16[512,512]{1,0:T(8,128)(2,1)S(1)} all-gather(bf16[128,512]{1,0:T(8,128)(2,1)} %get-tuple-element.15), channel_id=2, replica_groups=mesh['phase'=8,'x'=4,'za'=2,'zb'=2,'seq'=4] {'seq'}, dimensions={0}, use_global_device_ids=true | all-gather | bytes 655360 | tf_op jit(solution)/shard_map/all_gather | solution.py:477
  85.9 1.6 copy-done
  88.2 4.1 %project.1 = bf16[4,656,128]{2,1,0:T(8,128)(2,1)} custom-call(bf16[4,4,128,512]{3,2,1,0:T(8,128)(2,1)S(1)} %all-to-all-done.1.cols.cols_a, f32[4,1,512]{2,1,0:T(1,128)S(1)} %copy-done.6, bf16[1,2048,512]{2,1,0:T(8,128)(2,1)S(1)} %copy-done, bf16[1,64,2048]{2,1,0:T(8,128)(2,1)S(1)} %bitcast.15, bf16[1,64,2048]{2,1,0:T(8,128)(2,1)S(1)} %bitcast.16, ...), custom_call_target="tpu_custom_call" | custom-call | tf_op jit(solution)/shard_map/project/pallas_call | solution.py:71
  92.3 12.6 %all_to_all.36 = bf16[4,656,128]{2,1,0:T(8,128)(2,1)S(1)} all-to-all(bf16[4,656,128]{2,1,0:T(8,128)(2,1)} %project.1), channel_id=1, replica_groups=mesh['phase'=8,'x'=4,'za'=2,'zb'=2,'seq'=4] {'x'}, dimensions={0} | all-to-all | bytes 1343488 | tf_op jit(solution)/shard_map/all_to_all | solution.py:485
  104.9 31.2 %all_to_all.37.arrived.q_in = bf16[4,656,128]{2,1,0:T(8,128)(2,1)S(1)} all-to-all(bf16[4,656,128]{2,1,0:T(8,128)(2,1)S(1)} %all_to_all.36), channel_id=1, replica_groups=mesh['phase'=8,'x'=4,'za'=2,'zb'=2,'seq'=4] {'seq'}, dimensions={0} | all-to-all | bytes 1343488 | tf_op jit(solution)/shard_map/all_to_all | solution.py:485
  136.0 0.8 kv_sum.1
  136.8 11.0 %all_to_all.38.kv_in.kv = bf16[8,144,128]{2,1,0:T(8,128)(2,1)S(1)} all-to-all(bf16[8,144,128]{2,1,0:T(8,128)(2,1)} %kv_sum.1), channel_id=1, replica_groups=mesh['phase'=8,'x'=4,'za'=2,'zb'=2,'seq'=4] {'x','zb'}, dimensions={0} | all-to-all | bytes 589824 | tf_op jit(solution)/shard_map/all_to_all | solution.py:486
  147.8 5.1 %attend.1 = (bf16[4,128,512]{2,1,0:T(8,128)(2,1)}, bf16[128,512]{1,0:T(8,128)(2,1)}) custom-call(bf16[4,656,128]{2,1,0:T(8,128)(2,1)S(1)} %all_to_all.37.arrived.q_in, bf16[8,144,128]{2,1,0:T(8,128)(2,1)S(1)} %all_to_all.38.kv_in.kv, f32[512,128]{1,0:T(8,128)S(1)} %pad_maximum_fusion.second.table, bf16[128,512]{1,0:T(8,128)(2,1)S(1)} %collective-permute-done.resid), custom_call_target="tpu_custom_call" | custom-call | tf_op jit(solution)/shard_map/attend/pallas_call | solution.py:315
  153.0 13.2 %all-to-all-start.5 = ((bf16[4,128,512]{2,1,0:T(8,128)(2,1)}), bf16[4,128,512]{2,1,0:T(8,128)(2,1)}, u32[]{:S(2)}, u32[]{:S(2)}) async-start(bf16[4,128,512]{2,1,0:T(8,128)(2,1)} %get-tuple-element.16), calls=%async_computation.5 | async-start | bytes 1048576 | tf_op jit(solution)/shard_map/all_to_all | solution.py:490
  166.1 1.6 collective-permute-start.2
  168.7 13.6 %all-to-all-done.5.group = bf16[4,128,512]{2,1,0:T(8,128)(2,1)} async-done(((bf16[4,128,512]{2,1,0:T(8,128)(2,1)}), bf16[4,128,512]{2,1,0:T(8,128)(2,1)}, u32[]{:S(2)}, u32[]{:S(2)}) %all-to-all-start.5) | async-done | bytes 524320 | tf_op jit(solution)/shard_map/all_to_all | solution.py:490
  182.3 0.9 copy-done.4
  183.2 3.7 %ffn_copies.1 = (bf16[4,4,128,512]{3,2,1,0:T(8,128)(2,1)}, bf16[144,512]{1,0:T(8,128)(2,1)S(1)}) custom-call(bf16[4,128,512]{2,1,0:T(8,128)(2,1)} %all-to-all-done.5.group, bf16[128,512]{1,0:T(8,128)(2,1)S(1)} %copy-done.4, bf16[512,512]{1,0:T(8,128)(2,1)S(1)} %attn_left.1.after.left_a), custom_call_target="tpu_custom_call" | custom-call | tf_op jit(solution)/shard_map/ffn_copies/pallas_call | solution.py:191
  186.9 4.6 %all-to-all-start.6 = ((bf16[4,4,128,512]{3,2,1,0:T(8,128)(2,1)}), bf16[4,4,128,512]{3,2,1,0:T(8,128)(2,1)}, u32[]{:S(2)}, u32[]{:S(2)}) async-start(bf16[4,4,128,512]{3,2,1,0:T(8,128)(2,1)} %get-tuple-element.19), calls=%async_computation.6 | async-start | bytes 4194304 | tf_op jit(solution)/shard_map/all_to_all | solution.py:492
  191.6 23.8 %all-gather.1 = bf16[576,512]{1,0:T(8,128)(2,1)S(1)} all-gather(bf16[144,512]{1,0:T(8,128)(2,1)S(1)} %get-tuple-element.18), channel_id=3, replica_groups=mesh['phase'=8,'x'=4,'za'=2,'zb'=2,'seq'=4] {'seq'}, dimensions={0}, use_global_device_ids=true | all-gather | bytes 737280 | tf_op jit(solution)/shard_map/all_gather | solution.py:493
  215.5 16.5 %collective-permute-start.3 = (bf16[1,128,512]{2,1,0:T(8,128)(2,1)S(1)}, bf16[1,128,512]{2,1,0:T(8,128)(2,1)S(1)}, u32[]{:S(2)}, u32[]{:S(2)}) collective-permute-start(bf16[1,128,512]{2,1,0:T(8,128)(2,1)S(1)} %constant_dynamic-slice_fusion), channel_id=1, source_target_pairs={{0,64},{64,128},{128,192},{192,256},{256,320},{320,384},{384,448},... | collective-permute-start | bytes 393224 | tf_op jit(solution)/shard_map/ppermute | solution.py:497
  232.1 8.5 %all-gather.3.r_ffn = f32[4,1,128]{2,1,0:T(1,128)S(1)} all-gather(f32[1,1,128]{2,1,0:T(1,128)S(1)} %rsqrt_bitcast_fusion), channel_id=4, replica_groups=mesh['phase'=8,'x'=4,'za'=2,'zb'=2,'seq'=4] {'x'}, dimensions={0}, use_global_device_ids=true | all-gather | bytes 2560 | tf_op jit(solution)/shard_map/all_gather | solution.py:494
  240.6 5.5 %hessian.1 = (bf16[512,2048]{1,0:T(8,128)(2,1)}, f32[1,128]{1,0:T(1,128)}) custom-call(s32[2]{0:T(128)S(1)} %pad_add_fusion.place, bf16[512,512]{1,0:T(8,128)(2,1)S(1)} %attn_left.1.after.left_a, bf16[4,4,128,512]{3,2,1,0:T(8,128)(2,1)S(1)} %all-to-all-done.1.cols.cols_a, f32[4,1,512]{2,1,0:T(1,128)S(1)} %copy-done.7, bf16[4,144,512]{2,1,0:T(8,128)(2,1)S(1)} %bitcast.12, ...), custom_call_target="tpu_custom_call" | custom-call | tf_op jit(solution)/shard_map/hessian/pallas_call | solution.py:430
  (39 shorter events, 4.1 us)
Async XLA Ops:
  0.6 25.5 %copy-start.5 = (bf16[1,128,512]{2,1,0:T(8,128)(2,1)S(1)}, bf16[1,128,512]{2,1,0:T(8,128)(2,1)}, u32[]{:S(2)}) copy-start(bf16[1,128,512]{2,1,0:T(8,128)(2,1)} %param.7) | copy-start | bytes 393220
  0.6 3.7 %collective-permute-start = (bf16[128,512]{1,0:T(8,128)(2,1)}, bf16[128,512]{1,0:T(8,128)(2,1)S(1)}, u32[]{:S(2)}, u32[]{:S(2)}) collective-permute-start(bf16[128,512]{1,0:T(8,128)(2,1)} %bitcast.17), channel_id=1, source_target_pairs={{0,0},{1,16},{2,32},{3,48},{4,4},{5,20},{6,36},{7,52},{8,8},{9,24}... | collective-permute-start | bytes 393224 | tf_op jit(solution)/shard_map/ppermute | solution.py:29
  3.7 0.7 collective-permute-start.1
  28.0 57.9 %copy-start.1 = (bf16[1,2048,64]{1,2,0:T(8,128)(2,1)S(1)}, bf16[1,2048,64]{1,2,0:T(8,128)(2,1)}, u32[]{:S(2)}) copy-start(bf16[1,2048,64]{1,2,0:T(8,128)(2,1)} %param.12) | copy-start | bytes 786436
  28.0 57.9 %copy-start.2 = (bf16[1,2048,64]{1,2,0:T(8,128)(2,1)S(1)}, bf16[1,2048,64]{1,2,0:T(8,128)(2,1)}, u32[]{:S(2)}) copy-start(bf16[1,2048,64]{1,2,0:T(8,128)(2,1)} %param.13) | copy-start | bytes 786436
  28.1 57.8 %all-to-all-start.1 = ((bf16[4,4,128,512]{3,2,1,0:T(8,128)(2,1)}), bf16[4,4,128,512]{3,2,1,0:T(8,128)(2,1)S(1)}, u32[]{:S(2)}, u32[]{:S(2)}) async-start(bf16[4,4,128,512]{3,2,1,0:T(8,128)(2,1)} %get-tuple-element.13), calls=%async_computation.1 | async-start | bytes 4194304 | tf_op jit(solution)/shard_map/all_to_all | solution.py:478
  85.9 1.6 copy-start
  87.5 0.7 copy-start.6
  136.0 31.7 %copy-start.9 = (bf16[1,512]{1,0:T(2,128)(2,1)S(1)}, bf16[1,512]{1,0:T(2,128)(2,1)}, u32[]{:S(2)}) copy-start(bf16[1,512]{1,0:T(2,128)(2,1)} %gain.1) | copy-start | bytes 3076
  153.0 29.3 %all-to-all-start.5 = ((bf16[4,128,512]{2,1,0:T(8,128)(2,1)}), bf16[4,128,512]{2,1,0:T(8,128)(2,1)}, u32[]{:S(2)}, u32[]{:S(2)}) async-start(bf16[4,128,512]{2,1,0:T(8,128)(2,1)} %get-tuple-element.16), calls=%async_computation.5 | async-start | bytes 1048576 | tf_op jit(solution)/shard_map/all_to_all | solution.py:490
  166.1 1.9 collective-permute-start.2
  168.1 0.7 copy-start.3
  182.3 0.9 copy-start.4
  186.9 53.6 %all-to-all-start.6 = ((bf16[4,4,128,512]{3,2,1,0:T(8,128)(2,1)}), bf16[4,4,128,512]{3,2,1,0:T(8,128)(2,1)}, u32[]{:S(2)}, u32[]{:S(2)}) async-start(bf16[4,4,128,512]{3,2,1,0:T(8,128)(2,1)} %get-tuple-element.19), calls=%async_computation.6 | async-start | bytes 4194304 | tf_op jit(solution)/shard_map/all_to_all | solution.py:492
  191.5 49.1 %copy-start.7 = (f32[4,1,512]{2,1,0:T(1,128)S(1)}, f32[4,1,512]{2,1,0:T(1,128)}, u32[]{:S(2)}) copy-start(f32[4,1,512]{2,1,0:T(1,128)} %get-tuple-element.14.gain.gain_a) | copy-start | bytes 24580
  191.5 49.1 %copy-start.8 = (f32[4,1,512]{2,1,0:T(1,128)S(1)}, f32[4,1,512]{2,1,0:T(1,128)}, u32[]{:S(2)}) copy-start(f32[4,1,512]{2,1,0:T(1,128)} %get-tuple-element.20.gain_f) | copy-start | bytes 24580
  191.5 49.1 %copy-start.10 = (bf16[1,512]{1,0:T(2,128)(2,1)S(1)}, bf16[1,512]{1,0:T(2,128)(2,1)}, u32[]{:S(2)}) copy-start(bf16[1,512]{1,0:T(2,128)(2,1)} %gain_row.1) | copy-start | bytes 3076
  215.5 25.1 %collective-permute-start.3 = (bf16[1,128,512]{2,1,0:T(8,128)(2,1)S(1)}, bf16[1,128,512]{2,1,0:T(8,128)(2,1)S(1)}, u32[]{:S(2)}, u32[]{:S(2)}) collective-permute-start(bf16[1,128,512]{2,1,0:T(8,128)(2,1)S(1)} %constant_dynamic-slice_fusion), channel_id=1, source_target_pairs={{0,64},{64,128},{128,192},{192,256},{256,320},{320,384},{384,448},... | collective-permute-start | bytes 393224 | tf_op jit(solution)/shard_map/ppermute | solution.py:497

commit v8 on v7

--- a/solution.py
+++ b/solution.py
@@ -16,6 +16,7 @@
 f32 = jnp.float32
 bf16 = jnp.bfloat16
 LIMIT = 24 * 1024 * 1024
+WIDE = 57 * 1024 * 1024
 
 
 def swap_x_seq(value):
@@ -29,15 +30,42 @@
     return lax.ppermute(value, GROUP, pairs)
 
 
-def project_kernel(cols, gain, wq, wk, wv, first, second, out, q_acc, kv_acc, squares):
+def project_kernel(
+    cols, gain, wq, wk, wv, first, second,
+    out, q_acc, kv_acc, squares, gain_in, wq_in, wk_in, wv_in, done,
+):
     step = pl.program_id(0)
     blocks, rows, feats = cols.shape
+
+    def query_copy(z):
+        part = pl.ds(pl.multiple_of(z * feats, feats), feats)
+        return pltpu.make_async_copy(wq.at[0, part, :], wq_in.at[z], done.at[z])
+
+    parts = wq_in.shape[0]
+    others = [
+        pltpu.make_async_copy(source, target, done.at[parts + i])
+        for i, (source, target) in enumerate(
+            [(gain, gain_in), (wk.at[0], wk_in), (wv.at[0], wv_in)]
+        )
+    ]
+
+    @pl.when(step == 0)
+    def _():
+        for copy in others:
+            copy.start()
+        for z in range(parts):
+            query_copy(z).start()
+        for copy in others:
+            copy.wait()
+
+    query_copy(step).wait()
     raw = cols[...].reshape(blocks * rows, feats).astype(f32)
-    left = (raw * gain[...]).astype(bf16)
+    left = (raw * gain_in[step]).astype(bf16)
     part = jnp.sum(raw * raw, axis=1, keepdims=True)
-    kv_w = jnp.concatenate([wk[...], wv[...]], 0)
+    here = pl.ds(pl.multiple_of(step * feats, feats), feats)
+    kv_w = jnp.concatenate([wk_in[:, here], wv_in[:, here]], 0)
     kv = lax.dot_general(left, kv_w, (((1,), (1,)), ((), ())), preferred_element_type=f32)
-    q = jnp.dot(left, wq[...], preferred_element_type=f32)
+    q = jnp.dot(left, wq_in[step], preferred_element_type=f32)
 
     @pl.when(step == 0)
     def _():
@@ -67,16 +95,16 @@
     blocks, parts, rows, feats = cols.shape
     q_width, kv_width = w_query.shape[2], 2 * w_key.shape[2]
     heads = q_width // HD
-    kv_spec = pl.BlockSpec((None, w_key.shape[2], feats), lambda z: (0, 0, z))
+    kept = pl.BlockSpec(memory_space=pltpu.HBM)
     return pl.pallas_call(
         project_kernel,
         grid=(parts,),
         in_specs=[
             pl.BlockSpec((blocks, None, rows, feats), lambda z: (0, z, 0, 0)),
-            pl.BlockSpec((None, 1, feats), lambda z: (z, 0, 0)),
-            pl.BlockSpec((None, feats, q_width), lambda z: (0, z, 0)),
-            kv_spec,
-            kv_spec,
+            kept,
+            kept,
+            kept,
+            kept,
         ]
         + [pl.BlockSpec(memory_space=pl.ANY)] * len(after),
         out_specs=fixed((blocks, (heads + 1) * rows + 16, HD)),
@@ -85,8 +113,13 @@
             pltpu.VMEM((blocks * rows, q_width), f32),
             pltpu.VMEM((blocks * rows, kv_width), f32),
             pltpu.VMEM((blocks * rows, 1), f32),
-        ],
-        compiler_params=params(),
+            pltpu.VMEM(gain.shape, f32),
+            pltpu.VMEM((parts, feats, q_width), bf16),
+            pltpu.VMEM((w_key.shape[2], parts * feats), bf16),
+            pltpu.VMEM((w_value.shape[2], parts * feats), bf16),
+            pltpu.SemaphoreType.DMA((parts + 3,)),
+        ],
+        compiler_params=params(WIDE),
         name="project",
     )(cols, gain, w_query, w_key.swapaxes(1, 2), w_value.swapaxes(1, 2), *after)
 
@@ -95,8 +128,8 @@
     return pl.BlockSpec(shape, lambda *at: (0,) * len(shape))
 
 
-def params():
-    return pltpu.CompilerParams(vmem_limit_bytes=LIMIT)
+def params(limit=LIMIT):
+    return pltpu.CompilerParams(vmem_limit_bytes=limit)
 
 
 def three_parts(value):
@@ -118,20 +151,6 @@
     rows = list(parts) + list(more)
     rows.append(jnp.zeros((16 - len(rows), rows[0].shape[1]), f32))
     return jnp.concatenate([row.astype(f32) for row in rows]).astype(bf16)
-
-
-def add_squares(group, squares):
-    rows = squares.shape[0]
-    block = group[pl.ds(0, rows), :].astype(f32)
-    part = jnp.sum(block * block, axis=1, keepdims=True)
-
-    @pl.when(pl.program_id(0) == 0)
-    def _():
-        squares[...] = part
-
-    @pl.when(pl.program_id(0) > 0)
-    def _():
-        squares[...] += part
 
 
 def attn_copies_kernel(group, own, copies, kept, gain_a, gain_f):
@@ -173,41 +192,38 @@
     )(group, own)
 
 
-def ffn_copies_kernel(group, own, after, copies, message, squares):
-    rows, feats = own.shape
+def ffn_copies_kernel(width, group, sums, own, after, copies, weight):
+    step = pl.program_id(0)
+    rows, feats = group.shape
+    bottom = copies.shape[1] - 16
+
+    @pl.when(step == 0)
+    def _():
+        r_sq = 1.0 / (jnp.sum(sums[...], axis=0) / width + norm_eps)
+        weight[...] = column_of(r_sq)
+        tail = jnp.concatenate([stacked(three_parts(r_sq))] * (feats // rows), 1)
+        for k in range(copies.shape[0]):
+            copies[k, pl.ds(bottom, 16), :] = tail
+
+    block = (group[...].astype(f32) * weight[...]).astype(bf16)
     for k in range(copies.shape[0]):
-        copies[k] = group[...]
-    add_squares(group, squares)
-
-    @pl.when(pl.program_id(0) == pl.num_programs(0) - 1)
-    def _():
-        message[pl.ds(0, rows), :] = own[...]
-        sums = stacked(three_parts(row_of(squares[...])))
-        message[pl.ds(rows, 16), :] = jnp.concatenate([sums] * (feats // rows), 1)
-
-
-def ffn_copies(group, own, after, count):
+        copies[k, pl.ds(pl.multiple_of(step * rows, rows), rows), :] = block
+
+
+def ffn_copies(width, group, sums, count, *after):
     parts, rows, feats = group.shape
-    return pl.pallas_call(
-        ffn_copies_kernel,
+    shape = (count, parts * rows + 16, feats)
+    return pl.pallas_call(
+        functools.partial(ffn_copies_kernel, width),
         grid=(parts,),
-        in_specs=[
-            pl.BlockSpec((None, rows, feats), lambda z: (z, 0, 0)),
-            fixed(own.shape),
-            pl.BlockSpec(memory_space=pl.ANY),
-        ],
-        out_specs=[
-            pl.BlockSpec((count, None, rows, feats), lambda z: (0, z, 0, 0)),
-            fixed((rows + 16, feats)),
-        ],
-        out_shape=[
-            pltpu.HBM((count, parts, rows, feats), bf16),
-            jax.ShapeDtypeStruct((rows + 16, feats), bf16),
-        ],
+        in_specs=[pl.BlockSpec((None, rows, feats), lambda z: (z, 0, 0)), fixed(sums.shape)]
+        + [pl.BlockSpec(memory_space=pl.ANY)] * len(after),
+        out_specs=fixed(shape),
+        out_shape=pltpu.HBM(shape, bf16),
         scratch_shapes=[pltpu.VMEM((rows, 1), f32)],
         compiler_params=params(),
         name="ffn_copies",
-    )(group, own, after)
+    )(group, sums, *after)
 
 
 def kv_sum_kernel(width, arrived, docs, out):
@@ -257,8 +273,8 @@
 
 
 def attend_kernel(
-    q_in, kv_in, table, resid, copies, out,
-    keys, values, r_all, docs_all, r_own, docs_own,
+    q_in, kv_in, table, resid, out, sums,
+    keys, values, r_all, docs_all, r_own, docs_own, squares,
 ):
     rows = out.shape[0]
     tokens = keys.shape[0]
@@ -305,8 +321,20 @@
     ) / total
     result = (resid[...].astype(f32) + context).astype(bf16)
     out[...] = result
-    for copy in range(copies.shape[0]):
-        copies[copy] = result
+    result = result.astype(f32)
+    part = jnp.sum(result * result, axis=1, keepdims=True)
+
+    @pl.when(pl.program_id(0) == 0)
+    def _():
+        squares[...] = part
+
+    @pl.when(pl.program_id(0) > 0)
+    def _():
+        squares[...] += part
+
+    @pl.when(pl.program_id(0) == pl.num_programs(0) - 1)
+    def _():
+        sums[...] = jnp.broadcast_to(row_of(squares[...])[None], sums.shape)
 
 
 def attend(q_in, kv_in, table, resid, copies):
@@ -321,12 +349,12 @@
         + [fixed(kv_in.shape), fixed(table.shape)]
         + [pl.BlockSpec((rows, HD), lambda h: (0, h))],
         out_specs=[
-            pl.BlockSpec((copies, rows, HD), lambda h: (0, 0, h)),
             pl.BlockSpec((rows, HD), lambda h: (0, h)),
+            fixed((copies, 1, rows)),
         ],
         out_shape=[
-            pltpu.HBM((copies, rows, feats), bf16),
             pltpu.HBM((rows, feats), bf16),
+            pltpu.HBM((copies, 1, rows), f32),
         ],
         scratch_shapes=[
             pltpu.VMEM((tokens, HD), f32),
@@ -335,15 +363,11 @@
             pltpu.VMEM((1, tokens), f32),
             pltpu.VMEM((rows, 1), f32),
             pltpu.VMEM((rows, 1), f32),
+            pltpu.VMEM((rows, 1), f32),
         ],
         compiler_params=params(),
         name="attend",
     )(q_in, kv_in, table, resid)
-
-
-def left_block(block, gain, r, scale):
-    turned = (block.astype(f32) * gain).T
-    return turned, r * r * scale
 
 
 def attn_left_kernel(scale, own_rows, gain, kv, out):
@@ -351,8 +375,8 @@
     for k in range(blocks):
         parts = kv[2 * k, pl.ds(rows, 16), :].astype(f32)
         r = parts[0:1] + parts[1:2] + parts[2:3]
-        turned, weight = left_block(own_rows[k], gain[...].astype(f32), r, scale)
-        out[:, pl.ds(k * rows, rows)] = (turned * weight).astype(bf16)
+        turned = (own_rows[k].astype(f32) * gain[...].astype(f32)).T
+        out[:, pl.ds(k * rows, rows)] = (turned * (r * r * scale)).astype(bf16)
 
 
 def attn_left(scale, own_rows, gain, kv_all):
@@ -370,7 +394,7 @@
 
 
 def hessian_kernel(
-    scale, place, left_a, cols_a, gain_a, ffn_rows, gain_row, r_ffn, cols_f, gain_f,
+    scale, place, left_a, cols_a, gain_a, ffn_rows, gain_row, r_sq, cols_f, gain_f,
     out, diagonal, left_f, turned_f,
 ):
     blocks, rows, feats = cols_a.shape
@@ -381,13 +405,13 @@
         squares = jnp.zeros((rows, 1), f32)
         part = pl.multiple_of(lax.axis_index("seq") * rows, rows)
         for k in range(blocks):
-            turned, weight = left_block(
-                ffn_rows[k, pl.ds(0, rows), :], gain_row[...].astype(f32), r_ffn[k], scale
-            )
+            turned = (ffn_rows[k].astype(f32) * gain_row[...].astype(f32)).T * scale
+            parts = r_sq[k].astype(f32)[:, :rows]
+            weight = (parts[0:1] + parts[1:2] + parts[2:3]) / scale
             turned_f[...] = turned
             mine = turned_f[pl.ds(part, rows), :]
             squares += jnp.sum(mine * mine * weight, axis=1, keepdims=True)
-            left_f[:, pl.ds(k * rows, rows)] = (turned * weight).astype(bf16)
+            left_f[:, pl.ds(k * rows, rows)] = turned.astype(bf16)
         diagonal[...] = row_of(squares)
 
     def product(left, cols, gain):
@@ -411,7 +435,7 @@
         out[...] = jnp.where(row_ids <= col_ids, upper, lower)
 
 
-def hessian(scale, place, left_a, cols_a, gain_a, ffn_rows, gain_row, r_ffn, cols_f, gain_f):
+def hessian(scale, place, left_a, cols_a, gain_a, ffn_rows, gain_row, cols_f, gain_f):
     blocks, parts, rows, feats = cols_a.shape
     tokens = blocks * rows
 
@@ -421,21 +445,22 @@
     def lower_at(z, at):
         return jnp.clip(jnp.minimum(z, at[0] - at[1]), 0, parts - 1)
 
-    def side(pick):
-        return [
-            pl.BlockSpec((blocks, None, rows, feats), lambda z, at: (0, pick(z, at), 0, 0)),
-            pl.BlockSpec((None, 1, feats), lambda z, at: (z, 0, 0)),
-        ]
-
+    gain = pl.BlockSpec((None, 1, feats), lambda z, at: (z, 0, 0))
     return pl.pallas_call(
         functools.partial(hessian_kernel, scale),
         grid_spec=pltpu.PrefetchScalarGridSpec(
             num_scalar_prefetch=1,
             grid=(parts,),
-            in_specs=[fixed(left_a.shape)]
-            + side(upper_at)
-            + [fixed(ffn_rows.shape), fixed(gain_row.shape), fixed(r_ffn.shape)]
-            + side(lower_at),
+            in_specs=[
+                fixed(left_a.shape),
+                pl.BlockSpec((blocks, None, rows, feats), lambda z, at: (0, upper_at(z, at), 0, 0)),
+                gain,
+                fixed(ffn_rows.shape),
+                fixed(gain_row.shape),
+                pl.BlockSpec((blocks, 16, feats), lambda z, at: (0, parts * rows // 16, 0)),
+                pl.BlockSpec((blocks, rows, feats), lambda z, at: (0, lower_at(z, at), 0)),
+                gain,
+            ],
             out_specs=[
                 pl.BlockSpec((feats, feats), lambda z, at: (0, z)),
                 fixed((1, rows)),
@@ -446,9 +471,9 @@
             jax.ShapeDtypeStruct((feats, parts * feats), bf16),
             jax.ShapeDtypeStruct((1, rows), f32),
         ],
-        compiler_params=params(),
+        compiler_params=params(WIDE),
         name="hessian",
-    )(place, left_a, cols_a, gain_a, ffn_rows, gain_row, r_ffn, cols_f, gain_f)
+    )(place, left_a, cols_a, gain_a, ffn_rows, gain_row, cols_f, cols_f, gain_f)
 
 
 def on_device(hidden, segment_ids, gain_attn, gain_ffn, w_query, w_key, w_value):
@@ -463,16 +488,10 @@
     place = jnp.stack([x_pos * nz + zl_pos, seq_pos * nz])
     place = place.astype(jnp.int32)
 
-    def copied(value, count):
-        return jnp.broadcast_to(value[None], (count,) + value.shape)
-
-    def r_of(parts):
-        return lax.rsqrt(jnp.sum(parts.astype(f32), axis=(0, 1)) / width + norm_eps)
-
     resid = swap_x_seq(hidden[0])
     docs = jnp.pad(segment_ids.astype(bf16), ((0, 13), (0, feats - rows)))
     extra = swap_x_seq(jnp.concatenate([gain_attn, gain_ffn, docs]))
-    group = lax.all_to_all(copied(jnp.concatenate([resid, extra]), nz), ZL, 0, 0)
+    group = lax.all_gather(jnp.concatenate([resid, extra]), ZL)
     copies, own_rows, gain_a, gain_f = attn_copies(group, hidden[0], nx)
     attn_rows = lax.all_gather(own_rows, "seq")
     attn_cols = lax.all_to_all(copies, "x", 0, 0)
@@ -484,19 +503,21 @@
     message = project(attn_cols, gain_a, w_query, w_key, w_value, attn_rows, table)
     arrived = lax.all_to_all(lax.all_to_all(message, "x", 0, 0), "seq", 0, 0)
     kv = lax.all_to_all(kv_sum(width, arrived, extra, 2 * nx), ("x", "zb"), 0, 0)
-    copies, section_out = attend(arrived, kv, table, resid, nz)
+    ring = ZL + ("seq",)
+    section_out, sums = attend(arrived, kv, table, resid, lax.axis_size(ring))
     left_a = attn_left(scale, attn_rows, gain_attn, kv)
 
-    group = lax.all_to_all(copies, ZL, 0, 0)
-    copies, message = ffn_copies(group, swap_x_seq(section_out), left_a, nx)
+    sums = lax.all_to_all(sums, ring, 0, 0)
+    out_rows = swap_x_seq(section_out)
+    group = lax.all_gather(section_out, ZL)
+    copies = ffn_copies(width, group, sums, nx, out_rows, left_a)
     ffn_cols = lax.all_to_all(copies, "x", 0, 0)
-    ffn_rows = lax.all_gather(message, "seq")
-    r_ffn = lax.all_gather(r_of(ffn_rows[:, rows : rows + 3, :rows])[None], "x")
+    ffn_rows = lax.all_gather(out_rows, "seq")
     count = lax.axis_size("phase")
-    passed = lax.dynamic_slice_in_dim(ffn_rows[:, :rows], seq_pos, 1, 0)
+    passed = lax.dynamic_slice_in_dim(ffn_rows, seq_pos, 1, 0)
     passed = lax.ppermute(passed, "phase", [(p, (p + 1) % count) for p in range(count)])
     hessians, ffn_diagonal = hessian(
-        scale, place, left_a, attn_cols, gain_a, ffn_rows, gain_ffn, r_ffn, ffn_cols, gain_f
+        scale, place, left_a, attn_cols, gain_a, ffn_rows, gain_ffn, ffn_cols, gain_f
     )
     return (passed, hessians[None], ffn_diagonal)
 

time: 248 us -> 240 us (0.968)
  blocking collectives: 136 us -> 159 us
  starting transfers between devices: 67.6 us -> 46.4 us
  waiting for transfers between devices: 13.6 us -> 1.32 us
    all_gather x2 -> x3, blocking collectives: 32.3 us -> 69 us  [the longest x1 28 us: on_device(): group = lax.all_gather(jnp.concatenate([resid, extra]), ZL)]
    all_to_all x1 -> x0, blocking collectives: 21.7 us -> none  [on_device(): lax.all_to_all(copied(jnp.concatenate([resid, extra]), nz), ZL, 0, 0)]
    all_to_all x1, waiting for transfers between devices: 13.6 us -> 0.01 us  [on_device(): sums = lax.all_to_all(sums, ring, 0, 0)]
    ppermute x1, starting transfers between devices: 16.5 us -> 6.02 us  [on_device(): lax.ppermute(passed, 'phase', [(p, (p + 1) % count) for p in range(count)])]
    all_to_all x1, starting transfers between devices: 29.4 us -> 19.3 us  [on_device(): attn_cols = lax.all_to_all(copies, 'x', 0, 0)]
    all_to_all x2, blocking collectives: 43.7 us -> 52.1 us  [on_device(): arrived = lax.all_to_all(lax.all_to_all(message, 'x', 0, 0), 'seq', 0, 0)]
    pallas_call x1, Pallas kernels: 4.12 us -> 6.62 us  [project(): pl.pallas_call(project_kernel, grid=(parts,), in_specs=[pl.BlockSpec((blo...]
  transfers between devices with their start and end apart: 7 -> 7, of which waited for: 1 -> 1; matrix products, arithmetic and copies ran while one was open for 1% -> 2% of each run, Pallas kernels for 0% -> 0%
where the time goes in v8:
time: 240 us; the launch traced here: 238 us
  blocking collectives  159 us (66%)
  starting transfers between devices  46.4 us (19%)
  Pallas kernels  23.6 us (10%)
  other arithmetic  3.85 us (2%)
  local copies, waits for them, and re-layouts  2.96 us (1%)
    all_to_all x2, blocking collectives, on_device(): arrived = lax.all_to_all(lax.all_to_all(message, 'x', 0, 0), 'seq', 0, 0)  52.1 us
    all_gather x1, blocking collectives, on_device(): attn_rows = lax.all_gather(own_rows, 'seq')  28.3 us
    all_gather x1, blocking collectives, on_device(): group = lax.all_gather(jnp.concatenate([resid, extra]), ZL)  28 us
    all_gather x1, blocking collectives, on_device(): ffn_rows = lax.all_gather(out_rows, 'seq')  23.3 us
    all_to_all x1, starting transfers between devices, on_device(): attn_cols = lax.all_to_all(copies, 'x', 0, 0)  19.3 us
    all_gather x1, blocking collectives, on_device(): group = lax.all_gather(section_out, ZL)  17.6 us
    all_to_all x1, starting transfers between devices, on_device(): sums = lax.all_to_all(sums, ring, 0, 0)  12.8 us
    all_to_all x1, blocking collectives, on_device(): lax.all_to_all(kv_sum(width, arrived, extra, 2 * nx), ('x', 'zb'), 0, 0)  9.94 us
  transfers between devices with their start and end apart: 7, of which 1 were waited for; matrix products, arithmetic and copies ran while one was open for 2% of the time, Pallas kernels for 0%

profile of v8, /device:TPU:1, one launch (start us, length us, event | category | flops | bytes accessed | tf_op | source)
XLA Modules:
  0.0 238.2 jit_solution(12823456677587295687)
XLA Ops:
  0.6 1.6 collective-permute-start
  4.3 28.0 %all-gather = bf16[576,512]{1,0:T(8,128)(2,1)S(1)} all-gather(bf16[144,512]{1,0:T(8,128)(2,1)S(1)} %pad_maximum_fusion.1), channel_id=2, replica_groups=mesh['phase'=8,'x'=4,'za'=2,'zb'=2,'seq'=4] {'za','zb'}, dimensions={0}, use_global_device_ids=true | all-gather | bytes 737280 | tf_op jit(solution)/shard_map/all_gather | solution.py:494
  32.3 0.9 copy-done.3
  33.2 1.9 attn_copies.1
  35.1 19.3 %all-to-all-start = ((bf16[4,4,128,512]{3,2,1,0:T(8,128)(2,1)}), bf16[4,4,128,512]{3,2,1,0:T(8,128)(2,1)S(1)}, u32[]{:S(2)}, u32[]{:S(2)}) async-start(bf16[4,4,128,512]{3,2,1,0:T(8,128)(2,1)} %get-tuple-element.11), calls=%async_computation | async-start | bytes 4194304 | tf_op jit(solution)/shard_map/all_to_all | solution.py:497
  54.5 1.0 fusion.1
  55.5 0.8 pad_maximum_fusion.second.table
  56.3 28.3 %all-gather.1 = bf16[512,512]{1,0:T(8,128)(2,1)} all-gather(bf16[128,512]{1,0:T(8,128)(2,1)S(1)} %copy-done.7), channel_id=3, replica_groups=mesh['phase'=8,'x'=4,'za'=2,'zb'=2,'seq'=4] {'seq'}, dimensions={0}, use_global_device_ids=true | all-gather | bytes 655360 | tf_op jit(solution)/shard_map/all_gather | solution.py:496
  84.6 1.4 copy-done.5
  86.0 6.6 %project.1 = bf16[4,656,128]{2,1,0:T(8,128)(2,1)} custom-call(bf16[4,4,128,512]{3,2,1,0:T(8,128)(2,1)} %copy-done.5, f32[4,1,512]{2,1,0:T(1,128)} %get-tuple-element.12.gain.gain_a, bf16[1,2048,512]{2,1,0:T(8,128)(2,1)} %wq.1, bf16[1,64,2048]{2,1,0:T(8,128)(2,1)} %bitcast.18, bf16[1,64,2048]{2,1,0:T(8,128)(2,1)} %bitcast.19, bf16[4,128,512]{2,1,0:T(8,128)(2,1)} %bitcast.10, ...), custom_call_target="tpu_custom_call" | custom-call | tf_op jit(solution)/shard_map/project/pallas_call | solution.py:99
  92.6 12.2 %all_to_all.30 = bf16[4,656,128]{2,1,0:T(8,128)(2,1)S(1)} all-to-all(bf16[4,656,128]{2,1,0:T(8,128)(2,1)} %project.1), channel_id=1, replica_groups=mesh['phase'=8,'x'=4,'za'=2,'zb'=2,'seq'=4] {'x'}, dimensions={0} | all-to-all | bytes 1343488 | tf_op jit(solution)/shard_map/all_to_all | solution.py:504
  104.9 39.9 %all_to_all.31.arrived.q_in = bf16[4,656,128]{2,1,0:T(8,128)(2,1)S(1)} all-to-all(bf16[4,656,128]{2,1,0:T(8,128)(2,1)S(1)} %all_to_all.30), channel_id=1, replica_groups=mesh['phase'=8,'x'=4,'za'=2,'zb'=2,'seq'=4] {'seq'}, dimensions={0} | all-to-all | bytes 1343488 | tf_op jit(solution)/shard_map/all_to_all | solution.py:504
  144.8 0.8 kv_sum.1
  145.5 9.9 %all_to_all.32.kv_in.kv = bf16[8,144,128]{2,1,0:T(8,128)(2,1)S(1)} all-to-all(bf16[8,144,128]{2,1,0:T(8,128)(2,1)} %kv_sum.1), channel_id=1, replica_groups=mesh['phase'=8,'x'=4,'za'=2,'zb'=2,'seq'=4] {'x','zb'}, dimensions={0} | all-to-all | bytes 589824 | tf_op jit(solution)/shard_map/all_to_all | solution.py:505
  155.5 5.5 %attend.1 = (bf16[128,512]{1,0:T(8,128)(2,1)}, f32[16,1,128]{2,1,0:T(1,128)}) custom-call(bf16[4,656,128]{2,1,0:T(8,128)(2,1)S(1)} %all_to_all.31.arrived.q_in, bf16[8,144,128]{2,1,0:T(8,128)(2,1)S(1)} %all_to_all.32.kv_in.kv, f32[512,128]{1,0:T(8,128)S(1)} %copy-done.2, bf16[128,512]{1,0:T(8,128)(2,1)S(1)} %collective-permute-done.resid), custom_call_target="tpu_custom_call" | custom-call | tf_op jit(solution)/shard_map/attend/pallas_call | solution.py:343
  160.9 1.6 collective-permute-start.2
  162.5 12.8 %all-to-all-start.4 = ((f32[16,1,128]{2,1,0:T(1,128)}), f32[16,1,128]{2,1,0:T(1,128)S(1)}, u32[]{:S(2)}, u32[]{:S(2)}) async-start(f32[16,1,128]{2,1,0:T(1,128)} %get-tuple-element.15), calls=%async_computation.4 | async-start | bytes 16384 | tf_op jit(solution)/shard_map/all_to_all | solution.py:510
  175.3 17.6 %all-gather.3 = bf16[512,512]{1,0:T(8,128)(2,1)S(1)} all-gather(bf16[128,512]{1,0:T(8,128)(2,1)} %get-tuple-element.14), channel_id=5, replica_groups=mesh['phase'=8,'x'=4,'za'=2,'zb'=2,'seq'=4] {'za','zb'}, dimensions={0}, use_global_device_ids=true | all-gather | bytes 655360 | tf_op jit(solution)/shard_map/all_gather | solution.py:512
  193.3 1.9 ffn_copies.1
  195.2 4.5 %all-to-all-start.5 = ((bf16[4,528,512]{2,1,0:T(8,128)(2,1)}), bf16[4,528,512]{2,1,0:T(8,128)(2,1)}, u32[]{:S(2)}, u32[]{:S(2)}) async-start(bf16[4,528,512]{2,1,0:T(8,128)(2,1)} %ffn_copies.1), calls=%async_computation.5 | async-start | bytes 4325376 | tf_op jit(solution)/shard_map/all_to_all | solution.py:514
  199.7 23.3 %all-gather.2 = bf16[512,512]{1,0:T(8,128)(2,1)S(1)} all-gather(bf16[128,512]{1,0:T(8,128)(2,1)S(1)} %collective-permute-done.2.own), channel_id=4, replica_groups=mesh['phase'=8,'x'=4,'za'=2,'zb'=2,'seq'=4] {'seq'}, dimensions={0}, use_global_device_ids=true | all-gather | bytes 655360 | tf_op jit(solution)/shard_map/all_gather | solution.py:515
  223.0 6.0 %collective-permute-start.3 = (bf16[1,128,512]{2,1,0:T(8,128)(2,1)S(1)}, bf16[1,128,512]{2,1,0:T(8,128)(2,1)S(1)}, u32[]{:S(2)}, u32[]{:S(2)}) collective-permute-start(bf16[1,128,512]{2,1,0:T(8,128)(2,1)S(1)} %constant_dynamic-slice_fusion), channel_id=1, source_target_pairs={{0,64},{64,128},{128,192},{192,256},{256,320},{320,384},{384,448},... | collective-permute-start | bytes 393224 | tf_op jit(solution)/shard_map/ppermute | solution.py:518
  229.6 1.3 collective-permute-done.3
  231.0 6.6 %hessian.1 = (bf16[512,2048]{1,0:T(8,128)(2,1)}, f32[1,128]{1,0:T(1,128)}) custom-call(s32[2]{0:T(128)} %pad_add_fusion.place, bf16[512,512]{1,0:T(8,128)(2,1)} %copy-done, bf16[4,4,128,512]{3,2,1,0:T(8,128)(2,1)} %copy-done.5, f32[4,1,512]{2,1,0:T(1,128)} %get-tuple-element.12.gain.gain_a, bf16[4,128,512]{2,1,0:T(8,128)(2,1)} %bitcast.17, ...), custom_call_target="tpu_custom_call" | custom-call | tf_op jit(solution)/shard_map/hessian/pallas_call | solution.py:449
  (29 shorter events, 3.7 us)
Async XLA Ops:
  0.6 3.6 %collective-permute-start = (bf16[128,512]{1,0:T(8,128)(2,1)}, bf16[128,512]{1,0:T(8,128)(2,1)S(1)}, u32[]{:S(2)}, u32[]{:S(2)}) collective-permute-start(bf16[128,512]{1,0:T(8,128)(2,1)} %bitcast.14), channel_id=1, source_target_pairs={{0,0},{1,16},{2,32},{3,48},{4,4},{5,20},{6,36},{7,52},{8,8},{9,24}... | collective-permute-start | bytes 393224 | tf_op jit(solution)/shard_map/ppermute | solution.py:30
  3.6 0.7 collective-permute-start.1
  32.3 0.9 copy-start.3
  35.1 21.2 %copy-start.7 = (bf16[128,512]{1,0:T(8,128)(2,1)S(1)}, bf16[128,512]{1,0:T(8,128)(2,1)}, u32[]{:S(2)}) copy-start(bf16[128,512]{1,0:T(8,128)(2,1)} %get-tuple-element.13) | copy-start | bytes 393220
  35.1 49.5 %all-to-all-start = ((bf16[4,4,128,512]{3,2,1,0:T(8,128)(2,1)}), bf16[4,4,128,512]{3,2,1,0:T(8,128)(2,1)S(1)}, u32[]{:S(2)}, u32[]{:S(2)}) async-start(bf16[4,4,128,512]{3,2,1,0:T(8,128)(2,1)} %get-tuple-element.11), calls=%async_computation | async-start | bytes 4194304 | tf_op jit(solution)/shard_map/all_to_all | solution.py:497
  84.6 1.4 copy-start.5
  92.6 62.9 %copy-start.2 = (f32[512,128]{1,0:T(8,128)S(1)}, f32[512,128]{1,0:T(8,128)}, u32[]{:S(2)}) copy-start(f32[512,128]{1,0:T(8,128)} %pad_maximum_fusion.second.table) | copy-start | bytes 786436
  144.8 48.1 %copy-start.1 = (bf16[512,512]{1,0:T(8,128)(2,1)S(1)}, bf16[512,512]{1,0:T(8,128)(2,1)}, u32[]{:S(2)}) copy-start(bf16[512,512]{1,0:T(8,128)(2,1)} %all-gather.1) | copy-start | bytes 1572868
  144.8 48.1 %copy-start.4 = (bf16[1,512]{1,0:T(2,128)(2,1)S(1)}, bf16[1,512]{1,0:T(2,128)(2,1)}, u32[]{:S(2)}) copy-start(bf16[1,512]{1,0:T(2,128)(2,1)} %gain.1) | copy-start | bytes 3076
  160.9 32.3 %collective-permute-start.2 = (bf16[128,512]{1,0:T(8,128)(2,1)}, bf16[128,512]{1,0:T(8,128)(2,1)S(1)}, u32[]{:S(2)}, u32[]{:S(2)}) collective-permute-start(bf16[128,512]{1,0:T(8,128)(2,1)} %get-tuple-element.14), channel_id=1, source_target_pairs={{0,0},{1,16},{2,32},{3,48},{4,4},{5,20},{6,36},{7,52},{8,8},{9,24}... | collective-permute-start | bytes 393224 | tf_op jit(solution)/shard_map/ppermute | solution.py:30
  162.5 30.8 %all-to-all-start.4 = ((f32[16,1,128]{2,1,0:T(1,128)}), f32[16,1,128]{2,1,0:T(1,128)S(1)}, u32[]{:S(2)}, u32[]{:S(2)}) async-start(f32[16,1,128]{2,1,0:T(1,128)} %get-tuple-element.15), calls=%async_computation.4 | async-start | bytes 16384 | tf_op jit(solution)/shard_map/all_to_all | solution.py:510
  193.2 1.9 copy-start
  195.2 35.8 %all-to-all-start.5 = ((bf16[4,528,512]{2,1,0:T(8,128)(2,1)}), bf16[4,528,512]{2,1,0:T(8,128)(2,1)}, u32[]{:S(2)}, u32[]{:S(2)}) async-start(bf16[4,528,512]{2,1,0:T(8,128)(2,1)} %ffn_copies.1), calls=%async_computation.5 | async-start | bytes 4325376 | tf_op jit(solution)/shard_map/all_to_all | solution.py:514
  223.0 8.0 %copy-start.6 = (bf16[512,512]{1,0:T(8,128)(2,1)}, bf16[512,512]{1,0:T(8,128)(2,1)S(1)}, u32[]{:S(2)}) copy-start(bf16[512,512]{1,0:T(8,128)(2,1)S(1)} %all-gather.2) | copy-start | bytes 1572868
  223.0 8.0 %collective-permute-start.3 = (bf16[1,128,512]{2,1,0:T(8,128)(2,1)S(1)}, bf16[1,128,512]{2,1,0:T(8,128)(2,1)S(1)}, u32[]{:S(2)}, u32[]{:S(2)}) collective-permute-start(bf16[1,128,512]{2,1,0:T(8,128)(2,1)S(1)} %constant_dynamic-slice_fusion), channel_id=1, source_target_pairs={{0,64},{64,128},{128,192},{192,256},{256,320},{320,384},{384,448},... | collective-permute-start | bytes 393224 | tf_op jit(solution)/shard_map/ppermute | solution.py:518

commit v9 on v8

--- a/solution.py
+++ b/solution.py
@@ -17,6 +17,7 @@
 bf16 = jnp.bfloat16
 LIMIT = 24 * 1024 * 1024
 WIDE = 57 * 1024 * 1024
+PROJECT = 55 * 1024 * 1024
 
 
 def swap_x_seq(value):
@@ -30,42 +31,15 @@
     return lax.ppermute(value, GROUP, pairs)
 
 
-def project_kernel(
-    cols, gain, wq, wk, wv, first, second,
-    out, q_acc, kv_acc, squares, gain_in, wq_in, wk_in, wv_in, done,
-):
+def project_kernel(cols, gain, wq, wk, wv, after, out, q_acc, kv_acc, squares):
     step = pl.program_id(0)
     blocks, rows, feats = cols.shape
-
-    def query_copy(z):
-        part = pl.ds(pl.multiple_of(z * feats, feats), feats)
-        return pltpu.make_async_copy(wq.at[0, part, :], wq_in.at[z], done.at[z])
-
-    parts = wq_in.shape[0]
-    others = [
-        pltpu.make_async_copy(source, target, done.at[parts + i])
-        for i, (source, target) in enumerate(
-            [(gain, gain_in), (wk.at[0], wk_in), (wv.at[0], wv_in)]
-        )
-    ]
-
-    @pl.when(step == 0)
-    def _():
-        for copy in others:
-            copy.start()
-        for z in range(parts):
-            query_copy(z).start()
-        for copy in others:
-            copy.wait()
-
-    query_copy(step).wait()
     raw = cols[...].reshape(blocks * rows, feats).astype(f32)
-    left = (raw * gain_in[step]).astype(bf16)
+    left = (raw * gain[...]).astype(bf16)
     part = jnp.sum(raw * raw, axis=1, keepdims=True)
-    here = pl.ds(pl.multiple_of(step * feats, feats), feats)
-    kv_w = jnp.concatenate([wk_in[:, here], wv_in[:, here]], 0)
+    kv_w = jnp.concatenate([wk[...], wv[...]], 0)
     kv = lax.dot_general(left, kv_w, (((1,), (1,)), ((), ())), preferred_element_type=f32)
-    q = jnp.dot(left, wq_in[step], preferred_element_type=f32)
+    q = jnp.dot(left, wq[...], preferred_element_type=f32)
 
     @pl.when(step == 0)
     def _():
@@ -91,37 +65,32 @@
                 out[k, pl.ds(h * rows, rows), :] = q_acc[block, pl.ds(h * HD, HD)].astype(bf16)
 
 
-def project(cols, gain, w_query, w_key, w_value, *after):
+def project(cols, gain, w_query, w_key, w_value, after):
     blocks, parts, rows, feats = cols.shape
     q_width, kv_width = w_query.shape[2], 2 * w_key.shape[2]
     heads = q_width // HD
-    kept = pl.BlockSpec(memory_space=pltpu.HBM)
+    kv_spec = pl.BlockSpec((None, w_key.shape[2], feats), lambda z: (0, 0, z))
     return pl.pallas_call(
         project_kernel,
         grid=(parts,),
         in_specs=[
             pl.BlockSpec((blocks, None, rows, feats), lambda z: (0, z, 0, 0)),
-            kept,
-            kept,
-            kept,
-            kept,
-        ]
-        + [pl.BlockSpec(memory_space=pl.ANY)] * len(after),
+            pl.BlockSpec((None, 1, feats), lambda z: (z, 0, 0)),
+            pl.BlockSpec((None, feats, q_width), lambda z: (0, z, 0)),
+            kv_spec,
+            kv_spec,
+            pl.BlockSpec(memory_space=pl.ANY),
+        ],
         out_specs=fixed((blocks, (heads + 1) * rows + 16, HD)),
         out_shape=pltpu.HBM((blocks, (heads + 1) * rows + 16, HD), bf16),
         scratch_shapes=[
             pltpu.VMEM((blocks * rows, q_width), f32),
             pltpu.VMEM((blocks * rows, kv_width), f32),
             pltpu.VMEM((blocks * rows, 1), f32),
-            pltpu.VMEM(gain.shape, f32),
-            pltpu.VMEM((parts, feats, q_width), bf16),
-            pltpu.VMEM((w_key.shape[2], parts * feats), bf16),
-            pltpu.VMEM((w_value.shape[2], parts * feats), bf16),
-            pltpu.SemaphoreType.DMA((parts + 3,)),
-        ],
-        compiler_params=params(WIDE),
+        ],
+        compiler_params=params(PROJECT),
         name="project",
-    )(cols, gain, w_query, w_key.swapaxes(1, 2), w_value.swapaxes(1, 2), *after)
+    )(cols, gain, w_query, w_key.swapaxes(1, 2), w_value.swapaxes(1, 2), after)
 
 
 def fixed(shape):
@@ -153,43 +122,72 @@
     return jnp.concatenate([row.astype(f32) for row in rows]).astype(bf16)
 
 
-def attn_copies_kernel(group, own, copies, kept, gain_a, gain_f):
-    rows = own.shape[0]
+def attn_copies_kernel(group, copies, gain_a, gain_f):
+    rows = copies.shape[1]
     for k in range(copies.shape[0]):
         copies[k] = group[pl.ds(0, rows), :]
     gains = group[pl.ds(rows, 16), :].astype(f32)
     gain_a[...] = gains[0:1]
     gain_f[...] = gains[1:2]
 
-    @pl.when(pl.program_id(0) == 0)
-    def _():
-        kept[...] = own[...]
-
-
-def attn_copies(group, own, count):
+
+def attn_copies(group, count):
     parts, tall, feats = group.shape
-    rows = own.shape[0]
+    rows = tall - 16
     gain = pl.BlockSpec((None, 1, feats), lambda z: (z, 0, 0))
     gain_shape = pltpu.HBM((parts, 1, feats), f32)
     return pl.pallas_call(
         attn_copies_kernel,
         grid=(parts,),
-        in_specs=[pl.BlockSpec((None, tall, feats), lambda z: (z, 0, 0)), fixed(own.shape)],
+        in_specs=[pl.BlockSpec((None, tall, feats), lambda z: (z, 0, 0))],
         out_specs=[
             pl.BlockSpec((count, None, rows, feats), lambda z: (0, z, 0, 0)),
-            fixed(own.shape),
             gain,
             gain,
         ],
         out_shape=[
             pltpu.HBM((count, parts, rows, feats), bf16),
-            pltpu.HBM(own.shape, bf16),
             gain_shape,
             gain_shape,
         ],
         compiler_params=params(),
         name="attn_copies",
-    )(group, own)
+    )(group)
+
+
+def take_kernel(value, after, out):
+    out[...] = value[...]
+
+
+def take_after(value, after):
+    return pl.pallas_call(
+        take_kernel,
+        grid=(1,),
+        in_specs=[fixed(value.shape), pl.BlockSpec(memory_space=pl.ANY)],
+        out_specs=fixed(value.shape),
+        out_shape=pltpu.HBM(value.shape, value.dtype),
+        compiler_params=params(),
+        name="take_after",
+    )(value, after)
+
+
+def pile_kernel(top, bottom, after, out):
+    rows = top.shape[0]
+    out[pl.ds(0, rows), :] = top[...]
+    out[pl.ds(rows, bottom.shape[0]), :] = bottom[...]
+
+
+def pile(top, bottom, after):
+    shape = (top.shape[0] + bottom.shape[0], top.shape[1])
+    return pl.pallas_call(
+        pile_kernel,
+        grid=(1,),
+        in_specs=[fixed(top.shape), fixed(bottom.shape), pl.BlockSpec(memory_space=pl.ANY)],
+        out_specs=fixed(shape),
+        out_shape=jax.ShapeDtypeStruct(shape, top.dtype),
+        compiler_params=params(),
+        name="pile",
+    )(top, bottom, after)
 
 
 def ffn_copies_kernel(width, group, sums, own, after, copies, weight):
@@ -491,16 +489,16 @@
     resid = swap_x_seq(hidden[0])
     docs = jnp.pad(segment_ids.astype(bf16), ((0, 13), (0, feats - rows)))
     extra = swap_x_seq(jnp.concatenate([gain_attn, gain_ffn, docs]))
-    group = lax.all_gather(jnp.concatenate([resid, extra]), ZL)
-    copies, own_rows, gain_a, gain_f = attn_copies(group, hidden[0], nx)
-    attn_rows = lax.all_gather(own_rows, "seq")
-    attn_cols = lax.all_to_all(copies, "x", 0, 0)
-
     half = HD // 2
     freq = rope_base ** (-(jnp.arange(half, dtype=f32) * 2.0 / HD))
     angle = jnp.arange(tokens, dtype=f32)[:, None] * freq[None, :]
     table = jnp.concatenate([jnp.cos(angle), jnp.sin(angle)], 1)
-    message = project(attn_cols, gain_a, w_query, w_key, w_value, attn_rows, table)
+    group = lax.all_gather(pile(resid, extra, table), ZL)
+    copies, gain_a, gain_f = attn_copies(group, nx)
+    attn_rows = lax.all_gather(take_after(hidden[0], gain_a), "seq")
+    attn_cols = lax.all_to_all(copies, "x", 0, 0)
+
+    message = project(attn_cols, gain_a, w_query, w_key, w_value, attn_rows)
     arrived = lax.all_to_all(lax.all_to_all(message, "x", 0, 0), "seq", 0, 0)
     kv = lax.all_to_all(kv_sum(width, arrived, extra, 2 * nx), ("x", "zb"), 0, 0)
     ring = ZL + ("seq",)
@@ -514,8 +512,7 @@
     ffn_cols = lax.all_to_all(copies, "x", 0, 0)
     ffn_rows = lax.all_gather(out_rows, "seq")
     count = lax.axis_size("phase")
-    passed = lax.dynamic_slice_in_dim(ffn_rows, seq_pos, 1, 0)
-    passed = lax.ppermute(passed, "phase", [(p, (p + 1) % count) for p in range(count)])
+    passed = lax.ppermute(out_rows, "phase", [(p, (p + 1) % count) for p in range(count)])[None]
     hessians, ffn_diagonal = hessian(
         scale, place, left_a, attn_cols, gain_a, ffn_rows, gain_ffn, ffn_cols, gain_f
     )

time: 240 us -> 237 us (0.988)
  blocking collectives: 159 us -> 164 us
  starting transfers between devices: 46.4 us -> 43.6 us
    all_gather x1, blocking collectives: 23.3 us -> 27.5 us  [on_device(): ffn_rows = lax.all_gather(out_rows, 'seq')]
    ppermute x1, starting transfers between devices: 6.02 us -> 3.24 us  [on_device(): lax.ppermute(out_rows, 'phase', [(p, (p + 1) % count) for p in range(coun...]
  transfers between devices with their start and end apart: 7 -> 7, of which waited for: 1 -> 0; matrix products, arithmetic and copies ran while one was open for 2% -> 1% of each run, Pallas kernels for 0% -> 0%
where the time goes in v9:
time: 237 us; the launch traced here: 235 us
  blocking collectives  164 us (69%)
  starting transfers between devices  43.6 us (18%)
  Pallas kernels  23.4 us (10%)
  other arithmetic  3.09 us (1%)
    all_to_all x2, blocking collectives, on_device(): arrived = lax.all_to_all(lax.all_to_all(message, 'x', 0, 0), 'seq', 0, 0)  53.2 us
    all_gather x1, blocking collectives, on_device(): attn_rows = lax.all_gather(take_after(hidden[0], gain_a), 'seq')  28.6 us
    all_gather x1, blocking collectives, on_device(): ffn_rows = lax.all_gather(out_rows, 'seq')  27.5 us
    all_gather x1, blocking collectives, on_device(): group = lax.all_gather(pile(resid, extra, table), ZL)  26.9 us
    all_to_all x1, starting transfers between devices, on_device(): attn_cols = lax.all_to_all(copies, 'x', 0, 0)  19.3 us
    all_gather x1, blocking collectives, on_device(): group = lax.all_gather(section_out, ZL)  17.7 us
    all_to_all x1, starting transfers between devices, on_device(): sums = lax.all_to_all(sums, ring, 0, 0)  12.8 us
    all_to_all x1, blocking collectives, on_device(): lax.all_to_all(kv_sum(width, arrived, extra, 2 * nx), ('x', 'zb'), 0, 0)  9.94 us
  transfers between devices with their start and end apart: 7, of which 0 were waited for; matrix products, arithmetic and copies ran while one was open for 1% of the time, Pallas kernels for 0%

profile of v9, /device:TPU:1, one launch (start us, length us, event | category | flops | bytes accessed | tf_op | source)
XLA Modules:
  0.0 235.3 jit_solution(8334614179215604053)
XLA Ops:
  0.6 1.6 collective-permute-start
  2.2 0.7 convert_element_type.5
  2.9 0.7 fusion.3
  3.6 0.7 collective-permute-start.1
  4.3 1.0 fusion.1
  5.4 26.9 %all-gather = bf16[576,512]{1,0:T(8,128)(2,1)S(1)} all-gather(bf16[144,512]{1,0:T(8,128)(2,1)S(1)} %pile.1), channel_id=2, replica_groups=mesh['phase'=8,'x'=4,'za'=2,'zb'=2,'seq'=4] {'za','zb'}, dimensions={0}, use_global_device_ids=true | all-gather | bytes 737280 | tf_op jit(solution)/shard_map/all_gather | solution.py:496
  32.3 1.8 attn_copies.1
  34.2 19.3 %all-to-all-start = ((bf16[4,4,128,512]{3,2,1,0:T(8,128)(2,1)}), bf16[4,4,128,512]{3,2,1,0:T(8,128)(2,1)}, u32[]{:S(2)}, u32[]{:S(2)}) async-start(bf16[4,4,128,512]{3,2,1,0:T(8,128)(2,1)} %get-tuple-element.10), calls=%async_computation | async-start | bytes 4194304 | tf_op jit(solution)/shard_map/all_to_all | solution.py:499
  53.5 0.7 take_after.1
  54.2 28.6 %all-gather.1 = bf16[512,512]{1,0:T(8,128)(2,1)} all-gather(bf16[128,512]{1,0:T(8,128)(2,1)} %take_after.1), channel_id=3, replica_groups=mesh['phase'=8,'x'=4,'za'=2,'zb'=2,'seq'=4] {'seq'}, dimensions={0}, use_global_device_ids=true | all-gather | bytes 655360 | tf_op jit(solution)/shard_map/all_gather | solution.py:498
  82.8 5.7 %project.1 = bf16[4,656,128]{2,1,0:T(8,128)(2,1)} custom-call(bf16[4,4,128,512]{3,2,1,0:T(8,128)(2,1)} %all-to-all-done.cols.cols_a, f32[4,1,512]{2,1,0:T(1,128)} %get-tuple-element.11.after.gain.gain_a, bf16[1,2048,512]{2,1,0:T(8,128)(2,1)} %wq.1, bf16[1,64,2048]{2,1,0:T(8,128)(2,1)} %bitcast.18, bf16[1,64,2048]{2,1,0:T(8,128)(2,1)} %bitcast.19, ...), custom_call_target="tpu_custom_call" | custom-call | tf_op jit(solution)/shard_map/project/pallas_call | solution.py:73
  88.5 12.9 %all_to_all.30 = bf16[4,656,128]{2,1,0:T(8,128)(2,1)S(1)} all-to-all(bf16[4,656,128]{2,1,0:T(8,128)(2,1)} %project.1), channel_id=1, replica_groups=mesh['phase'=8,'x'=4,'za'=2,'zb'=2,'seq'=4] {'x'}, dimensions={0} | all-to-all | bytes 1343488 | tf_op jit(solution)/shard_map/all_to_all | solution.py:502
  101.4 40.3 %all_to_all.31.arrived.q_in = bf16[4,656,128]{2,1,0:T(8,128)(2,1)S(1)} all-to-all(bf16[4,656,128]{2,1,0:T(8,128)(2,1)S(1)} %all_to_all.30), channel_id=1, replica_groups=mesh['phase'=8,'x'=4,'za'=2,'zb'=2,'seq'=4] {'seq'}, dimensions={0} | all-to-all | bytes 1343488 | tf_op jit(solution)/shard_map/all_to_all | solution.py:502
  141.7 0.8 kv_sum.1
  142.4 9.9 %all_to_all.32.kv_in.kv = bf16[8,144,128]{2,1,0:T(8,128)(2,1)S(1)} all-to-all(bf16[8,144,128]{2,1,0:T(8,128)(2,1)} %kv_sum.1), channel_id=1, replica_groups=mesh['phase'=8,'x'=4,'za'=2,'zb'=2,'seq'=4] {'x','zb'}, dimensions={0} | all-to-all | bytes 589824 | tf_op jit(solution)/shard_map/all_to_all | solution.py:503
  152.4 5.5 %attend.1 = (bf16[128,512]{1,0:T(8,128)(2,1)}, f32[16,1,128]{2,1,0:T(1,128)}) custom-call(bf16[4,656,128]{2,1,0:T(8,128)(2,1)S(1)} %all_to_all.31.arrived.q_in, bf16[8,144,128]{2,1,0:T(8,128)(2,1)S(1)} %all_to_all.32.kv_in.kv, f32[512,128]{1,0:T(8,128)S(1)} %pad_maximum_fusion.after.table, bf16[128,512]{1,0:T(8,128)(2,1)S(1)} %collective-permute-done.top.resid), custom_call_target="tpu_custom_call" | custom-call | tf_op jit(solution)/shard_map/attend/pallas_call | solution.py:341
  157.8 1.6 collective-permute-start.2
  159.4 12.8 %all-to-all-start.4 = ((f32[16,1,128]{2,1,0:T(1,128)}), f32[16,1,128]{2,1,0:T(1,128)S(1)}, u32[]{:S(2)}, u32[]{:S(2)}) async-start(f32[16,1,128]{2,1,0:T(1,128)} %get-tuple-element.13), calls=%async_computation.4 | async-start | bytes 16384 | tf_op jit(solution)/shard_map/all_to_all | solution.py:508
  172.2 17.7 %all-gather.3 = bf16[512,512]{1,0:T(8,128)(2,1)S(1)} all-gather(bf16[128,512]{1,0:T(8,128)(2,1)} %get-tuple-element.12), channel_id=5, replica_groups=mesh['phase'=8,'x'=4,'za'=2,'zb'=2,'seq'=4] {'za','zb'}, dimensions={0}, use_global_device_ids=true | all-gather | bytes 655360 | tf_op jit(solution)/shard_map/all_gather | solution.py:510
  190.2 1.9 ffn_copies.1
  192.1 4.5 %all-to-all-start.5 = ((bf16[4,528,512]{2,1,0:T(8,128)(2,1)}), bf16[4,528,512]{2,1,0:T(8,128)(2,1)}, u32[]{:S(2)}, u32[]{:S(2)}) async-start(bf16[4,528,512]{2,1,0:T(8,128)(2,1)} %ffn_copies.1), calls=%async_computation.5 | async-start | bytes 4325376 | tf_op jit(solution)/shard_map/all_to_all | solution.py:512
  197.2 3.2 %collective-permute-start.3 = (bf16[128,512]{1,0:T(8,128)(2,1)S(1)}, bf16[128,512]{1,0:T(8,128)(2,1)S(1)}, u32[]{:S(2)}, u32[]{:S(2)}) collective-permute-start(bf16[128,512]{1,0:T(8,128)(2,1)S(1)} %collective-permute-done.2.own), channel_id=1, source_target_pairs={{0,64},{64,128},{128,192},{192,256},{256,320},{320,384},{384,448},... | collective-permute-start | bytes 393224 | tf_op jit(solution)/shard_map/ppermute | solution.py:515
  200.5 27.5 %all-gather.2 = bf16[512,512]{1,0:T(8,128)(2,1)} all-gather(bf16[128,512]{1,0:T(8,128)(2,1)S(1)} %collective-permute-done.2.own), channel_id=4, replica_groups=mesh['phase'=8,'x'=4,'za'=2,'zb'=2,'seq'=4] {'seq'}, dimensions={0}, use_global_device_ids=true | all-gather | bytes 655360 | tf_op jit(solution)/shard_map/all_gather | solution.py:513
  228.0 6.6 %hessian.1 = (bf16[512,2048]{1,0:T(8,128)(2,1)}, f32[1,128]{1,0:T(1,128)}) custom-call(s32[2]{0:T(128)} %pad_add_fusion.place, bf16[512,512]{1,0:T(8,128)(2,1)} %copy-done, bf16[4,4,128,512]{3,2,1,0:T(8,128)(2,1)} %all-to-all-done.cols.cols_a, f32[4,1,512]{2,1,0:T(1,128)} %get-tuple-element.11.after.gain.gain_a, bf16[4,128,512]{2,1,0:T(8,128)(2,1)} %bitcast.17, ...), custom_call_target="tpu_custom_call" | custom-call | tf_op jit(solution)/shard_map/hessian/pallas_call | solution.py:447
  (23 shorter events, 1.8 us)
Async XLA Ops:
  0.6 4.8 %collective-permute-start = (bf16[128,512]{1,0:T(8,128)(2,1)}, bf16[128,512]{1,0:T(8,128)(2,1)S(1)}, u32[]{:S(2)}, u32[]{:S(2)}) collective-permute-start(bf16[128,512]{1,0:T(8,128)(2,1)} %bitcast.15), channel_id=1, source_target_pairs={{0,0},{1,16},{2,32},{3,48},{4,4},{5,20},{6,36},{7,52},{8,8},{9,24}... | collective-permute-start | bytes 393224 | tf_op jit(solution)/shard_map/ppermute | solution.py:31
  3.6 1.8 collective-permute-start.1
  34.2 19.3 %copy-start.2 = (bf16[1,128,512]{2,1,0:T(8,128)(2,1)S(1)}, bf16[1,128,512]{2,1,0:T(8,128)(2,1)}, u32[]{:S(2)}) copy-start(bf16[1,128,512]{2,1,0:T(8,128)(2,1)} %param.7) | copy-start | bytes 393220
  34.2 19.3 %copy-start.3 = (f32[4,1,512]{2,1,0:T(1,128)S(1)}, f32[4,1,512]{2,1,0:T(1,128)}, u32[]{:S(2)}) copy-start(f32[4,1,512]{2,1,0:T(1,128)} %get-tuple-element.11.after.gain.gain_a) | copy-start | bytes 24580
  34.2 48.6 %all-to-all-start = ((bf16[4,4,128,512]{3,2,1,0:T(8,128)(2,1)}), bf16[4,4,128,512]{3,2,1,0:T(8,128)(2,1)}, u32[]{:S(2)}, u32[]{:S(2)}) async-start(bf16[4,4,128,512]{3,2,1,0:T(8,128)(2,1)} %get-tuple-element.10), calls=%async_computation | async-start | bytes 4194304 | tf_op jit(solution)/shard_map/all_to_all | solution.py:499
  141.7 48.2 %copy-start.1 = (bf16[512,512]{1,0:T(8,128)(2,1)S(1)}, bf16[512,512]{1,0:T(8,128)(2,1)}, u32[]{:S(2)}) copy-start(bf16[512,512]{1,0:T(8,128)(2,1)} %all-gather.1) | copy-start | bytes 1572868
  141.7 48.2 %copy-start.4 = (bf16[1,512]{1,0:T(2,128)(2,1)S(1)}, bf16[1,512]{1,0:T(2,128)(2,1)}, u32[]{:S(2)}) copy-start(bf16[1,512]{1,0:T(2,128)(2,1)} %gain.1) | copy-start | bytes 3076
  157.8 32.4 %collective-permute-start.2 = (bf16[128,512]{1,0:T(8,128)(2,1)}, bf16[128,512]{1,0:T(8,128)(2,1)S(1)}, u32[]{:S(2)}, u32[]{:S(2)}) collective-permute-start(bf16[128,512]{1,0:T(8,128)(2,1)} %get-tuple-element.12), channel_id=1, source_target_pairs={{0,0},{1,16},{2,32},{3,48},{4,4},{5,20},{6,36},{7,52},{8,8},{9,24}... | collective-permute-start | bytes 393224 | tf_op jit(solution)/shard_map/ppermute | solution.py:31
  159.4 30.8 %all-to-all-start.4 = ((f32[16,1,128]{2,1,0:T(1,128)}), f32[16,1,128]{2,1,0:T(1,128)S(1)}, u32[]{:S(2)}, u32[]{:S(2)}) async-start(f32[16,1,128]{2,1,0:T(1,128)} %get-tuple-element.13), calls=%async_computation.4 | async-start | bytes 16384 | tf_op jit(solution)/shard_map/all_to_all | solution.py:508
  190.2 1.9 copy-start
  192.1 35.9 %all-to-all-start.5 = ((bf16[4,528,512]{2,1,0:T(8,128)(2,1)}), bf16[4,528,512]{2,1,0:T(8,128)(2,1)}, u32[]{:S(2)}, u32[]{:S(2)}) async-start(bf16[4,528,512]{2,1,0:T(8,128)(2,1)} %ffn_copies.1), calls=%async_computation.5 | async-start | bytes 4325376 | tf_op jit(solution)/shard_map/all_to_all | solution.py:512
  197.2 30.8 %collective-permute-start.3 = (bf16[128,512]{1,0:T(8,128)(2,1)S(1)}, bf16[128,512]{1,0:T(8,128)(2,1)S(1)}, u32[]{:S(2)}, u32[]{:S(2)}) collective-permute-start(bf16[128,512]{1,0:T(8,128)(2,1)S(1)} %collective-permute-done.2.own), channel_id=1, source_target_pairs={{0,64},{64,128},{128,192},{192,256},{256,320},{320,384},{384,448},... | collective-permute-start | bytes 393224 | tf_op jit(solution)/shard_map/ppermute | solution.py:515

commit v10 on v9

--- a/solution.py
+++ b/solution.py
@@ -190,38 +190,59 @@
     )(top, bottom, after)
 
 
-def ffn_copies_kernel(width, group, sums, own, after, copies, weight):
+def total_of(parts):
+    parts = parts.astype(f32)
+    return parts[0:1] + parts[1:2] + parts[2:3]
+
+
+def below(row, feats):
+    return jnp.concatenate([stacked(three_parts(row))] * (feats // row.shape[1]), 1)
+
+
+def ffn_copies_kernel(group, own, after, copies, message, sums):
     step = pl.program_id(0)
-    rows, feats = group.shape
-    bottom = copies.shape[1] - 16
+    rows, feats = own.shape
+    for k in range(copies.shape[0]):
+        copies[k] = group[pl.ds(0, rows), :]
+    part = total_of(group[pl.ds(rows, 16), :])[:, :rows]
 
     @pl.when(step == 0)
     def _():
-        r_sq = 1.0 / (jnp.sum(sums[...], axis=0) / width + norm_eps)
-        weight[...] = column_of(r_sq)
-        tail = jnp.concatenate([stacked(three_parts(r_sq))] * (feats // rows), 1)
-        for k in range(copies.shape[0]):
-            copies[k, pl.ds(bottom, 16), :] = tail
-
-    block = (group[...].astype(f32) * weight[...]).astype(bf16)
-    for k in range(copies.shape[0]):
-        copies[k, pl.ds(pl.multiple_of(step * rows, rows), rows), :] = block
-
-
-def ffn_copies(width, group, sums, count, *after):
-    parts, rows, feats = group.shape
-    shape = (count, parts * rows + 16, feats)
-    return pl.pallas_call(
-        functools.partial(ffn_copies_kernel, width),
+        message[pl.ds(0, rows), :] = own[...]
+        sums[...] = part
+
+    @pl.when(step > 0)
+    def _():
+        sums[...] += part
+
+    @pl.when(step == pl.num_programs(0) - 1)
+    def _():
+        message[pl.ds(rows, 16), :] = below(sums[...], feats)
+
+
+def ffn_copies(group, own, count, after):
+    parts, tall, feats = group.shape
+    rows = own.shape[0]
+    return pl.pallas_call(
+        ffn_copies_kernel,
         grid=(parts,),
-        in_specs=[pl.BlockSpec((None, rows, feats), lambda z: (z, 0, 0)), fixed(sums.shape)]
-        + [pl.BlockSpec(memory_space=pl.ANY)] * len(after),
-        out_specs=fixed(shape),
-        out_shape=pltpu.HBM(shape, bf16),
-        scratch_shapes=[pltpu.VMEM((rows, 1), f32)],
+        in_specs=[
+            pl.BlockSpec((None, tall, feats), lambda z: (z, 0, 0)),
+            fixed(own.shape),
+            pl.BlockSpec(memory_space=pl.ANY),
+        ],
+        out_specs=[
+            pl.BlockSpec((count, None, rows, feats), lambda z: (0, z, 0, 0)),
+            fixed((tall, feats)),
+        ],
+        out_shape=[
+            pltpu.HBM((count, parts, rows, feats), bf16),
+            pltpu.HBM((tall, feats), bf16),
+        ],
+        scratch_shapes=[pltpu.VMEM((1, rows), f32)],
         compiler_params=params(),
         name="ffn_copies",
-    )(group, sums, *after)
+    )(group, own, after)
 
 
 def kv_sum_kernel(width, arrived, docs, out):
@@ -270,98 +291,82 @@
     return jnp.sum(jnp.where(same, row, f32(0.0)), axis=1, keepdims=True)
 
 
-def attend_kernel(
-    q_in, kv_in, table, resid, out, sums,
-    keys, values, r_all, docs_all, r_own, docs_own, squares,
-):
-    rows = out.shape[0]
+def halves(value):
+    high = value.astype(bf16)
+    return high, (value - high.astype(f32)).astype(bf16)
+
+
+def attend_kernel(q_in, kv_in, table, resid, copies, out, keys, values, r_all, docs_all):
+    rows, feats = out.shape
+    heads = feats // HD
     tokens = keys.shape[0]
     x_pos = lax.axis_index("x")
-
-    @pl.when(pl.program_id(0) == 0)
-    def _():
-        lower = lax.broadcasted_iota(jnp.int32, (rows, HD), 1) < HD // 2
-        for k in range(tokens // rows):
-            first = kv_in[2 * k, pl.ds(0, rows), :].astype(f32)
-            second = kv_in[2 * k + 1, pl.ds(0, rows), :].astype(f32)
-            tail = kv_in[2 * k, pl.ds(rows, 16), :].astype(f32)
-            block = pl.ds(k * rows, rows)
-            key = jnp.where(lower, first, pltpu.roll(second, HD // 2, 1))
-            keys[block, :] = rotate(key, table[block, :])
-            values[block, :] = jnp.where(lower, pltpu.roll(first, HD // 2, 1), second)
-            r = tail[0:1] + tail[1:2] + tail[2:3]
-            r_all[:, block] = r
-            docs_all[:, block] = tail[3:4]
-
-            @pl.when(x_pos == k)
-            def _():
-                r_own[...] = column_of(r) * (1.0 / HD**0.5)
-                docs_own[...] = column_of(tail[3:4])
-
-    query = jnp.sum(q_in[...].astype(f32), axis=0)
+    lower = lax.broadcasted_iota(jnp.int32, (rows, HD), 1) < HD // 2
+    for k in range(tokens // rows):
+        first = kv_in[2 * k, pl.ds(0, rows), :].astype(f32)
+        second = kv_in[2 * k + 1, pl.ds(0, rows), :].astype(f32)
+        tail = kv_in[2 * k, pl.ds(rows, 16), :].astype(f32)
+        block = pl.ds(k * rows, rows)
+        key = jnp.where(lower, first, pltpu.roll(second, HD // 2, 1))
+        high, low = halves(rotate(key, table[block, :]))
+        keys[block, :] = jnp.concatenate([high, high, low], 1)
+        value = jnp.where(lower, pltpu.roll(first, HD // 2, 1), second).astype(bf16)
+        values[block, :] = value
+        values[pl.ds(tokens + k * rows, rows), :] = value
+        r_all[:, block] = total_of(tail)
+        docs_all[:, block] = tail[3:4]
+
     own = pl.ds(pl.multiple_of(x_pos * rows, rows), rows)
-    query = rotate(query, table[own, :]) * r_own[...]
-    scores = lax.dot_general(
-        query, keys[...], (((1,), (1,)), ((), ())),
-        preferred_element_type=f32, precision=lax.Precision.HIGHEST,
-    )
-    scores = scores * r_all[...]
-    key_ids = lax.broadcasted_iota(jnp.int32, scores.shape, 1)
-    own_ids = lax.broadcasted_iota(jnp.int32, scores.shape, 0) + x_pos * rows
-    allowed = (key_ids <= own_ids) & (docs_all[...] == docs_own[...])
-    scores = jnp.where(allowed, scores, f32(-1e30))
-    peak = jnp.max(scores, axis=-1, keepdims=True)
-    weights = jnp.where(allowed, jnp.exp(scores - peak), f32(0.0))
-    total = jnp.sum(weights, axis=-1, keepdims=True)
-    context = jnp.dot(
-        weights * r_all[...], values[...],
-        preferred_element_type=f32, precision=lax.Precision.HIGHEST,
-    ) / total
-    result = (resid[...].astype(f32) + context).astype(bf16)
-    out[...] = result
-    result = result.astype(f32)
-    part = jnp.sum(result * result, axis=1, keepdims=True)
-
-    @pl.when(pl.program_id(0) == 0)
-    def _():
-        squares[...] = part
-
-    @pl.when(pl.program_id(0) > 0)
-    def _():
-        squares[...] += part
-
-    @pl.when(pl.program_id(0) == pl.num_programs(0) - 1)
-    def _():
-        sums[...] = jnp.broadcast_to(row_of(squares[...])[None], sums.shape)
+    r_own = column_of(r_all[:, own]) * (1.0 / HD**0.5)
+    key_ids = lax.broadcasted_iota(jnp.int32, (rows, tokens), 1)
+    own_ids = lax.broadcasted_iota(jnp.int32, (rows, tokens), 0) + x_pos * rows
+    allowed = (key_ids <= own_ids) & (docs_all[...] == column_of(docs_all[:, own]))
+    squares = jnp.zeros((rows, 1), f32)
+    for h in range(heads):
+        query = jnp.sum(q_in[:, pl.ds(h * rows, rows), :].astype(f32), axis=0)
+        high, low = halves(rotate(query, table[own, :]) * r_own)
+        scores = lax.dot_general(
+            jnp.concatenate([high, low, high], 1), keys[...], (((1,), (1,)), ((), ())),
+            preferred_element_type=f32,
+        )
+        scores = jnp.where(allowed, scores * r_all[...], f32(-1e30))
+        peak = jnp.max(scores, axis=-1, keepdims=True)
+        weights = jnp.where(allowed, jnp.exp(scores - peak), f32(0.0))
+        total = jnp.sum(weights, axis=-1, keepdims=True)
+        weights = jnp.concatenate(halves(weights * r_all[...]), 1)
+        context = jnp.dot(weights, values[...], preferred_element_type=f32) / total
+        lanes = pl.ds(h * HD, HD)
+        result = (resid[:, lanes].astype(f32) + context).astype(bf16)
+        out[:, lanes] = result
+        for copy in range(copies.shape[0]):
+            copies[copy, pl.ds(0, rows), lanes] = result
+        result = result.astype(f32)
+        squares += jnp.sum(result * result, axis=1, keepdims=True)
+    tail = below(row_of(squares), feats)
+    for copy in range(copies.shape[0]):
+        copies[copy, pl.ds(rows, 16), :] = tail
 
 
 def attend(q_in, kv_in, table, resid, copies):
     rows, feats = resid.shape
     heads, tokens = feats // HD, table.shape[0]
+    shape = (copies, rows + 16, feats)
     return pl.pallas_call(
         attend_kernel,
-        grid=(heads,),
+        grid=(1,),
         in_specs=[
-            pl.BlockSpec((q_in.shape[0], rows, HD), lambda h: (0, h, 0)),
-        ]
-        + [fixed(kv_in.shape), fixed(table.shape)]
-        + [pl.BlockSpec((rows, HD), lambda h: (0, h))],
-        out_specs=[
-            pl.BlockSpec((rows, HD), lambda h: (0, h)),
-            fixed((copies, 1, rows)),
-        ],
-        out_shape=[
-            pltpu.HBM((rows, feats), bf16),
-            pltpu.HBM((copies, 1, rows), f32),
-        ],
+            fixed((q_in.shape[0], heads * rows, HD)),
+            fixed(kv_in.shape),
+            fixed(table.shape),
+            fixed(resid.shape),
+        ],
+        out_specs=[fixed(shape), fixed(resid.shape)],
+        out_shape=[pltpu.HBM(shape, bf16), pltpu.HBM(resid.shape, bf16)],
         scratch_shapes=[
-            pltpu.VMEM((tokens, HD), f32),
-            pltpu.VMEM((tokens, HD), f32),
+            pltpu.VMEM((tokens, 3 * HD), bf16),
+            pltpu.VMEM((2 * tokens, HD), bf16),
             pltpu.VMEM((1, tokens), f32),
             pltpu.VMEM((1, tokens), f32),
-            pltpu.VMEM((rows, 1), f32),
-            pltpu.VMEM((rows, 1), f32),
-            pltpu.VMEM((rows, 1), f32),
         ],
         compiler_params=params(),
         name="attend",
@@ -392,25 +397,23 @@
 
 
 def hessian_kernel(
-    scale, place, left_a, cols_a, gain_a, ffn_rows, gain_row, r_sq, cols_f, gain_f,
-    out, diagonal, left_f, turned_f,
+    scale, width, place, left_a, cols_a, gain_a, ffn_rows, gain_row, total, cols_f, gain_f,
+    out, diagonal, left_f,
 ):
     blocks, rows, feats = cols_a.shape
     row, col = place[0], place[1] + pl.program_id(0)
 
     @pl.when(pl.program_id(0) == 0)
     def _():
-        squares = jnp.zeros((rows, 1), f32)
-        part = pl.multiple_of(lax.axis_index("seq") * rows, rows)
+        part = pl.ds(pl.multiple_of(lax.axis_index("seq") * rows, rows), rows)
+        squares = jnp.zeros((1, rows), f32)
         for k in range(blocks):
-            turned = (ffn_rows[k].astype(f32) * gain_row[...].astype(f32)).T * scale
-            parts = r_sq[k].astype(f32)[:, :rows]
-            weight = (parts[0:1] + parts[1:2] + parts[2:3]) / scale
-            turned_f[...] = turned
-            mine = turned_f[pl.ds(part, rows), :]
-            squares += jnp.sum(mine * mine * weight, axis=1, keepdims=True)
-            left_f[:, pl.ds(k * rows, rows)] = turned.astype(bf16)
-        diagonal[...] = row_of(squares)
+            weight = column_of(scale / (total[k] / width + norm_eps))
+            block = ffn_rows[k, pl.ds(0, rows), :].astype(f32) * gain_row[...].astype(f32)
+            left_f[:, pl.ds(k * rows, rows)] = (block * weight).astype(bf16).T
+            mine = ffn_rows[k, pl.ds(0, rows), part].astype(f32) * gain_row[:, part].astype(f32)
+            squares += jnp.sum(mine * mine * weight, axis=0, keepdims=True)
+        diagonal[...] = squares
 
     def product(left, cols, gain):
         right = cols[...].reshape(blocks * rows, feats)
@@ -433,7 +436,9 @@
         out[...] = jnp.where(row_ids <= col_ids, upper, lower)
 
 
-def hessian(scale, place, left_a, cols_a, gain_a, ffn_rows, gain_row, cols_f, gain_f):
+def hessian(
+    scale, width, place, left_a, cols_a, gain_a, ffn_rows, gain_row, total, cols_f, gain_f
+):
     blocks, parts, rows, feats = cols_a.shape
     tokens = blocks * rows
 
@@ -445,7 +450,7 @@
 
     gain = pl.BlockSpec((None, 1, feats), lambda z, at: (z, 0, 0))
     return pl.pallas_call(
-        functools.partial(hessian_kernel, scale),
+        functools.partial(hessian_kernel, scale, width),
         grid_spec=pltpu.PrefetchScalarGridSpec(
             num_scalar_prefetch=1,
             grid=(parts,),
@@ -455,15 +460,15 @@
                 gain,
                 fixed(ffn_rows.shape),
                 fixed(gain_row.shape),
-                pl.BlockSpec((blocks, 16, feats), lambda z, at: (0, parts * rows // 16, 0)),
-                pl.BlockSpec((blocks, rows, feats), lambda z, at: (0, lower_at(z, at), 0)),
+                fixed(total.shape),
+                pl.BlockSpec((blocks, None, rows, feats), lambda z, at: (0, lower_at(z, at), 0, 0)),
                 gain,
             ],
             out_specs=[
                 pl.BlockSpec((feats, feats), lambda z, at: (0, z)),
                 fixed((1, rows)),
             ],
-            scratch_shapes=[pltpu.VMEM((feats, tokens), bf16), pltpu.VMEM((feats, rows), f32)],
+            scratch_shapes=[pltpu.VMEM((feats, tokens), bf16)],
         ),
         out_shape=[
             jax.ShapeDtypeStruct((feats, parts * feats), bf16),
@@ -471,7 +476,7 @@
         ],
         compiler_params=params(WIDE),
         name="hessian",
-    )(place, left_a, cols_a, gain_a, ffn_rows, gain_row, cols_f, cols_f, gain_f)
+    )(place, left_a, cols_a, gain_a, ffn_rows, gain_row, total, cols_f, gain_f)
 
 
 def on_device(hidden, segment_ids, gain_attn, gain_ffn, w_query, w_key, w_value):
@@ -501,20 +506,21 @@
     message = project(attn_cols, gain_a, w_query, w_key, w_value, attn_rows)
     arrived = lax.all_to_all(lax.all_to_all(message, "x", 0, 0), "seq", 0, 0)
     kv = lax.all_to_all(kv_sum(width, arrived, extra, 2 * nx), ("x", "zb"), 0, 0)
-    ring = ZL + ("seq",)
-    section_out, sums = attend(arrived, kv, table, resid, lax.axis_size(ring))
+    copies, section_out = attend(arrived, kv, table, resid, nz)
     left_a = attn_left(scale, attn_rows, gain_attn, kv)
 
-    sums = lax.all_to_all(sums, ring, 0, 0)
     out_rows = swap_x_seq(section_out)
-    group = lax.all_gather(section_out, ZL)
-    copies = ffn_copies(width, group, sums, nx, out_rows, left_a)
+    group = lax.all_to_all(copies, ZL, 0, 0)
+    copies, message = ffn_copies(group, out_rows, nx, left_a)
     ffn_cols = lax.all_to_all(copies, "x", 0, 0)
-    ffn_rows = lax.all_gather(out_rows, "seq")
+    ffn_rows = lax.all_gather(message, "seq")
+    total = jnp.sum(ffn_rows[:, rows : rows + 3, :rows].astype(f32), axis=(0, 1))
+    total = lax.all_gather(total[None], "x")
     count = lax.axis_size("phase")
-    passed = lax.ppermute(out_rows, "phase", [(p, (p + 1) % count) for p in range(count)])[None]
+    passed = lax.dynamic_slice_in_dim(ffn_rows[:, :rows], seq_pos, 1, 0)
+    passed = lax.ppermute(passed, "phase", [(p, (p + 1) % count) for p in range(count)])
     hessians, ffn_diagonal = hessian(
-        scale, place, left_a, attn_cols, gain_a, ffn_rows, gain_ffn, ffn_cols, gain_f
+        scale, width, place, left_a, attn_cols, gain_a, ffn_rows, gain_ffn, total, ffn_cols, gain_f
     )
     return (passed, hessians[None], ffn_diagonal)
 

time: 237 us -> 238 us (level)
  blocking collectives: 164 us -> 125 us
  starting transfers between devices: 43.6 us -> 70.9 us
  waiting for transfers between devices: 0.02 us -> 14.6 us
  Pallas kernels: 23.4 us -> 20.8 us
    all_gather x2, blocking collectives: 45.2 us -> 24.2 us  [the longest x1 16 us: on_device(): ffn_rows = lax.all_gather(message, 'seq')]
    ppermute x1, starting transfers between devices: 3.24 us -> 20.2 us  [on_device(): lax.ppermute(passed, 'phase', [(p, (p + 1) % count) for p in range(count)])]
    all_to_all x1, waiting for transfers between devices: 0.01 us -> 14.6 us  [on_device(): group = lax.all_to_all(copies, ZL, 0, 0)]
    all_to_all x1, starting transfers between devices: 19.3 us -> 32.5 us  [on_device(): attn_cols = lax.all_to_all(copies, 'x', 0, 0)]
    all_to_all x2, blocking collectives: 53.2 us -> 45.4 us  [on_device(): arrived = lax.all_to_all(lax.all_to_all(message, 'x', 0, 0), 'seq', 0, 0)]
    all_gather x1, blocking collectives: 26.9 us -> 21.1 us  [on_device(): group = lax.all_gather(pile(resid, extra, table), ZL)]
    all_gather x1, blocking collectives: 28.6 us -> 24.4 us  [on_device(): attn_rows = lax.all_gather(take_after(hidden[0], gain_a), 'seq')]
    pallas_call x3, Pallas kernels: 14 us -> 11.4 us  [the longest x1 6.42 us: hessian(): pl.pallas_call(functools.partial(hessian_kernel, scale, width), grid_spec...]
  transfers between devices with their start and end apart: 7 -> 7, of which waited for: 0 -> 1; matrix products, arithmetic and copies ran while one was open for 1% -> 1% of each run, Pallas kernels for 0% -> 0%
where the time goes in v10:
time: 238 us
  blocking collectives  125 us (53%)
  starting transfers between devices  70.9 us (30%)
  Pallas kernels  20.8 us (9%)
  waiting for transfers between devices  14.6 us (6%)
  other arithmetic  3.11 us (1%)
    all_to_all x2, blocking collectives, on_device(): arrived = lax.all_to_all(lax.all_to_all(message, 'x', 0, 0), 'seq', 0, 0)  45.4 us
    all_to_all x1, starting transfers between devices, on_device(): attn_cols = lax.all_to_all(copies, 'x', 0, 0)  32.5 us
    all_gather x1, blocking collectives, on_device(): attn_rows = lax.all_gather(take_after(hidden[0], gain_a), 'seq')  24.4 us
    all_gather x1, blocking collectives, on_device(): group = lax.all_gather(pile(resid, extra, table), ZL)  21.1 us
    ppermute x1, starting transfers between devices, on_device(): lax.ppermute(passed, 'phase', [(p, (p + 1) % count) for p in range(count)])  20.2 us
    all_gather x1, blocking collectives, on_device(): ffn_rows = lax.all_gather(message, 'seq')  16 us
    all_to_all x1, waiting for transfers between devices, on_device(): group = lax.all_to_all(copies, ZL, 0, 0)  14.6 us
    all_to_all x1, starting transfers between devices, on_device(): group = lax.all_to_all(copies, ZL, 0, 0)  10.4 us
  transfers between devices with their start and end apart: 7, of which 1 were waited for; matrix products, arithmetic and copies ran while one was open for 1% of the time, Pallas kernels for 0%

profile of v10, /device:TPU:1, one launch (start us, length us, event | category | flops | bytes accessed | tf_op | source)
XLA Modules:
  0.0 237.6 jit_solution(5633178087843183506)
XLA Ops:
  1.3 0.7 fusion.3
  2.7 1.6 collective-permute-start
  4.2 1.0 fusion.1
  5.4 21.1 %all-gather = bf16[576,512]{1,0:T(8,128)(2,1)S(1)} all-gather(bf16[144,512]{1,0:T(8,128)(2,1)S(1)} %pile.1), channel_id=2, replica_groups=mesh['phase'=8,'x'=4,'za'=2,'zb'=2,'seq'=4] {'za','zb'}, dimensions={0}, use_global_device_ids=true | all-gather | bytes 737280 | tf_op jit(solution)/shard_map/all_gather | solution.py:501
  26.5 1.8 attn_copies.1
  28.4 32.5 %all-to-all-start = ((bf16[4,4,128,512]{3,2,1,0:T(8,128)(2,1)}), bf16[4,4,128,512]{3,2,1,0:T(8,128)(2,1)}, u32[]{:S(2)}, u32[]{:S(2)}) async-start(bf16[4,4,128,512]{3,2,1,0:T(8,128)(2,1)} %get-tuple-element.12), calls=%async_computation | async-start | bytes 4194304 | tf_op jit(solution)/shard_map/all_to_all | solution.py:504
  60.9 0.7 take_after.1
  61.6 24.4 %all-gather.1 = bf16[512,512]{1,0:T(8,128)(2,1)} all-gather(bf16[128,512]{1,0:T(8,128)(2,1)} %take_after.1), channel_id=3, replica_groups=mesh['phase'=8,'x'=4,'za'=2,'zb'=2,'seq'=4] {'seq'}, dimensions={0}, use_global_device_ids=true | all-gather | bytes 655360 | tf_op jit(solution)/shard_map/all_gather | solution.py:503
  86.0 5.7 %project.1 = bf16[4,656,128]{2,1,0:T(8,128)(2,1)} custom-call(bf16[4,4,128,512]{3,2,1,0:T(8,128)(2,1)} %all-to-all-done.cols.cols_a, f32[4,1,512]{2,1,0:T(1,128)} %get-tuple-element.13.after.gain.gain_a, bf16[1,2048,512]{2,1,0:T(8,128)(2,1)} %wq.1, bf16[1,64,2048]{2,1,0:T(8,128)(2,1)} %bitcast.18, bf16[1,64,2048]{2,1,0:T(8,128)(2,1)} %bitcast.19, ...), custom_call_target="tpu_custom_call" | custom-call | tf_op jit(solution)/shard_map/project/pallas_call | solution.py:73
  91.7 12.3 %all_to_all.30 = bf16[4,656,128]{2,1,0:T(8,128)(2,1)S(1)} all-to-all(bf16[4,656,128]{2,1,0:T(8,128)(2,1)} %project.1), channel_id=1, replica_groups=mesh['phase'=8,'x'=4,'za'=2,'zb'=2,'seq'=4] {'x'}, dimensions={0} | all-to-all | bytes 1343488 | tf_op jit(solution)/shard_map/all_to_all | solution.py:507
  104.0 33.2 %all_to_all.31.arrived.q_in = bf16[4,656,128]{2,1,0:T(8,128)(2,1)S(1)} all-to-all(bf16[4,656,128]{2,1,0:T(8,128)(2,1)S(1)} %all_to_all.30), channel_id=1, replica_groups=mesh['phase'=8,'x'=4,'za'=2,'zb'=2,'seq'=4] {'seq'}, dimensions={0} | all-to-all | bytes 1343488 | tf_op jit(solution)/shard_map/all_to_all | solution.py:507
  137.1 0.8 kv_sum.1
  137.9 10.3 %all_to_all.32.kv_in.kv = bf16[8,144,128]{2,1,0:T(8,128)(2,1)S(1)} all-to-all(bf16[8,144,128]{2,1,0:T(8,128)(2,1)} %kv_sum.1), channel_id=1, replica_groups=mesh['phase'=8,'x'=4,'za'=2,'zb'=2,'seq'=4] {'x','zb'}, dimensions={0} | all-to-all | bytes 589824 | tf_op jit(solution)/shard_map/all_to_all | solution.py:508
  148.2 3.1 %attend.1 = (bf16[4,144,512]{2,1,0:T(8,128)(2,1)}, bf16[128,512]{1,0:T(8,128)(2,1)}) custom-call(bf16[4,656,128]{2,1,0:T(8,128)(2,1)S(1)} %all_to_all.31.arrived.q_in, bf16[8,144,128]{2,1,0:T(8,128)(2,1)S(1)} %all_to_all.32.kv_in.kv, f32[512,128]{1,0:T(8,128)S(1)} %pad_maximum_fusion.after.table, bf16[128,512]{1,0:T(8,128)(2,1)S(1)} %collective-permute-done.top.resid), custom_call_target="tpu_custom_call" | custom-call | tf_op jit(solution)/shard_map/attend/pallas_call | solution.py:354
  151.3 10.4 %all-to-all-start.4 = ((bf16[4,144,512]{2,1,0:T(8,128)(2,1)}), bf16[4,144,512]{2,1,0:T(8,128)(2,1)S(1)}, u32[]{:S(2)}, u32[]{:S(2)}) async-start(bf16[4,144,512]{2,1,0:T(8,128)(2,1)} %get-tuple-element.14), calls=%async_computation.4 | async-start | bytes 1179648 | tf_op jit(solution)/shard_map/all_to_all | solution.py:513
  161.7 1.6 collective-permute-start.2
  163.6 14.6 %all-to-all-done.4.group = bf16[4,144,512]{2,1,0:T(8,128)(2,1)S(1)} async-done(((bf16[4,144,512]{2,1,0:T(8,128)(2,1)}), bf16[4,144,512]{2,1,0:T(8,128)(2,1)S(1)}, u32[]{:S(2)}, u32[]{:S(2)}) %all-to-all-start.4) | async-done | bytes 589856 | tf_op jit(solution)/shard_map/all_to_all | solution.py:513
  178.2 1.9 ffn_copies.1
  180.1 3.9 %all-to-all-start.5 = ((bf16[4,4,128,512]{3,2,1,0:T(8,128)(2,1)}), bf16[4,4,128,512]{3,2,1,0:T(8,128)(2,1)S(1)}, u32[]{:S(2)}, u32[]{:S(2)}) async-start(bf16[4,4,128,512]{3,2,1,0:T(8,128)(2,1)} %get-tuple-element.17), calls=%async_computation.5 | async-start | bytes 4194304 | tf_op jit(solution)/shard_map/all_to_all | solution.py:515
  184.1 16.0 %all-gather.2 = bf16[576,512]{1,0:T(8,128)(2,1)S(1)} all-gather(bf16[144,512]{1,0:T(8,128)(2,1)S(1)} %copy-done.7), channel_id=4, replica_groups=mesh['phase'=8,'x'=4,'za'=2,'zb'=2,'seq'=4] {'seq'}, dimensions={0}, use_global_device_ids=true | all-gather | bytes 737280 | tf_op jit(solution)/shard_map/all_gather | solution.py:516
  200.1 20.2 %collective-permute-start.3 = (bf16[1,128,512]{2,1,0:T(8,128)(2,1)S(1)}, bf16[1,128,512]{2,1,0:T(8,128)(2,1)S(1)}, u32[]{:S(2)}, u32[]{:S(2)}) collective-permute-start(bf16[1,128,512]{2,1,0:T(8,128)(2,1)S(1)} %constant_dynamic-slice_fusion), channel_id=1, source_target_pairs={{0,64},{64,128},{128,192},{192,256},{256,320},{320,384},{384,448},... | collective-permute-start | bytes 393224 | tf_op jit(solution)/shard_map/ppermute | solution.py:521
  221.0 8.2 %all-gather.4.total = f32[4,1,128]{2,1,0:T(1,128)} all-gather(f32[1,1,128]{2,1,0:T(1,128)S(1)} %bitcast.20), channel_id=5, replica_groups=mesh['phase'=8,'x'=4,'za'=2,'zb'=2,'seq'=4] {'x'}, dimensions={0}, use_global_device_ids=true | all-gather | bytes 2560 | tf_op jit(solution)/shard_map/all_gather | solution.py:518
  229.2 1.3 copy-done.5
  230.5 6.4 %hessian.1 = (bf16[512,2048]{1,0:T(8,128)(2,1)}, f32[1,128]{1,0:T(1,128)}) custom-call(s32[2]{0:T(128)} %pad_add_fusion.place, bf16[512,512]{1,0:T(8,128)(2,1)} %copy-done, bf16[4,4,128,512]{3,2,1,0:T(8,128)(2,1)} %all-to-all-done.cols.cols_a, f32[4,1,512]{2,1,0:T(1,128)} %get-tuple-element.13.after.gain.gain_a, bf16[4,144,512]{2,1,0:T(8,128)(2,1)} %bitcast.17, ...), custom_call_target="tpu_custom_call" | custom-call | tf_op jit(solution)/shard_map/hessian/pallas_call | solution.py:452
  (32 shorter events, 3.2 us)
Async XLA Ops:
  2.0 3.4 %collective-permute-start.1 = (bf16[16,512]{1,0:T(8,128)(2,1)S(1)}, bf16[16,512]{1,0:T(8,128)(2,1)S(1)}, u32[]{:S(2)}, u32[]{:S(2)}) collective-permute-start(bf16[16,512]{1,0:T(8,128)(2,1)S(1)} %fusion.3), channel_id=1, source_target_pairs={{0,0},{1,16},{2,32},{3,48},{4,4},{5,20},{6,36},{7,52},{8,8},{9,24}... | collective-permute-start | bytes 49160 | tf_op jit(solution)/shard_map/ppermute | solution.py:31
  2.7 2.7 %collective-permute-start = (bf16[128,512]{1,0:T(8,128)(2,1)}, bf16[128,512]{1,0:T(8,128)(2,1)S(1)}, u32[]{:S(2)}, u32[]{:S(2)}) collective-permute-start(bf16[128,512]{1,0:T(8,128)(2,1)} %bitcast.13), channel_id=1, source_target_pairs={{0,0},{1,16},{2,32},{3,48},{4,4},{5,20},{6,36},{7,52},{8,8},{9,24}... | collective-permute-start | bytes 393224 | tf_op jit(solution)/shard_map/ppermute | solution.py:31
  28.4 32.5 %copy-start.2 = (bf16[1,128,512]{2,1,0:T(8,128)(2,1)S(1)}, bf16[1,128,512]{2,1,0:T(8,128)(2,1)}, u32[]{:S(2)}) copy-start(bf16[1,128,512]{2,1,0:T(8,128)(2,1)} %param.7) | copy-start | bytes 393220
  28.4 32.5 %copy-start.3 = (f32[4,1,512]{2,1,0:T(1,128)S(1)}, f32[4,1,512]{2,1,0:T(1,128)}, u32[]{:S(2)}) copy-start(f32[4,1,512]{2,1,0:T(1,128)} %get-tuple-element.13.after.gain.gain_a) | copy-start | bytes 24580
  28.4 57.6 %all-to-all-start = ((bf16[4,4,128,512]{3,2,1,0:T(8,128)(2,1)}), bf16[4,4,128,512]{3,2,1,0:T(8,128)(2,1)}, u32[]{:S(2)}, u32[]{:S(2)}) async-start(bf16[4,4,128,512]{3,2,1,0:T(8,128)(2,1)} %get-tuple-element.12), calls=%async_computation | async-start | bytes 4194304 | tf_op jit(solution)/shard_map/all_to_all | solution.py:504
  137.1 26.1 %copy-start.1 = (bf16[512,512]{1,0:T(8,128)(2,1)S(1)}, bf16[512,512]{1,0:T(8,128)(2,1)}, u32[]{:S(2)}) copy-start(bf16[512,512]{1,0:T(8,128)(2,1)} %all-gather.1) | copy-start | bytes 1572868
  137.1 26.1 %copy-start.4 = (bf16[1,512]{1,0:T(2,128)(2,1)S(1)}, bf16[1,512]{1,0:T(2,128)(2,1)}, u32[]{:S(2)}) copy-start(bf16[1,512]{1,0:T(2,128)(2,1)} %gain.1) | copy-start | bytes 3076
  151.3 26.9 %all-to-all-start.4 = ((bf16[4,144,512]{2,1,0:T(8,128)(2,1)}), bf16[4,144,512]{2,1,0:T(8,128)(2,1)S(1)}, u32[]{:S(2)}, u32[]{:S(2)}) async-start(bf16[4,144,512]{2,1,0:T(8,128)(2,1)} %get-tuple-element.14), calls=%async_computation.4 | async-start | bytes 1179648 | tf_op jit(solution)/shard_map/all_to_all | solution.py:513
  161.7 1.9 collective-permute-start.2
  163.6 16.5 %copy-start = (bf16[512,512]{1,0:T(8,128)(2,1)}, bf16[512,512]{1,0:T(8,128)(2,1)S(1)}, u32[]{:S(2)}) copy-start(bf16[512,512]{1,0:T(8,128)(2,1)S(1)} %attn_left.1.after.left_a) | copy-start | bytes 1572868
  180.1 3.9 %copy-start.7 = (bf16[144,512]{1,0:T(8,128)(2,1)S(1)}, bf16[144,512]{1,0:T(8,128)(2,1)}, u32[]{:S(2)}) copy-start(bf16[144,512]{1,0:T(8,128)(2,1)} %get-tuple-element.16) | copy-start | bytes 442372
  180.1 49.1 %all-to-all-start.5 = ((bf16[4,4,128,512]{3,2,1,0:T(8,128)(2,1)}), bf16[4,4,128,512]{3,2,1,0:T(8,128)(2,1)S(1)}, u32[]{:S(2)}, u32[]{:S(2)}) async-start(bf16[4,4,128,512]{3,2,1,0:T(8,128)(2,1)} %get-tuple-element.17), calls=%async_computation.5 | async-start | bytes 4194304 | tf_op jit(solution)/shard_map/all_to_all | solution.py:515
  200.1 29.1 %copy-start.6 = (bf16[576,512]{1,0:T(8,128)(2,1)}, bf16[576,512]{1,0:T(8,128)(2,1)S(1)}, u32[]{:S(2)}) copy-start(bf16[576,512]{1,0:T(8,128)(2,1)S(1)} %all-gather.2) | copy-start | bytes 1769476
  200.1 29.1 %collective-permute-start.3 = (bf16[1,128,512]{2,1,0:T(8,128)(2,1)S(1)}, bf16[1,128,512]{2,1,0:T(8,128)(2,1)S(1)}, u32[]{:S(2)}, u32[]{:S(2)}) collective-permute-start(bf16[1,128,512]{2,1,0:T(8,128)(2,1)S(1)} %constant_dynamic-slice_fusion), channel_id=1, source_target_pairs={{0,64},{64,128},{128,192},{192,256},{256,320},{320,384},{384,448},... | collective-permute-start | bytes 393224 | tf_op jit(solution)/shard_map/ppermute | solution.py:521
  229.2 1.3 copy-start.5

commit v11 on v10

--- a/solution.py
+++ b/solution.py
@@ -122,7 +122,7 @@
     return jnp.concatenate([row.astype(f32) for row in rows]).astype(bf16)
 
 
-def attn_copies_kernel(group, copies, gain_a, gain_f):
+def attn_copies_kernel(group, table, place, copies, gain_a, gain_f):
     rows = copies.shape[1]
     for k in range(copies.shape[0]):
         copies[k] = group[pl.ds(0, rows), :]
@@ -131,7 +131,7 @@
     gain_f[...] = gains[1:2]
 
 
-def attn_copies(group, count):
+def attn_copies(group, count, *after):
     parts, tall, feats = group.shape
     rows = tall - 16
     gain = pl.BlockSpec((None, 1, feats), lambda z: (z, 0, 0))
@@ -139,7 +139,8 @@
     return pl.pallas_call(
         attn_copies_kernel,
         grid=(parts,),
-        in_specs=[pl.BlockSpec((None, tall, feats), lambda z: (z, 0, 0))],
+        in_specs=[pl.BlockSpec((None, tall, feats), lambda z: (z, 0, 0))]
+        + [pl.BlockSpec(memory_space=pl.ANY)] * len(after),
         out_specs=[
             pl.BlockSpec((count, None, rows, feats), lambda z: (0, z, 0, 0)),
             gain,
@@ -152,7 +153,7 @@
         ],
         compiler_params=params(),
         name="attn_copies",
-    )(group)
+    )(group, *after)
 
 
 def take_kernel(value, after, out):
@@ -166,28 +167,30 @@
         in_specs=[fixed(value.shape), pl.BlockSpec(memory_space=pl.ANY)],
         out_specs=fixed(value.shape),
         out_shape=pltpu.HBM(value.shape, value.dtype),
-        compiler_params=params(),
+        compiler_params=params(WIDE),
         name="take_after",
     )(value, after)
 
 
-def pile_kernel(top, bottom, after, out):
-    rows = top.shape[0]
-    out[pl.ds(0, rows), :] = top[...]
-    out[pl.ds(rows, bottom.shape[0]), :] = bottom[...]
-
-
-def pile(top, bottom, after):
-    shape = (top.shape[0] + bottom.shape[0], top.shape[1])
-    return pl.pallas_call(
-        pile_kernel,
+def first_message_kernel(hidden, gain_a, gain_f, ids, out):
+    rows, feats = hidden.shape
+    out[pl.ds(0, rows), :] = hidden[...]
+    docs = jnp.concatenate([ids[...].astype(f32)] * (feats // rows), 1)
+    out[pl.ds(rows, 16), :] = stacked([gain_a[...], gain_f[...], docs])
+
+
+def first_message(hidden, gain_a, gain_f, ids):
+    shape = (hidden.shape[0] + 16, hidden.shape[1])
+    arrays = (hidden, gain_a, gain_f, ids)
+    return pl.pallas_call(
+        first_message_kernel,
         grid=(1,),
-        in_specs=[fixed(top.shape), fixed(bottom.shape), pl.BlockSpec(memory_space=pl.ANY)],
+        in_specs=[fixed(a.shape) for a in arrays],
         out_specs=fixed(shape),
-        out_shape=jax.ShapeDtypeStruct(shape, top.dtype),
-        compiler_params=params(),
-        name="pile",
-    )(top, bottom, after)
+        out_shape=pltpu.HBM(shape, bf16),
+        compiler_params=params(WIDE),
+        name="first_message",
+    )(*arrays)
 
 
 def total_of(parts):
@@ -268,7 +271,7 @@
                 (pl.Element(blocks), pl.Element(rows + 16), pl.Element(lanes)),
                 lambda i: (0, last, 0),
             ),
-            fixed(docs.shape),
+            pl.BlockSpec((16, docs.shape[1]), lambda i: (rows // 16, 0)),
         ],
         out_specs=fixed((copies, rows + 16, lanes)),
         out_shape=pltpu.HBM((copies, rows + 16, lanes), bf16),
@@ -347,8 +350,8 @@
         copies[copy, pl.ds(rows, 16), :] = tail
 
 
-def attend(q_in, kv_in, table, resid, copies):
-    rows, feats = resid.shape
+def attend(q_in, kv_in, table, swapped, copies):
+    rows, feats = swapped.shape[0] - 16, swapped.shape[1]
     heads, tokens = feats // HD, table.shape[0]
     shape = (copies, rows + 16, feats)
     return pl.pallas_call(
@@ -358,10 +361,10 @@
             fixed((q_in.shape[0], heads * rows, HD)),
             fixed(kv_in.shape),
             fixed(table.shape),
-            fixed(resid.shape),
-        ],
-        out_specs=[fixed(shape), fixed(resid.shape)],
-        out_shape=[pltpu.HBM(shape, bf16), pltpu.HBM(resid.shape, bf16)],
+            fixed((rows, feats)),
+        ],
+        out_specs=[fixed(shape), fixed((rows, feats))],
+        out_shape=[pltpu.HBM(shape, bf16), pltpu.HBM((rows, feats), bf16)],
         scratch_shapes=[
             pltpu.VMEM((tokens, 3 * HD), bf16),
             pltpu.VMEM((2 * tokens, HD), bf16),
@@ -370,7 +373,7 @@
         ],
         compiler_params=params(),
         name="attend",
-    )(q_in, kv_in, table, resid)
+    )(q_in, kv_in, table, swapped)
 
 
 def attn_left_kernel(scale, own_rows, gain, kv, out):
@@ -474,7 +477,7 @@
             jax.ShapeDtypeStruct((feats, parts * feats), bf16),
             jax.ShapeDtypeStruct((1, rows), f32),
         ],
-        compiler_params=params(WIDE),
+        compiler_params=params(),
         name="hessian",
     )(place, left_a, cols_a, gain_a, ffn_rows, gain_row, total, cols_f, gain_f)
 
@@ -491,22 +494,20 @@
     place = jnp.stack([x_pos * nz + zl_pos, seq_pos * nz])
     place = place.astype(jnp.int32)
 
-    resid = swap_x_seq(hidden[0])
-    docs = jnp.pad(segment_ids.astype(bf16), ((0, 13), (0, feats - rows)))
-    extra = swap_x_seq(jnp.concatenate([gain_attn, gain_ffn, docs]))
+    swapped = swap_x_seq(first_message(hidden[0], gain_attn, gain_ffn, segment_ids))
     half = HD // 2
     freq = rope_base ** (-(jnp.arange(half, dtype=f32) * 2.0 / HD))
     angle = jnp.arange(tokens, dtype=f32)[:, None] * freq[None, :]
     table = jnp.concatenate([jnp.cos(angle), jnp.sin(angle)], 1)
-    group = lax.all_gather(pile(resid, extra, table), ZL)
-    copies, gain_a, gain_f = attn_copies(group, nx)
+    group = lax.all_gather(swapped, ZL)
+    copies, gain_a, gain_f = attn_copies(group, nx, table, place)
     attn_rows = lax.all_gather(take_after(hidden[0], gain_a), "seq")
     attn_cols = lax.all_to_all(copies, "x", 0, 0)
 
     message = project(attn_cols, gain_a, w_query, w_key, w_value, attn_rows)
     arrived = lax.all_to_all(lax.all_to_all(message, "x", 0, 0), "seq", 0, 0)
-    kv = lax.all_to_all(kv_sum(width, arrived, extra, 2 * nx), ("x", "zb"), 0, 0)
-    copies, section_out = attend(arrived, kv, table, resid, nz)
+    kv = lax.all_to_all(kv_sum(width, arrived, swapped, 2 * nx), ("x", "zb"), 0, 0)
+    copies, section_out = attend(arrived, kv, table, swapped, nz)
     left_a = attn_left(scale, attn_rows, gain_attn, kv)
 
     out_rows = swap_x_seq(section_out)

time: 238 us -> 236 us (level)
  blocking collectives: 125 us -> 149 us
  starting transfers between devices: 70.9 us -> 47.3 us
  waiting for transfers between devices: 14.6 us -> 12.2 us
    all_to_all x1, starting transfers between devices: 32.5 us -> 18.5 us  [on_device(): attn_cols = lax.all_to_all(copies, 'x', 0, 0)]
    all_gather x1, blocking collectives: 21.1 us -> 28.9 us  [on_device(): group = lax.all_gather(swapped, ZL)]
    all_to_all x1, starting transfers between devices: 10.4 us -> 3.48 us  [on_device(): group = lax.all_to_all(copies, ZL, 0, 0)]
    all_to_all x2, blocking collectives: 45.4 us -> 50.4 us  [on_device(): arrived = lax.all_to_all(lax.all_to_all(message, 'x', 0, 0), 'seq', 0, 0)]
    all_gather x1, blocking collectives: 16 us -> 20.8 us  [on_device(): ffn_rows = lax.all_gather(message, 'seq')]
    all_gather x1, blocking collectives: 24.4 us -> 29.1 us  [on_device(): attn_rows = lax.all_gather(take_after(hidden[0], gain_a), 'seq')]
    ppermute x1, starting transfers between devices: 20.2 us -> 16.4 us  [on_device(): lax.ppermute(passed, 'phase', [(p, (p + 1) % count) for p in range(count)])]
  transfers between devices with their start and end apart: 7 -> 6, of which waited for: 1 -> 1; matrix products, arithmetic and copies ran while one was open for 1% -> 1% of each run, Pallas kernels for 0% -> 1%
where the time goes in v11:
time: 236 us; the launch traced here: 235 us
  blocking collectives  149 us (63%)
  starting transfers between devices  47.3 us (20%)
  Pallas kernels  22.3 us (9%)
  waiting for transfers between devices  12.2 us (5%)
    all_to_all x2, blocking collectives, on_device(): arrived = lax.all_to_all(lax.all_to_all(message, 'x', 0, 0), 'seq', 0, 0)  50.4 us
    all_gather x1, blocking collectives, on_device(): attn_rows = lax.all_gather(take_after(hidden[0], gain_a), 'seq')  29.1 us
    all_gather x1, blocking collectives, on_device(): group = lax.all_gather(swapped, ZL)  28.9 us
    all_gather x1, blocking collectives, on_device(): ffn_rows = lax.all_gather(message, 'seq')  20.8 us
    all_to_all x1, starting transfers between devices, on_device(): attn_cols = lax.all_to_all(copies, 'x', 0, 0)  18.5 us
    ppermute x1, starting transfers between devices, on_device(): lax.ppermute(passed, 'phase', [(p, (p + 1) % count) for p in range(count)])  16.4 us
    all_to_all x1, waiting for transfers between devices, on_device(): group = lax.all_to_all(copies, ZL, 0, 0)  12.2 us
    all_to_all x1, blocking collectives, on_device(): lax.all_to_all(kv_sum(width, arrived, swapped, 2 * nx), ('x', 'zb'), 0, 0)  9.84 us
  transfers between devices with their start and end apart: 6, of which 1 were waited for; matrix products, arithmetic and copies ran while one was open for 1% of the time, Pallas kernels for 1%

profile of v11, /device:TPU:1, one launch (start us, length us, event | category | flops | bytes accessed | tf_op | source)
XLA Modules:
  0.0 234.7 jit_solution(1763613247210369057)
XLA Ops:
  0.6 1.6 first_message.1
  2.2 1.6 collective-permute-start
  3.8 1.0 fusion.1
  5.0 28.9 %all-gather = bf16[576,512]{1,0:T(8,128)(2,1)S(1)} all-gather(bf16[144,512]{1,0:T(8,128)(2,1)S(1)} %collective-permute-done.docs.resid), channel_id=2, replica_groups=mesh['phase'=8,'x'=4,'za'=2,'zb'=2,'seq'=4] {'za','zb'}, dimensions={0}, use_global_device_ids=true | all-gather | bytes 737280 | tf_op jit(solution)/shard_map/all_gather | solution.py:502
  33.9 1.8 attn_copies.1
  35.8 18.5 %all-to-all-start = ((bf16[4,4,128,512]{3,2,1,0:T(8,128)(2,1)}), bf16[4,4,128,512]{3,2,1,0:T(8,128)(2,1)S(1)}, u32[]{:S(2)}, u32[]{:S(2)}) async-start(bf16[4,4,128,512]{3,2,1,0:T(8,128)(2,1)} %get-tuple-element.12), calls=%async_computation | async-start | bytes 4194304 | tf_op jit(solution)/shard_map/all_to_all | solution.py:505
  54.3 1.6 take_after.1
  55.8 29.1 %all-gather.1 = bf16[512,512]{1,0:T(8,128)(2,1)} all-gather(bf16[128,512]{1,0:T(8,128)(2,1)} %take_after.1), channel_id=3, replica_groups=mesh['phase'=8,'x'=4,'za'=2,'zb'=2,'seq'=4] {'seq'}, dimensions={0}, use_global_device_ids=true | all-gather | bytes 655360 | tf_op jit(solution)/shard_map/all_gather | solution.py:504
  84.9 1.3 copy-done
  86.3 5.7 %project.1 = bf16[4,656,128]{2,1,0:T(8,128)(2,1)} custom-call(bf16[4,4,128,512]{3,2,1,0:T(8,128)(2,1)} %copy-done, f32[4,1,512]{2,1,0:T(1,128)} %get-tuple-element.13.after.gain.gain_a, bf16[1,2048,512]{2,1,0:T(8,128)(2,1)} %wq.1, bf16[1,64,2048]{2,1,0:T(8,128)(2,1)} %bitcast.18, bf16[1,64,2048]{2,1,0:T(8,128)(2,1)} %bitcast.19, bf16[4,128,512]{2,1,0:T(8,128)(2,1)} %bitcast.13), custom_call_target="tpu_custom_call" | custom-call | tf_op jit(solution)/shard_map/project/pallas_call | solution.py:73
  92.0 11.8 %all_to_all.30 = bf16[4,656,128]{2,1,0:T(8,128)(2,1)S(1)} all-to-all(bf16[4,656,128]{2,1,0:T(8,128)(2,1)} %project.1), channel_id=1, replica_groups=mesh['phase'=8,'x'=4,'za'=2,'zb'=2,'seq'=4] {'x'}, dimensions={0} | all-to-all | bytes 1343488 | tf_op jit(solution)/shard_map/all_to_all | solution.py:508
  103.8 38.6 %all_to_all.31.arrived.q_in = bf16[4,656,128]{2,1,0:T(8,128)(2,1)S(1)} all-to-all(bf16[4,656,128]{2,1,0:T(8,128)(2,1)S(1)} %all_to_all.30), channel_id=1, replica_groups=mesh['phase'=8,'x'=4,'za'=2,'zb'=2,'seq'=4] {'seq'}, dimensions={0} | all-to-all | bytes 1343488 | tf_op jit(solution)/shard_map/all_to_all | solution.py:508
  142.4 0.8 kv_sum.1
  143.2 9.8 %all_to_all.32.kv_in.kv = bf16[8,144,128]{2,1,0:T(8,128)(2,1)S(1)} all-to-all(bf16[8,144,128]{2,1,0:T(8,128)(2,1)} %kv_sum.1), channel_id=1, replica_groups=mesh['phase'=8,'x'=4,'za'=2,'zb'=2,'seq'=4] {'x','zb'}, dimensions={0} | all-to-all | bytes 589824 | tf_op jit(solution)/shard_map/all_to_all | solution.py:509
  153.0 3.2 %attend.1 = (bf16[4,144,512]{2,1,0:T(8,128)(2,1)}, bf16[128,512]{1,0:T(8,128)(2,1)}) custom-call(bf16[4,656,128]{2,1,0:T(8,128)(2,1)S(1)} %all_to_all.31.arrived.q_in, bf16[8,144,128]{2,1,0:T(8,128)(2,1)S(1)} %all_to_all.32.kv_in.kv, f32[512,128]{1,0:T(8,128)S(1)} %pad_maximum_fusion.table, bf16[144,512]{1,0:T(8,128)(2,1)S(1)} %collective-permute-done.docs.resid), custom_call_target="tpu_custom_call" | custom-call | tf_op jit(solution)/shard_map/attend/pallas_call | solution.py:357
  156.2 3.5 %all-to-all-start.4 = ((bf16[4,144,512]{2,1,0:T(8,128)(2,1)}), bf16[4,144,512]{2,1,0:T(8,128)(2,1)S(1)}, u32[]{:S(2)}, u32[]{:S(2)}) async-start(bf16[4,144,512]{2,1,0:T(8,128)(2,1)} %get-tuple-element.14), calls=%async_computation.4 | async-start | bytes 1179648 | tf_op jit(solution)/shard_map/all_to_all | solution.py:514
  159.6 1.6 collective-permute-start.1
  161.6 12.2 %all-to-all-done.4.group = bf16[4,144,512]{2,1,0:T(8,128)(2,1)S(1)} async-done(((bf16[4,144,512]{2,1,0:T(8,128)(2,1)}), bf16[4,144,512]{2,1,0:T(8,128)(2,1)S(1)}, u32[]{:S(2)}, u32[]{:S(2)}) %all-to-all-start.4) | async-done | bytes 589856 | tf_op jit(solution)/shard_map/all_to_all | solution.py:514
  173.8 2.0 ffn_copies.1
  175.8 5.8 %all-to-all-start.5 = ((bf16[4,4,128,512]{3,2,1,0:T(8,128)(2,1)}), bf16[4,4,128,512]{3,2,1,0:T(8,128)(2,1)}, u32[]{:S(2)}, u32[]{:S(2)}) async-start(bf16[4,4,128,512]{3,2,1,0:T(8,128)(2,1)} %get-tuple-element.17), calls=%async_computation.5 | async-start | bytes 4194304 | tf_op jit(solution)/shard_map/all_to_all | solution.py:516
  181.6 20.8 %all-gather.2 = bf16[576,512]{1,0:T(8,128)(2,1)S(1)} all-gather(bf16[144,512]{1,0:T(8,128)(2,1)S(1)} %copy-done.7), channel_id=4, replica_groups=mesh['phase'=8,'x'=4,'za'=2,'zb'=2,'seq'=4] {'seq'}, dimensions={0}, use_global_device_ids=true | all-gather | bytes 737280 | tf_op jit(solution)/shard_map/all_gather | solution.py:517
  202.5 16.4 %collective-permute-start.2 = (bf16[1,128,512]{2,1,0:T(8,128)(2,1)S(1)}, bf16[1,128,512]{2,1,0:T(8,128)(2,1)S(1)}, u32[]{:S(2)}, u32[]{:S(2)}) collective-permute-start(bf16[1,128,512]{2,1,0:T(8,128)(2,1)S(1)} %constant_dynamic-slice_fusion), channel_id=1, source_target_pairs={{0,64},{64,128},{128,192},{192,256},{256,320},{320,384},{384,448},... | collective-permute-start | bytes 393224 | tf_op jit(solution)/shard_map/ppermute | solution.py:522
  218.9 9.8 %all-gather.4.total = f32[4,1,128]{2,1,0:T(1,128)S(1)} all-gather(f32[1,1,128]{2,1,0:T(1,128)S(1)} %bitcast.20), channel_id=5, replica_groups=mesh['phase'=8,'x'=4,'za'=2,'zb'=2,'seq'=4] {'x'}, dimensions={0}, use_global_device_ids=true | all-gather | bytes 2560 | tf_op jit(solution)/shard_map/all_gather | solution.py:519
  228.8 5.3 %hessian.1 = (bf16[512,2048]{1,0:T(8,128)(2,1)}, f32[1,128]{1,0:T(1,128)}) custom-call(s32[2]{0:T(128)S(1)} %pad_add_fusion.place, bf16[512,512]{1,0:T(8,128)(2,1)S(1)} %attn_left.1.after.left_a, bf16[4,4,128,512]{3,2,1,0:T(8,128)(2,1)S(1)} %copy-done.1, f32[4,1,512]{2,1,0:T(1,128)S(1)} %copy-done.3, bf16[4,144,512]{2,1,0:T(8,128)(2,1)S(1)} %bitcast.12, ...), custom_call_target="tpu_custom_call" | custom-call | tf_op jit(solution)/shard_map/hessian/pallas_call | solution.py:455
  (28 shorter events, 1.3 us)
Async XLA Ops:
  2.2 2.8 %collective-permute-start = (bf16[144,512]{1,0:T(8,128)(2,1)}, bf16[144,512]{1,0:T(8,128)(2,1)S(1)}, u32[]{:S(2)}, u32[]{:S(2)}) collective-permute-start(bf16[144,512]{1,0:T(8,128)(2,1)} %first_message.1), channel_id=1, source_target_pairs={{0,0},{1,16},{2,32},{3,48},{4,4},{5,20},{6,36},{7,52},{8,8},{9,24}... | collective-permute-start | bytes 442376 | tf_op jit(solution)/shard_map/ppermute | solution.py:31
  35.8 49.2 %all-to-all-start = ((bf16[4,4,128,512]{3,2,1,0:T(8,128)(2,1)}), bf16[4,4,128,512]{3,2,1,0:T(8,128)(2,1)S(1)}, u32[]{:S(2)}, u32[]{:S(2)}) async-start(bf16[4,4,128,512]{3,2,1,0:T(8,128)(2,1)} %get-tuple-element.12), calls=%async_computation | async-start | bytes 4194304 | tf_op jit(solution)/shard_map/all_to_all | solution.py:505
  84.9 1.3 copy-start
  142.4 18.8 %copy-start.2 = (bf16[512,512]{1,0:T(8,128)(2,1)S(1)}, bf16[512,512]{1,0:T(8,128)(2,1)}, u32[]{:S(2)}) copy-start(bf16[512,512]{1,0:T(8,128)(2,1)} %all-gather.1) | copy-start | bytes 1572868
  142.4 18.8 %copy-start.5 = (bf16[1,512]{1,0:T(2,128)(2,1)S(1)}, bf16[1,512]{1,0:T(2,128)(2,1)}, u32[]{:S(2)}) copy-start(bf16[1,512]{1,0:T(2,128)(2,1)} %gain.1) | copy-start | bytes 3076
  156.2 17.6 %all-to-all-start.4 = ((bf16[4,144,512]{2,1,0:T(8,128)(2,1)}), bf16[4,144,512]{2,1,0:T(8,128)(2,1)S(1)}, u32[]{:S(2)}, u32[]{:S(2)}) async-start(bf16[4,144,512]{2,1,0:T(8,128)(2,1)} %get-tuple-element.14), calls=%async_computation.4 | async-start | bytes 1179648 | tf_op jit(solution)/shard_map/all_to_all | solution.py:514
  159.6 1.9 collective-permute-start.1
  175.8 5.8 %copy-start.7 = (bf16[144,512]{1,0:T(8,128)(2,1)S(1)}, bf16[144,512]{1,0:T(8,128)(2,1)}, u32[]{:S(2)}) copy-start(bf16[144,512]{1,0:T(8,128)(2,1)} %get-tuple-element.16) | copy-start | bytes 442372
  175.8 53.0 %copy-start.1 = (bf16[4,4,128,512]{3,2,1,0:T(8,128)(2,1)S(1)}, bf16[4,4,128,512]{3,2,1,0:T(8,128)(2,1)}, u32[]{:S(2)}) copy-start(bf16[4,4,128,512]{3,2,1,0:T(8,128)(2,1)} %copy-done) | copy-start | bytes 6291460
  175.8 53.0 %copy-start.3 = (f32[4,1,512]{2,1,0:T(1,128)S(1)}, f32[4,1,512]{2,1,0:T(1,128)}, u32[]{:S(2)}) copy-start(f32[4,1,512]{2,1,0:T(1,128)} %get-tuple-element.13.after.gain.gain_a) | copy-start | bytes 24580
  175.8 53.0 %copy-start.4 = (f32[4,1,512]{2,1,0:T(1,128)S(1)}, f32[4,1,512]{2,1,0:T(1,128)}, u32[]{:S(2)}) copy-start(f32[4,1,512]{2,1,0:T(1,128)} %get-tuple-element.18.gain_f) | copy-start | bytes 24580
  175.8 53.0 %copy-start.6 = (bf16[1,512]{1,0:T(2,128)(2,1)S(1)}, bf16[1,512]{1,0:T(2,128)(2,1)}, u32[]{:S(2)}) copy-start(bf16[1,512]{1,0:T(2,128)(2,1)} %gain_row.1) | copy-start | bytes 3076
  175.8 53.0 %all-to-all-start.5 = ((bf16[4,4,128,512]{3,2,1,0:T(8,128)(2,1)}), bf16[4,4,128,512]{3,2,1,0:T(8,128)(2,1)}, u32[]{:S(2)}, u32[]{:S(2)}) async-start(bf16[4,4,128,512]{3,2,1,0:T(8,128)(2,1)} %get-tuple-element.17), calls=%async_computation.5 | async-start | bytes 4194304 | tf_op jit(solution)/shard_map/all_to_all | solution.py:516
  202.5 26.3 %collective-permute-start.2 = (bf16[1,128,512]{2,1,0:T(8,128)(2,1)S(1)}, bf16[1,128,512]{2,1,0:T(8,128)(2,1)S(1)}, u32[]{:S(2)}, u32[]{:S(2)}) collective-permute-start(bf16[1,128,512]{2,1,0:T(8,128)(2,1)S(1)} %constant_dynamic-slice_fusion), channel_id=1, source_target_pairs={{0,64},{64,128},{128,192},{192,256},{256,320},{320,384},{384,448},... | collective-permute-start | bytes 393224 | tf_op jit(solution)/shard_map/ppermute | solution.py:522

commit v12 on v11

--- a/solution.py
+++ b/solution.py
@@ -17,7 +17,7 @@
 bf16 = jnp.bfloat16
 LIMIT = 24 * 1024 * 1024
 WIDE = 57 * 1024 * 1024
-PROJECT = 55 * 1024 * 1024
+PROJECT = 57 * 1024 * 1024
 
 
 def swap_x_seq(value):
@@ -31,15 +31,17 @@
     return lax.ppermute(value, GROUP, pairs)
 
 
-def project_kernel(cols, gain, wq, wk, wv, after, out, q_acc, kv_acc, squares):
+def project_kernel(cols, gain, wq, wk, wv, after, out, q_acc, kv_acc, squares, left):
     step = pl.program_id(0)
-    blocks, rows, feats = cols.shape
-    raw = cols[...].reshape(blocks * rows, feats).astype(f32)
-    left = (raw * gain[...]).astype(bf16)
-    part = jnp.sum(raw * raw, axis=1, keepdims=True)
+    blocks, parts, rows, feats = cols.shape
+    part = jnp.zeros((blocks * rows, 1), f32)
+    for z in range(parts):
+        raw = cols[:, z].reshape(blocks * rows, feats).astype(f32)
+        left[:, pl.ds(z * feats, feats)] = (raw * gain[z]).astype(bf16)
+        part += jnp.sum(raw * raw, axis=1, keepdims=True)
     kv_w = jnp.concatenate([wk[...], wv[...]], 0)
-    kv = lax.dot_general(left, kv_w, (((1,), (1,)), ((), ())), preferred_element_type=f32)
-    q = jnp.dot(left, wq[...], preferred_element_type=f32)
+    kv = lax.dot_general(left[...], kv_w, (((1,), (1,)), ((), ())), preferred_element_type=f32)
+    q = jnp.dot(left[...], wq[...], preferred_element_type=f32)
 
     @pl.when(step == 0)
     def _():
@@ -69,14 +71,15 @@
     blocks, parts, rows, feats = cols.shape
     q_width, kv_width = w_query.shape[2], 2 * w_key.shape[2]
     heads = q_width // HD
-    kv_spec = pl.BlockSpec((None, w_key.shape[2], feats), lambda z: (0, 0, z))
+    pair = 2
+    kv_spec = pl.BlockSpec((None, w_key.shape[2], pair * feats), lambda z: (0, 0, z))
     return pl.pallas_call(
         project_kernel,
-        grid=(parts,),
+        grid=(parts // pair,),
         in_specs=[
-            pl.BlockSpec((blocks, None, rows, feats), lambda z: (0, z, 0, 0)),
-            pl.BlockSpec((None, 1, feats), lambda z: (z, 0, 0)),
-            pl.BlockSpec((None, feats, q_width), lambda z: (0, z, 0)),
+            pl.BlockSpec((blocks, pair, rows, feats), lambda z: (0, z, 0, 0)),
+            pl.BlockSpec((pair, 1, feats), lambda z: (z, 0, 0)),
+            pl.BlockSpec((None, pair * feats, q_width), lambda z: (0, z, 0)),
             kv_spec,
             kv_spec,
             pl.BlockSpec(memory_space=pl.ANY),
@@ -87,6 +90,7 @@
             pltpu.VMEM((blocks * rows, q_width), f32),
             pltpu.VMEM((blocks * rows, kv_width), f32),
             pltpu.VMEM((blocks * rows, 1), f32),
+            pltpu.VMEM((blocks * rows, pair * feats), bf16),
         ],
         compiler_params=params(PROJECT),
         name="project",
@@ -167,7 +171,7 @@
         in_specs=[fixed(value.shape), pl.BlockSpec(memory_space=pl.ANY)],
         out_specs=fixed(value.shape),
         out_shape=pltpu.HBM(value.shape, value.dtype),
-        compiler_params=params(WIDE),
+        compiler_params=params(),
         name="take_after",
     )(value, after)
 
@@ -401,7 +405,7 @@
 
 def hessian_kernel(
     scale, width, place, left_a, cols_a, gain_a, ffn_rows, gain_row, total, cols_f, gain_f,
-    out, diagonal, left_f,
+    passed, out, diagonal, passed_out, left_f,
 ):
     blocks, rows, feats = cols_a.shape
     row, col = place[0], place[1] + pl.program_id(0)
@@ -417,6 +421,7 @@
             mine = ffn_rows[k, pl.ds(0, rows), part].astype(f32) * gain_row[:, part].astype(f32)
             squares += jnp.sum(mine * mine * weight, axis=0, keepdims=True)
         diagonal[...] = squares
+        passed_out[...] = passed[...]
 
     def product(left, cols, gain):
         right = cols[...].reshape(blocks * rows, feats)
@@ -440,7 +445,7 @@
 
 
 def hessian(
-    scale, width, place, left_a, cols_a, gain_a, ffn_rows, gain_row, total, cols_f, gain_f
+    scale, width, place, left_a, cols_a, gain_a, ffn_rows, gain_row, total, cols_f, gain_f, passed
 ):
     blocks, parts, rows, feats = cols_a.shape
     tokens = blocks * rows
@@ -466,20 +471,23 @@
                 fixed(total.shape),
                 pl.BlockSpec((blocks, None, rows, feats), lambda z, at: (0, lower_at(z, at), 0, 0)),
                 gain,
+                fixed(passed.shape),
             ],
             out_specs=[
                 pl.BlockSpec((feats, feats), lambda z, at: (0, z)),
                 fixed((1, rows)),
+                fixed(passed.shape),
             ],
             scratch_shapes=[pltpu.VMEM((feats, tokens), bf16)],
         ),
         out_shape=[
             jax.ShapeDtypeStruct((feats, parts * feats), bf16),
             jax.ShapeDtypeStruct((1, rows), f32),
+            jax.ShapeDtypeStruct(passed.shape, bf16),
         ],
         compiler_params=params(),
         name="hessian",
-    )(place, left_a, cols_a, gain_a, ffn_rows, gain_row, total, cols_f, gain_f)
+    )(place, left_a, cols_a, gain_a, ffn_rows, gain_row, total, cols_f, gain_f, passed)
 
 
 def on_device(hidden, segment_ids, gain_attn, gain_ffn, w_query, w_key, w_value):
@@ -520,8 +528,19 @@
     count = lax.axis_size("phase")
     passed = lax.dynamic_slice_in_dim(ffn_rows[:, :rows], seq_pos, 1, 0)
     passed = lax.ppermute(passed, "phase", [(p, (p + 1) % count) for p in range(count)])
-    hessians, ffn_diagonal = hessian(
-        scale, width, place, left_a, attn_cols, gain_a, ffn_rows, gain_ffn, total, ffn_cols, gain_f
+    hessians, ffn_diagonal, passed = hessian(
+        scale,
+        width,
+        place,
+        left_a,
+        attn_cols,
+        gain_a,
+        ffn_rows,
+        gain_ffn,
+        total,
+        ffn_cols,
+        gain_f,
+        passed,
     )
     return (passed, hessians[None], ffn_diagonal)
 

time: 236 us -> 235 us (level)
  blocking collectives: 149 us -> 143 us
  starting transfers between devices: 47.3 us -> 51.7 us
    ppermute x1, starting transfers between devices: 16.4 us -> 21 us  [on_device(): lax.ppermute(passed, 'phase', [(p, (p + 1) % count) for p in range(count)])]
    all_gather x1, blocking collectives: 20.8 us -> 17.1 us  [on_device(): ffn_rows = lax.all_gather(message, 'seq')]
  transfers between devices with their start and end apart: 6 -> 6, of which waited for: 1 -> 1; matrix products, arithmetic and copies ran while one was open for 1% -> 1% of each run, Pallas kernels for 1% -> 0%
where the time goes in v12:
time: 235 us; the launch traced here: 232 us
  blocking collectives  143 us (61%)
  starting transfers between devices  51.7 us (22%)
  Pallas kernels  20.5 us (9%)
  waiting for transfers between devices  12.6 us (5%)
    all_to_all x2, blocking collectives, on_device(): arrived = lax.all_to_all(lax.all_to_all(message, 'x', 0, 0), 'seq', 0, 0)  51.2 us
    all_gather x1, blocking collectives, on_device(): attn_rows = lax.all_gather(take_after(hidden[0], gain_a), 'seq')  29 us
    all_gather x1, blocking collectives, on_device(): group = lax.all_gather(swapped, ZL)  28.9 us
    ppermute x1, starting transfers between devices, on_device(): lax.ppermute(passed, 'phase', [(p, (p + 1) % count) for p in range(count)])  21 us
    all_to_all x1, starting transfers between devices, on_device(): attn_cols = lax.all_to_all(copies, 'x', 0, 0)  18.6 us
    all_gather x1, blocking collectives, on_device(): ffn_rows = lax.all_gather(message, 'seq')  17.1 us
    all_to_all x1, waiting for transfers between devices, on_device(): group = lax.all_to_all(copies, ZL, 0, 0)  12.6 us
    all_to_all x1, blocking collectives, on_device(): lax.all_to_all(kv_sum(width, arrived, swapped, 2 * nx), ('x', 'zb'), 0, 0)  9.84 us
  transfers between devices with their start and end apart: 6, of which 1 were waited for; matrix products, arithmetic and copies ran while one was open for 1% of the time, Pallas kernels for 0%

profile of v12, /device:TPU:1, one launch (start us, length us, event | category | flops | bytes accessed | tf_op | source)
XLA Modules:
  0.0 231.7 jit_solution(16548087841982313525)
XLA Ops:
  0.6 1.6 first_message.1
  2.2 1.6 collective-permute-start
  3.8 1.0 fusion.1
  5.0 28.9 %all-gather = bf16[576,512]{1,0:T(8,128)(2,1)S(1)} all-gather(bf16[144,512]{1,0:T(8,128)(2,1)S(1)} %collective-permute-done.docs.resid), channel_id=2, replica_groups=mesh['phase'=8,'x'=4,'za'=2,'zb'=2,'seq'=4] {'za','zb'}, dimensions={0}, use_global_device_ids=true | all-gather | bytes 737280 | tf_op jit(solution)/shard_map/all_gather | solution.py:510
  33.9 1.8 attn_copies.1
  35.8 18.6 %all-to-all-start = ((bf16[4,4,128,512]{3,2,1,0:T(8,128)(2,1)}), bf16[4,4,128,512]{3,2,1,0:T(8,128)(2,1)S(1)}, u32[]{:S(2)}, u32[]{:S(2)}) async-start(bf16[4,4,128,512]{3,2,1,0:T(8,128)(2,1)} %get-tuple-element.14), calls=%async_computation | async-start | bytes 4194304 | tf_op jit(solution)/shard_map/all_to_all | solution.py:513
  54.4 0.7 take_after.1
  55.1 29.0 %all-gather.1 = bf16[512,512]{1,0:T(8,128)(2,1)} all-gather(bf16[128,512]{1,0:T(8,128)(2,1)} %take_after.1), channel_id=3, replica_groups=mesh['phase'=8,'x'=4,'za'=2,'zb'=2,'seq'=4] {'seq'}, dimensions={0}, use_global_device_ids=true | all-gather | bytes 655360 | tf_op jit(solution)/shard_map/all_gather | solution.py:512
  84.1 1.3 copy-done
  85.4 4.9 %project.1 = bf16[4,656,128]{2,1,0:T(8,128)(2,1)} custom-call(bf16[4,4,128,512]{3,2,1,0:T(8,128)(2,1)} %copy-done, f32[4,1,512]{2,1,0:T(1,128)} %get-tuple-element.13.after.gain.gain_a, bf16[1,2048,512]{2,1,0:T(8,128)(2,1)} %wq.1, bf16[1,64,2048]{2,1,0:T(8,128)(2,1)} %bitcast.18, bf16[1,64,2048]{2,1,0:T(8,128)(2,1)} %bitcast.19, bf16[4,128,512]{2,1,0:T(8,128)(2,1)} %bitcast.13), custom_call_target="tpu_custom_call" | custom-call | tf_op jit(solution)/shard_map/project/pallas_call | solution.py:76
  90.3 11.8 %all_to_all.30 = bf16[4,656,128]{2,1,0:T(8,128)(2,1)S(1)} all-to-all(bf16[4,656,128]{2,1,0:T(8,128)(2,1)} %project.1), channel_id=1, replica_groups=mesh['phase'=8,'x'=4,'za'=2,'zb'=2,'seq'=4] {'x'}, dimensions={0} | all-to-all | bytes 1343488 | tf_op jit(solution)/shard_map/all_to_all | solution.py:516
  102.1 39.4 %all_to_all.31.arrived.q_in = bf16[4,656,128]{2,1,0:T(8,128)(2,1)S(1)} all-to-all(bf16[4,656,128]{2,1,0:T(8,128)(2,1)S(1)} %all_to_all.30), channel_id=1, replica_groups=mesh['phase'=8,'x'=4,'za'=2,'zb'=2,'seq'=4] {'seq'}, dimensions={0} | all-to-all | bytes 1343488 | tf_op jit(solution)/shard_map/all_to_all | solution.py:516
  141.5 0.8 kv_sum.1
  142.3 9.8 %all_to_all.32.kv.kv_in = bf16[8,144,128]{2,1,0:T(8,128)(2,1)S(1)} all-to-all(bf16[8,144,128]{2,1,0:T(8,128)(2,1)} %kv_sum.1), channel_id=1, replica_groups=mesh['phase'=8,'x'=4,'za'=2,'zb'=2,'seq'=4] {'x','zb'}, dimensions={0} | all-to-all | bytes 589824 | tf_op jit(solution)/shard_map/all_to_all | solution.py:517
  152.1 3.2 %attend.1 = (bf16[4,144,512]{2,1,0:T(8,128)(2,1)}, bf16[128,512]{1,0:T(8,128)(2,1)}) custom-call(bf16[4,656,128]{2,1,0:T(8,128)(2,1)S(1)} %all_to_all.31.arrived.q_in, bf16[8,144,128]{2,1,0:T(8,128)(2,1)S(1)} %all_to_all.32.kv.kv_in, f32[512,128]{1,0:T(8,128)S(1)} %pad_maximum_fusion.table, bf16[144,512]{1,0:T(8,128)(2,1)S(1)} %collective-permute-done.docs.resid), custom_call_target="tpu_custom_call" | custom-call | tf_op jit(solution)/shard_map/attend/pallas_call | solution.py:361
  155.3 3.5 %all-to-all-start.4 = ((bf16[4,144,512]{2,1,0:T(8,128)(2,1)}), bf16[4,144,512]{2,1,0:T(8,128)(2,1)S(1)}, u32[]{:S(2)}, u32[]{:S(2)}) async-start(bf16[4,144,512]{2,1,0:T(8,128)(2,1)} %get-tuple-element.15), calls=%async_computation.4 | async-start | bytes 1179648 | tf_op jit(solution)/shard_map/all_to_all | solution.py:522
  158.7 1.6 collective-permute-start.1
  160.7 12.6 %all-to-all-done.4.group = bf16[4,144,512]{2,1,0:T(8,128)(2,1)S(1)} async-done(((bf16[4,144,512]{2,1,0:T(8,128)(2,1)}), bf16[4,144,512]{2,1,0:T(8,128)(2,1)S(1)}, u32[]{:S(2)}, u32[]{:S(2)}) %all-to-all-start.4) | async-done | bytes 589856 | tf_op jit(solution)/shard_map/all_to_all | solution.py:522
  173.3 2.0 ffn_copies.1
  175.3 5.5 %all-to-all-start.5 = ((bf16[4,4,128,512]{3,2,1,0:T(8,128)(2,1)}), bf16[4,4,128,512]{3,2,1,0:T(8,128)(2,1)}, u32[]{:S(2)}, u32[]{:S(2)}) async-start(bf16[4,4,128,512]{3,2,1,0:T(8,128)(2,1)} %get-tuple-element.18), calls=%async_computation.5 | async-start | bytes 4194304 | tf_op jit(solution)/shard_map/all_to_all | solution.py:524
  180.8 17.1 %all-gather.2 = bf16[576,512]{1,0:T(8,128)(2,1)S(1)} all-gather(bf16[144,512]{1,0:T(8,128)(2,1)S(1)} %copy-done.9), channel_id=4, replica_groups=mesh['phase'=8,'x'=4,'za'=2,'zb'=2,'seq'=4] {'seq'}, dimensions={0}, use_global_device_ids=true | all-gather | bytes 737280 | tf_op jit(solution)/shard_map/all_gather | solution.py:525
  197.9 21.0 %collective-permute-start.2 = (bf16[1,128,512]{2,1,0:T(8,128)(2,1)S(1)}, bf16[1,128,512]{2,1,0:T(8,128)(2,1)S(1)}, u32[]{:S(2)}, u32[]{:S(2)}) collective-permute-start(bf16[1,128,512]{2,1,0:T(8,128)(2,1)S(1)} %constant_dynamic-slice_fusion), channel_id=1, source_target_pairs={{0,64},{64,128},{128,192},{192,256},{256,320},{320,384},{384,448},... | collective-permute-start | bytes 393224 | tf_op jit(solution)/shard_map/ppermute | solution.py:530
  218.9 7.5 %all-gather.4.total = f32[4,1,128]{2,1,0:T(1,128)S(1)} all-gather(f32[1,1,128]{2,1,0:T(1,128)S(1)} %bitcast.20), channel_id=5, replica_groups=mesh['phase'=8,'x'=4,'za'=2,'zb'=2,'seq'=4] {'x'}, dimensions={0}, use_global_device_ids=true | all-gather | bytes 2560 | tf_op jit(solution)/shard_map/all_gather | solution.py:527
  226.4 5.3 %hessian.1 = (bf16[512,2048]{1,0:T(8,128)(2,1)}, f32[1,128]{1,0:T(1,128)}, bf16[1,128,512]{2,1,0:T(8,128)(2,1)}) custom-call(s32[2]{0:T(128)S(1)} %pad_add_fusion.place, bf16[512,512]{1,0:T(8,128)(2,1)S(1)} %attn_left.1.after.left_a, bf16[4,4,128,512]{3,2,1,0:T(8,128)(2,1)S(1)} %copy-done.1, f32[4,1,512]{2,1,0:T(1,128)S(1)} %copy-done.5, ...), custom_call_target="tpu_custom_call" | custom-call | tf_op jit(solution)/shard_map/hessian/pallas_call | solution.py:460
  (31 shorter events, 0.7 us)
Async XLA Ops:
  2.2 2.8 %collective-permute-start = (bf16[144,512]{1,0:T(8,128)(2,1)}, bf16[144,512]{1,0:T(8,128)(2,1)S(1)}, u32[]{:S(2)}, u32[]{:S(2)}) collective-permute-start(bf16[144,512]{1,0:T(8,128)(2,1)} %first_message.1), channel_id=1, source_target_pairs={{0,0},{1,16},{2,32},{3,48},{4,4},{5,20},{6,36},{7,52},{8,8},{9,24}... | collective-permute-start | bytes 442376 | tf_op jit(solution)/shard_map/ppermute | solution.py:31
  35.8 18.6 %copy-start.3 = (bf16[1,128,512]{2,1,0:T(8,128)(2,1)S(1)}, bf16[1,128,512]{2,1,0:T(8,128)(2,1)}, u32[]{:S(2)}) copy-start(bf16[1,128,512]{2,1,0:T(8,128)(2,1)} %param.7) | copy-start | bytes 393220
  35.8 18.6 %copy-start.4 = (f32[4,1,512]{2,1,0:T(1,128)S(1)}, f32[4,1,512]{2,1,0:T(1,128)}, u32[]{:S(2)}) copy-start(f32[4,1,512]{2,1,0:T(1,128)} %get-tuple-element.13.after.gain.gain_a) | copy-start | bytes 24580
  35.8 48.3 %all-to-all-start = ((bf16[4,4,128,512]{3,2,1,0:T(8,128)(2,1)}), bf16[4,4,128,512]{3,2,1,0:T(8,128)(2,1)S(1)}, u32[]{:S(2)}, u32[]{:S(2)}) async-start(bf16[4,4,128,512]{3,2,1,0:T(8,128)(2,1)} %get-tuple-element.14), calls=%async_computation | async-start | bytes 4194304 | tf_op jit(solution)/shard_map/all_to_all | solution.py:513
  84.1 1.3 copy-start
  141.5 18.8 %copy-start.2 = (bf16[512,512]{1,0:T(8,128)(2,1)S(1)}, bf16[512,512]{1,0:T(8,128)(2,1)}, u32[]{:S(2)}) copy-start(bf16[512,512]{1,0:T(8,128)(2,1)} %all-gather.1) | copy-start | bytes 1572868
  141.5 18.8 %copy-start.8 = (bf16[1,512]{1,0:T(2,128)(2,1)S(1)}, bf16[1,512]{1,0:T(2,128)(2,1)}, u32[]{:S(2)}) copy-start(bf16[1,512]{1,0:T(2,128)(2,1)} %gain.1) | copy-start | bytes 3076
  155.3 18.0 %all-to-all-start.4 = ((bf16[4,144,512]{2,1,0:T(8,128)(2,1)}), bf16[4,144,512]{2,1,0:T(8,128)(2,1)S(1)}, u32[]{:S(2)}, u32[]{:S(2)}) async-start(bf16[4,144,512]{2,1,0:T(8,128)(2,1)} %get-tuple-element.15), calls=%async_computation.4 | async-start | bytes 1179648 | tf_op jit(solution)/shard_map/all_to_all | solution.py:522
  158.7 1.9 collective-permute-start.1
  175.2 5.5 %copy-start.9 = (bf16[144,512]{1,0:T(8,128)(2,1)S(1)}, bf16[144,512]{1,0:T(8,128)(2,1)}, u32[]{:S(2)}) copy-start(bf16[144,512]{1,0:T(8,128)(2,1)} %get-tuple-element.17) | copy-start | bytes 442372
  175.2 51.1 %copy-start.1 = (bf16[4,4,128,512]{3,2,1,0:T(8,128)(2,1)S(1)}, bf16[4,4,128,512]{3,2,1,0:T(8,128)(2,1)}, u32[]{:S(2)}) copy-start(bf16[4,4,128,512]{3,2,1,0:T(8,128)(2,1)} %copy-done) | copy-start | bytes 6291460
  175.2 51.1 %copy-start.5 = (f32[4,1,512]{2,1,0:T(1,128)S(1)}, f32[4,1,512]{2,1,0:T(1,128)}, u32[]{:S(2)}) copy-start(f32[4,1,512]{2,1,0:T(1,128)} %get-tuple-element.13.after.gain.gain_a) | copy-start | bytes 24580
  175.3 51.1 %copy-start.6 = (bf16[1,512]{1,0:T(2,128)(2,1)S(1)}, bf16[1,512]{1,0:T(2,128)(2,1)}, u32[]{:S(2)}) copy-start(bf16[1,512]{1,0:T(2,128)(2,1)} %gain_row.1) | copy-start | bytes 3076
  175.3 51.1 %copy-start.7 = (f32[4,1,512]{2,1,0:T(1,128)S(1)}, f32[4,1,512]{2,1,0:T(1,128)}, u32[]{:S(2)}) copy-start(f32[4,1,512]{2,1,0:T(1,128)} %get-tuple-element.19.gain_f) | copy-start | bytes 24580
  175.3 51.1 %all-to-all-start.5 = ((bf16[4,4,128,512]{3,2,1,0:T(8,128)(2,1)}), bf16[4,4,128,512]{3,2,1,0:T(8,128)(2,1)}, u32[]{:S(2)}, u32[]{:S(2)}) async-start(bf16[4,4,128,512]{3,2,1,0:T(8,128)(2,1)} %get-tuple-element.18), calls=%async_computation.5 | async-start | bytes 4194304 | tf_op jit(solution)/shard_map/all_to_all | solution.py:524
  197.9 28.5 %collective-permute-start.2 = (bf16[1,128,512]{2,1,0:T(8,128)(2,1)S(1)}, bf16[1,128,512]{2,1,0:T(8,128)(2,1)S(1)}, u32[]{:S(2)}, u32[]{:S(2)}) collective-permute-start(bf16[1,128,512]{2,1,0:T(8,128)(2,1)S(1)} %constant_dynamic-slice_fusion), channel_id=1, source_target_pairs={{0,64},{64,128},{128,192},{192,256},{256,320},{320,384},{384,448},... | collective-permute-start | bytes 393224 | tf_op jit(solution)/shard_map/ppermute | solution.py:530

commit v13 on v12

--- a/solution.py
+++ b/solution.py
@@ -31,7 +31,7 @@
     return lax.ppermute(value, GROUP, pairs)
 
 
-def project_kernel(cols, gain, wq, wk, wv, after, out, q_acc, kv_acc, squares, left):
+def project_kernel(cols, gain, wq, wk, wv, out, q_acc, kv_acc, squares, left):
     step = pl.program_id(0)
     blocks, parts, rows, feats = cols.shape
     part = jnp.zeros((blocks * rows, 1), f32)
@@ -67,7 +67,7 @@
                 out[k, pl.ds(h * rows, rows), :] = q_acc[block, pl.ds(h * HD, HD)].astype(bf16)
 
 
-def project(cols, gain, w_query, w_key, w_value, after):
+def project(cols, gain, w_query, w_key, w_value):
     blocks, parts, rows, feats = cols.shape
     q_width, kv_width = w_query.shape[2], 2 * w_key.shape[2]
     heads = q_width // HD
@@ -82,7 +82,6 @@
             pl.BlockSpec((None, pair * feats, q_width), lambda z: (0, z, 0)),
             kv_spec,
             kv_spec,
-            pl.BlockSpec(memory_space=pl.ANY),
         ],
         out_specs=fixed((blocks, (heads + 1) * rows + 16, HD)),
         out_shape=pltpu.HBM((blocks, (heads + 1) * rows + 16, HD), bf16),
@@ -94,7 +93,7 @@
         ],
         compiler_params=params(PROJECT),
         name="project",
-    )(cols, gain, w_query, w_key.swapaxes(1, 2), w_value.swapaxes(1, 2), after)
+    )(cols, gain, w_query, w_key.swapaxes(1, 2), w_value.swapaxes(1, 2))
 
 
 def fixed(shape):
@@ -126,7 +125,7 @@
     return jnp.concatenate([row.astype(f32) for row in rows]).astype(bf16)
 
 
-def attn_copies_kernel(group, table, place, copies, gain_a, gain_f):
+def attn_copies_kernel(group, own_rows, copies, gain_a, gain_f):
     rows = copies.shape[1]
     for k in range(copies.shape[0]):
         copies[k] = group[pl.ds(0, rows), :]
@@ -160,22 +159,6 @@
     )(group, *after)
 
 
-def take_kernel(value, after, out):
-    out[...] = value[...]
-
-
-def take_after(value, after):
-    return pl.pallas_call(
-        take_kernel,
-        grid=(1,),
-        in_specs=[fixed(value.shape), pl.BlockSpec(memory_space=pl.ANY)],
-        out_specs=fixed(value.shape),
-        out_shape=pltpu.HBM(value.shape, value.dtype),
-        compiler_params=params(),
-        name="take_after",
-    )(value, after)
-
-
 def first_message_kernel(hidden, gain_a, gain_f, ids, out):
     rows, feats = hidden.shape
     out[pl.ds(0, rows), :] = hidden[...]
@@ -252,7 +235,7 @@
     )(group, own, after)
 
 
-def kv_sum_kernel(width, arrived, docs, out):
+def kv_sum_kernel(width, arrived, docs, table, place, out):
     rows = out.shape[1] - 16
     kv = jnp.sum(arrived[:, pl.ds(0, rows), :].astype(f32), axis=0).astype(bf16)
     sums = jnp.sum(arrived[:, pl.ds(rows, 16), :].astype(f32), axis=0)
@@ -263,7 +246,7 @@
         out[copy, pl.ds(rows, 16), :] = tail
 
 
-def kv_sum(width, arrived, docs, copies):
+def kv_sum(width, arrived, docs, copies, *after):
     blocks, tall, lanes = arrived.shape
     rows = HD
     last = tall - rows - 16
@@ -276,12 +259,13 @@
                 lambda i: (0, last, 0),
             ),
             pl.BlockSpec((16, docs.shape[1]), lambda i: (rows // 16, 0)),
-        ],
+        ]
+        + [pl.BlockSpec(memory_space=pl.ANY)] * len(after),
         out_specs=fixed((copies, rows + 16, lanes)),
         out_shape=pltpu.HBM((copies, rows + 16, lanes), bf16),
         compiler_params=params(),
         name="kv_sum",
-    )(arrived, docs)
+    )(arrived, docs, *after)
 
 
 def rotate(values, table):
@@ -508,13 +492,13 @@
     angle = jnp.arange(tokens, dtype=f32)[:, None] * freq[None, :]
     table = jnp.concatenate([jnp.cos(angle), jnp.sin(angle)], 1)
     group = lax.all_gather(swapped, ZL)
-    copies, gain_a, gain_f = attn_copies(group, nx, table, place)
-    attn_rows = lax.all_gather(take_after(hidden[0], gain_a), "seq")
+    attn_rows = lax.all_gather(hidden[0], "seq")
+    copies, gain_a, gain_f = attn_copies(group, nx, attn_rows)
     attn_cols = lax.all_to_all(copies, "x", 0, 0)
 
-    message = project(attn_cols, gain_a, w_query, w_key, w_value, attn_rows)
+    message = project(attn_cols, gain_a, w_query, w_key, w_value)
     arrived = lax.all_to_all(lax.all_to_all(message, "x", 0, 0), "seq", 0, 0)
-    kv = lax.all_to_all(kv_sum(width, arrived, swapped, 2 * nx), ("x", "zb"), 0, 0)
+    kv = lax.all_to_all(kv_sum(width, arrived, swapped, 2 * nx, table, place), ("x", "zb"), 0, 0)
     copies, section_out = attend(arrived, kv, table, swapped, nz)
     left_a = attn_left(scale, attn_rows, gain_attn, kv)
 

time: 235 us -> 244 us (1.038)
  waiting for transfers between devices: 12.6 us -> 40.8 us
  starting transfers between devices: 51.7 us -> 33.2 us
    all_to_all x2 -> x1, blocking collectives: 51.2 us -> 11.9 us  [on_device(): arrived = lax.all_to_all(lax.all_to_all(message, 'x', 0, 0), 'seq', 0, 0)]
    all_to_all x1 -> x2, blocking collectives: 9.84 us -> 42.1 us  [the longest x1 32.2 us: on_device(): attn_cols = lax.all_to_all(copies, 'x', 0, 0)]
    all_to_all x1, waiting for transfers between devices: 0.01 us -> 30.7 us  [on_device(): arrived = lax.all_to_all(lax.all_to_all(message, 'x', 0, 0), 'seq', 0, 0)]
    all_gather x1, blocking collectives: 29 us -> 43.7 us  [on_device(): attn_rows = lax.all_gather(hidden[0], 'seq')]
    all_to_all x1, starting transfers between devices: 18.6 us -> 5.15 us  [on_device(): arrived = lax.all_to_all(lax.all_to_all(message, 'x', 0, 0), 'seq', 0, 0)]
    all_gather x1, blocking collectives: 28.9 us -> 16.9 us  [on_device(): group = lax.all_gather(swapped, ZL)]
    ppermute x1, starting transfers between devices: 21 us -> 12.2 us  [on_device(): lax.ppermute(passed, 'phase', [(p, (p + 1) % count) for p in range(count)])]
    all_gather x1, blocking collectives: 17.1 us -> 22.7 us  [on_device(): ffn_rows = lax.all_gather(message, 'seq')]
  transfers between devices with their start and end apart: 6 -> 6, of which waited for: 1 -> 2; matrix products, arithmetic and copies ran while one was open for 1% -> 1% of each run, Pallas kernels for 0% -> 0%
where the time goes in v13:
time: 244 us; the launch traced here: 241 us
  blocking collectives  145 us (59%)
  waiting for transfers between devices  40.8 us (17%)
  starting transfers between devices  33.2 us (14%)
  Pallas kernels  19.8 us (8%)
    all_gather x1, blocking collectives, on_device(): attn_rows = lax.all_gather(hidden[0], 'seq')  43.7 us
    all_to_all x1, blocking collectives, on_device(): attn_cols = lax.all_to_all(copies, 'x', 0, 0)  32.2 us
    all_to_all x1, waiting for transfers between devices, on_device(): arrived = lax.all_to_all(lax.all_to_all(message, 'x', 0, 0), 'seq', 0, 0)  30.7 us
    all_gather x1, blocking collectives, on_device(): ffn_rows = lax.all_gather(message, 'seq')  22.7 us
    all_gather x1, blocking collectives, on_device(): group = lax.all_gather(swapped, ZL)  16.9 us
    ppermute x1, starting transfers between devices, on_device(): lax.ppermute(passed, 'phase', [(p, (p + 1) % count) for p in range(count)])  12.2 us
    all_to_all x1, blocking collectives, on_device(): arrived = lax.all_to_all(lax.all_to_all(message, 'x', 0, 0), 'seq', 0, 0)  11.9 us
    all_to_all x1, waiting for transfers between devices, on_device(): group = lax.all_to_all(copies, ZL, 0, 0)  10.2 us
  transfers between devices with their start and end apart: 6, of which 2 were waited for; matrix products, arithmetic and copies ran while one was open for 1% of the time, Pallas kernels for 0%

profile of v13, /device:TPU:1, one launch (start us, length us, event | category | flops | bytes accessed | tf_op | source)
XLA Modules:
  0.0 241.3 jit_solution(9010202277583137484)
XLA Ops:
  0.6 1.6 first_message.1
  2.2 1.6 collective-permute-start
  3.8 43.7 %all_gather.18.own_rows = bf16[4,128,512]{2,1,0:T(8,128)(2,1)S(1)} all-gather(bf16[1,128,512]{2,1,0:T(8,128)(2,1)} %param.7), channel_id=1, replica_groups=mesh['phase'=8,'x'=4,'za'=2,'zb'=2,'seq'=4] {'seq'}, dimensions={0}, use_global_device_ids=true | all-gather | bytes 655360 | tf_op jit(solution)/shard_map/all_gather | solution.py:495
  47.4 16.9 %all-gather = bf16[576,512]{1,0:T(8,128)(2,1)S(1)} all-gather(bf16[144,512]{1,0:T(8,128)(2,1)S(1)} %collective-permute-done.docs.resid), channel_id=2, replica_groups=mesh['phase'=8,'x'=4,'za'=2,'zb'=2,'seq'=4] {'za','zb'}, dimensions={0}, use_global_device_ids=true | all-gather | bytes 737280 | tf_op jit(solution)/shard_map/all_gather | solution.py:494
  64.3 1.8 attn_copies.1
  66.2 32.2 %all_to_all.30.cols.cols_a = bf16[4,4,128,512]{3,2,1,0:T(8,128)(2,1)} all-to-all(bf16[4,4,128,512]{3,2,1,0:T(8,128)(2,1)} %get-tuple-element.13), channel_id=1, replica_groups=mesh['phase'=8,'x'=4,'za'=2,'zb'=2,'seq'=4] {'x'}, dimensions={0} | all-to-all | bytes 4194304 | tf_op jit(solution)/shard_map/all_to_all | solution.py:497
  98.4 4.8 %project.1 = bf16[4,656,128]{2,1,0:T(8,128)(2,1)} custom-call(bf16[4,4,128,512]{3,2,1,0:T(8,128)(2,1)} %all_to_all.30.cols.cols_a, f32[4,1,512]{2,1,0:T(1,128)} %get-tuple-element.14.gain.gain_a, bf16[1,2048,512]{2,1,0:T(8,128)(2,1)} %wq.1, bf16[1,64,2048]{2,1,0:T(8,128)(2,1)} %bitcast.14, bf16[1,64,2048]{2,1,0:T(8,128)(2,1)} %bitcast.15), custom_call_target="tpu_custom_call" | custom-call | tf_op jit(solution)/shard_map/project/pallas_call | solution.py:76
  103.2 11.9 %all_to_all.31 = bf16[4,656,128]{2,1,0:T(8,128)(2,1)} all-to-all(bf16[4,656,128]{2,1,0:T(8,128)(2,1)} %project.1), channel_id=1, replica_groups=mesh['phase'=8,'x'=4,'za'=2,'zb'=2,'seq'=4] {'x'}, dimensions={0} | all-to-all | bytes 1343488 | tf_op jit(solution)/shard_map/all_to_all | solution.py:500
  115.2 5.1 %all-to-all-start.2 = ((bf16[4,656,128]{2,1,0:T(8,128)(2,1)}), bf16[4,656,128]{2,1,0:T(8,128)(2,1)S(1)}, u32[]{:S(2)}, u32[]{:S(2)}) async-start(bf16[4,656,128]{2,1,0:T(8,128)(2,1)} %all_to_all.31), calls=%async_computation.2 | async-start | bytes 1343488 | tf_op jit(solution)/shard_map/all_to_all | solution.py:500
  120.4 1.0 fusion.1
  121.5 30.7 %all-to-all-done.2.arrived.q_in = bf16[4,656,128]{2,1,0:T(8,128)(2,1)S(1)} async-done(((bf16[4,656,128]{2,1,0:T(8,128)(2,1)}), bf16[4,656,128]{2,1,0:T(8,128)(2,1)S(1)}, u32[]{:S(2)}, u32[]{:S(2)}) %all-to-all-start.2) | async-done | bytes 671776 | tf_op jit(solution)/shard_map/all_to_all | solution.py:500
  152.2 0.8 kv_sum.1
  153.0 9.8 %all_to_all.32.kv.kv_in = bf16[8,144,128]{2,1,0:T(8,128)(2,1)S(1)} all-to-all(bf16[8,144,128]{2,1,0:T(8,128)(2,1)} %kv_sum.1), channel_id=1, replica_groups=mesh['phase'=8,'x'=4,'za'=2,'zb'=2,'seq'=4] {'x','zb'}, dimensions={0} | all-to-all | bytes 589824 | tf_op jit(solution)/shard_map/all_to_all | solution.py:501
  162.8 3.1 %attend.1 = (bf16[4,144,512]{2,1,0:T(8,128)(2,1)}, bf16[128,512]{1,0:T(8,128)(2,1)}) custom-call(bf16[4,656,128]{2,1,0:T(8,128)(2,1)S(1)} %all-to-all-done.2.arrived.q_in, bf16[8,144,128]{2,1,0:T(8,128)(2,1)S(1)} %all_to_all.32.kv.kv_in, f32[512,128]{1,0:T(8,128)S(1)} %pad_maximum_fusion.table, bf16[144,512]{1,0:T(8,128)(2,1)S(1)} %collective-permute-done.docs.resid), custom_call_target="tpu_custom_call" | custom-call | tf_op jit(solution)/shard_map/attend/pallas_call | solution.py:345
  166.0 3.5 %all-to-all-start.4 = ((bf16[4,144,512]{2,1,0:T(8,128)(2,1)}), bf16[4,144,512]{2,1,0:T(8,128)(2,1)S(1)}, u32[]{:S(2)}, u32[]{:S(2)}) async-start(bf16[4,144,512]{2,1,0:T(8,128)(2,1)} %get-tuple-element.15), calls=%async_computation.4 | async-start | bytes 1179648 | tf_op jit(solution)/shard_map/all_to_all | solution.py:506
  169.4 1.6 collective-permute-start.1
  171.0 0.3 attn_left.1.after.left_a
  171.4 10.2 %all-to-all-done.4.group = bf16[4,144,512]{2,1,0:T(8,128)(2,1)S(1)} async-done(((bf16[4,144,512]{2,1,0:T(8,128)(2,1)}), bf16[4,144,512]{2,1,0:T(8,128)(2,1)S(1)}, u32[]{:S(2)}, u32[]{:S(2)}) %all-to-all-start.4) | async-done | bytes 589856 | tf_op jit(solution)/shard_map/all_to_all | solution.py:506
  181.5 1.9 ffn_copies.1
  183.5 9.2 %all-to-all-start.5 = ((bf16[4,4,128,512]{3,2,1,0:T(8,128)(2,1)}), bf16[4,4,128,512]{3,2,1,0:T(8,128)(2,1)}, u32[]{:S(2)}, u32[]{:S(2)}) async-start(bf16[4,4,128,512]{3,2,1,0:T(8,128)(2,1)} %get-tuple-element.18), calls=%async_computation.5 | async-start | bytes 4194304 | tf_op jit(solution)/shard_map/all_to_all | solution.py:508
  192.7 22.7 %all-gather.1 = bf16[576,512]{1,0:T(8,128)(2,1)S(1)} all-gather(bf16[144,512]{1,0:T(8,128)(2,1)S(1)} %copy-done.5), channel_id=3, replica_groups=mesh['phase'=8,'x'=4,'za'=2,'zb'=2,'seq'=4] {'seq'}, dimensions={0}, use_global_device_ids=true | all-gather | bytes 737280 | tf_op jit(solution)/shard_map/all_gather | solution.py:509
  215.5 12.2 %collective-permute-start.2 = (bf16[1,128,512]{2,1,0:T(8,128)(2,1)S(1)}, bf16[1,128,512]{2,1,0:T(8,128)(2,1)S(1)}, u32[]{:S(2)}, u32[]{:S(2)}) collective-permute-start(bf16[1,128,512]{2,1,0:T(8,128)(2,1)S(1)} %constant_dynamic-slice_fusion), channel_id=1, source_target_pairs={{0,64},{64,128},{128,192},{192,256},{256,320},{320,384},{384,448},... | collective-permute-start | bytes 393224 | tf_op jit(solution)/shard_map/ppermute | solution.py:514
  227.7 8.2 %all-gather.3.total = f32[4,1,128]{2,1,0:T(1,128)S(1)} all-gather(f32[1,1,128]{2,1,0:T(1,128)S(1)} %bitcast.16), channel_id=4, replica_groups=mesh['phase'=8,'x'=4,'za'=2,'zb'=2,'seq'=4] {'x'}, dimensions={0}, use_global_device_ids=true | all-gather | bytes 2560 | tf_op jit(solution)/shard_map/all_gather | solution.py:511
  236.0 5.3 %hessian.1 = (bf16[512,2048]{1,0:T(8,128)(2,1)}, f32[1,128]{1,0:T(1,128)}, bf16[1,128,512]{2,1,0:T(8,128)(2,1)}) custom-call(s32[2]{0:T(128)S(1)} %pad_add_fusion.place, bf16[512,512]{1,0:T(8,128)(2,1)S(1)} %attn_left.1.after.left_a, bf16[4,4,128,512]{3,2,1,0:T(8,128)(2,1)S(1)} %copy-done, f32[4,1,512]{2,1,0:T(1,128)S(1)} %copy-done.1, ...), custom_call_target="tpu_custom_call" | custom-call | tf_op jit(solution)/shard_map/hessian/pallas_call | solution.py:444
  (22 shorter events, 0.3 us)
Async XLA Ops:
  2.2 45.2 %collective-permute-start = (bf16[144,512]{1,0:T(8,128)(2,1)}, bf16[144,512]{1,0:T(8,128)(2,1)S(1)}, u32[]{:S(2)}, u32[]{:S(2)}) collective-permute-start(bf16[144,512]{1,0:T(8,128)(2,1)} %first_message.1), channel_id=1, source_target_pairs={{0,0},{1,16},{2,32},{3,48},{4,4},{5,20},{6,36},{7,52},{8,8},{9,24}... | collective-permute-start | bytes 442376 | tf_op jit(solution)/shard_map/ppermute | solution.py:31
  115.2 37.0 %all-to-all-start.2 = ((bf16[4,656,128]{2,1,0:T(8,128)(2,1)}), bf16[4,656,128]{2,1,0:T(8,128)(2,1)S(1)}, u32[]{:S(2)}, u32[]{:S(2)}) async-start(bf16[4,656,128]{2,1,0:T(8,128)(2,1)} %all_to_all.31), calls=%async_computation.2 | async-start | bytes 1343488 | tf_op jit(solution)/shard_map/all_to_all | solution.py:500
  121.5 49.5 %copy-start.4 = (bf16[1,512]{1,0:T(2,128)(2,1)S(1)}, bf16[1,512]{1,0:T(2,128)(2,1)}, u32[]{:S(2)}) copy-start(bf16[1,512]{1,0:T(2,128)(2,1)} %gain.1) | copy-start | bytes 3076
  166.0 15.6 %all-to-all-start.4 = ((bf16[4,144,512]{2,1,0:T(8,128)(2,1)}), bf16[4,144,512]{2,1,0:T(8,128)(2,1)S(1)}, u32[]{:S(2)}, u32[]{:S(2)}) async-start(bf16[4,144,512]{2,1,0:T(8,128)(2,1)} %get-tuple-element.15), calls=%async_computation.4 | async-start | bytes 1179648 | tf_op jit(solution)/shard_map/all_to_all | solution.py:506
  169.4 1.9 collective-permute-start.1
  183.4 9.3 %copy-start.5 = (bf16[144,512]{1,0:T(8,128)(2,1)S(1)}, bf16[144,512]{1,0:T(8,128)(2,1)}, u32[]{:S(2)}) copy-start(bf16[144,512]{1,0:T(8,128)(2,1)} %get-tuple-element.17) | copy-start | bytes 442372
  183.4 52.5 %copy-start = (bf16[4,4,128,512]{3,2,1,0:T(8,128)(2,1)S(1)}, bf16[4,4,128,512]{3,2,1,0:T(8,128)(2,1)}, u32[]{:S(2)}) copy-start(bf16[4,4,128,512]{3,2,1,0:T(8,128)(2,1)} %all_to_all.30.cols.cols_a) | copy-start | bytes 6291460
  183.4 52.5 %copy-start.1 = (f32[4,1,512]{2,1,0:T(1,128)S(1)}, f32[4,1,512]{2,1,0:T(1,128)}, u32[]{:S(2)}) copy-start(f32[4,1,512]{2,1,0:T(1,128)} %get-tuple-element.14.gain.gain_a) | copy-start | bytes 24580
  183.4 52.5 %copy-start.2 = (bf16[1,512]{1,0:T(2,128)(2,1)S(1)}, bf16[1,512]{1,0:T(2,128)(2,1)}, u32[]{:S(2)}) copy-start(bf16[1,512]{1,0:T(2,128)(2,1)} %gain_row.1) | copy-start | bytes 3076
  183.5 52.5 %copy-start.3 = (f32[4,1,512]{2,1,0:T(1,128)S(1)}, f32[4,1,512]{2,1,0:T(1,128)}, u32[]{:S(2)}) copy-start(f32[4,1,512]{2,1,0:T(1,128)} %get-tuple-element.19.gain_f) | copy-start | bytes 24580
  183.5 52.5 %all-to-all-start.5 = ((bf16[4,4,128,512]{3,2,1,0:T(8,128)(2,1)}), bf16[4,4,128,512]{3,2,1,0:T(8,128)(2,1)}, u32[]{:S(2)}, u32[]{:S(2)}) async-start(bf16[4,4,128,512]{3,2,1,0:T(8,128)(2,1)} %get-tuple-element.18), calls=%async_computation.5 | async-start | bytes 4194304 | tf_op jit(solution)/shard_map/all_to_all | solution.py:508
  215.5 20.5 %collective-permute-start.2 = (bf16[1,128,512]{2,1,0:T(8,128)(2,1)S(1)}, bf16[1,128,512]{2,1,0:T(8,128)(2,1)S(1)}, u32[]{:S(2)}, u32[]{:S(2)}) collective-permute-start(bf16[1,128,512]{2,1,0:T(8,128)(2,1)S(1)} %constant_dynamic-slice_fusion), channel_id=1, source_target_pairs={{0,64},{64,128},{128,192},{192,256},{256,320},{320,384},{384,448},... | collective-permute-start | bytes 393224 | tf_op jit(solution)/shard_map/ppermute | solution.py:514

commit v14 on v13

--- a/solution.py
+++ b/solution.py
@@ -31,7 +31,7 @@
     return lax.ppermute(value, GROUP, pairs)
 
 
-def project_kernel(cols, gain, wq, wk, wv, out, q_acc, kv_acc, squares, left):
+def project_kernel(cols, gain, wq, wk, wv, after, out, q_acc, kv_acc, squares, left):
     step = pl.program_id(0)
     blocks, parts, rows, feats = cols.shape
     part = jnp.zeros((blocks * rows, 1), f32)
@@ -67,7 +67,7 @@
                 out[k, pl.ds(h * rows, rows), :] = q_acc[block, pl.ds(h * HD, HD)].astype(bf16)
 
 
-def project(cols, gain, w_query, w_key, w_value):
+def project(cols, gain, w_query, w_key, w_value, after):
     blocks, parts, rows, feats = cols.shape
     q_width, kv_width = w_query.shape[2], 2 * w_key.shape[2]
     heads = q_width // HD
@@ -82,6 +82,7 @@
             pl.BlockSpec((None, pair * feats, q_width), lambda z: (0, z, 0)),
             kv_spec,
             kv_spec,
+            pl.BlockSpec(memory_space=pl.ANY),
         ],
         out_specs=fixed((blocks, (heads + 1) * rows + 16, HD)),
         out_shape=pltpu.HBM((blocks, (heads + 1) * rows + 16, HD), bf16),
@@ -93,7 +94,7 @@
         ],
         compiler_params=params(PROJECT),
         name="project",
-    )(cols, gain, w_query, w_key.swapaxes(1, 2), w_value.swapaxes(1, 2))
+    )(cols, gain, w_query, w_key.swapaxes(1, 2), w_value.swapaxes(1, 2), after)
 
 
 def fixed(shape):
@@ -125,7 +126,7 @@
     return jnp.concatenate([row.astype(f32) for row in rows]).astype(bf16)
 
 
-def attn_copies_kernel(group, own_rows, copies, gain_a, gain_f):
+def attn_copies_kernel(group, copies, gain_a, gain_f):
     rows = copies.shape[1]
     for k in range(copies.shape[0]):
         copies[k] = group[pl.ds(0, rows), :]
@@ -134,7 +135,7 @@
     gain_f[...] = gains[1:2]
 
 
-def attn_copies(group, count, *after):
+def attn_copies(group, count):
     parts, tall, feats = group.shape
     rows = tall - 16
     gain = pl.BlockSpec((None, 1, feats), lambda z: (z, 0, 0))
@@ -142,8 +143,7 @@
     return pl.pallas_call(
         attn_copies_kernel,
         grid=(parts,),
-        in_specs=[pl.BlockSpec((None, tall, feats), lambda z: (z, 0, 0))]
-        + [pl.BlockSpec(memory_space=pl.ANY)] * len(after),
+        in_specs=[pl.BlockSpec((None, tall, feats), lambda z: (z, 0, 0))],
         out_specs=[
             pl.BlockSpec((count, None, rows, feats), lambda z: (0, z, 0, 0)),
             gain,
@@ -156,7 +156,7 @@
         ],
         compiler_params=params(),
         name="attn_copies",
-    )(group, *after)
+    )(group)
 
 
 def first_message_kernel(hidden, gain_a, gain_f, ids, out):
@@ -287,7 +287,7 @@
     return high, (value - high.astype(f32)).astype(bf16)
 
 
-def attend_kernel(q_in, kv_in, table, resid, copies, out, keys, values, r_all, docs_all):
+def attend_kernel(q_in, kv_in, table, resid, message, out, keys, values, r_all, docs_all):
     rows, feats = out.shape
     heads = feats // HD
     tokens = keys.shape[0]
@@ -329,19 +329,16 @@
         lanes = pl.ds(h * HD, HD)
         result = (resid[:, lanes].astype(f32) + context).astype(bf16)
         out[:, lanes] = result
-        for copy in range(copies.shape[0]):
-            copies[copy, pl.ds(0, rows), lanes] = result
+        message[pl.ds(0, rows), lanes] = result
         result = result.astype(f32)
         squares += jnp.sum(result * result, axis=1, keepdims=True)
-    tail = below(row_of(squares), feats)
-    for copy in range(copies.shape[0]):
-        copies[copy, pl.ds(rows, 16), :] = tail
-
-
-def attend(q_in, kv_in, table, swapped, copies):
+    message[pl.ds(rows, 16), :] = below(row_of(squares), feats)
+
+
+def attend(q_in, kv_in, table, swapped):
     rows, feats = swapped.shape[0] - 16, swapped.shape[1]
     heads, tokens = feats // HD, table.shape[0]
-    shape = (copies, rows + 16, feats)
+    shape = swapped.shape
     return pl.pallas_call(
         attend_kernel,
         grid=(1,),
@@ -492,18 +489,18 @@
     angle = jnp.arange(tokens, dtype=f32)[:, None] * freq[None, :]
     table = jnp.concatenate([jnp.cos(angle), jnp.sin(angle)], 1)
     group = lax.all_gather(swapped, ZL)
+    copies, gain_a, gain_f = attn_copies(group, nx)
     attn_rows = lax.all_gather(hidden[0], "seq")
-    copies, gain_a, gain_f = attn_copies(group, nx, attn_rows)
     attn_cols = lax.all_to_all(copies, "x", 0, 0)
 
-    message = project(attn_cols, gain_a, w_query, w_key, w_value)
+    message = project(attn_cols, gain_a, w_query, w_key, w_value, attn_rows)
     arrived = lax.all_to_all(lax.all_to_all(message, "x", 0, 0), "seq", 0, 0)
     kv = lax.all_to_all(kv_sum(width, arrived, swapped, 2 * nx, table, place), ("x", "zb"), 0, 0)
-    copies, section_out = attend(arrived, kv, table, swapped, nz)
+    message, section_out = attend(arrived, kv, table, swapped)
     left_a = attn_left(scale, attn_rows, gain_attn, kv)
 
     out_rows = swap_x_seq(section_out)
-    group = lax.all_to_all(copies, ZL, 0, 0)
+    group = lax.all_gather(message, ZL)
     copies, message = ffn_copies(group, out_rows, nx, left_a)
     ffn_cols = lax.all_to_all(copies, "x", 0, 0)
     ffn_rows = lax.all_gather(message, "seq")

time: 244 us -> 236 us (0.967)
  starting transfers between devices: 33.2 us -> 58.5 us
  blocking collectives: 145 us -> 127 us
  waiting for transfers between devices: 40.8 us -> 26.5 us
    all_to_all x1 -> x0, blocking collectives: 32.2 us -> none  [on_device(): attn_cols = lax.all_to_all(copies, 'x', 0, 0)]
    all_gather x0 -> x1, blocking collectives: none -> 24.3 us  [on_device(): group = lax.all_gather(message, ZL)]
    all_to_all x1, starting transfers between devices: 3.48 us -> 26.2 us  [on_device(): attn_cols = lax.all_to_all(copies, 'x', 0, 0)]
    all_gather x1, blocking collectives: 43.7 us -> 28.8 us  [on_device(): attn_rows = lax.all_gather(hidden[0], 'seq')]
    all_to_all x1, waiting for transfers between devices: 10.2 us -> 0.01 us  [on_device(): attn_cols = lax.all_to_all(copies, 'x', 0, 0)]
    all_gather x1, blocking collectives: 16.9 us -> 22.5 us  [on_device(): group = lax.all_gather(swapped, ZL)]
    all_to_all x1, waiting for transfers between devices: 30.7 us -> 26.5 us  [on_device(): arrived = lax.all_to_all(lax.all_to_all(message, 'x', 0, 0), 'seq', 0, 0)]
  transfers between devices with their start and end apart: 6 -> 6, of which waited for: 2 -> 1; matrix products, arithmetic and copies ran while one was open for 1% -> 1% of each run, Pallas kernels for 0% -> 0%
where the time goes in v14:
time: 236 us; the launch traced here: 235 us
  blocking collectives  127 us (54%)
  starting transfers between devices  58.5 us (25%)
  waiting for transfers between devices  26.5 us (11%)
  Pallas kernels  19.7 us (8%)
    all_gather x1, blocking collectives, on_device(): attn_rows = lax.all_gather(hidden[0], 'seq')  28.8 us
    all_to_all x1, waiting for transfers between devices, on_device(): arrived = lax.all_to_all(lax.all_to_all(message, 'x', 0, 0), 'seq', 0, 0)  26.5 us
    all_to_all x1, starting transfers between devices, on_device(): attn_cols = lax.all_to_all(copies, 'x', 0, 0)  26.2 us
    all_gather x1, blocking collectives, on_device(): group = lax.all_gather(message, ZL)  24.3 us
    all_gather x1, blocking collectives, on_device(): group = lax.all_gather(swapped, ZL)  22.5 us
    all_gather x1, blocking collectives, on_device(): ffn_rows = lax.all_gather(message, 'seq')  20.6 us
    ppermute x1, starting transfers between devices, on_device(): lax.ppermute(passed, 'phase', [(p, (p + 1) % count) for p in range(count)])  12 us
    all_to_all x1, blocking collectives, on_device(): arrived = lax.all_to_all(lax.all_to_all(message, 'x', 0, 0), 'seq', 0, 0)  12 us
  transfers between devices with their start and end apart: 6, of which 1 were waited for; matrix products, arithmetic and copies ran while one was open for 1% of the time, Pallas kernels for 0%

profile of v14, /device:TPU:1, one launch (start us, length us, event | category | flops | bytes accessed | tf_op | source)
XLA Modules:
  0.0 235.2 jit_solution(12278907834685101140)
XLA Ops:
  0.6 1.6 first_message.1
  2.2 1.6 collective-permute-start
  3.8 22.5 %all-gather = bf16[576,512]{1,0:T(8,128)(2,1)S(1)} all-gather(bf16[144,512]{1,0:T(8,128)(2,1)S(1)} %collective-permute-done.docs.resid), channel_id=2, replica_groups=mesh['phase'=8,'x'=4,'za'=2,'zb'=2,'seq'=4] {'za','zb'}, dimensions={0}, use_global_device_ids=true | all-gather | bytes 737280 | tf_op jit(solution)/shard_map/all_gather | solution.py:491
  26.3 1.8 attn_copies.1
  28.1 26.2 %all-to-all-start = ((bf16[4,4,128,512]{3,2,1,0:T(8,128)(2,1)}), bf16[4,4,128,512]{3,2,1,0:T(8,128)(2,1)S(1)}, u32[]{:S(2)}, u32[]{:S(2)}) async-start(bf16[4,4,128,512]{3,2,1,0:T(8,128)(2,1)} %get-tuple-element.13), calls=%async_computation | async-start | bytes 4194304 | tf_op jit(solution)/shard_map/all_to_all | solution.py:494
  54.4 28.8 %all_gather.24.after.own_rows = bf16[4,128,512]{2,1,0:T(8,128)(2,1)} all-gather(bf16[1,128,512]{2,1,0:T(8,128)(2,1)S(1)} %copy-done.7), channel_id=1, replica_groups=mesh['phase'=8,'x'=4,'za'=2,'zb'=2,'seq'=4] {'seq'}, dimensions={0}, use_global_device_ids=true | all-gather | bytes 655360 | tf_op jit(solution)/shard_map/all_gather | solution.py:493
  83.2 1.3 copy-done
  84.5 4.9 %project.1 = bf16[4,656,128]{2,1,0:T(8,128)(2,1)} custom-call(bf16[4,4,128,512]{3,2,1,0:T(8,128)(2,1)} %copy-done, f32[4,1,512]{2,1,0:T(1,128)} %get-tuple-element.14.gain.gain_a, bf16[1,2048,512]{2,1,0:T(8,128)(2,1)} %wq.1, bf16[1,64,2048]{2,1,0:T(8,128)(2,1)} %bitcast.16, bf16[1,64,2048]{2,1,0:T(8,128)(2,1)} %bitcast.17, ...), custom_call_target="tpu_custom_call" | custom-call | tf_op jit(solution)/shard_map/project/pallas_call | solution.py:76
  89.4 12.0 %all_to_all.25 = bf16[4,656,128]{2,1,0:T(8,128)(2,1)} all-to-all(bf16[4,656,128]{2,1,0:T(8,128)(2,1)} %project.1), channel_id=1, replica_groups=mesh['phase'=8,'x'=4,'za'=2,'zb'=2,'seq'=4] {'x'}, dimensions={0} | all-to-all | bytes 1343488 | tf_op jit(solution)/shard_map/all_to_all | solution.py:497
  101.4 6.5 %all-to-all-start.2 = ((bf16[4,656,128]{2,1,0:T(8,128)(2,1)}), bf16[4,656,128]{2,1,0:T(8,128)(2,1)S(1)}, u32[]{:S(2)}, u32[]{:S(2)}) async-start(bf16[4,656,128]{2,1,0:T(8,128)(2,1)} %all_to_all.25), calls=%async_computation.2 | async-start | bytes 1343488 | tf_op jit(solution)/shard_map/all_to_all | solution.py:497
  107.9 1.0 fusion.1
  109.1 26.5 %all-to-all-done.2.arrived.q_in = bf16[4,656,128]{2,1,0:T(8,128)(2,1)S(1)} async-done(((bf16[4,656,128]{2,1,0:T(8,128)(2,1)}), bf16[4,656,128]{2,1,0:T(8,128)(2,1)S(1)}, u32[]{:S(2)}, u32[]{:S(2)}) %all-to-all-start.2) | async-done | bytes 671776 | tf_op jit(solution)/shard_map/all_to_all | solution.py:497
  135.5 0.8 kv_sum.1
  136.3 10.3 %all_to_all.26.kv.kv_in = bf16[8,144,128]{2,1,0:T(8,128)(2,1)S(1)} all-to-all(bf16[8,144,128]{2,1,0:T(8,128)(2,1)} %kv_sum.1), channel_id=1, replica_groups=mesh['phase'=8,'x'=4,'za'=2,'zb'=2,'seq'=4] {'x','zb'}, dimensions={0} | all-to-all | bytes 589824 | tf_op jit(solution)/shard_map/all_to_all | solution.py:498
  146.6 3.0 %attend.1 = (bf16[144,512]{1,0:T(8,128)(2,1)}, bf16[128,512]{1,0:T(8,128)(2,1)}) custom-call(bf16[4,656,128]{2,1,0:T(8,128)(2,1)S(1)} %all-to-all-done.2.arrived.q_in, bf16[8,144,128]{2,1,0:T(8,128)(2,1)S(1)} %all_to_all.26.kv.kv_in, f32[512,128]{1,0:T(8,128)S(1)} %pad_maximum_fusion.table, bf16[144,512]{1,0:T(8,128)(2,1)S(1)} %collective-permute-done.docs.resid), custom_call_target="tpu_custom_call" | custom-call | tf_op jit(solution)/shard_map/attend/pallas_call | solution.py:342
  149.6 1.6 collective-permute-start.1
  151.1 0.3 attn_left.1.after.left_a
  151.5 24.3 %all-gather.1 = bf16[576,512]{1,0:T(8,128)(2,1)S(1)} all-gather(bf16[144,512]{1,0:T(8,128)(2,1)} %get-tuple-element.15), channel_id=3, replica_groups=mesh['phase'=8,'x'=4,'za'=2,'zb'=2,'seq'=4] {'za','zb'}, dimensions={0}, use_global_device_ids=true | all-gather | bytes 737280 | tf_op jit(solution)/shard_map/all_gather | solution.py:503
  175.7 2.0 ffn_copies.1
  177.8 10.7 %all-to-all-start.4 = ((bf16[4,4,128,512]{3,2,1,0:T(8,128)(2,1)}), bf16[4,4,128,512]{3,2,1,0:T(8,128)(2,1)}, u32[]{:S(2)}, u32[]{:S(2)}) async-start(bf16[4,4,128,512]{3,2,1,0:T(8,128)(2,1)} %get-tuple-element.18), calls=%async_computation.4 | async-start | bytes 4194304 | tf_op jit(solution)/shard_map/all_to_all | solution.py:505
  188.4 20.6 %all-gather.2 = bf16[576,512]{1,0:T(8,128)(2,1)S(1)} all-gather(bf16[144,512]{1,0:T(8,128)(2,1)S(1)} %copy-done.8), channel_id=4, replica_groups=mesh['phase'=8,'x'=4,'za'=2,'zb'=2,'seq'=4] {'seq'}, dimensions={0}, use_global_device_ids=true | all-gather | bytes 737280 | tf_op jit(solution)/shard_map/all_gather | solution.py:506
  209.1 12.0 %collective-permute-start.2 = (bf16[1,128,512]{2,1,0:T(8,128)(2,1)S(1)}, bf16[1,128,512]{2,1,0:T(8,128)(2,1)S(1)}, u32[]{:S(2)}, u32[]{:S(2)}) collective-permute-start(bf16[1,128,512]{2,1,0:T(8,128)(2,1)S(1)} %constant_dynamic-slice_fusion), channel_id=1, source_target_pairs={{0,64},{64,128},{128,192},{192,256},{256,320},{320,384},{384,448},... | collective-permute-start | bytes 393224 | tf_op jit(solution)/shard_map/ppermute | solution.py:511
  221.1 8.7 %all-gather.4.total = f32[4,1,128]{2,1,0:T(1,128)S(1)} all-gather(f32[1,1,128]{2,1,0:T(1,128)S(1)} %bitcast.18), channel_id=5, replica_groups=mesh['phase'=8,'x'=4,'za'=2,'zb'=2,'seq'=4] {'x'}, dimensions={0}, use_global_device_ids=true | all-gather | bytes 2560 | tf_op jit(solution)/shard_map/all_gather | solution.py:508
  229.9 5.3 %hessian.1 = (bf16[512,2048]{1,0:T(8,128)(2,1)}, f32[1,128]{1,0:T(1,128)}, bf16[1,128,512]{2,1,0:T(8,128)(2,1)}) custom-call(s32[2]{0:T(128)S(1)} %pad_add_fusion.place, bf16[512,512]{1,0:T(8,128)(2,1)S(1)} %attn_left.1.after.left_a, bf16[4,4,128,512]{3,2,1,0:T(8,128)(2,1)S(1)} %copy-done.1, f32[4,1,512]{2,1,0:T(1,128)S(1)} %copy-done.3, ...), custom_call_target="tpu_custom_call" | custom-call | tf_op jit(solution)/shard_map/hessian/pallas_call | solution.py:441
  (28 shorter events, 0.3 us)
Async XLA Ops:
  2.2 1.6 collective-permute-start
  28.1 26.2 %copy-start.7 = (bf16[1,128,512]{2,1,0:T(8,128)(2,1)S(1)}, bf16[1,128,512]{2,1,0:T(8,128)(2,1)}, u32[]{:S(2)}) copy-start(bf16[1,128,512]{2,1,0:T(8,128)(2,1)} %param.7) | copy-start | bytes 393220
  28.1 55.1 %all-to-all-start = ((bf16[4,4,128,512]{3,2,1,0:T(8,128)(2,1)}), bf16[4,4,128,512]{3,2,1,0:T(8,128)(2,1)S(1)}, u32[]{:S(2)}, u32[]{:S(2)}) async-start(bf16[4,4,128,512]{3,2,1,0:T(8,128)(2,1)} %get-tuple-element.13), calls=%async_computation | async-start | bytes 4194304 | tf_op jit(solution)/shard_map/all_to_all | solution.py:494
  83.2 1.3 copy-start
  101.4 34.2 %all-to-all-start.2 = ((bf16[4,656,128]{2,1,0:T(8,128)(2,1)}), bf16[4,656,128]{2,1,0:T(8,128)(2,1)S(1)}, u32[]{:S(2)}, u32[]{:S(2)}) async-start(bf16[4,656,128]{2,1,0:T(8,128)(2,1)} %all_to_all.25), calls=%async_computation.2 | async-start | bytes 1343488 | tf_op jit(solution)/shard_map/all_to_all | solution.py:497
  108.9 42.2 %copy-start.2 = (bf16[4,128,512]{2,1,0:T(8,128)(2,1)S(1)}, bf16[4,128,512]{2,1,0:T(8,128)(2,1)}, u32[]{:S(2)}) copy-start(bf16[4,128,512]{2,1,0:T(8,128)(2,1)} %all_gather.24.after.own_rows) | copy-start | bytes 1572868
  108.9 42.2 %copy-start.6 = (bf16[1,512]{1,0:T(2,128)(2,1)S(1)}, bf16[1,512]{1,0:T(2,128)(2,1)}, u32[]{:S(2)}) copy-start(bf16[1,512]{1,0:T(2,128)(2,1)} %gain.1) | copy-start | bytes 3076
  149.6 26.2 %collective-permute-start.1 = (bf16[128,512]{1,0:T(8,128)(2,1)}, bf16[128,512]{1,0:T(8,128)(2,1)S(1)}, u32[]{:S(2)}, u32[]{:S(2)}) collective-permute-start(bf16[128,512]{1,0:T(8,128)(2,1)} %get-tuple-element.16), channel_id=1, source_target_pairs={{0,0},{1,16},{2,32},{3,48},{4,4},{5,20},{6,36},{7,52},{8,8},{9,24}... | collective-permute-start | bytes 393224 | tf_op jit(solution)/shard_map/ppermute | solution.py:31
  177.7 10.7 %copy-start.8 = (bf16[144,512]{1,0:T(8,128)(2,1)S(1)}, bf16[144,512]{1,0:T(8,128)(2,1)}, u32[]{:S(2)}) copy-start(bf16[144,512]{1,0:T(8,128)(2,1)} %get-tuple-element.17) | copy-start | bytes 442372
  177.7 52.1 %copy-start.1 = (bf16[4,4,128,512]{3,2,1,0:T(8,128)(2,1)S(1)}, bf16[4,4,128,512]{3,2,1,0:T(8,128)(2,1)}, u32[]{:S(2)}) copy-start(bf16[4,4,128,512]{3,2,1,0:T(8,128)(2,1)} %copy-done) | copy-start | bytes 6291460
  177.7 52.1 %copy-start.3 = (f32[4,1,512]{2,1,0:T(1,128)S(1)}, f32[4,1,512]{2,1,0:T(1,128)}, u32[]{:S(2)}) copy-start(f32[4,1,512]{2,1,0:T(1,128)} %get-tuple-element.14.gain.gain_a) | copy-start | bytes 24580
  177.7 52.1 %copy-start.4 = (bf16[1,512]{1,0:T(2,128)(2,1)S(1)}, bf16[1,512]{1,0:T(2,128)(2,1)}, u32[]{:S(2)}) copy-start(bf16[1,512]{1,0:T(2,128)(2,1)} %gain_row.1) | copy-start | bytes 3076
  177.8 52.1 %copy-start.5 = (f32[4,1,512]{2,1,0:T(1,128)S(1)}, f32[4,1,512]{2,1,0:T(1,128)}, u32[]{:S(2)}) copy-start(f32[4,1,512]{2,1,0:T(1,128)} %get-tuple-element.19.gain_f) | copy-start | bytes 24580
  177.8 52.1 %all-to-all-start.4 = ((bf16[4,4,128,512]{3,2,1,0:T(8,128)(2,1)}), bf16[4,4,128,512]{3,2,1,0:T(8,128)(2,1)}, u32[]{:S(2)}, u32[]{:S(2)}) async-start(bf16[4,4,128,512]{3,2,1,0:T(8,128)(2,1)} %get-tuple-element.18), calls=%async_computation.4 | async-start | bytes 4194304 | tf_op jit(solution)/shard_map/all_to_all | solution.py:505
  209.1 20.7 %collective-permute-start.2 = (bf16[1,128,512]{2,1,0:T(8,128)(2,1)S(1)}, bf16[1,128,512]{2,1,0:T(8,128)(2,1)S(1)}, u32[]{:S(2)}, u32[]{:S(2)}) collective-permute-start(bf16[1,128,512]{2,1,0:T(8,128)(2,1)S(1)} %constant_dynamic-slice_fusion), channel_id=1, source_target_pairs={{0,64},{64,128},{128,192},{192,256},{256,320},{320,384},{384,448},... | collective-permute-start | bytes 393224 | tf_op jit(solution)/shard_map/ppermute | solution.py:511

commit v15 on v14

--- a/solution.py
+++ b/solution.py
@@ -17,7 +17,7 @@
 bf16 = jnp.bfloat16
 LIMIT = 24 * 1024 * 1024
 WIDE = 57 * 1024 * 1024
-PROJECT = 57 * 1024 * 1024
+PROJECT = 24 * 1024 * 1024
 
 
 def swap_x_seq(value):
@@ -235,7 +235,7 @@
     )(group, own, after)
 
 
-def kv_sum_kernel(width, arrived, docs, table, place, out):
+def kv_sum_kernel(width, arrived, docs, table, out):
     rows = out.shape[1] - 16
     kv = jnp.sum(arrived[:, pl.ds(0, rows), :].astype(f32), axis=0).astype(bf16)
     sums = jnp.sum(arrived[:, pl.ds(rows, 16), :].astype(f32), axis=0)
@@ -287,7 +287,7 @@
     return high, (value - high.astype(f32)).astype(bf16)
 
 
-def attend_kernel(q_in, kv_in, table, resid, message, out, keys, values, r_all, docs_all):
+def attend_kernel(q_in, kv_in, table, resid, copies, out, keys, values, r_all, docs_all):
     rows, feats = out.shape
     heads = feats // HD
     tokens = keys.shape[0]
@@ -329,16 +329,19 @@
         lanes = pl.ds(h * HD, HD)
         result = (resid[:, lanes].astype(f32) + context).astype(bf16)
         out[:, lanes] = result
-        message[pl.ds(0, rows), lanes] = result
+        for copy in range(copies.shape[0]):
+            copies[copy, pl.ds(0, rows), lanes] = result
         result = result.astype(f32)
         squares += jnp.sum(result * result, axis=1, keepdims=True)
-    message[pl.ds(rows, 16), :] = below(row_of(squares), feats)
-
-
-def attend(q_in, kv_in, table, swapped):
+    tail = below(row_of(squares), feats)
+    for copy in range(copies.shape[0]):
+        copies[copy, pl.ds(rows, 16), :] = tail
+
+
+def attend(q_in, kv_in, table, swapped, copies):
     rows, feats = swapped.shape[0] - 16, swapped.shape[1]
     heads, tokens = feats // HD, table.shape[0]
-    shape = swapped.shape
+    shape = (copies, rows + 16, feats)
     return pl.pallas_call(
         attend_kernel,
         grid=(1,),
@@ -361,7 +364,7 @@
     )(q_in, kv_in, table, swapped)
 
 
-def attn_left_kernel(scale, own_rows, gain, kv, out):
+def attn_left_kernel(scale, own_rows, gain, kv, after, out):
     blocks, rows, feats = own_rows.shape
     for k in range(blocks):
         parts = kv[2 * k, pl.ds(rows, 16), :].astype(f32)
@@ -370,18 +373,18 @@
         out[:, pl.ds(k * rows, rows)] = (turned * (r * r * scale)).astype(bf16)
 
 
-def attn_left(scale, own_rows, gain, kv_all):
+def attn_left(scale, own_rows, gain, kv_all, after):
     blocks, rows, feats = own_rows.shape
     arrays = (own_rows, gain, kv_all)
     return pl.pallas_call(
         functools.partial(attn_left_kernel, scale),
         grid=(1,),
-        in_specs=[fixed(a.shape) for a in arrays],
+        in_specs=[fixed(a.shape) for a in arrays] + [pl.BlockSpec(memory_space=pl.ANY)],
         out_specs=fixed((feats, blocks * rows)),
         out_shape=jax.ShapeDtypeStruct((feats, blocks * rows), bf16),
         compiler_params=params(),
         name="attn_left",
-    )(*arrays)
+    )(*arrays, after)
 
 
 def hessian_kernel(
@@ -489,18 +492,20 @@
     angle = jnp.arange(tokens, dtype=f32)[:, None] * freq[None, :]
     table = jnp.concatenate([jnp.cos(angle), jnp.sin(angle)], 1)
     group = lax.all_gather(swapped, ZL)
+    swapped = pltpu.with_memory_space_constraint(swapped, pltpu.HBM)
     copies, gain_a, gain_f = attn_copies(group, nx)
     attn_rows = lax.all_gather(hidden[0], "seq")
     attn_cols = lax.all_to_all(copies, "x", 0, 0)
 
+    w_query = pltpu.with_memory_space_constraint(w_query, pltpu.HBM)
     message = project(attn_cols, gain_a, w_query, w_key, w_value, attn_rows)
     arrived = lax.all_to_all(lax.all_to_all(message, "x", 0, 0), "seq", 0, 0)
-    kv = lax.all_to_all(kv_sum(width, arrived, swapped, 2 * nx, table, place), ("x", "zb"), 0, 0)
-    message, section_out = attend(arrived, kv, table, swapped)
-    left_a = attn_left(scale, attn_rows, gain_attn, kv)
-
-    out_rows = swap_x_seq(section_out)
-    group = lax.all_gather(message, ZL)
+    kv = lax.all_to_all(kv_sum(width, arrived, swapped, 2 * nx, table), ("x", "zb"), 0, 0)
+    copies, section_out = attend(arrived, kv, table, swapped, nz)
+    left_a = attn_left(scale, attn_rows, gain_attn, kv, place)
+
+    out_rows = pltpu.with_memory_space_constraint(swap_x_seq(section_out), pltpu.HBM)
+    group = lax.all_to_all(copies, ZL, 0, 0)
     copies, message = ffn_copies(group, out_rows, nx, left_a)
     ffn_cols = lax.all_to_all(copies, "x", 0, 0)
     ffn_rows = lax.all_gather(message, "seq")

time: 236 us -> 238 us (level)
  blocking collectives: 127 us -> 106 us
  starting transfers between devices: 58.5 us -> 69.2 us
  waiting for transfers between devices: 26.5 us -> 34.5 us
  Pallas kernels: 19.7 us -> 22.9 us
    all_gather x1 -> x0, blocking collectives: 24.3 us -> none  [on_device(): group = lax.all_gather(message, ZL)]
    all_to_all x0 -> x1, waiting for transfers between devices: none -> 6.76 us  [on_device(): group = lax.all_to_all(copies, ZL, 0, 0)]
    ppermute x1, starting transfers between devices: 12 us -> 17.6 us  [on_device(): lax.ppermute(passed, 'phase', [(p, (p + 1) % count) for p in range(count)])]
    all_to_all x0 -> x1, starting transfers between devices: none -> 5.36 us  [on_device(): group = lax.all_to_all(copies, ZL, 0, 0)]
    all_gather x1, blocking collectives: 20.6 us -> 25.7 us  [on_device(): ffn_rows = lax.all_gather(message, 'seq')]
  transfers between devices with their start and end apart: 6 -> 7, of which waited for: 1 -> 2; matrix products, arithmetic and copies ran while one was open for 1% -> 1% of each run, Pallas kernels for 0% -> 0%
where the time goes in v15:
time: 238 us; the launch traced here: 237 us
  blocking collectives  106 us (45%)
  starting transfers between devices  69.2 us (29%)
  waiting for transfers between devices  34.5 us (14%)
  Pallas kernels  22.9 us (10%)
  local copies, waits for them, and re-layouts  2.41 us (1%)
    all_gather x1, blocking collectives, on_device(): attn_rows = lax.all_gather(hidden[0], 'seq')  28.9 us
    all_to_all x1, waiting for transfers between devices, on_device(): arrived = lax.all_to_all(lax.all_to_all(message, 'x', 0, 0), 'seq', 0, 0)  27.7 us
    all_to_all x1, starting transfers between devices, on_device(): attn_cols = lax.all_to_all(copies, 'x', 0, 0)  26.9 us
    all_gather x1, blocking collectives, on_device(): ffn_rows = lax.all_gather(message, 'seq')  25.7 us
    all_gather x1, blocking collectives, on_device(): group = lax.all_gather(swapped, ZL)  21.8 us
    ppermute x1, starting transfers between devices, on_device(): lax.ppermute(passed, 'phase', [(p, (p + 1) % count) for p in range(count)])  17.6 us
    all_to_all x1, blocking collectives, on_device(): arrived = lax.all_to_all(lax.all_to_all(message, 'x', 0, 0), 'seq', 0, 0)  12.2 us
    all_to_all x1, starting transfers between devices, on_device(): ffn_cols = lax.all_to_all(copies, 'x', 0, 0)  9.88 us
  transfers between devices with their start and end apart: 7, of which 2 were waited for; matrix products, arithmetic and copies ran while one was open for 1% of the time, Pallas kernels for 0%

profile of v15, /device:TPU:1, one launch (start us, length us, event | category | flops | bytes accessed | tf_op | source)
XLA Modules:
  0.0 237.4 jit_solution(8214408192300001259)
XLA Ops:
  0.6 1.6 first_message.1
  2.2 1.6 collective-permute-start
  4.5 21.8 %all-gather = bf16[576,512]{1,0:T(8,128)(2,1)S(1)} all-gather(bf16[144,512]{1,0:T(8,128)(2,1)S(1)} %collective-permute-done.docs.resid), channel_id=2, replica_groups=mesh['phase'=8,'x'=4,'za'=2,'zb'=2,'seq'=4] {'za','zb'}, dimensions={0}, use_global_device_ids=true | all-gather | bytes 737280 | tf_op jit(solution)/shard_map/all_gather | solution.py:494
  26.2 1.8 attn_copies.1
  28.1 26.9 %all-to-all-start = ((bf16[4,4,128,512]{3,2,1,0:T(8,128)(2,1)}), bf16[4,4,128,512]{3,2,1,0:T(8,128)(2,1)S(1)}, u32[]{:S(2)}, u32[]{:S(2)}) async-start(bf16[4,4,128,512]{3,2,1,0:T(8,128)(2,1)} %get-tuple-element.13), calls=%async_computation | async-start | bytes 4194304 | tf_op jit(solution)/shard_map/all_to_all | solution.py:498
  55.0 28.9 %all_gather.18.after.own_rows = bf16[4,128,512]{2,1,0:T(8,128)(2,1)S(1)} all-gather(bf16[1,128,512]{2,1,0:T(8,128)(2,1)S(1)} %copy-done.12), channel_id=1, replica_groups=mesh['phase'=8,'x'=4,'za'=2,'zb'=2,'seq'=4] {'seq'}, dimensions={0}, use_global_device_ids=true | all-gather | bytes 655360 | tf_op jit(solution)/shard_map/all_gather | solution.py:497
  84.0 4.5 %project.1 = bf16[4,656,128]{2,1,0:T(8,128)(2,1)} custom-call(bf16[4,4,128,512]{3,2,1,0:T(8,128)(2,1)S(1)} %all-to-all-done.cols.cols_a, f32[4,1,512]{2,1,0:T(1,128)S(1)} %copy-done.6, bf16[1,2048,512]{2,1,0:T(8,128)(2,1)} %wq.1, bf16[1,64,2048]{2,1,0:T(8,128)(2,1)S(1)} %bitcast.13, bf16[1,64,2048]{2,1,0:T(8,128)(2,1)S(1)} %bitcast.14, ...), custom_call_target="tpu_custom_call" | custom-call | tf_op jit(solution)/shard_map/project/pallas_call | solution.py:76
  88.5 12.2 %all_to_all.30 = bf16[4,656,128]{2,1,0:T(8,128)(2,1)} all-to-all(bf16[4,656,128]{2,1,0:T(8,128)(2,1)} %project.1), channel_id=1, replica_groups=mesh['phase'=8,'x'=4,'za'=2,'zb'=2,'seq'=4] {'x'}, dimensions={0} | all-to-all | bytes 1343488 | tf_op jit(solution)/shard_map/all_to_all | solution.py:502
  100.7 6.3 %all-to-all-start.2 = ((bf16[4,656,128]{2,1,0:T(8,128)(2,1)}), bf16[4,656,128]{2,1,0:T(8,128)(2,1)S(1)}, u32[]{:S(2)}, u32[]{:S(2)}) async-start(bf16[4,656,128]{2,1,0:T(8,128)(2,1)} %all_to_all.30), calls=%async_computation.2 | async-start | bytes 1343488 | tf_op jit(solution)/shard_map/all_to_all | solution.py:502
  107.1 1.0 fusion.1
  108.2 27.7 %all-to-all-done.2.arrived.q_in = bf16[4,656,128]{2,1,0:T(8,128)(2,1)S(1)} async-done(((bf16[4,656,128]{2,1,0:T(8,128)(2,1)}), bf16[4,656,128]{2,1,0:T(8,128)(2,1)S(1)}, u32[]{:S(2)}, u32[]{:S(2)}) %all-to-all-start.2) | async-done | bytes 671776 | tf_op jit(solution)/shard_map/all_to_all | solution.py:502
  136.0 1.5 kv_sum.1
  137.4 9.8 %all_to_all.31.kv.kv_in = bf16[8,144,128]{2,1,0:T(8,128)(2,1)S(1)} all-to-all(bf16[8,144,128]{2,1,0:T(8,128)(2,1)} %kv_sum.1), channel_id=1, replica_groups=mesh['phase'=8,'x'=4,'za'=2,'zb'=2,'seq'=4] {'x','zb'}, dimensions={0} | all-to-all | bytes 589824 | tf_op jit(solution)/shard_map/all_to_all | solution.py:503
  147.3 4.2 %attend.1 = (bf16[4,144,512]{2,1,0:T(8,128)(2,1)}, bf16[128,512]{1,0:T(8,128)(2,1)}) custom-call(bf16[4,656,128]{2,1,0:T(8,128)(2,1)S(1)} %all-to-all-done.2.arrived.q_in, bf16[8,144,128]{2,1,0:T(8,128)(2,1)S(1)} %all_to_all.31.kv.kv_in, f32[512,128]{1,0:T(8,128)S(1)} %pad_maximum_fusion.table, bf16[144,512]{1,0:T(8,128)(2,1)} %copy-done.11), custom_call_target="tpu_custom_call" | custom-call | tf_op jit(solution)/shard_map/attend/pallas_call | solution.py:345
  151.5 5.4 %all-to-all-start.4 = ((bf16[4,144,512]{2,1,0:T(8,128)(2,1)}), bf16[4,144,512]{2,1,0:T(8,128)(2,1)}, u32[]{:S(2)}, u32[]{:S(2)}) async-start(bf16[4,144,512]{2,1,0:T(8,128)(2,1)} %get-tuple-element.15), calls=%async_computation.4 | async-start | bytes 1179648 | tf_op jit(solution)/shard_map/all_to_all | solution.py:508
  156.8 1.6 collective-permute-start.1
  158.4 1.0 copy-done.3
  160.5 6.8 %all-to-all-done.4.group = bf16[4,144,512]{2,1,0:T(8,128)(2,1)} async-done(((bf16[4,144,512]{2,1,0:T(8,128)(2,1)}), bf16[4,144,512]{2,1,0:T(8,128)(2,1)}, u32[]{:S(2)}, u32[]{:S(2)}) %all-to-all-start.4) | async-done | bytes 589856 | tf_op jit(solution)/shard_map/all_to_all | solution.py:508
  167.2 3.6 %ffn_copies.1 = (bf16[4,4,128,512]{3,2,1,0:T(8,128)(2,1)}, bf16[144,512]{1,0:T(8,128)(2,1)}) custom-call(bf16[4,144,512]{2,1,0:T(8,128)(2,1)} %all-to-all-done.4.group, bf16[128,512]{1,0:T(8,128)(2,1)} %copy-done.14, bf16[512,512]{1,0:T(8,128)(2,1)S(1)} %attn_left.1.after.left_a), custom_call_target="tpu_custom_call" | custom-call | tf_op jit(solution)/shard_map/ffn_copies/pallas_call | solution.py:216
  170.9 9.9 %all-to-all-start.5 = ((bf16[4,4,128,512]{3,2,1,0:T(8,128)(2,1)}), bf16[4,4,128,512]{3,2,1,0:T(8,128)(2,1)}, u32[]{:S(2)}, u32[]{:S(2)}) async-start(bf16[4,4,128,512]{3,2,1,0:T(8,128)(2,1)} %get-tuple-element.18), calls=%async_computation.5 | async-start | bytes 4194304 | tf_op jit(solution)/shard_map/all_to_all | solution.py:510
  180.8 25.7 %all-gather.1 = bf16[576,512]{1,0:T(8,128)(2,1)S(1)} all-gather(bf16[144,512]{1,0:T(8,128)(2,1)S(1)} %copy-done.13), channel_id=3, replica_groups=mesh['phase'=8,'x'=4,'za'=2,'zb'=2,'seq'=4] {'seq'}, dimensions={0}, use_global_device_ids=true | all-gather | bytes 737280 | tf_op jit(solution)/shard_map/all_gather | solution.py:511
  206.6 17.6 %collective-permute-start.2 = (bf16[1,128,512]{2,1,0:T(8,128)(2,1)S(1)}, bf16[1,128,512]{2,1,0:T(8,128)(2,1)S(1)}, u32[]{:S(2)}, u32[]{:S(2)}) collective-permute-start(bf16[1,128,512]{2,1,0:T(8,128)(2,1)S(1)} %constant_dynamic-slice_fusion), channel_id=1, source_target_pairs={{0,64},{64,128},{128,192},{192,256},{256,320},{320,384},{384,448},... | collective-permute-start | bytes 393224 | tf_op jit(solution)/shard_map/ppermute | solution.py:516
  224.1 7.9 %all-gather.3.total = f32[4,1,128]{2,1,0:T(1,128)S(1)} all-gather(f32[1,1,128]{2,1,0:T(1,128)S(1)} %bitcast.16), channel_id=4, replica_groups=mesh['phase'=8,'x'=4,'za'=2,'zb'=2,'seq'=4] {'x'}, dimensions={0}, use_global_device_ids=true | all-gather | bytes 2560 | tf_op jit(solution)/shard_map/all_gather | solution.py:513
  232.1 5.3 %hessian.1 = (bf16[512,2048]{1,0:T(8,128)(2,1)}, f32[1,128]{1,0:T(1,128)}, bf16[1,128,512]{2,1,0:T(8,128)(2,1)}) custom-call(s32[2]{0:T(128)S(1)} %pad_add_fusion.after.place, bf16[512,512]{1,0:T(8,128)(2,1)S(1)} %copy-done.1, bf16[4,4,128,512]{3,2,1,0:T(8,128)(2,1)S(1)} %all-to-all-done.cols.cols_a, f32[4,1,512]{2,1,0:T(1,128)S(1)} %copy-done.7, ...), custom_call_target="tpu_custom_call" | custom-call | tf_op jit(solution)/shard_map/hessian/pallas_call | solution.py:444
  (41 shorter events, 2.1 us)
Async XLA Ops:
  2.2 1.6 collective-permute-start
  3.8 0.7 copy-start.11
  28.1 26.9 %copy-start.12 = (bf16[1,128,512]{2,1,0:T(8,128)(2,1)S(1)}, bf16[1,128,512]{2,1,0:T(8,128)(2,1)}, u32[]{:S(2)}) copy-start(bf16[1,128,512]{2,1,0:T(8,128)(2,1)} %param.7) | copy-start | bytes 393220
  28.1 55.9 %copy-start.4 = (bf16[1,2048,64]{1,2,0:T(8,128)(2,1)S(1)}, bf16[1,2048,64]{1,2,0:T(8,128)(2,1)}, u32[]{:S(2)}) copy-start(bf16[1,2048,64]{1,2,0:T(8,128)(2,1)} %param.12) | copy-start | bytes 786436
  28.1 55.9 %copy-start.5 = (bf16[1,2048,64]{1,2,0:T(8,128)(2,1)S(1)}, bf16[1,2048,64]{1,2,0:T(8,128)(2,1)}, u32[]{:S(2)}) copy-start(bf16[1,2048,64]{1,2,0:T(8,128)(2,1)} %param.13) | copy-start | bytes 786436
  28.1 55.9 %copy-start.6 = (f32[4,1,512]{2,1,0:T(1,128)S(1)}, f32[4,1,512]{2,1,0:T(1,128)}, u32[]{:S(2)}) copy-start(f32[4,1,512]{2,1,0:T(1,128)} %get-tuple-element.14.gain.gain_a) | copy-start | bytes 24580
  28.1 55.8 %all-to-all-start = ((bf16[4,4,128,512]{3,2,1,0:T(8,128)(2,1)}), bf16[4,4,128,512]{3,2,1,0:T(8,128)(2,1)S(1)}, u32[]{:S(2)}, u32[]{:S(2)}) async-start(bf16[4,4,128,512]{3,2,1,0:T(8,128)(2,1)} %get-tuple-element.13), calls=%async_computation | async-start | bytes 4194304 | tf_op jit(solution)/shard_map/all_to_all | solution.py:498
  100.7 35.2 %all-to-all-start.2 = ((bf16[4,656,128]{2,1,0:T(8,128)(2,1)}), bf16[4,656,128]{2,1,0:T(8,128)(2,1)S(1)}, u32[]{:S(2)}, u32[]{:S(2)}) async-start(bf16[4,656,128]{2,1,0:T(8,128)(2,1)} %all_to_all.30), calls=%async_computation.2 | async-start | bytes 1343488 | tf_op jit(solution)/shard_map/all_to_all | solution.py:502
  147.3 4.2 %copy-start.2 = (bf16[8,144,128]{2,1,0:T(8,128)(2,1)}, bf16[8,144,128]{2,1,0:T(8,128)(2,1)S(1)}, u32[]{:S(2)}) copy-start(bf16[8,144,128]{2,1,0:T(8,128)(2,1)S(1)} %all_to_all.31.kv.kv_in) | copy-start | bytes 884740
  151.5 15.8 %all-to-all-start.4 = ((bf16[4,144,512]{2,1,0:T(8,128)(2,1)}), bf16[4,144,512]{2,1,0:T(8,128)(2,1)}, u32[]{:S(2)}, u32[]{:S(2)}) async-start(bf16[4,144,512]{2,1,0:T(8,128)(2,1)} %get-tuple-element.15), calls=%async_computation.4 | async-start | bytes 1179648 | tf_op jit(solution)/shard_map/all_to_all | solution.py:508
  156.8 3.6 %collective-permute-start.1 = (bf16[128,512]{1,0:T(8,128)(2,1)}, bf16[128,512]{1,0:T(8,128)(2,1)S(1)}, u32[]{:S(2)}, u32[]{:S(2)}) collective-permute-start(bf16[128,512]{1,0:T(8,128)(2,1)} %get-tuple-element.16), channel_id=1, source_target_pairs={{0,0},{1,16},{2,32},{3,48},{4,4},{5,20},{6,36},{7,52},{8,8},{9,24}... | collective-permute-start | bytes 393224 | tf_op jit(solution)/shard_map/ppermute | solution.py:31
  158.4 1.0 copy-start.3
  159.4 0.7 copy-start.10
  160.4 10.5 %copy-start = (bf16[512,512]{1,0:T(8,128)(2,1)}, bf16[512,512]{1,0:T(8,128)(2,1)S(1)}, u32[]{:S(2)}) copy-start(bf16[512,512]{1,0:T(8,128)(2,1)S(1)} %attn_left.1.after.left_a) | copy-start | bytes 1572868
  160.5 6.8 %copy-start.14 = (bf16[128,512]{1,0:T(8,128)(2,1)}, bf16[128,512]{1,0:T(8,128)(2,1)S(1)}, u32[]{:S(2)}) copy-start(bf16[128,512]{1,0:T(8,128)(2,1)S(1)} %collective-permute-done.1.own) | copy-start | bytes 393220
  170.9 9.9 %copy-start.13 = (bf16[144,512]{1,0:T(8,128)(2,1)S(1)}, bf16[144,512]{1,0:T(8,128)(2,1)}, u32[]{:S(2)}) copy-start(bf16[144,512]{1,0:T(8,128)(2,1)} %get-tuple-element.17) | copy-start | bytes 442372
  170.9 61.1 %copy-start.7 = (f32[4,1,512]{2,1,0:T(1,128)S(1)}, f32[4,1,512]{2,1,0:T(1,128)}, u32[]{:S(2)}) copy-start(f32[4,1,512]{2,1,0:T(1,128)} %get-tuple-element.14.gain.gain_a) | copy-start | bytes 24580
  170.9 61.1 %copy-start.8 = (bf16[1,512]{1,0:T(2,128)(2,1)S(1)}, bf16[1,512]{1,0:T(2,128)(2,1)}, u32[]{:S(2)}) copy-start(bf16[1,512]{1,0:T(2,128)(2,1)} %gain_row.1) | copy-start | bytes 3076
  170.9 61.1 %copy-start.9 = (f32[4,1,512]{2,1,0:T(1,128)S(1)}, f32[4,1,512]{2,1,0:T(1,128)}, u32[]{:S(2)}) copy-start(f32[4,1,512]{2,1,0:T(1,128)} %get-tuple-element.19.gain_f) | copy-start | bytes 24580
  170.9 61.1 %all-to-all-start.5 = ((bf16[4,4,128,512]{3,2,1,0:T(8,128)(2,1)}), bf16[4,4,128,512]{3,2,1,0:T(8,128)(2,1)}, u32[]{:S(2)}, u32[]{:S(2)}) async-start(bf16[4,4,128,512]{3,2,1,0:T(8,128)(2,1)} %get-tuple-element.18), calls=%async_computation.5 | async-start | bytes 4194304 | tf_op jit(solution)/shard_map/all_to_all | solution.py:510
  180.8 51.3 %copy-start.1 = (bf16[512,512]{1,0:T(8,128)(2,1)S(1)}, bf16[512,512]{1,0:T(8,128)(2,1)}, u32[]{:S(2)}) copy-start(bf16[512,512]{1,0:T(8,128)(2,1)} %copy-done) | copy-start | bytes 1572868
  206.6 25.5 %collective-permute-start.2 = (bf16[1,128,512]{2,1,0:T(8,128)(2,1)S(1)}, bf16[1,128,512]{2,1,0:T(8,128)(2,1)S(1)}, u32[]{:S(2)}, u32[]{:S(2)}) collective-permute-start(bf16[1,128,512]{2,1,0:T(8,128)(2,1)S(1)} %constant_dynamic-slice_fusion), channel_id=1, source_target_pairs={{0,64},{64,128},{128,192},{192,256},{256,320},{320,384},{384,448},... | collective-permute-start | bytes 393224 | tf_op jit(solution)/shard_map/ppermute | solution.py:516

commit v16 on v14

--- a/solution.py
+++ b/solution.py
@@ -287,7 +287,7 @@
     return high, (value - high.astype(f32)).astype(bf16)
 
 
-def attend_kernel(q_in, kv_in, table, resid, message, out, keys, values, r_all, docs_all):
+def attend_kernel(q_in, kv_in, table, resid, copies, out, keys, values, r_all, docs_all):
     rows, feats = out.shape
     heads = feats // HD
     tokens = keys.shape[0]
@@ -329,16 +329,19 @@
         lanes = pl.ds(h * HD, HD)
         result = (resid[:, lanes].astype(f32) + context).astype(bf16)
         out[:, lanes] = result
-        message[pl.ds(0, rows), lanes] = result
+        for copy in range(copies.shape[0]):
+            copies[copy, pl.ds(0, rows), lanes] = result
         result = result.astype(f32)
         squares += jnp.sum(result * result, axis=1, keepdims=True)
-    message[pl.ds(rows, 16), :] = below(row_of(squares), feats)
-
-
-def attend(q_in, kv_in, table, swapped):
+    tail = below(row_of(squares), feats)
+    for copy in range(copies.shape[0]):
+        copies[copy, pl.ds(rows, 16), :] = tail
+
+
+def attend(q_in, kv_in, table, swapped, copies):
     rows, feats = swapped.shape[0] - 16, swapped.shape[1]
     heads, tokens = feats // HD, table.shape[0]
-    shape = swapped.shape
+    shape = (copies, rows + 16, feats)
     return pl.pallas_call(
         attend_kernel,
         grid=(1,),
@@ -496,11 +499,11 @@
     message = project(attn_cols, gain_a, w_query, w_key, w_value, attn_rows)
     arrived = lax.all_to_all(lax.all_to_all(message, "x", 0, 0), "seq", 0, 0)
     kv = lax.all_to_all(kv_sum(width, arrived, swapped, 2 * nx, table, place), ("x", "zb"), 0, 0)
-    message, section_out = attend(arrived, kv, table, swapped)
+    copies, section_out = attend(arrived, kv, table, swapped, nz)
     left_a = attn_left(scale, attn_rows, gain_attn, kv)
 
     out_rows = swap_x_seq(section_out)
-    group = lax.all_gather(message, ZL)
+    group = lax.all_to_all(copies, ZL, 0, 0)
     copies, message = ffn_copies(group, out_rows, nx, left_a)
     ffn_cols = lax.all_to_all(copies, "x", 0, 0)
     ffn_rows = lax.all_gather(message, "seq")

time: 236 us -> 231 us (0.979)
  blocking collectives: 127 us -> 97.6 us
  waiting for transfers between devices: 26.5 us -> 38.6 us
  starting transfers between devices: 58.5 us -> 70.1 us
    all_gather x1 -> x0, blocking collectives: 24.3 us -> none  [on_device(): group = lax.all_gather(message, ZL)]
    all_to_all x0 -> x1, waiting for transfers between devices: none -> 12.1 us  [on_device(): group = lax.all_to_all(copies, ZL, 0, 0)]
    ppermute x1, starting transfers between devices: 12 us -> 20.2 us  [on_device(): lax.ppermute(passed, 'phase', [(p, (p + 1) % count) for p in range(count)])]
    all_to_all x0 -> x1, starting transfers between devices: none -> 8.08 us  [on_device(): group = lax.all_to_all(copies, ZL, 0, 0)]
    all_gather x1, blocking collectives: 20.6 us -> 15.6 us  [on_device(): ffn_rows = lax.all_gather(message, 'seq')]
    all_to_all x1, starting transfers between devices: 10.7 us -> 6.06 us  [on_device(): ffn_cols = lax.all_to_all(copies, 'x', 0, 0)]
  transfers between devices with their start and end apart: 6 -> 7, of which waited for: 1 -> 2; matrix products, arithmetic and copies ran while one was open for 1% -> 1% of each run, Pallas kernels for 0% -> 0%
where the time goes in v16:
time: 231 us; the launch traced here: 230 us
  blocking collectives  97.6 us (42%)
  starting transfers between devices  70.1 us (30%)
  waiting for transfers between devices  38.6 us (17%)
  Pallas kernels  19.9 us (9%)
    all_gather x1, blocking collectives, on_device(): attn_rows = lax.all_gather(hidden[0], 'seq')  28.8 us
    all_to_all x1, waiting for transfers between devices, on_device(): arrived = lax.all_to_all(lax.all_to_all(message, 'x', 0, 0), 'seq', 0, 0)  26.4 us
    all_to_all x1, starting transfers between devices, on_device(): attn_cols = lax.all_to_all(copies, 'x', 0, 0)  26.2 us
    all_gather x1, blocking collectives, on_device(): group = lax.all_gather(swapped, ZL)  22.5 us
    ppermute x1, starting transfers between devices, on_device(): lax.ppermute(passed, 'phase', [(p, (p + 1) % count) for p in range(count)])  20.2 us
    all_gather x1, blocking collectives, on_device(): ffn_rows = lax.all_gather(message, 'seq')  15.6 us
    all_to_all x1, waiting for transfers between devices, on_device(): group = lax.all_to_all(copies, ZL, 0, 0)  12.1 us
    all_to_all x1, blocking collectives, on_device(): arrived = lax.all_to_all(lax.all_to_all(message, 'x', 0, 0), 'seq', 0, 0)  12 us
  transfers between devices with their start and end apart: 7, of which 2 were waited for; matrix products, arithmetic and copies ran while one was open for 1% of the time, Pallas kernels for 0%

profile of v16, /device:TPU:1, one launch (start us, length us, event | category | flops | bytes accessed | tf_op | source)
XLA Modules:
  0.0 229.6 jit_solution(18207132810464763849)
XLA Ops:
  0.6 1.6 first_message.1
  2.2 1.6 collective-permute-start
  3.8 22.5 %all-gather = bf16[576,512]{1,0:T(8,128)(2,1)S(1)} all-gather(bf16[144,512]{1,0:T(8,128)(2,1)S(1)} %collective-permute-done.docs.resid), channel_id=2, replica_groups=mesh['phase'=8,'x'=4,'za'=2,'zb'=2,'seq'=4] {'za','zb'}, dimensions={0}, use_global_device_ids=true | all-gather | bytes 737280 | tf_op jit(solution)/shard_map/all_gather | solution.py:494
  26.3 1.8 attn_copies.1
  28.1 26.2 %all-to-all-start = ((bf16[4,4,128,512]{3,2,1,0:T(8,128)(2,1)}), bf16[4,4,128,512]{3,2,1,0:T(8,128)(2,1)S(1)}, u32[]{:S(2)}, u32[]{:S(2)}) async-start(bf16[4,4,128,512]{3,2,1,0:T(8,128)(2,1)} %get-tuple-element.13), calls=%async_computation | async-start | bytes 4194304 | tf_op jit(solution)/shard_map/all_to_all | solution.py:497
  54.4 28.8 %all_gather.18.after.own_rows = bf16[4,128,512]{2,1,0:T(8,128)(2,1)} all-gather(bf16[1,128,512]{2,1,0:T(8,128)(2,1)S(1)} %copy-done.7), channel_id=1, replica_groups=mesh['phase'=8,'x'=4,'za'=2,'zb'=2,'seq'=4] {'seq'}, dimensions={0}, use_global_device_ids=true | all-gather | bytes 655360 | tf_op jit(solution)/shard_map/all_gather | solution.py:496
  83.2 1.3 copy-done
  84.5 4.9 %project.1 = bf16[4,656,128]{2,1,0:T(8,128)(2,1)} custom-call(bf16[4,4,128,512]{3,2,1,0:T(8,128)(2,1)} %copy-done, f32[4,1,512]{2,1,0:T(1,128)} %get-tuple-element.14.gain.gain_a, bf16[1,2048,512]{2,1,0:T(8,128)(2,1)} %wq.1, bf16[1,64,2048]{2,1,0:T(8,128)(2,1)} %bitcast.14, bf16[1,64,2048]{2,1,0:T(8,128)(2,1)} %bitcast.15, ...), custom_call_target="tpu_custom_call" | custom-call | tf_op jit(solution)/shard_map/project/pallas_call | solution.py:76
  89.4 12.0 %all_to_all.30 = bf16[4,656,128]{2,1,0:T(8,128)(2,1)} all-to-all(bf16[4,656,128]{2,1,0:T(8,128)(2,1)} %project.1), channel_id=1, replica_groups=mesh['phase'=8,'x'=4,'za'=2,'zb'=2,'seq'=4] {'x'}, dimensions={0} | all-to-all | bytes 1343488 | tf_op jit(solution)/shard_map/all_to_all | solution.py:500
  101.4 6.5 %all-to-all-start.2 = ((bf16[4,656,128]{2,1,0:T(8,128)(2,1)}), bf16[4,656,128]{2,1,0:T(8,128)(2,1)S(1)}, u32[]{:S(2)}, u32[]{:S(2)}) async-start(bf16[4,656,128]{2,1,0:T(8,128)(2,1)} %all_to_all.30), calls=%async_computation.2 | async-start | bytes 1343488 | tf_op jit(solution)/shard_map/all_to_all | solution.py:500
  107.9 1.0 fusion.1
  109.1 26.4 %all-to-all-done.2.arrived.q_in = bf16[4,656,128]{2,1,0:T(8,128)(2,1)S(1)} async-done(((bf16[4,656,128]{2,1,0:T(8,128)(2,1)}), bf16[4,656,128]{2,1,0:T(8,128)(2,1)S(1)}, u32[]{:S(2)}, u32[]{:S(2)}) %all-to-all-start.2) | async-done | bytes 671776 | tf_op jit(solution)/shard_map/all_to_all | solution.py:500
  135.5 0.8 kv_sum.1
  136.2 10.5 %all_to_all.31.kv.kv_in = bf16[8,144,128]{2,1,0:T(8,128)(2,1)S(1)} all-to-all(bf16[8,144,128]{2,1,0:T(8,128)(2,1)} %kv_sum.1), channel_id=1, replica_groups=mesh['phase'=8,'x'=4,'za'=2,'zb'=2,'seq'=4] {'x','zb'}, dimensions={0} | all-to-all | bytes 589824 | tf_op jit(solution)/shard_map/all_to_all | solution.py:501
  146.7 3.2 %attend.1 = (bf16[4,144,512]{2,1,0:T(8,128)(2,1)}, bf16[128,512]{1,0:T(8,128)(2,1)}) custom-call(bf16[4,656,128]{2,1,0:T(8,128)(2,1)S(1)} %all-to-all-done.2.arrived.q_in, bf16[8,144,128]{2,1,0:T(8,128)(2,1)S(1)} %all_to_all.31.kv.kv_in, f32[512,128]{1,0:T(8,128)S(1)} %pad_maximum_fusion.table, bf16[144,512]{1,0:T(8,128)(2,1)S(1)} %collective-permute-done.docs.resid), custom_call_target="tpu_custom_call" | custom-call | tf_op jit(solution)/shard_map/attend/pallas_call | solution.py:345
  149.9 8.1 %all-to-all-start.4 = ((bf16[4,144,512]{2,1,0:T(8,128)(2,1)}), bf16[4,144,512]{2,1,0:T(8,128)(2,1)S(1)}, u32[]{:S(2)}, u32[]{:S(2)}) async-start(bf16[4,144,512]{2,1,0:T(8,128)(2,1)} %get-tuple-element.15), calls=%async_computation.4 | async-start | bytes 1179648 | tf_op jit(solution)/shard_map/all_to_all | solution.py:506
  158.0 1.6 collective-permute-start.1
  159.9 12.1 %all-to-all-done.4.group = bf16[4,144,512]{2,1,0:T(8,128)(2,1)S(1)} async-done(((bf16[4,144,512]{2,1,0:T(8,128)(2,1)}), bf16[4,144,512]{2,1,0:T(8,128)(2,1)S(1)}, u32[]{:S(2)}, u32[]{:S(2)}) %all-to-all-start.4) | async-done | bytes 589856 | tf_op jit(solution)/shard_map/all_to_all | solution.py:506
  172.0 2.0 ffn_copies.1
  174.1 6.1 %all-to-all-start.5 = ((bf16[4,4,128,512]{3,2,1,0:T(8,128)(2,1)}), bf16[4,4,128,512]{3,2,1,0:T(8,128)(2,1)}, u32[]{:S(2)}, u32[]{:S(2)}) async-start(bf16[4,4,128,512]{3,2,1,0:T(8,128)(2,1)} %get-tuple-element.18), calls=%async_computation.5 | async-start | bytes 4194304 | tf_op jit(solution)/shard_map/all_to_all | solution.py:508
  180.1 15.6 %all-gather.1 = bf16[576,512]{1,0:T(8,128)(2,1)S(1)} all-gather(bf16[144,512]{1,0:T(8,128)(2,1)S(1)} %copy-done.8), channel_id=3, replica_groups=mesh['phase'=8,'x'=4,'za'=2,'zb'=2,'seq'=4] {'seq'}, dimensions={0}, use_global_device_ids=true | all-gather | bytes 737280 | tf_op jit(solution)/shard_map/all_gather | solution.py:509
  195.8 20.2 %collective-permute-start.2 = (bf16[1,128,512]{2,1,0:T(8,128)(2,1)S(1)}, bf16[1,128,512]{2,1,0:T(8,128)(2,1)S(1)}, u32[]{:S(2)}, u32[]{:S(2)}) collective-permute-start(bf16[1,128,512]{2,1,0:T(8,128)(2,1)S(1)} %constant_dynamic-slice_fusion), channel_id=1, source_target_pairs={{0,64},{64,128},{128,192},{192,256},{256,320},{320,384},{384,448},... | collective-permute-start | bytes 393224 | tf_op jit(solution)/shard_map/ppermute | solution.py:514
  216.0 8.2 %all-gather.3.total = f32[4,1,128]{2,1,0:T(1,128)S(1)} all-gather(f32[1,1,128]{2,1,0:T(1,128)S(1)} %bitcast.16), channel_id=4, replica_groups=mesh['phase'=8,'x'=4,'za'=2,'zb'=2,'seq'=4] {'x'}, dimensions={0}, use_global_device_ids=true | all-gather | bytes 2560 | tf_op jit(solution)/shard_map/all_gather | solution.py:511
  224.3 5.3 %hessian.1 = (bf16[512,2048]{1,0:T(8,128)(2,1)}, f32[1,128]{1,0:T(1,128)}, bf16[1,128,512]{2,1,0:T(8,128)(2,1)}) custom-call(s32[2]{0:T(128)S(1)} %pad_add_fusion.place, bf16[512,512]{1,0:T(8,128)(2,1)S(1)} %attn_left.1.after.left_a, bf16[4,4,128,512]{3,2,1,0:T(8,128)(2,1)S(1)} %copy-done.1, f32[4,1,512]{2,1,0:T(1,128)S(1)} %copy-done.3, ...), custom_call_target="tpu_custom_call" | custom-call | tf_op jit(solution)/shard_map/hessian/pallas_call | solution.py:444
  (29 shorter events, 0.7 us)
Async XLA Ops:
  2.2 1.6 collective-permute-start
  28.1 26.2 %copy-start.7 = (bf16[1,128,512]{2,1,0:T(8,128)(2,1)S(1)}, bf16[1,128,512]{2,1,0:T(8,128)(2,1)}, u32[]{:S(2)}) copy-start(bf16[1,128,512]{2,1,0:T(8,128)(2,1)} %param.7) | copy-start | bytes 393220
  28.1 55.1 %all-to-all-start = ((bf16[4,4,128,512]{3,2,1,0:T(8,128)(2,1)}), bf16[4,4,128,512]{3,2,1,0:T(8,128)(2,1)S(1)}, u32[]{:S(2)}, u32[]{:S(2)}) async-start(bf16[4,4,128,512]{3,2,1,0:T(8,128)(2,1)} %get-tuple-element.13), calls=%async_computation | async-start | bytes 4194304 | tf_op jit(solution)/shard_map/all_to_all | solution.py:497
  83.2 1.3 copy-start
  101.4 34.1 %all-to-all-start.2 = ((bf16[4,656,128]{2,1,0:T(8,128)(2,1)}), bf16[4,656,128]{2,1,0:T(8,128)(2,1)S(1)}, u32[]{:S(2)}, u32[]{:S(2)}) async-start(bf16[4,656,128]{2,1,0:T(8,128)(2,1)} %all_to_all.30), calls=%async_computation.2 | async-start | bytes 1343488 | tf_op jit(solution)/shard_map/all_to_all | solution.py:500
  109.0 50.5 %copy-start.2 = (bf16[4,128,512]{2,1,0:T(8,128)(2,1)S(1)}, bf16[4,128,512]{2,1,0:T(8,128)(2,1)}, u32[]{:S(2)}) copy-start(bf16[4,128,512]{2,1,0:T(8,128)(2,1)} %all_gather.18.after.own_rows) | copy-start | bytes 1572868
  109.1 50.5 %copy-start.6 = (bf16[1,512]{1,0:T(2,128)(2,1)S(1)}, bf16[1,512]{1,0:T(2,128)(2,1)}, u32[]{:S(2)}) copy-start(bf16[1,512]{1,0:T(2,128)(2,1)} %gain.1) | copy-start | bytes 3076
  149.9 22.1 %all-to-all-start.4 = ((bf16[4,144,512]{2,1,0:T(8,128)(2,1)}), bf16[4,144,512]{2,1,0:T(8,128)(2,1)S(1)}, u32[]{:S(2)}, u32[]{:S(2)}) async-start(bf16[4,144,512]{2,1,0:T(8,128)(2,1)} %get-tuple-element.15), calls=%async_computation.4 | async-start | bytes 1179648 | tf_op jit(solution)/shard_map/all_to_all | solution.py:506
  158.0 1.9 collective-permute-start.1
  174.0 6.1 %copy-start.8 = (bf16[144,512]{1,0:T(8,128)(2,1)S(1)}, bf16[144,512]{1,0:T(8,128)(2,1)}, u32[]{:S(2)}) copy-start(bf16[144,512]{1,0:T(8,128)(2,1)} %get-tuple-element.17) | copy-start | bytes 442372
  174.0 50.2 %copy-start.1 = (bf16[4,4,128,512]{3,2,1,0:T(8,128)(2,1)S(1)}, bf16[4,4,128,512]{3,2,1,0:T(8,128)(2,1)}, u32[]{:S(2)}) copy-start(bf16[4,4,128,512]{3,2,1,0:T(8,128)(2,1)} %copy-done) | copy-start | bytes 6291460
  174.0 50.2 %copy-start.3 = (f32[4,1,512]{2,1,0:T(1,128)S(1)}, f32[4,1,512]{2,1,0:T(1,128)}, u32[]{:S(2)}) copy-start(f32[4,1,512]{2,1,0:T(1,128)} %get-tuple-element.14.gain.gain_a) | copy-start | bytes 24580
  174.0 50.2 %copy-start.4 = (bf16[1,512]{1,0:T(2,128)(2,1)S(1)}, bf16[1,512]{1,0:T(2,128)(2,1)}, u32[]{:S(2)}) copy-start(bf16[1,512]{1,0:T(2,128)(2,1)} %gain_row.1) | copy-start | bytes 3076
  174.0 50.2 %copy-start.5 = (f32[4,1,512]{2,1,0:T(1,128)S(1)}, f32[4,1,512]{2,1,0:T(1,128)}, u32[]{:S(2)}) copy-start(f32[4,1,512]{2,1,0:T(1,128)} %get-tuple-element.19.gain_f) | copy-start | bytes 24580
  174.1 50.2 %all-to-all-start.5 = ((bf16[4,4,128,512]{3,2,1,0:T(8,128)(2,1)}), bf16[4,4,128,512]{3,2,1,0:T(8,128)(2,1)}, u32[]{:S(2)}, u32[]{:S(2)}) async-start(bf16[4,4,128,512]{3,2,1,0:T(8,128)(2,1)} %get-tuple-element.18), calls=%async_computation.5 | async-start | bytes 4194304 | tf_op jit(solution)/shard_map/all_to_all | solution.py:508
  195.8 28.4 %collective-permute-start.2 = (bf16[1,128,512]{2,1,0:T(8,128)(2,1)S(1)}, bf16[1,128,512]{2,1,0:T(8,128)(2,1)S(1)}, u32[]{:S(2)}, u32[]{:S(2)}) collective-permute-start(bf16[1,128,512]{2,1,0:T(8,128)(2,1)S(1)} %constant_dynamic-slice_fusion), channel_id=1, source_target_pairs={{0,64},{64,128},{128,192},{192,256},{256,320},{320,384},{384,448},... | collective-permute-start | bytes 393224 | tf_op jit(solution)/shard_map/ppermute | solution.py:514
